TPU v7x, 32 devices: a whole 2x2x4 slice. The times are simulated.
32 devices in a mesh: dp: 16 (over z, y, x), feat: 2 (over core).
Axes of the slice: x: 2, y: 2, z: 4, core: 2. Of those that a mesh axis runs over, the one named last changes fastest.
Arguments:
- grads: bfloat16 [2, 8192, 4, 128], P('feat', 'dp'), may hold values from -6 to 6
- block_ids: int32 [2, 8192, 4], P('feat', 'dp'), may hold values from 0 to 511, all different within a row; in each aligned block of 512 rows (0 to 511, 512 to 1023, ..., all dimensions but the last counted through in order) at most 6 rows name the same one
- probe: bfloat16 [512, 2, 128, 512], P('dp', 'feat'), may hold values from -0.1875 to 0.1875
Outputs:
- whitened: float32 [8192, 512], P(('dp', 'feat'))
Inputs may be any that keep to these rules, and one draw needn't show every extreme that they name: block_ids[j, s, k] is a local block number in slice j; the ids of one sample in one slice are distinct; among the 512 samples of one index of dp, no number appears more than 6 times in one slice, and some number appears exactly 6 times.
All inputs are finite; a program needn't handle non-finite values.
Results may differ from a plain program's by a relative error of at most 0.012.
Values may be sent and summed in bfloat16 or wider, within the bound.
No kernel may reach another device: no remote copies, remote signals or barrier semaphores. Data moves between devices by JAX's collectives and lax.ppermute only.
A program may use at most 128 MiB of HBM per device.

v0:
```python
import math

import jax
import jax.numpy as jnp
from jax import lax
from jax.sharding import PartitionSpec as P

ridge = 0.1
root_steps = 4


def shifted(value, axis, steps):
    count = lax.axis_size(axis)
    pairs = [(source, (source + steps) % count) for source in range(count)]
    return lax.ppermute(value, axis, pairs)


def gram_of(rows):
    return lax.dot_general(rows, rows, (((0,), (0,)), ((), ())), preferred_element_type=jnp.float32)


def inverse_root(gram):
    width = gram.shape[0]
    ident = jnp.eye(width, dtype=jnp.float32)
    scale = jnp.trace(gram) / width
    current = gram / scale
    result = ident
    for step in range(root_steps):
        middle = 1.5 * ident - 0.5 * jnp.dot(result, current, precision=lax.Precision.HIGHEST)
        if step + 1 < root_steps:
            current = jnp.dot(current, middle, precision=lax.Precision.HIGHEST)
        result = jnp.dot(middle, result, precision=lax.Precision.HIGHEST)
    return result / jnp.sqrt(scale)


def local(grads, block_ids, probe):
    values = grads[0]
    ids = block_ids[0]
    s_dev, k_j, b_width = values.shape
    n_dp = lax.axis_size("dp")
    n_feat = lax.axis_size("feat")
    per_dev = probe.shape[0]
    width = probe.shape[3]
    b_slice = per_dev * n_dp
    bound = max(2, 3 * s_dev * k_j // (2 * b_slice))
    slots = per_dev * bound
    flat_ids = ids.reshape(-1)
    target = flat_ids // per_dev
    within = flat_ids % per_dev
    onehot = (target[:, None] == jnp.arange(n_dp, dtype=jnp.int32)[None, :]).astype(jnp.int32)
    rank_in = jnp.sum((jnp.cumsum(onehot, axis=0) - onehot) * onehot, axis=1)
    position = target * slots + rank_in
    send_tiles = (
        jnp.zeros((n_dp * slots, b_width), jnp.bfloat16)
        .at[position]
        .set(values.reshape(-1, b_width))
    )
    send_which = jnp.full((n_dp * slots,), per_dev, jnp.int32).at[position].set(within)
    send_tiles = send_tiles.reshape(n_dp, slots, b_width)
    send_which = send_which.reshape(n_dp, slots)
    local_probe = probe[:, 0].reshape(per_dev * b_width, width)
    tiles = lax.all_to_all(send_tiles, "dp", split_axis=0, concat_axis=0, tiled=True)
    which = lax.all_to_all(send_which, "dp", split_axis=0, concat_axis=0, tiled=True)
    pick = (which[..., None] == jnp.arange(per_dev, dtype=jnp.int32)).astype(jnp.bfloat16)
    spread = (pick[..., None] * tiles[..., None, :]).reshape(
        tiles.shape[0], tiles.shape[1], per_dev * b_width
    )
    product = jnp.einsum("ncf,fr->ncr", spread, local_probe, preferred_element_type=jnp.float32)
    returned = lax.all_to_all(
        product.astype(jnp.bfloat16), "dp", split_axis=0, concat_axis=0, tiled=True
    )
    per_tile = returned.reshape(n_dp * slots, width)[position]
    partial_value = jnp.sum(per_tile.reshape(s_dev, k_j, width).astype(jnp.float32), axis=1)
    own_rows = s_dev // n_feat
    summed = lax.psum(partial_value, "feat")
    sketch = summed.astype(jnp.bfloat16)
    gram = gram_of(sketch)
    mine = lax.dynamic_slice_in_dim(sketch, lax.axis_index("feat") * own_rows, own_rows, 0)
    gram = gram + ridge * s_dev * jnp.eye(width, dtype=jnp.float32)
    levels = n_dp.bit_length() - 1
    total = gram
    for level in range(levels):
        total = total + shifted(total, "dp", -(1 << level))
    root = inverse_root(total)
    samples = s_dev * n_dp
    return math.sqrt(samples) * jnp.dot(
        mine.astype(jnp.float32), root, precision=lax.Precision.HIGHEST
    )


def solution(mesh):
    return jax.shard_map(
        local,
        mesh=mesh,
        in_specs=(P("feat", "dp", None, None), P("feat", "dp", None), P("dp", "feat", None, None)),
        out_specs=P(("dp", "feat"), None),
        check_vma=False,
    )
```

profile of v0, /device:TPU:0, one launch (start us, length us, event | category | flops | bytes accessed | tf_op | source)
XLA Modules:
  0.0 376.2 jit_solution(12673517842278320416)
XLA Ops:
  1.4 4.5 %reduce-window.6 = s32[16,16,128]{2,1,0:T(8,128)S(1)} reduce-window(s32[16,16,128]{2,1,0:T(8,128)S(1)} %fusion.9, s32[]{:T(128)} %constant.52.clone.1), window={size=1x1x128 pad=0_0x0_0x127_0}, to_apply=%region_0.1 | reduce-window | flops 4161536 | bytes 262148 | tf_op jit(solution)/shard_map/reduce-window
  6.8 8.1 %scatter_custom_fusion = s32[3072]{0:T(1024)S(1)} fusion(s32[2048]{0:T(1024)S(1)} %bitcast.58, s32[2048]{0:T(1024)S(1)} %get-tuple-element.7, s32[]{:T(128)} %constant.50.clone.1), kind=kCustom, calls=%fused_computation.55 | custom fusion | bytes 12292 | tf_op jit(solution)/shard_map/scatter | solution.py:58
  15.6 8.3 %all-to-all-start = ((s32[16,1,192]{2,1,0:T(1,128)}), s32[16,1,192]{2,1,0:T(1,128)S(1)}, u32[]{:S(2)}, u32[]{:S(2)}) async-start(s32[16,1,192]{2,1,0:T(1,128)} %all_to_all.12), calls=%async_computation | async-start | bytes 32768 | tf_op jit(solution)/shard_map/all_to_all | solution.py:63
  23.9 7.0 %scatter_custom_fusion.1 = bf16[3072,128]{1,0:T(8,128)(2,1)} fusion(s32[2048]{0:T(1024)S(1)} %bitcast.59, bf16[2048,128]{1,0:T(8,128)(2,1)} %bitcast.63, bf16[]{:T(256)} %constant.58.clone.1), kind=kCustom, calls=%fused_computation.23 | custom fusion | bytes 786944 | tf_op jit(solution)/shard_map/scatter | solution.py:56
  31.2 6.6 %all-to-all-start.1 = ((bf16[16,192,128]{2,1,0:T(8,128)(2,1)}), bf16[16,192,128]{2,1,0:T(8,128)(2,1)S(1)}, u32[]{:S(2)}, u32[]{:S(2)}) async-start(bf16[16,192,128]{2,1,0:T(8,128)(2,1)} %bitcast.4), calls=%async_computation.1 | async-start | bytes 1572864 | tf_op jit(solution)/shard_map/all_to_all | solution.py:62
  38.4 18.6 %all-to-all-done.1 = bf16[16,192,128]{2,1,0:T(8,128)(2,1)S(1)} async-done(((bf16[16,192,128]{2,1,0:T(8,128)(2,1)}), bf16[16,192,128]{2,1,0:T(8,128)(2,1)S(1)}, u32[]{:S(2)}, u32[]{:S(2)}) %all-to-all-start.1) | async-done | bytes 786464 | tf_op jit(solution)/shard_map/all_to_all | solution.py:62
  57.0 15.9 %broadcast_multiply_fusion = bf16[16,192,32,128]{3,2,1,0:T(8,128)(2,1)} fusion(bf16[16,192,128]{2,1,0:T(8,128)(2,1)S(1)} %all-to-all-done.1, bf16[16,192,32]{2,1,0:T(8,128)(2,1)S(1)} %fusion), kind=kLoop, calls=%fused_computation.3 | loop fusion | flops 12582912 | bytes 26148864 | tf_op jit(solution)/shard_map/mul | solution.py:65
  72.9 37.3 %mul.84 = bf16[16,192,4096]{2,1,0:T(8,128)(2,1)} reshape(bf16[16,192,32,128]{3,2,1,0:T(8,128)(2,1)} %broadcast_multiply_fusion) | data formatting | bytes 50331648 | tf_op jit(solution)/shard_map/mul | solution.py:65
  110.2 20.3 %convolution_convert_fusion = bf16[16,192,512]{2,1,0:T(8,128)(2,1)} fusion(bf16[16,192,4096]{2,1,0:T(8,128)(2,1)} %mul.84, bf16[4096,512,1]{1,0,2:T(8,128)(2,1)} %bitcast.62), kind=kOutput, calls=%fused_computation.4 | convolution fusion | flops 12886474752 | bytes 32505856 | tf_op jit(solution)/shard_map/ncf,fr->ncr/dot_general | solution.py:68
  130.5 4.9 %all-to-all-start.2 = ((bf16[16,192,512]{2,1,0:T(8,128)(2,1)}), bf16[16,192,512]{2,1,0:T(8,128)(2,1)S(1)}, u32[]{:S(2)}, u32[]{:S(2)}) async-start(bf16[16,192,512]{2,1,0:T(8,128)(2,1)} %convolution_convert_fusion), calls=%async_computation.2 | async-start | bytes 6291456 | tf_op jit(solution)/shard_map/all_to_all | solution.py:69
  135.5 60.3 %all-to-all-done.2 = bf16[16,192,512]{2,1,0:T(8,128)(2,1)S(1)} async-done(((bf16[16,192,512]{2,1,0:T(8,128)(2,1)}), bf16[16,192,512]{2,1,0:T(8,128)(2,1)S(1)}, u32[]{:S(2)}, u32[]{:S(2)}) %all-to-all-start.2) | async-done | bytes 3145760 | tf_op jit(solution)/shard_map/all_to_all | solution.py:69
  195.8 9.2 %gather_fusion = bf16[2048,512]{1,0:T(8,128)(2,1)} fusion(bf16[3072,512]{1,0:T(8,128)(2,1)S(1)} %bitcast.54, s32[2048]{0:T(1024)S(1)} %broadcast_clamp_fusion), kind=kCustom, calls=%fused_computation | custom fusion | bytes 4202496 | tf_op jit(solution)/shard_map/gather | solution.py:72
  204.9 4.8 %reshape.154 = f32[512,4,512]{2,1,0:T(4,128)} reshape(bf16[2048,512]{1,0:T(8,128)(2,1)} %gather_fusion) | data formatting | bytes 6291456 | tf_op jit(solution)/shard_map/convert_element_type | solution.py:73
  209.7 4.7 %reduce_sum.32 = f32[512,512]{1,0:T(8,128)S(1)} reduce(f32[512,4,512]{2,1,0:T(4,128)} %reshape.154, f32[]{:T(128)} %constant.59.clone.1), dimensions={1}, to_apply=%region_5.6 | reduce | flops 786432 | bytes 5242884 | tf_op jit(solution)/shard_map/reduce_sum | solution.py:73
  214.4 6.3 %all-reduce.1 = bf16[512,512]{1,0:T(8,128)(2,1)S(1)} all-reduce(f32[512,512]{1,0:T(8,128)S(1)} %reduce_sum.32), channel_id=1, replica_groups=mesh['dp'=16,'feat'=2] {'feat'}, use_global_device_ids=true, to_apply=%region_6.7 | all-reduce | flops 262144 | bytes 1572864 | tf_op jit(solution)/shard_map/psum | solution.py:75
  221.1 12.5 %collective-permute-start = (f32[512,512]{1,0:T(8,128)S(1)}, f32[512,512]{1,0:T(8,128)S(1)}, u32[]{:S(2)}, u32[]{:S(2)}) collective-permute-start(f32[512,512]{1,0:T(8,128)S(1)} %convolution_add_fusion), channel_id=1, source_target_pairs={{0,30},{2,0},{4,2},{6,4},{8,6},{10,8},{12,10},{14,12},{16,14},{18,... | collective-permute-start | bytes 3145736 | tf_op jit(solution)/shard_map/ppermute | solution.py:15
  233.6 22.9 %collective-permute-done = f32[512,512]{1,0:T(8,128)S(1)} collective-permute-done((f32[512,512]{1,0:T(8,128)S(1)}, f32[512,512]{1,0:T(8,128)S(1)}, u32[]{:S(2)}, u32[]{:S(2)}) %collective-permute-start) | collective-permute-done | bytes 1048608 | tf_op jit(solution)/shard_map/ppermute | solution.py:15
  256.8 2.5 collective-permute-start.1
  259.3 22.1 %collective-permute-done.1 = f32[512,512]{1,0:T(8,128)S(1)} collective-permute-done((f32[512,512]{1,0:T(8,128)S(1)}, f32[512,512]{1,0:T(8,128)S(1)}, u32[]{:S(2)}, u32[]{:S(2)}) %collective-permute-start.1) | collective-permute-done | bytes 1048608 | tf_op jit(solution)/shard_map/ppermute | solution.py:15
  283.0 22.4 %collective-permute-done.2 = f32[512,512]{1,0:T(8,128)S(1)} collective-permute-done((f32[512,512]{1,0:T(8,128)S(1)}, f32[512,512]{1,0:T(8,128)S(1)}, u32[]{:S(2)}, u32[]{:S(2)}) %collective-permute-start.2) | collective-permute-done | bytes 1048608 | tf_op jit(solution)/shard_map/ppermute | solution.py:15
  307.4 44.5 %collective-permute-done.3 = f32[512,512]{1,0:T(8,128)S(1)} collective-permute-done((f32[512,512]{1,0:T(8,128)S(1)}, f32[512,512]{1,0:T(8,128)S(1)}, u32[]{:S(2)}, u32[]{:S(2)}) %collective-permute-start.3) | collective-permute-done | bytes 1048608 | tf_op jit(solution)/shard_map/ppermute | solution.py:15
  351.9 1.8 select_reduce_fusion
  354.4 2.3 select_subtract_fusion.3
  356.7 1.9 fusion.2
  359.6 1.9 select_subtract_fusion.2
  361.5 1.8 fusion.18
  363.3 1.8 fusion.17
  365.2 1.8 select_subtract_fusion.1
  367.0 2.1 fusion.20
  369.1 1.8 fusion.19
  371.0 1.9 select_subtract_fusion
  372.9 1.8 convolution_divide_fusion
  (27 shorter events, 10.4 us)
Async XLA Ops:
  15.6 15.7 %all-to-all-start = ((s32[16,1,192]{2,1,0:T(1,128)}), s32[16,1,192]{2,1,0:T(1,128)S(1)}, u32[]{:S(2)}, u32[]{:S(2)}) async-start(s32[16,1,192]{2,1,0:T(1,128)} %all_to_all.12), calls=%async_computation | async-start | bytes 32768 | tf_op jit(solution)/shard_map/all_to_all | solution.py:63
  31.2 25.8 %all-to-all-start.1 = ((bf16[16,192,128]{2,1,0:T(8,128)(2,1)}), bf16[16,192,128]{2,1,0:T(8,128)(2,1)S(1)}, u32[]{:S(2)}, u32[]{:S(2)}) async-start(bf16[16,192,128]{2,1,0:T(8,128)(2,1)} %bitcast.4), calls=%async_computation.1 | async-start | bytes 1572864 | tf_op jit(solution)/shard_map/all_to_all | solution.py:62
  130.5 65.2 %all-to-all-start.2 = ((bf16[16,192,512]{2,1,0:T(8,128)(2,1)}), bf16[16,192,512]{2,1,0:T(8,128)(2,1)S(1)}, u32[]{:S(2)}, u32[]{:S(2)}) async-start(bf16[16,192,512]{2,1,0:T(8,128)(2,1)} %convolution_convert_fusion), calls=%async_computation.2 | async-start | bytes 6291456 | tf_op jit(solution)/shard_map/all_to_all | solution.py:69
  221.1 35.4 %collective-permute-start = (f32[512,512]{1,0:T(8,128)S(1)}, f32[512,512]{1,0:T(8,128)S(1)}, u32[]{:S(2)}, u32[]{:S(2)}) collective-permute-start(f32[512,512]{1,0:T(8,128)S(1)} %convolution_add_fusion), channel_id=1, source_target_pairs={{0,30},{2,0},{4,2},{6,4},{8,6},{10,8},{12,10},{14,12},{16,14},{18,... | collective-permute-start | bytes 3145736 | tf_op jit(solution)/shard_map/ppermute | solution.py:15
  256.8 24.7 %collective-permute-start.1 = (f32[512,512]{1,0:T(8,128)S(1)}, f32[512,512]{1,0:T(8,128)S(1)}, u32[]{:S(2)}, u32[]{:S(2)}) collective-permute-start(f32[512,512]{1,0:T(8,128)S(1)} %add.65), channel_id=1, source_target_pairs={{0,28},{2,30},{4,0},{6,2},{8,4},{10,6},{12,8},{14,10},{16,12},{18,... | collective-permute-start | bytes 3145736 | tf_op jit(solution)/shard_map/ppermute | solution.py:15
  281.7 23.8 %collective-permute-start.2 = (f32[512,512]{1,0:T(8,128)S(1)}, f32[512,512]{1,0:T(8,128)S(1)}, u32[]{:S(2)}, u32[]{:S(2)}) collective-permute-start(f32[512,512]{1,0:T(8,128)S(1)} %add.66), channel_id=1, source_target_pairs={{0,24},{2,26},{4,28},{6,30},{8,0},{10,2},{12,4},{14,6},{16,8},{18,... | collective-permute-start | bytes 3145736 | tf_op jit(solution)/shard_map/ppermute | solution.py:15
  305.6 46.2 %collective-permute-start.3 = (f32[512,512]{1,0:T(8,128)S(1)}, f32[512,512]{1,0:T(8,128)S(1)}, u32[]{:S(2)}, u32[]{:S(2)}) collective-permute-start(f32[512,512]{1,0:T(8,128)S(1)} %add.67), channel_id=1, source_target_pairs={{0,16},{2,18},{4,20},{6,22},{8,24},{10,26},{12,28},{14,30},{16,0},... | collective-permute-start | bytes 3145736 | tf_op jit(solution)/shard_map/ppermute | solution.py:15
  353.7 3.1 copy-start
where the time goes:
time: 381 us; the launch traced here: 376 us
  waiting for transfers between devices  191 us (50%)
  local copies, waits for them, and re-layouts  68.8 us (18%)
  matrix products  42.5 us (11%)
  starting transfers between devices  37.9 us (10%)
  other arithmetic  28.5 us (7%)
  blocking collectives  6.27 us (2%)
    ppermute x4, waiting for transfers between devices, shifted(): return lax.ppermute(value, axis, pairs)  112 us
    all_to_all x1, waiting for transfers between devices, local(): lax.all_to_all(product.astype(jnp.bfloat16), 'dp', split_axis=0, concat_a...  60.3 us
    mul x1, local copies, waits for them, and re-layouts, local(): pick[..., None] * tiles[..., None, :]  37.3 us
    dot_general x1, matrix products, local(): jnp.einsum('ncf,fr->ncr', spread, local_probe, preferred_element_type=jnp...  20.3 us
    all_to_all x1, waiting for transfers between devices, local(): lax.all_to_all(send_tiles, 'dp', split_axis=0, concat_axis=0, tiled=True)  18.6 us
    ppermute x4, starting transfers between devices, shifted(): return lax.ppermute(value, axis, pairs)  18.1 us
    mul x1, other arithmetic, local(): pick[..., None] * tiles[..., None, :]  15.9 us
    gather x1, local copies, waits for them, and re-layouts, local(): per_tile = returned.reshape(n_dp * slots, width)[position]  9.17 us
  transfers between devices with their start and end apart: 7, of which 7 were waited for; matrix products, arithmetic and copies ran while one was open for 2% of the time, Pallas kernels for 0%

commit v1 on v0

v1 whole, which is shorter than its diff:
```python
import functools
import math

import jax
import jax.numpy as jnp
import numpy as np
from jax import lax
from jax.experimental import pallas as pl
from jax.experimental.pallas import tpu as pltpu
from jax.sharding import PartitionSpec as P

ridge = 0.1
root_steps = 4
f32 = jnp.float32
bf16 = jnp.bfloat16
lane = 128
vmem_limit = 48 << 20

COLS = (((0,), (0,)), ((), ()))


def params(**kw):
    return pltpu.CompilerParams(vmem_limit_bytes=vmem_limit, **kw)


def whole():
    return pl.BlockSpec(memory_space=pltpu.VMEM)


def pack_kernel(per_dev, bound, direct, ids_ref, values_ref, send_ref, position_ref):
    k_j, s_dev = ids_ref.shape
    n_ids = send_ref.shape[0] * per_dev if direct else send_ref.shape[1]
    width = lane
    ids_rows = ids_ref[...]
    padded = jnp.concatenate([ids_rows.astype(f32), jnp.zeros((lane - k_j, s_dev), f32)], axis=0)
    ids_cols = jnp.transpose(padded)
    numbers = lax.broadcasted_iota(jnp.int32, (s_dev, n_ids), 1).astype(f32)
    number_rows = lax.broadcasted_iota(jnp.int32, (n_ids, s_dev), 0)
    earlier = (
        lax.broadcasted_iota(jnp.int32, (s_dev, s_dev), 0) > lax.broadcasted_iota(jnp.int32, (s_dev, s_dev), 1)
    )
    earlier = jnp.where(earlier, 1.0, 0.0).astype(bf16)
    used = jnp.zeros((1, n_ids), f32)
    total = jnp.zeros((n_ids, bound * width), f32)
    places = []
    for k in range(k_j):
        column = ids_cols[:, k : k + 1]
        named = jnp.where(column == numbers, 1.0, 0.0)
        before = jnp.dot(earlier, named.astype(bf16), preferred_element_type=f32) + used
        rank = jnp.sum(named * before, axis=1, keepdims=True)
        used = used + jnp.sum(named, axis=0, keepdims=True)
        tile = values_ref[:, k * width : (k + 1) * width].astype(f32)
        by_rank = jnp.concatenate([jnp.where(rank == r, tile, 0.0).astype(bf16) for r in range(bound)], axis=1)
        named_rows = jnp.where(ids_rows[k : k + 1, :] == number_rows, 1.0, 0.0).astype(bf16)
        total = total + jnp.dot(named_rows, by_rank, preferred_element_type=f32)
        id_col = column.astype(jnp.int32)
        target = id_col // per_dev
        within = id_col - target * per_dev
        places.append((target * bound + rank.astype(jnp.int32)) * per_dev + within)
    position_ref[...] = jnp.concatenate(places, axis=1)
    for r in range(bound):
        rows = total[:, r * width : (r + 1) * width].astype(bf16)
        if direct:
            send_ref[:, r * per_dev : (r + 1) * per_dev, :] = rows.reshape(n_ids // per_dev, per_dev, width)
        else:
            send_ref[r] = rows


def pack(ids, values, n_dp, per_dev, bound):
    k_j, s_dev = ids.shape
    direct = per_dev % 16 == 0
    shape = (n_dp, bound * per_dev, lane) if direct else (bound, n_dp * per_dev, lane)
    send, position = pl.pallas_call(
        functools.partial(pack_kernel, per_dev, bound, direct),
        out_shape=(
            jax.ShapeDtypeStruct(shape, bf16),
            jax.ShapeDtypeStruct((s_dev, k_j), jnp.int32),
        ),
        in_specs=[whole(), whole()],
        out_specs=(whole(), whole()),
        compiler_params=params(),
        name="pack",
    )(ids, values)
    if not direct:
        send = send.reshape(bound, n_dp, per_dev, lane).transpose(1, 0, 2, 3).reshape(n_dp, bound * per_dev, lane)
    return send, position


def product_kernel(per_dev, per_step, tiles_ref, probe_ref, out_ref, tiles, products):
    step = pl.program_id(0)
    count = tiles.shape[0] // per_dev

    @pl.when(step == 0)
    def _():
        tiles[...] = tiles_ref[...].astype(f32)

    for at in range(per_step):
        block = step * per_step + at
        rows = pl.ds(block, count, stride=per_dev)
        value = jnp.dot(tiles[rows, :].astype(bf16), probe_ref[at], preferred_element_type=f32)
        for c in range(products.shape[0]):
            products[c, rows, :] = value[:, c * lane : (c + 1) * lane]

    @pl.when(step == pl.num_programs(0) - 1)
    def _():
        for c in range(products.shape[0]):
            out_ref[:, c * lane : (c + 1) * lane] = products[c].astype(bf16)


def product(tiles, probe):
    rows = tiles.shape[0]
    per_dev, _, width = probe.shape
    per_step = math.gcd(per_dev, 4)
    return pl.pallas_call(
        functools.partial(product_kernel, per_dev, per_step),
        out_shape=jax.ShapeDtypeStruct((rows, width), bf16),
        grid=(per_dev // per_step,),
        in_specs=[
            pl.BlockSpec((rows, lane), lambda i: (0, 0)),
            pl.BlockSpec((per_step, lane, width), lambda i: (i, 0, 0)),
        ],
        out_specs=pl.BlockSpec((rows, width), lambda i: (0, 0)),
        scratch_shapes=[pltpu.VMEM((rows, lane), f32), pltpu.VMEM((width // lane, rows, lane), f32)],
        compiler_params=params(),
        name="product",
    )(tiles, probe)


def combine_kernel(position_ref, rows_ref, out_ref):
    step = pl.program_id(0)
    s_dev, k_j = position_ref.shape
    count = rows_ref.shape[0]
    here = lax.broadcasted_iota(jnp.int32, (s_dev, count), 1) + step * count
    position = position_ref[...]
    hit = position[:, 0:1] == here
    for k in range(1, k_j):
        hit = jnp.logical_or(hit, position[:, k : k + 1] == here)
    part = jnp.dot(jnp.where(hit, 1.0, 0.0).astype(bf16), rows_ref[...], preferred_element_type=f32)

    @pl.when(step == 0)
    def _():
        out_ref[...] = part

    @pl.when(step > 0)
    def _():
        out_ref[...] += part


def combine(position, rows):
    s_dev, k_j = position.shape
    total, width = rows.shape
    count = total // 6 if total % (6 * lane) == 0 else total
    return pl.pallas_call(
        combine_kernel,
        out_shape=jax.ShapeDtypeStruct((s_dev, width), f32),
        grid=(total // count,),
        in_specs=[
            pl.BlockSpec((s_dev, k_j), lambda i: (0, 0)),
            pl.BlockSpec((count, width), lambda i: (i, 0)),
        ],
        out_specs=pl.BlockSpec((s_dev, width), lambda i: (0, 0)),
        compiler_params=params(),
        name="combine",
    )(position, rows)


def block_pairs(width):
    n = width // lane
    return [(i, j) for i in range(n) for j in range(i, n)]


def gram_kernel(own_rows, pairs_ref, place_ref, sum_a_ref, sum_b_ref, gram_ref, mine_ref, sketch):
    sketch[...] = (sum_a_ref[...] + sum_b_ref[...]).astype(bf16)
    start = pl.multiple_of(place_ref[0] * own_rows, own_rows)
    mine_ref[...] = sketch[pl.ds(start, own_rows), :]
    for at in range(gram_ref.shape[0]):
        left = sketch[:, pl.ds(pl.multiple_of(pairs_ref[2 * at] * lane, lane), lane)]
        right = sketch[:, pl.ds(pl.multiple_of(pairs_ref[2 * at + 1] * lane, lane), lane)]
        gram_ref[at] = lax.dot_general(left, right, COLS, preferred_element_type=f32)


def gram_blocks(sum_a, sum_b, place, n_feat):
    s_dev, width = sum_a.shape
    pairs = block_pairs(width)
    half = len(pairs) // 2
    table = jnp.asarray(np.array(pairs, np.int32).reshape(2, 2 * half))
    own_rows = s_dev // n_feat
    smem = pl.BlockSpec(memory_space=pltpu.SMEM)
    return pl.pallas_call(
        functools.partial(gram_kernel, own_rows),
        out_shape=(
            jax.ShapeDtypeStruct((half, lane, lane), f32),
            jax.ShapeDtypeStruct((own_rows, width), bf16),
        ),
        in_specs=[smem, smem, whole(), whole()],
        out_specs=(whole(), whole()),
        scratch_shapes=[pltpu.VMEM((s_dev, width), bf16)],
        compiler_params=params(),
        name="gram",
    )(table[place % 2], place.reshape(1), sum_a, sum_b)


def halves(value):
    high = value.astype(bf16)
    return high, (value - high.astype(f32)).astype(bf16)


def dot3(a, b):
    (ah, al), (bh, bl) = a, b
    out = jnp.dot(ah, bl, preferred_element_type=f32)
    if al is not None:
        out = out + jnp.dot(al, bh, preferred_element_type=f32)
    return out + jnp.dot(ah, bh, preferred_element_type=f32)


def root_kernel(samples, place_ref, mine_gram_ref, other_gram_ref, mine_ref, out_ref, gram):
    width = mine_ref.shape[1]
    pairs = block_pairs(width)
    half = len(pairs) // 2
    odd = place_ref[0] % 2 == 1
    for at, (i, j) in enumerate(pairs):
        mine, other = mine_gram_ref[at % half], other_gram_ref[at % half]
        block = jnp.where(odd, other, mine) if at < half else jnp.where(odd, mine, other)
        gram[i * lane : (i + 1) * lane, j * lane : (j + 1) * lane] = block
        if i != j:
            gram[j * lane : (j + 1) * lane, i * lane : (i + 1) * lane] = jnp.transpose(block)
    rows = lax.broadcasted_iota(jnp.int32, (width, width), 0)
    ident = jnp.where(rows == lax.broadcasted_iota(jnp.int32, (width, width), 1), 1.0, 0.0)
    total = gram[...] + ridge * samples * ident
    scale = jnp.sum(total * ident, axis=(0, 1), keepdims=True) / width
    current = total / scale
    result = (mine_ref[...], None)
    for step in range(root_steps):
        middle = halves(1.5 * ident - 0.5 * current)
        if step + 1 < root_steps:
            current = dot3(halves(dot3(halves(current), middle)), middle)
        value = dot3(result, middle)
        result = halves(value)
    out_ref[...] = (math.sqrt(samples) * lax.rsqrt(scale)) * value


def whiten(mine_gram, other_gram, mine, place, samples):
    width = mine.shape[1]
    return pl.pallas_call(
        functools.partial(root_kernel, samples),
        out_shape=jax.ShapeDtypeStruct(mine.shape, f32),
        in_specs=[pl.BlockSpec(memory_space=pltpu.SMEM), whole(), whole(), whole()],
        out_specs=whole(),
        scratch_shapes=[pltpu.VMEM((width, width), f32)],
        compiler_params=params(),
        name="root",
    )(place.reshape(1), mine_gram, other_gram, mine)


def crossed(value, axis, bits):
    count = lax.axis_size(axis)
    return lax.ppermute(value, axis, [(source, source ^ bits) for source in range(count)])


def sum_over_dp(value):
    n_dp = lax.axis_size("dp")
    index = lax.axis_index("dp")
    inner = math.gcd(n_dp, 4)
    flat = value.reshape(-1, lane)
    rows = flat.shape[0] // inner
    me = index % inner
    part = lax.dynamic_slice_in_dim(flat, me * rows, rows, 0)
    arrived = [
        crossed(lax.dynamic_slice_in_dim(flat, (me ^ bits) * rows, rows, 0), "dp", bits) for bits in range(1, inner)
    ]
    for other in arrived:
        part = part + other
    if n_dp // inner == 4:
        arrived = [crossed(part, "dp", bits * inner) for bits in range(1, 4)]
        for other in arrived:
            part = part + other
    else:
        bits = inner
        while bits < n_dp:
            part = part + crossed(part, "dp", bits)
            bits *= 2
    pieces = [part] + [crossed(part, "dp", bits) for bits in range(1, inner)]
    stacked = jnp.stack(pieces)
    ordered = [stacked[me ^ at] for at in range(inner)]
    return jnp.concatenate(ordered, axis=0).reshape(value.shape)


def local(grads, block_ids, probe):
    values = grads[0]
    s_dev, k_j, b_width = values.shape
    n_dp = lax.axis_size("dp")
    n_feat = lax.axis_size("feat")
    per_dev = probe.shape[0]
    width = probe.shape[3]
    b_slice = per_dev * n_dp
    bound = max(2, 3 * s_dev * k_j // (2 * b_slice))
    place = lax.axis_index("feat")
    send, position = pack(block_ids[0].T, values.reshape(s_dev, k_j * b_width), n_dp, per_dev, bound)
    tiles = lax.all_to_all(send, "dp", split_axis=0, concat_axis=0, tiled=True)
    products = product(tiles.reshape(-1, b_width), probe[:, 0])
    returned = lax.all_to_all(
        products.reshape(n_dp, -1, width), "dp", split_axis=0, concat_axis=0, tiled=True
    )
    part = combine(position, returned.reshape(-1, width))
    bits = n_feat // 2
    while bits > 1:
        part = part + crossed(part, "feat", bits)
        bits //= 2
    mine_gram, mine = gram_blocks(part, crossed(part, "feat", 1), place, n_feat)
    mine_gram = sum_over_dp(mine_gram)
    other_gram = crossed(mine_gram, "feat", 1)
    return whiten(mine_gram, other_gram, mine, place, s_dev * n_dp)


def solution(mesh):
    return jax.shard_map(
        local,
        mesh=mesh,
        in_specs=(P("feat", "dp", None, None), P("feat", "dp", None), P("dp", "feat", None, None)),
        out_specs=P(("dp", "feat"), None),
        check_vma=False,
    )
```

time: 381 us -> 164 us (0.43); the launches traced: 376 us -> 163 us
  waiting for transfers between devices: 191 us -> 17 us
  blocking collectives: 6.27 us -> 103 us
  local copies, waits for them, and re-layouts: 68.8 us -> 1.89 us
  matrix products: 42.5 us -> 0 us
  Pallas kernels: 0 us -> 29 us
  other arithmetic: 28.5 us -> 0.08 us
  starting transfers between devices: 37.9 us -> 11.7 us
    all_to_all x0 -> x2, blocking collectives: none -> 103 us  [the longest x1 74 us: local(): lax.all_to_all(products.reshape(n_dp, -1, width), 'dp', split_axis=0, con...]
    ppermute x4 -> x11, waiting for transfers between devices: 112 us -> 17 us  [crossed(): lax.ppermute(value, axis, [(source, source ^ bits) for source in range(co...]
    all_to_all x3 -> x0, waiting for transfers between devices: 79.2 us -> none  [the longest x1 60.3 us: local(): lax.all_to_all(product.astype(jnp.bfloat16), 'dp', split_axis=0, concat_a...]
    dot_general x14 -> x0, matrix products: 42.5 us -> none  [the longest x1 20.3 us: local(): jnp.einsum('ncf,fr->ncr', spread, local_probe, preferred_element_type=jnp...]
    mul x1 -> x0, local copies, waits for them, and re-layouts: 37.3 us -> none  [local(): pick[..., None] * tiles[..., None, :]]
    pallas_call x0 -> x5, Pallas kernels: none -> 29 us  [the longest x1 10 us: product(): pl.pallas_call(functools.partial(product_kernel, per_dev, per_step), out_...]
    all_to_all x3 -> x0, starting transfers between devices: 19.8 us -> none  [the longest x1 8.31 us: local(): lax.all_to_all(send_which, 'dp', split_axis=0, concat_axis=0, tiled=True)]
    mul x1 -> x0, other arithmetic: 15.9 us -> none  [local(): pick[..., None] * tiles[..., None, :]]
  transfers between devices with their start and end apart: 7 -> 11, of which waited for: 7 -> 9; matrix products, arithmetic and copies ran while one was open for 2% -> 0% of each run, Pallas kernels for 0% -> 0%
where the time goes in v1:
time: 164 us; the launch traced here: 163 us
  blocking collectives  103 us (63%)
  Pallas kernels  29 us (18%)
  waiting for transfers between devices  17 us (10%)
  starting transfers between devices  11.7 us (7%)
  local copies, waits for them, and re-layouts  1.89 us (1%)
    all_to_all x1, blocking collectives, local(): lax.all_to_all(products.reshape(n_dp, -1, width), 'dp', split_axis=0, con...  74 us
    all_to_all x1, blocking collectives, local(): tiles = lax.all_to_all(send, 'dp', split_axis=0, concat_axis=0, tiled=True)  29.4 us
    ppermute x11, waiting for transfers between devices, crossed(): lax.ppermute(value, axis, [(source, source ^ bits) for source in range(co...  17 us
    ppermute x11, starting transfers between devices, crossed(): lax.ppermute(value, axis, [(source, source ^ bits) for source in range(co...  11.7 us
    pallas_call x1, Pallas kernels, product(): pl.pallas_call(functools.partial(product_kernel, per_dev, per_step), out_...  10 us
    pallas_call x1, Pallas kernels, whiten(): pl.pallas_call(functools.partial(root_kernel, samples), out_shape=jax.Sha...  8 us
    pallas_call x1, Pallas kernels, combine(): pl.pallas_call(combine_kernel, out_shape=jax.ShapeDtypeStruct((s_dev, wid...  5.64 us
    pallas_call x1, Pallas kernels, pack(): pl.pallas_call(functools.partial(pack_kernel, per_dev, bound, direct), ou...  4.34 us
  transfers between devices with their start and end apart: 11, of which 9 were waited for; matrix products, arithmetic and copies ran while one was open for 0% of the time, Pallas kernels for 0%

profile of v1, /device:TPU:0, one launch (start us, length us, event | category | flops | bytes accessed | tf_op | source)
XLA Modules:
  0.0 163.3 jit_solution(14766102647329898603)
XLA Ops:
  0.0 1.1 copy.7
  1.1 0.0 copy-start
  1.1 0.7 copy-done
  1.8 4.3 %pack.1 = (bf16[16,192,128]{2,1,0:T(8,128)(2,1)S(1)}, s32[512,4]{1,0:T(8,128)S(1)}) custom-call(s32[4,512]{1,0:T(4,128)S(1)} %bitcast.37, bf16[512,512]{1,0:T(8,128)(2,1)S(1)} %bitcast.32), custom_call_target="tpu_custom_call" | custom-call | tf_op jit(solution)/shard_map/pack/pallas_call | solution.py:73
  6.2 29.4 %all_to_all.10 = bf16[16,192,128]{2,1,0:T(8,128)(2,1)S(1)} all-to-all(bf16[16,192,128]{2,1,0:T(8,128)(2,1)S(1)} %get-tuple-element.10), channel_id=1, replica_groups=mesh['dp'=16,'feat'=2] {'dp'}, dimensions={0} | all-to-all | bytes 1572864 | tf_op jit(solution)/shard_map/all_to_all | solution.py:299
  35.6 10.0 %product.1 = bf16[3072,512]{1,0:T(8,128)(2,1)S(1)} custom-call(bf16[3072,128]{1,0:T(8,128)(2,1)S(1)} %bitcast.31, bf16[32,128,512]{2,1,0:T(8,128)(2,1)} %bitcast.38), custom_call_target="tpu_custom_call" | custom-call | tf_op jit(solution)/shard_map/product/pallas_call | solution.py:114
  45.6 74.0 %all_to_all.11 = bf16[16,192,512]{2,1,0:T(8,128)(2,1)S(1)} all-to-all(bf16[16,192,512]{2,1,0:T(8,128)(2,1)S(1)} %bitcast.30), channel_id=1, replica_groups=mesh['dp'=16,'feat'=2] {'dp'}, dimensions={0} | all-to-all | bytes 6291456 | tf_op jit(solution)/shard_map/all_to_all | solution.py:301
  119.6 5.6 %combine.1.sum_a_ref = f32[512,512]{1,0:T(8,128)S(1)} custom-call(s32[512,4]{1,0:T(8,128)S(1)} %get-tuple-element.9.position_ref, bf16[3072,512]{1,0:T(8,128)(2,1)S(1)} %bitcast.29), custom_call_target="tpu_custom_call" | custom-call | tf_op jit(solution)/shard_map/combine/pallas_call | solution.py:153
  125.3 0.1 collective-permute-start
  125.4 2.6 %collective-permute-done.sum_b_ref = f32[512,512]{1,0:T(8,128)S(1)} collective-permute-done((f32[512,512]{1,0:T(8,128)S(1)}, f32[512,512]{1,0:T(8,128)S(1)}, u32[]{:S(2)}, u32[]{:S(2)}) %collective-permute-start) | collective-permute-done | bytes 1048608 | tf_op jit(solution)/shard_map/ppermute | solution.py:257
  128.0 1.0 gram.1
  129.1 1.0 collective-permute-start.3
  130.0 1.1 collective-permute-start.2
  131.1 1.5 collective-permute-start.1
  132.6 2.7 %collective-permute-done.3 = f32[160,128]{1,0:T(8,128)S(1)} collective-permute-done((f32[160,128]{1,0:T(8,128)S(1)}, f32[160,128]{1,0:T(8,128)S(1)}, u32[]{:S(2)}, u32[]{:S(2)}) %collective-permute-start.3) | collective-permute-done | bytes 81952 | tf_op jit(solution)/shard_map/ppermute | solution.py:257
  135.3 0.7 collective-permute-done.2
  136.0 0.0 collective-permute-done.1
  136.0 2.2 %collective-permute-start.6 = (f32[160,128]{1,0:T(8,128)S(1)}, f32[160,128]{1,0:T(8,128)S(1)}, u32[]{:S(2)}, u32[]{:S(2)}) collective-permute-start(f32[160,128]{1,0:T(8,128)S(1)} %add_add_fusion.1), channel_id=1, source_target_pairs={{0,24},{2,26},{4,28},{6,30},{8,16},{10,18},{12,20},{14,22},{16,8},... | collective-permute-start | bytes 245768 | tf_op jit(solution)/shard_map/ppermute | solution.py:257
  138.2 0.6 collective-permute-start.5
  138.8 1.7 %collective-permute-start.4 = (f32[160,128]{1,0:T(8,128)S(1)}, f32[160,128]{1,0:T(8,128)S(1)}, u32[]{:S(2)}, u32[]{:S(2)}) collective-permute-start(f32[160,128]{1,0:T(8,128)S(1)} %add_add_fusion.1), channel_id=1, source_target_pairs={{0,8},{2,10},{4,12},{6,14},{8,0},{10,2},{12,4},{14,6},{16,24},{18,... | collective-permute-start | bytes 245768 | tf_op jit(solution)/shard_map/ppermute | solution.py:257
  140.5 2.7 %collective-permute-done.6 = f32[160,128]{1,0:T(8,128)S(1)} collective-permute-done((f32[160,128]{1,0:T(8,128)S(1)}, f32[160,128]{1,0:T(8,128)S(1)}, u32[]{:S(2)}, u32[]{:S(2)}) %collective-permute-start.6) | collective-permute-done | bytes 81952 | tf_op jit(solution)/shard_map/ppermute | solution.py:257
  143.2 3.2 %collective-permute-done.5 = f32[160,128]{1,0:T(8,128)S(1)} collective-permute-done((f32[160,128]{1,0:T(8,128)S(1)}, f32[160,128]{1,0:T(8,128)S(1)}, u32[]{:S(2)}, u32[]{:S(2)}) %collective-permute-start.5) | collective-permute-done | bytes 81952 | tf_op jit(solution)/shard_map/ppermute | solution.py:257
  146.4 0.0 collective-permute-done.4
  146.4 1.4 collective-permute-start.9
  147.8 1.2 collective-permute-start.8
  149.0 0.9 collective-permute-start.7
  149.9 2.5 %collective-permute-done.9 = f32[160,128]{1,0:T(8,128)S(1)} collective-permute-done((f32[160,128]{1,0:T(8,128)S(1)}, f32[160,128]{1,0:T(8,128)S(1)}, u32[]{:S(2)}, u32[]{:S(2)}) %collective-permute-start.9) | collective-permute-done | bytes 81952 | tf_op jit(solution)/shard_map/ppermute | solution.py:257
  152.5 0.4 collective-permute-done.8
  152.9 0.6 collective-permute-done.7
  153.6 0.1 collective-permute-start.10
  153.6 1.6 collective-permute-done.10.other_gram_ref
  155.3 8.0 %root.1 = f32[256,512]{1,0:T(8,128)} custom-call(s32[1]{0:T(128)} %bitcast.place_ref, f32[5,128,128]{2,1,0:T(8,128)S(1)} %bitcast.34, f32[5,128,128]{2,1,0:T(8,128)S(1)} %collective-permute-done.10.other_gram_ref, bf16[256,512]{1,0:T(8,128)(2,1)S(1)} %get-tuple-element.12.mine_ref), custom_call_target="tpu_custom_call" | custom-call | tf_op jit(solution)/shard_map/root/pallas_call | solution.py:244
  (9 shorter events, 0.2 us)
Async XLA Ops:
  1.1 0.7 copy-start
  119.6 5.8 %copy-start.1 = (s32[2,10]{1,0:T(2,128)S(1)}, s32[2,10]{1,0:T(2,128)}, u32[]{:S(2)}) copy-start(s32[2,10]{1,0:T(2,128)} %constant.40.clone) | copy-start | bytes 244
  125.3 2.7 %collective-permute-start = (f32[512,512]{1,0:T(8,128)S(1)}, f32[512,512]{1,0:T(8,128)S(1)}, u32[]{:S(2)}, u32[]{:S(2)}) collective-permute-start(f32[512,512]{1,0:T(8,128)S(1)} %combine.1.sum_a_ref), channel_id=1, source_target_pairs={{0,1},{1,0},{2,3},{3,2},{4,5},{5,4},{6,7},{7,6},{8,9},{9,8},{10,11... | collective-permute-start | bytes 3145736 | tf_op jit(solution)/shard_map/ppermute | solution.py:257
  129.1 6.3 %collective-permute-start.3 = (f32[160,128]{1,0:T(8,128)S(1)}, f32[160,128]{1,0:T(8,128)S(1)}, u32[]{:S(2)}, u32[]{:S(2)}) collective-permute-start(f32[160,128]{1,0:T(8,128)S(1)} %get-tuple-element.18), channel_id=1, source_target_pairs={{0,6},{2,4},{4,2},{6,0},{8,14},{10,12},{12,10},{14,8},{16,22},{18,... | collective-permute-start | bytes 245768 | tf_op jit(solution)/shard_map/ppermute | solution.py:257
  130.0 6.0 %collective-permute-start.2 = (f32[160,128]{1,0:T(8,128)S(1)}, f32[160,128]{1,0:T(8,128)S(1)}, u32[]{:S(2)}, u32[]{:S(2)}) collective-permute-start(f32[160,128]{1,0:T(8,128)S(1)} %get-tuple-element.19), channel_id=1, source_target_pairs={{0,4},{2,6},{4,0},{6,2},{8,12},{10,14},{12,8},{14,10},{16,20},{18,... | collective-permute-start | bytes 245768 | tf_op jit(solution)/shard_map/ppermute | solution.py:257
  131.1 4.9 %collective-permute-start.1 = (f32[160,128]{1,0:T(8,128)S(1)}, f32[160,128]{1,0:T(8,128)S(1)}, u32[]{:S(2)}, u32[]{:S(2)}) collective-permute-start(f32[160,128]{1,0:T(8,128)S(1)} %get-tuple-element.17), channel_id=1, source_target_pairs={{0,2},{2,0},{4,6},{6,4},{8,10},{10,8},{12,14},{14,12},{16,18},{18,... | collective-permute-start | bytes 245768 | tf_op jit(solution)/shard_map/ppermute | solution.py:257
  136.0 7.2 %collective-permute-start.6 = (f32[160,128]{1,0:T(8,128)S(1)}, f32[160,128]{1,0:T(8,128)S(1)}, u32[]{:S(2)}, u32[]{:S(2)}) collective-permute-start(f32[160,128]{1,0:T(8,128)S(1)} %add_add_fusion.1), channel_id=1, source_target_pairs={{0,24},{2,26},{4,28},{6,30},{8,16},{10,18},{12,20},{14,22},{16,8},... | collective-permute-start | bytes 245768 | tf_op jit(solution)/shard_map/ppermute | solution.py:257
  138.2 8.1 %collective-permute-start.5 = (f32[160,128]{1,0:T(8,128)S(1)}, f32[160,128]{1,0:T(8,128)S(1)}, u32[]{:S(2)}, u32[]{:S(2)}) collective-permute-start(f32[160,128]{1,0:T(8,128)S(1)} %add_add_fusion.1), channel_id=1, source_target_pairs={{0,16},{2,18},{4,20},{6,22},{8,24},{10,26},{12,28},{14,30},{16,0},... | collective-permute-start | bytes 245768 | tf_op jit(solution)/shard_map/ppermute | solution.py:257
  138.8 7.5 %collective-permute-start.4 = (f32[160,128]{1,0:T(8,128)S(1)}, f32[160,128]{1,0:T(8,128)S(1)}, u32[]{:S(2)}, u32[]{:S(2)}) collective-permute-start(f32[160,128]{1,0:T(8,128)S(1)} %add_add_fusion.1), channel_id=1, source_target_pairs={{0,8},{2,10},{4,12},{6,14},{8,0},{10,2},{12,4},{14,6},{16,24},{18,... | collective-permute-start | bytes 245768 | tf_op jit(solution)/shard_map/ppermute | solution.py:257
  146.4 6.1 %collective-permute-start.9 = (f32[160,128]{1,0:T(8,128)S(1)}, f32[160,128]{1,0:T(8,128)S(1)}, u32[]{:S(2)}, u32[]{:S(2)}) collective-permute-start(f32[160,128]{1,0:T(8,128)S(1)} %add_add_fusion), channel_id=1, source_target_pairs={{0,6},{2,4},{4,2},{6,0},{8,14},{10,12},{12,10},{14,8},{16,22},{18,... | collective-permute-start | bytes 245768 | tf_op jit(solution)/shard_map/ppermute | solution.py:257
  147.8 5.1 %collective-permute-start.8 = (f32[160,128]{1,0:T(8,128)S(1)}, f32[160,128]{1,0:T(8,128)S(1)}, u32[]{:S(2)}, u32[]{:S(2)}) collective-permute-start(f32[160,128]{1,0:T(8,128)S(1)} %add_add_fusion), channel_id=1, source_target_pairs={{0,4},{2,6},{4,0},{6,2},{8,12},{10,14},{12,8},{14,10},{16,20},{18,... | collective-permute-start | bytes 245768 | tf_op jit(solution)/shard_map/ppermute | solution.py:257
  149.0 4.4 %collective-permute-start.7 = (f32[160,128]{1,0:T(8,128)S(1)}, f32[160,128]{1,0:T(8,128)S(1)}, u32[]{:S(2)}, u32[]{:S(2)}) collective-permute-start(f32[160,128]{1,0:T(8,128)S(1)} %add_add_fusion), channel_id=1, source_target_pairs={{0,2},{2,0},{4,6},{6,4},{8,10},{10,8},{12,14},{14,12},{16,18},{18,... | collective-permute-start | bytes 245768 | tf_op jit(solution)/shard_map/ppermute | solution.py:257
  153.6 1.7 %collective-permute-start.10 = (f32[5,128,128]{2,1,0:T(8,128)S(1)}, f32[5,128,128]{2,1,0:T(8,128)S(1)}, u32[]{:S(2)}, u32[]{:S(2)}) collective-permute-start(f32[5,128,128]{2,1,0:T(8,128)S(1)} %bitcast.33), channel_id=1, source_target_pairs={{0,1},{1,0},{2,3},{3,2},{4,5},{5,4},{6,7},{7,6},{8,9},{9,8},{10,11... | collective-permute-start | bytes 983048 | tf_op jit(solution)/shard_map/ppermute | solution.py:257

commit v2 on v1

--- a/solution.py
+++ b/solution.py
@@ -14,6 +14,7 @@
 f32 = jnp.float32
 bf16 = jnp.bfloat16
 lane = 128
+chunk = 256
 vmem_limit = 48 << 20
 
 COLS = (((0,), (0,)), ((), ()))
@@ -27,10 +28,15 @@
     return pl.BlockSpec(memory_space=pltpu.VMEM)
 
 
-def pack_kernel(per_dev, bound, direct, ids_ref, values_ref, send_ref, position_ref):
+def joint_of(per_dev):
+    return math.gcd(per_dev, 4)
+
+
+def pack_kernel(per_dev, bound, ids_ref, values_ref, send_ref, position_ref):
     k_j, s_dev = ids_ref.shape
-    n_ids = send_ref.shape[0] * per_dev if direct else send_ref.shape[1]
-    width = lane
+    n_dp, slots, width = send_ref.shape
+    n_ids = n_dp * per_dev
+    joint = joint_of(per_dev)
     ids_rows = ids_ref[...]
     padded = jnp.concatenate([ids_rows.astype(f32), jnp.zeros((lane - k_j, s_dev), f32)], axis=0)
     ids_cols = jnp.transpose(padded)
@@ -54,84 +60,154 @@
         named_rows = jnp.where(ids_rows[k : k + 1, :] == number_rows, 1.0, 0.0).astype(bf16)
         total = total + jnp.dot(named_rows, by_rank, preferred_element_type=f32)
         id_col = column.astype(jnp.int32)
-        target = id_col // per_dev
-        within = id_col - target * per_dev
-        places.append((target * bound + rank.astype(jnp.int32)) * per_dev + within)
-    position_ref[...] = jnp.concatenate(places, axis=1)
-    for r in range(bound):
-        rows = total[:, r * width : (r + 1) * width].astype(bf16)
-        if direct:
-            send_ref[:, r * per_dev : (r + 1) * per_dev, :] = rows.reshape(n_ids // per_dev, per_dev, width)
-        else:
-            send_ref[r] = rows
+        group = id_col // joint
+        places.append((group * bound + rank.astype(jnp.int32)) * joint + id_col - group * joint)
+    position = jnp.concatenate(places + [jnp.zeros((s_dev, lane - k_j), jnp.int32)], axis=1).astype(f32)
+    position_ref[...] = jnp.transpose(position)[: position_ref.shape[0]]
+    slot = lax.broadcasted_iota(jnp.int32, (slots, slots), 0)
+    origin = lax.broadcasted_iota(jnp.int32, (slots, slots), 1)
+    group = slot // (joint * bound)
+    rank = (slot - group * (joint * bound)) // joint
+    block = group * joint + slot % joint
+    order = jnp.where(origin == rank * per_dev + block, 1.0, 0.0).astype(bf16)
+    for to in range(n_dp):
+        rows = total[to * per_dev : (to + 1) * per_dev, :]
+        rows = jnp.concatenate([rows[:, r * width : (r + 1) * width] for r in range(bound)], axis=0)
+        send_ref[to] = jnp.dot(order, rows.astype(bf16), preferred_element_type=f32).astype(bf16)
 
 
 def pack(ids, values, n_dp, per_dev, bound):
     k_j, s_dev = ids.shape
-    direct = per_dev % 16 == 0
-    shape = (n_dp, bound * per_dev, lane) if direct else (bound, n_dp * per_dev, lane)
-    send, position = pl.pallas_call(
-        functools.partial(pack_kernel, per_dev, bound, direct),
+    return pl.pallas_call(
+        functools.partial(pack_kernel, per_dev, bound),
         out_shape=(
-            jax.ShapeDtypeStruct(shape, bf16),
-            jax.ShapeDtypeStruct((s_dev, k_j), jnp.int32),
+            jax.ShapeDtypeStruct((n_dp, bound * per_dev, lane), bf16),
+            jax.ShapeDtypeStruct((8, s_dev), f32),
         ),
         in_specs=[whole(), whole()],
         out_specs=(whole(), whole()),
         compiler_params=params(),
         name="pack",
     )(ids, values)
-    if not direct:
-        send = send.reshape(bound, n_dp, per_dev, lane).transpose(1, 0, 2, 3).reshape(n_dp, bound * per_dev, lane)
-    return send, position
-
-
-def product_kernel(per_dev, per_step, tiles_ref, probe_ref, out_ref, tiles, products):
+
+
+def product_kernel(bound, joint, groups, place_ref, tiles_ref, probe_ref, out_ref):
+    inner, outer, unit, width = out_ref.shape
+    count = inner * outer
+    rows = bound * joint
+    start = pl.multiple_of(pl.program_id(0) * unit, unit)
+    place = place_ref[0]
+    tiles = [
+        tiles_ref[b * inner + (place ^ a), pl.ds(start, unit), :].astype(f32)
+        for a in range(inner)
+        for b in range(outer)
+    ]
+    own = lax.broadcasted_iota(jnp.int32, (count * rows, lane), 0) % joint
+    parts = []
+    for g in range(groups):
+        tile = jnp.concatenate([t[g * rows : (g + 1) * rows] for t in tiles], axis=0)
+        spread = jnp.concatenate([jnp.where(own == j, tile, 0.0).astype(bf16) for j in range(joint)], axis=1)
+        probe = probe_ref[g * joint : (g + 1) * joint].reshape(joint * lane, width)
+        parts.append(jnp.dot(spread, probe, preferred_element_type=f32))
+    for a in range(inner):
+        for b in range(outer):
+            at = (a * outer + b) * rows
+            value = jnp.concatenate([part[at : at + rows] for part in parts], axis=0)
+            out_ref[a, b] = value.astype(bf16)
+
+
+def product(place, tiles, probe, inner, bound, first, width):
+    n_dp, slots, _ = tiles.shape
+    per_dev = probe.shape[0]
+    joint = joint_of(per_dev)
+    groups = 1 if bound * joint % 16 == 0 else 2
+    unit = groups * bound * joint
+    return pl.pallas_call(
+        functools.partial(product_kernel, bound, joint, groups),
+        out_shape=jax.ShapeDtypeStruct((inner, n_dp // inner, slots, width), bf16),
+        grid=(slots // unit,),
+        in_specs=[
+            pl.BlockSpec(memory_space=pltpu.SMEM),
+            pl.BlockSpec((n_dp, slots, lane), lambda i: (0, 0, 0)),
+            pl.BlockSpec((groups * joint, lane, width), lambda i: (i, 0, first // width)),
+        ],
+        out_specs=pl.BlockSpec((inner, n_dp // inner, unit, width), lambda i: (0, 0, i, 0)),
+        compiler_params=params(),
+        cost_estimate=pl.CostEstimate(flops=2 * n_dp * slots * joint * lane * width, bytes_accessed=1 << 22, transcendentals=0),
+        name="product",
+    )(place.reshape(1), tiles, probe)
+
+
+def choose_kernel(k_j, slots, inner, place_ref, *refs):
+    position_refs, out_ref = refs[:-1], refs[-1]
+    _, s_dev, count = out_ref.shape
+    place, outer_at = place_ref[0], place_ref[1]
+    at = lax.broadcasted_iota(jnp.int32, (1, count), 1)
+    expect = jnp.zeros((1, count), jnp.int32)
+    for a in range(inner):
+        inside = jnp.logical_and(at >= a * slots, at < (a + 1) * slots)
+        expect = jnp.where(inside, (outer_at * inner + (place ^ a)) * slots + at - a * slots, expect)
+    expect = expect.astype(f32)
+    rows = [ref[...] for ref in position_refs]
+    rows = jnp.concatenate(rows + [jnp.zeros((lane - 8 * len(rows), s_dev), f32)], axis=0)
+    columns = jnp.transpose(rows)
+    for c in range(len(position_refs)):
+        hit = columns[:, 8 * c : 8 * c + 1] == expect
+        for k in range(1, k_j):
+            hit = jnp.logical_or(hit, columns[:, 8 * c + k : 8 * c + k + 1] == expect)
+        out_ref[c] = jnp.where(hit, 1.0, 0.0).astype(bf16)
+
+
+def choose(place, outer_at, positions, k_j, slots, inner):
+    s_dev = positions[0].shape[1]
+    return pl.pallas_call(
+        functools.partial(choose_kernel, k_j, slots, inner),
+        out_shape=jax.ShapeDtypeStruct((len(positions), s_dev, inner * slots), bf16),
+        in_specs=[pl.BlockSpec(memory_space=pltpu.SMEM)] + [whole()] * len(positions),
+        out_specs=whole(),
+        compiler_params=params(),
+        cost_estimate=pl.CostEstimate(flops=1 << 24, bytes_accessed=1 << 23, transcendentals=0),
+        name="choose",
+    )(jnp.stack([place, outer_at]), *positions)
+
+
+def gather_kernel(outer, place_ref, hits_ref, *refs):
+    rows_refs, keep_ref, give_ref = refs[:-2], refs[-2], refs[-1]
+    half = keep_ref.shape[1]
+    slots = rows_refs[0].shape[1]
+    feat, outer_at = place_ref[0], place_ref[1]
+    for c in range(outer):
+        rows = jnp.concatenate([ref[outer_at ^ c] for ref in rows_refs], axis=0)
+        give = hits_ref[c, pl.ds(pl.multiple_of((1 - feat) * half, half), half), :]
+        give_ref[c] = jnp.dot(give, rows, preferred_element_type=f32).astype(bf16)
+        keep = hits_ref[c, pl.ds(pl.multiple_of(feat * half, half), half), :]
+        keep_ref[c] = jnp.dot(keep, rows, preferred_element_type=f32)
+
+
+def gather(feat, outer_at, hits, rows):
+    outer, s_dev, _ = hits.shape
+    width = rows[0].shape[2]
+    return pl.pallas_call(
+        functools.partial(gather_kernel, outer),
+        out_shape=(
+            jax.ShapeDtypeStruct((outer, s_dev // 2, width), f32),
+            jax.ShapeDtypeStruct((outer, s_dev // 2, width), bf16),
+        ),
+        in_specs=[pl.BlockSpec(memory_space=pltpu.SMEM)] + [whole()] * (1 + len(rows)),
+        out_specs=(whole(), whole()),
+        compiler_params=params(),
+        cost_estimate=pl.CostEstimate(flops=2 * hits.size * width, bytes_accessed=1 << 23, transcendentals=0),
+        name="gather",
+    )(jnp.stack([feat, outer_at]), hits, *rows)
+
+
+def combine_kernel(k_j, position_ref, rows_ref, out_ref):
     step = pl.program_id(0)
-    count = tiles.shape[0] // per_dev
-
-    @pl.when(step == 0)
-    def _():
-        tiles[...] = tiles_ref[...].astype(f32)
-
-    for at in range(per_step):
-        block = step * per_step + at
-        rows = pl.ds(block, count, stride=per_dev)
-        value = jnp.dot(tiles[rows, :].astype(bf16), probe_ref[at], preferred_element_type=f32)
-        for c in range(products.shape[0]):
-            products[c, rows, :] = value[:, c * lane : (c + 1) * lane]
-
-    @pl.when(step == pl.num_programs(0) - 1)
-    def _():
-        for c in range(products.shape[0]):
-            out_ref[:, c * lane : (c + 1) * lane] = products[c].astype(bf16)
-
-
-def product(tiles, probe):
-    rows = tiles.shape[0]
-    per_dev, _, width = probe.shape
-    per_step = math.gcd(per_dev, 4)
-    return pl.pallas_call(
-        functools.partial(product_kernel, per_dev, per_step),
-        out_shape=jax.ShapeDtypeStruct((rows, width), bf16),
-        grid=(per_dev // per_step,),
-        in_specs=[
-            pl.BlockSpec((rows, lane), lambda i: (0, 0)),
-            pl.BlockSpec((per_step, lane, width), lambda i: (i, 0, 0)),
-        ],
-        out_specs=pl.BlockSpec((rows, width), lambda i: (0, 0)),
-        scratch_shapes=[pltpu.VMEM((rows, lane), f32), pltpu.VMEM((width // lane, rows, lane), f32)],
-        compiler_params=params(),
-        name="product",
-    )(tiles, probe)
-
-
-def combine_kernel(position_ref, rows_ref, out_ref):
-    step = pl.program_id(0)
-    s_dev, k_j = position_ref.shape
+    s_dev = position_ref.shape[1]
     count = rows_ref.shape[0]
     here = lax.broadcasted_iota(jnp.int32, (s_dev, count), 1) + step * count
-    position = position_ref[...]
+    rows = jnp.concatenate([position_ref[...], jnp.zeros((lane - 8, s_dev), f32)], axis=0)
+    position = jnp.transpose(rows).astype(jnp.int32)
     hit = position[:, 0:1] == here
     for k in range(1, k_j):
         hit = jnp.logical_or(hit, position[:, k : k + 1] == here)
@@ -146,16 +222,16 @@
         out_ref[...] += part
 
 
-def combine(position, rows):
-    s_dev, k_j = position.shape
+def combine(position, rows, k_j):
+    s_dev = position.shape[1]
     total, width = rows.shape
     count = total // 6 if total % (6 * lane) == 0 else total
     return pl.pallas_call(
-        combine_kernel,
+        functools.partial(combine_kernel, k_j),
         out_shape=jax.ShapeDtypeStruct((s_dev, width), f32),
         grid=(total // count,),
         in_specs=[
-            pl.BlockSpec((s_dev, k_j), lambda i: (0, 0)),
+            pl.BlockSpec((8, s_dev), lambda i: (0, 0)),
             pl.BlockSpec((count, width), lambda i: (i, 0)),
         ],
         out_specs=pl.BlockSpec((s_dev, width), lambda i: (0, 0)),
@@ -169,35 +245,27 @@
     return [(i, j) for i in range(n) for j in range(i, n)]
 
 
-def gram_kernel(own_rows, pairs_ref, place_ref, sum_a_ref, sum_b_ref, gram_ref, mine_ref, sketch):
-    sketch[...] = (sum_a_ref[...] + sum_b_ref[...]).astype(bf16)
-    start = pl.multiple_of(place_ref[0] * own_rows, own_rows)
-    mine_ref[...] = sketch[pl.ds(start, own_rows), :]
+def gram_kernel(pairs_ref, sketch_ref, gram_ref):
     for at in range(gram_ref.shape[0]):
-        left = sketch[:, pl.ds(pl.multiple_of(pairs_ref[2 * at] * lane, lane), lane)]
-        right = sketch[:, pl.ds(pl.multiple_of(pairs_ref[2 * at + 1] * lane, lane), lane)]
+        left = sketch_ref[:, pl.ds(pl.multiple_of(pairs_ref[2 * at] * lane, lane), lane)]
+        right = sketch_ref[:, pl.ds(pl.multiple_of(pairs_ref[2 * at + 1] * lane, lane), lane)]
         gram_ref[at] = lax.dot_general(left, right, COLS, preferred_element_type=f32)
 
 
-def gram_blocks(sum_a, sum_b, place, n_feat):
-    s_dev, width = sum_a.shape
+def gram_blocks(sketch, feat):
+    width = sketch.shape[1]
     pairs = block_pairs(width)
     half = len(pairs) // 2
     table = jnp.asarray(np.array(pairs, np.int32).reshape(2, 2 * half))
-    own_rows = s_dev // n_feat
     smem = pl.BlockSpec(memory_space=pltpu.SMEM)
     return pl.pallas_call(
-        functools.partial(gram_kernel, own_rows),
-        out_shape=(
-            jax.ShapeDtypeStruct((half, lane, lane), f32),
-            jax.ShapeDtypeStruct((own_rows, width), bf16),
-        ),
-        in_specs=[smem, smem, whole(), whole()],
-        out_specs=(whole(), whole()),
-        scratch_shapes=[pltpu.VMEM((s_dev, width), bf16)],
+        gram_kernel,
+        out_shape=jax.ShapeDtypeStruct((half, lane, lane), f32),
+        in_specs=[smem, whole()],
+        out_specs=whole(),
         compiler_params=params(),
         name="gram",
-    )(table[place % 2], place.reshape(1), sum_a, sum_b)
+    )(table[feat % 2], sketch)
 
 
 def halves(value):
@@ -285,31 +353,64 @@
     return jnp.concatenate(ordered, axis=0).reshape(value.shape)
 
 
+def sketch_by_all_to_all(products, position, k_j):
+    n_feat = lax.axis_size("feat")
+    feat = lax.axis_index("feat")
+    width = products.shape[2]
+    returned = lax.all_to_all(products, "dp", split_axis=0, concat_axis=0, tiled=True)
+    part = combine(position, returned.reshape(-1, width), k_j)
+    bits = 1
+    while bits < n_feat:
+        part = part + crossed(part, "feat", bits)
+        bits *= 2
+    sketch = part.astype(bf16)
+    own_rows = sketch.shape[0] // n_feat
+    return lax.dynamic_slice_in_dim(sketch, feat * own_rows, own_rows, 0), sketch
+
+
+def sketch_by_planes(tiles, probe, position, inner, bound, k_j):
+    n_dp, slots, _ = tiles.shape
+    outer = n_dp // inner
+    index, feat = lax.axis_index("dp"), lax.axis_index("feat")
+    place, outer_at = index % inner, index // inner
+    width = probe.shape[2]
+    positions = [position] + [crossed(position, "dp", c * inner) for c in range(1, outer)]
+    hits = choose(place, outer_at, positions, k_j, slots, inner)
+    mine, others = [], []
+    for first in range(0, width, chunk):
+        sent = product(place, tiles, probe, inner, bound, first, chunk)
+        rows = [sent[0]] + [crossed(sent[a], "dp", a) for a in range(1, inner)]
+        keep, give = gather(feat, outer_at, hits, rows)
+        plane = keep + crossed(give, "feat", 1).astype(f32)
+        total = plane[0]
+        for c in range(1, outer):
+            total = total + crossed(plane[c].astype(bf16), "dp", c * inner).astype(f32)
+        mine.append(total.astype(bf16))
+        others.append(crossed(mine[-1], "feat", 1))
+    mine, others = jnp.concatenate(mine, axis=1), jnp.concatenate(others, axis=1)
+    return mine, jnp.concatenate([mine, others], axis=0)
+
+
 def local(grads, block_ids, probe):
     values = grads[0]
     s_dev, k_j, b_width = values.shape
-    n_dp = lax.axis_size("dp")
-    n_feat = lax.axis_size("feat")
+    n_dp, n_feat = lax.axis_size("dp"), lax.axis_size("feat")
+    feat = lax.axis_index("feat")
     per_dev = probe.shape[0]
     width = probe.shape[3]
     b_slice = per_dev * n_dp
     bound = max(2, 3 * s_dev * k_j // (2 * b_slice))
-    place = lax.axis_index("feat")
+    probe = probe[:, 0]
     send, position = pack(block_ids[0].T, values.reshape(s_dev, k_j * b_width), n_dp, per_dev, bound)
     tiles = lax.all_to_all(send, "dp", split_axis=0, concat_axis=0, tiled=True)
-    products = product(tiles.reshape(-1, b_width), probe[:, 0])
-    returned = lax.all_to_all(
-        products.reshape(n_dp, -1, width), "dp", split_axis=0, concat_axis=0, tiled=True
-    )
-    part = combine(position, returned.reshape(-1, width))
-    bits = n_feat // 2
-    while bits > 1:
-        part = part + crossed(part, "feat", bits)
-        bits //= 2
-    mine_gram, mine = gram_blocks(part, crossed(part, "feat", 1), place, n_feat)
-    mine_gram = sum_over_dp(mine_gram)
+    if n_feat == 2 and n_dp == 16:
+        mine, sketch = sketch_by_planes(tiles, probe, position, 4, bound, k_j)
+    else:
+        products = product(jnp.zeros((), jnp.int32), tiles, probe, 1, bound, 0, width)
+        mine, sketch = sketch_by_all_to_all(products[0], position, k_j)
+    mine_gram = sum_over_dp(gram_blocks(sketch, feat))
     other_gram = crossed(mine_gram, "feat", 1)
-    return whiten(mine_gram, other_gram, mine, place, s_dev * n_dp)
+    return whiten(mine_gram, other_gram, mine, feat, s_dev * n_dp)
 
 
 def solution(mesh):

time: 164 us -> 152 us (0.927)
  blocking collectives: 103 us -> 0 us
  waiting for transfers between devices: 17 us -> 72.7 us
  starting transfers between devices: 11.7 us -> 41.9 us
  local copies, waits for them, and re-layouts: 1.89 us -> 4.58 us
  Pallas kernels: 29 us -> 31 us
    all_to_all x2 -> x0, blocking collectives: 103 us -> none  [the longest x1 74 us: local(): lax.all_to_all(products.reshape(n_dp, -1, width), 'dp', split_axis=0, con...]
    ppermute x11 -> x29, waiting for transfers between devices: 17 us -> 53 us  [crossed(): lax.ppermute(value, axis, [(source, source ^ bits) for source in range(co...]
    ppermute x11 -> x29, starting transfers between devices: 11.7 us -> 33.6 us  [crossed(): lax.ppermute(value, axis, [(source, source ^ bits) for source in range(co...]
    all_to_all x0 -> x1, waiting for transfers between devices: none -> 19.7 us  [local(): tiles = lax.all_to_all(send, 'dp', split_axis=0, concat_axis=0, tiled=True)]
    all_to_all x0 -> x1, starting transfers between devices: none -> 8.31 us  [local(): tiles = lax.all_to_all(send, 'dp', split_axis=0, concat_axis=0, tiled=True)]
    pallas_call x4 -> x7, Pallas kernels: 21 us -> 22.9 us  [the longest x2 6.8 us: product(): pl.pallas_call(functools.partial(product_kernel, bound, joint, groups), o...]
    unnamed x5 -> x7, local copies, waits for them, and re-layouts: 1.82 us -> 3.45 us
  transfers between devices with their start and end apart: 11 -> 30, of which waited for: 9 -> 21; matrix products, arithmetic and copies ran while one was open for 0% -> 1% of each run, Pallas kernels for 0% -> 7%
where the time goes in v2:
time: 152 us; the launch traced here: 151 us
  waiting for transfers between devices  72.7 us (48%)
  starting transfers between devices  41.9 us (28%)
  Pallas kernels  31 us (20%)
  local copies, waits for them, and re-layouts  4.58 us (3%)
    ppermute x29, waiting for transfers between devices, crossed(): lax.ppermute(value, axis, [(source, source ^ bits) for source in range(co...  53 us
    ppermute x29, starting transfers between devices, crossed(): lax.ppermute(value, axis, [(source, source ^ bits) for source in range(co...  33.6 us
    all_to_all x1, waiting for transfers between devices, local(): tiles = lax.all_to_all(send, 'dp', split_axis=0, concat_axis=0, tiled=True)  19.7 us
    all_to_all x1, starting transfers between devices, local(): tiles = lax.all_to_all(send, 'dp', split_axis=0, concat_axis=0, tiled=True)  8.31 us
    pallas_call x1, Pallas kernels, whiten(): pl.pallas_call(functools.partial(root_kernel, samples), out_shape=jax.Sha...  8.02 us
    pallas_call x2, Pallas kernels, product(): pl.pallas_call(functools.partial(product_kernel, bound, joint, groups), o...  6.8 us
    pallas_call x2, Pallas kernels, gather(): pl.pallas_call(functools.partial(gather_kernel, outer), out_shape=(jax.Sh...  5.76 us
    pallas_call x1, Pallas kernels, pack(): pl.pallas_call(functools.partial(pack_kernel, per_dev, bound), out_shape=...  5.73 us
  transfers between devices with their start and end apart: 30, of which 21 were waited for; matrix products, arithmetic and copies ran while one was open for 1% of the time, Pallas kernels for 7%

profile of v2, /device:TPU:0, one launch (start us, length us, event | category | flops | bytes accessed | tf_op | source)
XLA Modules:
  0.0 151.3 jit_solution(15065586419294575548)
XLA Ops:
  1.8 5.7 %pack.1 = (bf16[16,192,128]{2,1,0:T(8,128)(2,1)}, f32[8,512]{1,0:T(8,128)S(1)}) custom-call(s32[4,512]{1,0:T(4,128)S(1)} %bitcast.81, bf16[512,512]{1,0:T(8,128)(2,1)S(1)} %bitcast.76), custom_call_target="tpu_custom_call" | custom-call | tf_op jit(solution)/shard_map/pack/pallas_call | solution.py:81
  7.6 8.3 %all-to-all-start = ((bf16[16,192,128]{2,1,0:T(8,128)(2,1)}), bf16[16,192,128]{2,1,0:T(8,128)(2,1)S(1)}, u32[]{:S(2)}, u32[]{:S(2)}) async-start(bf16[16,192,128]{2,1,0:T(8,128)(2,1)} %get-tuple-element.12), calls=%async_computation | async-start | bytes 1572864 | tf_op jit(solution)/shard_map/all_to_all | solution.py:405
  15.9 19.7 %all-to-all-done.tiles_ref = bf16[16,192,128]{2,1,0:T(8,128)(2,1)S(1)} async-done(((bf16[16,192,128]{2,1,0:T(8,128)(2,1)}), bf16[16,192,128]{2,1,0:T(8,128)(2,1)S(1)}, u32[]{:S(2)}, u32[]{:S(2)}) %all-to-all-start) | async-done | bytes 786464 | tf_op jit(solution)/shard_map/all_to_all | solution.py:405
  35.6 3.3 %product.2 = bf16[4,4,192,256]{3,2,1,0:T(8,128)(2,1)S(1)} custom-call(s32[1]{0:T(128)} %bitcast.3.place_ref, bf16[16,192,128]{2,1,0:T(8,128)(2,1)S(1)} %all-to-all-done.tiles_ref, bf16[32,128,512]{2,1,0:T(8,128)(2,1)} %bitcast.82), custom_call_target="tpu_custom_call" | custom-call | flops 805306368 | bytes 4194304 | tf_op jit(solution)/shard_map/product/pallas_call | solution.py:125
  40.4 1.6 %collective-permute-start.4 = (bf16[4,192,256]{2,1,0:T(8,128)(2,1)S(1)}, bf16[4,192,256]{2,1,0:T(8,128)(2,1)S(1)}, u32[]{:S(2)}, u32[]{:S(2)}) collective-permute-start(bf16[4,192,256]{2,1,0:T(8,128)(2,1)S(1)} %get-tuple-element.22), channel_id=1, source_target_pairs={{0,4},{2,6},{4,0},{6,2},{8,12},{10,14},{12,8},{14,10},{16,20},{18,... | collective-permute-start | bytes 1179656 | tf_op jit(solution)/shard_map/ppermute | solution.py:325
  43.3 2.1 %collective-permute-start = (f32[8,512]{1,0:T(8,128)S(1)}, f32[8,512]{1,0:T(8,128)S(1)}, u32[]{:S(2)}, u32[]{:S(2)}) collective-permute-start(f32[8,512]{1,0:T(8,128)S(1)} %get-tuple-element.11.refs_0_), channel_id=1, source_target_pairs={{0,8},{2,10},{4,12},{6,14},{8,0},{10,2},{12,4},{14,6},{16,24},{18,... | collective-permute-start | bytes 49160 | tf_op jit(solution)/shard_map/ppermute | solution.py:325
  47.2 2.0 %collective-permute-start.2 = (f32[8,512]{1,0:T(8,128)S(1)}, f32[8,512]{1,0:T(8,128)S(1)}, u32[]{:S(2)}, u32[]{:S(2)}) collective-permute-start(f32[8,512]{1,0:T(8,128)S(1)} %get-tuple-element.11.refs_0_), channel_id=1, source_target_pairs={{0,24},{2,26},{4,28},{6,30},{8,16},{10,18},{12,20},{14,22},{16,8},... | collective-permute-start | bytes 49160 | tf_op jit(solution)/shard_map/ppermute | solution.py:325
  50.1 2.6 %collective-permute-done.2.refs_3_ = f32[8,512]{1,0:T(8,128)S(1)} collective-permute-done((f32[8,512]{1,0:T(8,128)S(1)}, f32[8,512]{1,0:T(8,128)S(1)}, u32[]{:S(2)}, u32[]{:S(2)}) %collective-permute-start.2) | collective-permute-done | bytes 16416 | tf_op jit(solution)/shard_map/ppermute | solution.py:325
  52.7 3.7 %choose.1.hits_ref = bf16[4,512,768]{2,1,0:T(8,128)(2,1)S(1)} custom-call(s32[2]{0:T(128)S(1)} %pad_add_fusion.1.place_ref, f32[8,512]{1,0:T(8,128)S(1)} %get-tuple-element.11.refs_0_, f32[8,512]{1,0:T(8,128)S(1)} %collective-permute-done.refs_1_, f32[8,512]{1,0:T(8,128)S(1)} %collective-permute-done.1.refs_2_, f32[8,512]{1,0:T(8,128)S(1)} %collective-permute-done.2.refs_3_), custom_call_target="tpu_custom_call" | custom-call | flops 16777216 | bytes 8388608 | tf_op jit(solution)/shard_map/choose/pallas_call | solution.py:163
  56.4 1.6 %copy-done = bf16[4,512,768]{2,1,0:T(8,128)(2,1)} copy-done((bf16[4,512,768]{2,1,0:T(8,128)(2,1)}, bf16[4,512,768]{2,1,0:T(8,128)(2,1)S(1)}, u32[]{:S(2)}) %copy-start) | copy-done | bytes 3145752
  58.1 3.5 %product.3 = bf16[4,4,192,256]{3,2,1,0:T(8,128)(2,1)S(1)} custom-call(s32[1]{0:T(128)} %bitcast.3.place_ref, bf16[16,192,128]{2,1,0:T(8,128)(2,1)S(1)} %all-to-all-done.tiles_ref, bf16[32,128,512]{2,1,0:T(8,128)(2,1)} %bitcast.83), custom_call_target="tpu_custom_call" | custom-call | flops 805306368 | bytes 4194304 | tf_op jit(solution)/shard_map/product/pallas_call | solution.py:125
  61.6 2.9 %gather.2 = (f32[4,256,256]{2,1,0:T(8,128)S(1)}, bf16[4,256,256]{2,1,0:T(8,128)(2,1)S(1)}) custom-call(s32[2]{0:T(128)S(1)} %pad_add_fusion.place_ref, bf16[4,512,768]{2,1,0:T(8,128)(2,1)} %copy-done, bf16[4,192,256]{2,1,0:T(8,128)(2,1)S(1)} %get-tuple-element.24.refs_0_, bf16[4,192,256]{2,1,0:T(8,128)(2,1)S(1)} %collective-permute-done.3.refs_1_, ...), custom_call_target="tpu_custom_call" | custom-call | flops 805306368 | bytes 8388608 | tf_op jit(solution)/shard_map/gather/pallas_call | solution.py:190
  65.3 1.5 collective-permute-start.11
  66.8 1.4 collective-permute-start.12
  68.3 8.4 %collective-permute-done.10.refs_1_ = bf16[4,192,256]{2,1,0:T(8,128)(2,1)S(1)} collective-permute-done((bf16[4,192,256]{2,1,0:T(8,128)(2,1)S(1)}, bf16[4,192,256]{2,1,0:T(8,128)(2,1)S(1)}, u32[]{:S(2)}, u32[]{:S(2)}) %collective-permute-start.10) | collective-permute-done | bytes 393248 | tf_op jit(solution)/shard_map/ppermute | solution.py:325
  76.7 7.4 %collective-permute-done.11.refs_2_ = bf16[4,192,256]{2,1,0:T(8,128)(2,1)S(1)} collective-permute-done((bf16[4,192,256]{2,1,0:T(8,128)(2,1)S(1)}, bf16[4,192,256]{2,1,0:T(8,128)(2,1)S(1)}, u32[]{:S(2)}, u32[]{:S(2)}) %collective-permute-start.11) | collective-permute-done | bytes 393248 | tf_op jit(solution)/shard_map/ppermute | solution.py:325
  84.1 1.6 %collective-permute-done.12.refs_3_ = bf16[4,192,256]{2,1,0:T(8,128)(2,1)S(1)} collective-permute-done((bf16[4,192,256]{2,1,0:T(8,128)(2,1)S(1)}, bf16[4,192,256]{2,1,0:T(8,128)(2,1)S(1)}, u32[]{:S(2)}, u32[]{:S(2)}) %collective-permute-start.12) | collective-permute-done | bytes 393248 | tf_op jit(solution)/shard_map/ppermute | solution.py:325
  85.7 2.9 %gather.3 = (f32[4,256,256]{2,1,0:T(8,128)S(1)}, bf16[4,256,256]{2,1,0:T(8,128)(2,1)S(1)}) custom-call(s32[2]{0:T(128)S(1)} %pad_add_fusion.place_ref, bf16[4,512,768]{2,1,0:T(8,128)(2,1)} %copy-done, bf16[4,192,256]{2,1,0:T(8,128)(2,1)S(1)} %get-tuple-element.28.refs_0_, bf16[4,192,256]{2,1,0:T(8,128)(2,1)S(1)} %collective-permute-done.10.refs_1_, ...), custom_call_target="tpu_custom_call" | custom-call | flops 805306368 | bytes 8388608 | tf_op jit(solution)/shard_map/gather/pallas_call | solution.py:190
  88.9 3.0 %collective-permute-start.8 = (bf16[256,256]{1,0:T(8,128)(2,1)S(1)}, bf16[256,256]{1,0:T(8,128)(2,1)S(1)}, u32[]{:S(2)}, u32[]{:S(2)}) collective-permute-start(bf16[256,256]{1,0:T(8,128)(2,1)S(1)} %get-tuple-element.31), channel_id=1, source_target_pairs={{0,16},{2,18},{4,20},{6,22},{8,24},{10,26},{12,28},{14,30},{16,0},... | collective-permute-start | bytes 393224 | tf_op jit(solution)/shard_map/ppermute | solution.py:325
  91.9 1.4 collective-permute-start.9
  93.6 3.0 %collective-permute-start.15 = (bf16[256,256]{1,0:T(8,128)(2,1)S(1)}, bf16[256,256]{1,0:T(8,128)(2,1)S(1)}, u32[]{:S(2)}, u32[]{:S(2)}) collective-permute-start(bf16[256,256]{1,0:T(8,128)(2,1)S(1)} %get-tuple-element.34), channel_id=1, source_target_pairs={{0,16},{2,18},{4,20},{6,22},{8,24},{10,26},{12,28},{14,30},{16,0},... | collective-permute-start | bytes 393224 | tf_op jit(solution)/shard_map/ppermute | solution.py:325
  97.7 1.5 collective-permute-start.16
  99.2 2.7 %collective-permute-done.8 = bf16[256,256]{1,0:T(8,128)(2,1)S(1)} collective-permute-done((bf16[256,256]{1,0:T(8,128)(2,1)S(1)}, bf16[256,256]{1,0:T(8,128)(2,1)S(1)}, u32[]{:S(2)}, u32[]{:S(2)}) %collective-permute-start.8) | collective-permute-done | bytes 131104 | tf_op jit(solution)/shard_map/ppermute | solution.py:325
  103.2 9.9 %collective-permute-done.15 = bf16[256,256]{1,0:T(8,128)(2,1)S(1)} collective-permute-done((bf16[256,256]{1,0:T(8,128)(2,1)S(1)}, bf16[256,256]{1,0:T(8,128)(2,1)S(1)}, u32[]{:S(2)}, u32[]{:S(2)}) %collective-permute-start.15) | collective-permute-done | bytes 131104 | tf_op jit(solution)/shard_map/ppermute | solution.py:325
  121.2 2.2 %collective-permute-done.21 = f32[160,128]{1,0:T(8,128)S(1)} collective-permute-done((f32[160,128]{1,0:T(8,128)S(1)}, f32[160,128]{1,0:T(8,128)S(1)}, u32[]{:S(2)}, u32[]{:S(2)}) %collective-permute-start.21) | collective-permute-done | bytes 81952 | tf_op jit(solution)/shard_map/ppermute | solution.py:325
  123.4 3.0 %collective-permute-start.22 = (f32[160,128]{1,0:T(8,128)S(1)}, f32[160,128]{1,0:T(8,128)S(1)}, u32[]{:S(2)}, u32[]{:S(2)}) collective-permute-start(f32[160,128]{1,0:T(8,128)S(1)} %add_add_fusion.1), channel_id=1, source_target_pairs={{0,8},{2,10},{4,12},{6,14},{8,0},{10,2},{12,4},{14,6},{16,24},{18,... | collective-permute-start | bytes 245768 | tf_op jit(solution)/shard_map/ppermute | solution.py:325
  127.5 1.4 collective-permute-start.24
  129.6 4.6 %collective-permute-done.23 = f32[160,128]{1,0:T(8,128)S(1)} collective-permute-done((f32[160,128]{1,0:T(8,128)S(1)}, f32[160,128]{1,0:T(8,128)S(1)}, u32[]{:S(2)}, u32[]{:S(2)}) %collective-permute-start.23) | collective-permute-done | bytes 81952 | tf_op jit(solution)/shard_map/ppermute | solution.py:325
  136.2 1.6 %collective-permute-start.27 = (f32[160,128]{1,0:T(8,128)S(1)}, f32[160,128]{1,0:T(8,128)S(1)}, u32[]{:S(2)}, u32[]{:S(2)}) collective-permute-start(f32[160,128]{1,0:T(8,128)S(1)} %add_add_fusion), channel_id=1, source_target_pairs={{0,6},{2,4},{4,2},{6,0},{8,14},{10,12},{12,10},{14,8},{16,22},{18,... | collective-permute-start | bytes 245768 | tf_op jit(solution)/shard_map/ppermute | solution.py:325
  139.7 1.8 %collective-permute-done.27 = f32[160,128]{1,0:T(8,128)S(1)} collective-permute-done((f32[160,128]{1,0:T(8,128)S(1)}, f32[160,128]{1,0:T(8,128)S(1)}, u32[]{:S(2)}, u32[]{:S(2)}) %collective-permute-start.27) | collective-permute-done | bytes 81952 | tf_op jit(solution)/shard_map/ppermute | solution.py:325
  141.7 1.6 %collective-permute-done.28.other_gram_ref = f32[5,128,128]{2,1,0:T(8,128)S(1)} collective-permute-done((f32[5,128,128]{2,1,0:T(8,128)S(1)}, f32[5,128,128]{2,1,0:T(8,128)S(1)}, u32[]{:S(2)}, u32[]{:S(2)}) %collective-permute-start.28) | collective-permute-done | bytes 327712 | tf_op jit(solution)/shard_map/ppermute | solution.py:325
  143.3 8.0 %root.1 = f32[256,512]{1,0:T(8,128)} custom-call(s32[1]{0:T(128)} %bitcast.place_ref, f32[5,128,128]{2,1,0:T(8,128)S(1)} %bitcast.80, f32[5,128,128]{2,1,0:T(8,128)S(1)} %collective-permute-done.28.other_gram_ref, bf16[256,512]{1,0:T(8,128)(2,1)S(1)} %pad_maximum_fusion.2.mine_ref), custom_call_target="tpu_custom_call" | custom-call | tf_op jit(solution)/shard_map/root/pallas_call | solution.py:312
  (62 shorter events, 24.8 us)
Async XLA Ops:
  7.6 28.1 %all-to-all-start = ((bf16[16,192,128]{2,1,0:T(8,128)(2,1)}), bf16[16,192,128]{2,1,0:T(8,128)(2,1)S(1)}, u32[]{:S(2)}, u32[]{:S(2)}) async-start(bf16[16,192,128]{2,1,0:T(8,128)(2,1)} %get-tuple-element.12), calls=%async_computation | async-start | bytes 1572864 | tf_op jit(solution)/shard_map/all_to_all | solution.py:405
  39.8 21.8 %collective-permute-start.3 = (bf16[4,192,256]{2,1,0:T(8,128)(2,1)}, bf16[4,192,256]{2,1,0:T(8,128)(2,1)S(1)}, u32[]{:S(2)}, u32[]{:S(2)}) collective-permute-start(bf16[4,192,256]{2,1,0:T(8,128)(2,1)} %get-tuple-element.23), channel_id=1, source_target_pairs={{0,2},{2,0},{4,6},{6,4},{8,10},{10,8},{12,14},{14,12},{16,18},{18,... | collective-permute-start | bytes 1179656 | tf_op jit(solution)/shard_map/ppermute | solution.py:325
  40.4 21.2 %collective-permute-start.4 = (bf16[4,192,256]{2,1,0:T(8,128)(2,1)S(1)}, bf16[4,192,256]{2,1,0:T(8,128)(2,1)S(1)}, u32[]{:S(2)}, u32[]{:S(2)}) collective-permute-start(bf16[4,192,256]{2,1,0:T(8,128)(2,1)S(1)} %get-tuple-element.22), channel_id=1, source_target_pairs={{0,4},{2,6},{4,0},{6,2},{8,12},{10,14},{12,8},{14,10},{16,20},{18,... | collective-permute-start | bytes 1179656 | tf_op jit(solution)/shard_map/ppermute | solution.py:325
  42.0 19.6 %collective-permute-start.5 = (bf16[4,192,256]{2,1,0:T(8,128)(2,1)S(1)}, bf16[4,192,256]{2,1,0:T(8,128)(2,1)S(1)}, u32[]{:S(2)}, u32[]{:S(2)}) collective-permute-start(bf16[4,192,256]{2,1,0:T(8,128)(2,1)S(1)} %get-tuple-element.21), channel_id=1, source_target_pairs={{0,6},{2,4},{4,2},{6,0},{8,14},{10,12},{12,10},{14,8},{16,22},{18,... | collective-permute-start | bytes 1179656 | tf_op jit(solution)/shard_map/ppermute | solution.py:325
  43.3 3.9 %collective-permute-start = (f32[8,512]{1,0:T(8,128)S(1)}, f32[8,512]{1,0:T(8,128)S(1)}, u32[]{:S(2)}, u32[]{:S(2)}) collective-permute-start(f32[8,512]{1,0:T(8,128)S(1)} %get-tuple-element.11.refs_0_), channel_id=1, source_target_pairs={{0,8},{2,10},{4,12},{6,14},{8,0},{10,2},{12,4},{14,6},{16,24},{18,... | collective-permute-start | bytes 49160 | tf_op jit(solution)/shard_map/ppermute | solution.py:325
  45.5 4.6 %collective-permute-start.1 = (f32[8,512]{1,0:T(8,128)S(1)}, f32[8,512]{1,0:T(8,128)S(1)}, u32[]{:S(2)}, u32[]{:S(2)}) collective-permute-start(f32[8,512]{1,0:T(8,128)S(1)} %get-tuple-element.11.refs_0_), channel_id=1, source_target_pairs={{0,16},{2,18},{4,20},{6,22},{8,24},{10,26},{12,28},{14,30},{16,0},... | collective-permute-start | bytes 49160 | tf_op jit(solution)/shard_map/ppermute | solution.py:325
  47.2 5.5 %collective-permute-start.2 = (f32[8,512]{1,0:T(8,128)S(1)}, f32[8,512]{1,0:T(8,128)S(1)}, u32[]{:S(2)}, u32[]{:S(2)}) collective-permute-start(f32[8,512]{1,0:T(8,128)S(1)} %get-tuple-element.11.refs_0_), channel_id=1, source_target_pairs={{0,24},{2,26},{4,28},{6,30},{8,16},{10,18},{12,20},{14,22},{16,8},... | collective-permute-start | bytes 49160 | tf_op jit(solution)/shard_map/ppermute | solution.py:325
  56.4 1.6 %copy-start = (bf16[4,512,768]{2,1,0:T(8,128)(2,1)}, bf16[4,512,768]{2,1,0:T(8,128)(2,1)S(1)}, u32[]{:S(2)}) copy-start(bf16[4,512,768]{2,1,0:T(8,128)(2,1)S(1)} %choose.1.hits_ref) | copy-start | bytes 9437188
  64.5 24.1 %collective-permute-start.6 = (bf16[4,256,256]{2,1,0:T(8,128)(2,1)S(1)}, bf16[4,256,256]{2,1,0:T(8,128)(2,1)S(1)}, u32[]{:S(2)}, u32[]{:S(2)}) collective-permute-start(bf16[4,256,256]{2,1,0:T(8,128)(2,1)S(1)} %get-tuple-element.14), channel_id=1, source_target_pairs={{0,1},{1,0},{2,3},{3,2},{4,5},{5,4},{6,7},{7,6},{8,9},{9,8},{10,11... | collective-permute-start | bytes 1572872 | tf_op jit(solution)/shard_map/ppermute | solution.py:325
  64.7 12.0 %collective-permute-start.10 = (bf16[4,192,256]{2,1,0:T(8,128)(2,1)S(1)}, bf16[4,192,256]{2,1,0:T(8,128)(2,1)S(1)}, u32[]{:S(2)}, u32[]{:S(2)}) collective-permute-start(bf16[4,192,256]{2,1,0:T(8,128)(2,1)S(1)} %get-tuple-element.27), channel_id=1, source_target_pairs={{0,2},{2,0},{4,6},{6,4},{8,10},{10,8},{12,14},{14,12},{16,18},{18,... | collective-permute-start | bytes 1179656 | tf_op jit(solution)/shard_map/ppermute | solution.py:325
  65.3 18.7 %collective-permute-start.11 = (bf16[4,192,256]{2,1,0:T(8,128)(2,1)S(1)}, bf16[4,192,256]{2,1,0:T(8,128)(2,1)S(1)}, u32[]{:S(2)}, u32[]{:S(2)}) collective-permute-start(bf16[4,192,256]{2,1,0:T(8,128)(2,1)S(1)} %get-tuple-element.26), channel_id=1, source_target_pairs={{0,4},{2,6},{4,0},{6,2},{8,12},{10,14},{12,8},{14,10},{16,20},{18,... | collective-permute-start | bytes 1179656 | tf_op jit(solution)/shard_map/ppermute | solution.py:325
  66.8 18.8 %collective-permute-start.12 = (bf16[4,192,256]{2,1,0:T(8,128)(2,1)S(1)}, bf16[4,192,256]{2,1,0:T(8,128)(2,1)S(1)}, u32[]{:S(2)}, u32[]{:S(2)}) collective-permute-start(bf16[4,192,256]{2,1,0:T(8,128)(2,1)S(1)} %get-tuple-element.25), channel_id=1, source_target_pairs={{0,6},{2,4},{4,2},{6,0},{8,14},{10,12},{12,10},{14,8},{16,22},{18,... | collective-permute-start | bytes 1179656 | tf_op jit(solution)/shard_map/ppermute | solution.py:325
  88.5 4.8 %collective-permute-start.13 = (bf16[4,256,256]{2,1,0:T(8,128)(2,1)S(1)}, bf16[4,256,256]{2,1,0:T(8,128)(2,1)S(1)}, u32[]{:S(2)}, u32[]{:S(2)}) collective-permute-start(bf16[4,256,256]{2,1,0:T(8,128)(2,1)S(1)} %get-tuple-element.16), channel_id=1, source_target_pairs={{0,1},{1,0},{2,3},{3,2},{4,5},{5,4},{6,7},{7,6},{8,9},{9,8},{10,11... | collective-permute-start | bytes 1572872 | tf_op jit(solution)/shard_map/ppermute | solution.py:325
  88.8 8.9 %collective-permute-start.7 = (bf16[256,256]{1,0:T(8,128)(2,1)S(1)}, bf16[256,256]{1,0:T(8,128)(2,1)S(1)}, u32[]{:S(2)}, u32[]{:S(2)}) collective-permute-start(bf16[256,256]{1,0:T(8,128)(2,1)S(1)} %get-tuple-element.29), channel_id=1, source_target_pairs={{0,8},{2,10},{4,12},{6,14},{8,0},{10,2},{12,4},{14,6},{16,24},{18,... | collective-permute-start | bytes 393224 | tf_op jit(solution)/shard_map/ppermute | solution.py:325
  88.9 13.0 %collective-permute-start.8 = (bf16[256,256]{1,0:T(8,128)(2,1)S(1)}, bf16[256,256]{1,0:T(8,128)(2,1)S(1)}, u32[]{:S(2)}, u32[]{:S(2)}) collective-permute-start(bf16[256,256]{1,0:T(8,128)(2,1)S(1)} %get-tuple-element.31), channel_id=1, source_target_pairs={{0,16},{2,18},{4,20},{6,22},{8,24},{10,26},{12,28},{14,30},{16,0},... | collective-permute-start | bytes 393224 | tf_op jit(solution)/shard_map/ppermute | solution.py:325
  91.9 10.0 %collective-permute-start.9 = (bf16[256,256]{1,0:T(8,128)(2,1)S(1)}, bf16[256,256]{1,0:T(8,128)(2,1)S(1)}, u32[]{:S(2)}, u32[]{:S(2)}) collective-permute-start(bf16[256,256]{1,0:T(8,128)(2,1)S(1)} %get-tuple-element.30), channel_id=1, source_target_pairs={{0,24},{2,26},{4,28},{6,30},{8,16},{10,18},{12,20},{14,22},{16,8},... | collective-permute-start | bytes 393224 | tf_op jit(solution)/shard_map/ppermute | solution.py:325
  93.5 19.9 %copy-start.2 = (s32[2,10]{1,0:T(2,128)S(1)}, s32[2,10]{1,0:T(2,128)}, u32[]{:S(2)}) copy-start(s32[2,10]{1,0:T(2,128)} %constant.53.clone) | copy-start | bytes 244
  93.5 9.7 %collective-permute-start.14 = (bf16[256,256]{1,0:T(8,128)(2,1)S(1)}, bf16[256,256]{1,0:T(8,128)(2,1)S(1)}, u32[]{:S(2)}, u32[]{:S(2)}) collective-permute-start(bf16[256,256]{1,0:T(8,128)(2,1)S(1)} %get-tuple-element.32), channel_id=1, source_target_pairs={{0,8},{2,10},{4,12},{6,14},{8,0},{10,2},{12,4},{14,6},{16,24},{18,... | collective-permute-start | bytes 393224 | tf_op jit(solution)/shard_map/ppermute | solution.py:325
  93.6 19.5 %collective-permute-start.15 = (bf16[256,256]{1,0:T(8,128)(2,1)S(1)}, bf16[256,256]{1,0:T(8,128)(2,1)S(1)}, u32[]{:S(2)}, u32[]{:S(2)}) collective-permute-start(bf16[256,256]{1,0:T(8,128)(2,1)S(1)} %get-tuple-element.34), channel_id=1, source_target_pairs={{0,16},{2,18},{4,20},{6,22},{8,24},{10,26},{12,28},{14,30},{16,0},... | collective-permute-start | bytes 393224 | tf_op jit(solution)/shard_map/ppermute | solution.py:325
  97.7 15.5 %collective-permute-start.16 = (bf16[256,256]{1,0:T(8,128)(2,1)S(1)}, bf16[256,256]{1,0:T(8,128)(2,1)S(1)}, u32[]{:S(2)}, u32[]{:S(2)}) collective-permute-start(bf16[256,256]{1,0:T(8,128)(2,1)S(1)} %get-tuple-element.33), channel_id=1, source_target_pairs={{0,24},{2,26},{4,28},{6,30},{8,16},{10,18},{12,20},{14,22},{16,8},... | collective-permute-start | bytes 393224 | tf_op jit(solution)/shard_map/ppermute | solution.py:325
  102.0 11.4 %collective-permute-start.17 = (bf16[256,256]{1,0:T(8,128)(2,1)S(1)}, bf16[256,256]{1,0:T(8,128)(2,1)S(1)}, u32[]{:S(2)}, u32[]{:S(2)}) collective-permute-start(bf16[256,256]{1,0:T(8,128)(2,1)S(1)} %fusion.7), channel_id=1, source_target_pairs={{0,1},{1,0},{2,3},{3,2},{4,5},{5,4},{6,7},{7,6},{8,9},{9,8},{10,11... | collective-permute-start | bytes 393224 | tf_op jit(solution)/shard_map/ppermute | solution.py:325
  113.2 1.4 collective-permute-start.18
  115.6 4.6 %collective-permute-start.19 = (f32[160,128]{1,0:T(8,128)S(1)}, f32[160,128]{1,0:T(8,128)S(1)}, u32[]{:S(2)}, u32[]{:S(2)}) collective-permute-start(f32[160,128]{1,0:T(8,128)S(1)} %get-tuple-element.39), channel_id=1, source_target_pairs={{0,2},{2,0},{4,6},{6,4},{8,10},{10,8},{12,14},{14,12},{16,18},{18,... | collective-permute-start | bytes 245768 | tf_op jit(solution)/shard_map/ppermute | solution.py:325
  116.7 4.5 %collective-permute-start.20 = (f32[160,128]{1,0:T(8,128)S(1)}, f32[160,128]{1,0:T(8,128)S(1)}, u32[]{:S(2)}, u32[]{:S(2)}) collective-permute-start(f32[160,128]{1,0:T(8,128)S(1)} %get-tuple-element.41), channel_id=1, source_target_pairs={{0,4},{2,6},{4,0},{6,2},{8,12},{10,14},{12,8},{14,10},{16,20},{18,... | collective-permute-start | bytes 245768 | tf_op jit(solution)/shard_map/ppermute | solution.py:325
  118.0 5.3 %collective-permute-start.21 = (f32[160,128]{1,0:T(8,128)S(1)}, f32[160,128]{1,0:T(8,128)S(1)}, u32[]{:S(2)}, u32[]{:S(2)}) collective-permute-start(f32[160,128]{1,0:T(8,128)S(1)} %get-tuple-element.40), channel_id=1, source_target_pairs={{0,6},{2,4},{4,2},{6,0},{8,14},{10,12},{12,10},{14,8},{16,22},{18,... | collective-permute-start | bytes 245768 | tf_op jit(solution)/shard_map/ppermute | solution.py:325
  123.4 6.2 %collective-permute-start.22 = (f32[160,128]{1,0:T(8,128)S(1)}, f32[160,128]{1,0:T(8,128)S(1)}, u32[]{:S(2)}, u32[]{:S(2)}) collective-permute-start(f32[160,128]{1,0:T(8,128)S(1)} %add_add_fusion.1), channel_id=1, source_target_pairs={{0,8},{2,10},{4,12},{6,14},{8,0},{10,2},{12,4},{14,6},{16,24},{18,... | collective-permute-start | bytes 245768 | tf_op jit(solution)/shard_map/ppermute | solution.py:325
  126.4 7.8 %collective-permute-start.23 = (f32[160,128]{1,0:T(8,128)S(1)}, f32[160,128]{1,0:T(8,128)S(1)}, u32[]{:S(2)}, u32[]{:S(2)}) collective-permute-start(f32[160,128]{1,0:T(8,128)S(1)} %add_add_fusion.1), channel_id=1, source_target_pairs={{0,16},{2,18},{4,20},{6,22},{8,24},{10,26},{12,28},{14,30},{16,0},... | collective-permute-start | bytes 245768 | tf_op jit(solution)/shard_map/ppermute | solution.py:325
  127.5 6.7 %collective-permute-start.24 = (f32[160,128]{1,0:T(8,128)S(1)}, f32[160,128]{1,0:T(8,128)S(1)}, u32[]{:S(2)}, u32[]{:S(2)}) collective-permute-start(f32[160,128]{1,0:T(8,128)S(1)} %add_add_fusion.1), channel_id=1, source_target_pairs={{0,24},{2,26},{4,28},{6,30},{8,16},{10,18},{12,20},{14,22},{16,8},... | collective-permute-start | bytes 245768 | tf_op jit(solution)/shard_map/ppermute | solution.py:325
  134.2 4.5 %collective-permute-start.25 = (f32[160,128]{1,0:T(8,128)S(1)}, f32[160,128]{1,0:T(8,128)S(1)}, u32[]{:S(2)}, u32[]{:S(2)}) collective-permute-start(f32[160,128]{1,0:T(8,128)S(1)} %add_add_fusion), channel_id=1, source_target_pairs={{0,2},{2,0},{4,6},{6,4},{8,10},{10,8},{12,14},{14,12},{16,18},{18,... | collective-permute-start | bytes 245768 | tf_op jit(solution)/shard_map/ppermute | solution.py:325
  135.2 4.4 %collective-permute-start.26 = (f32[160,128]{1,0:T(8,128)S(1)}, f32[160,128]{1,0:T(8,128)S(1)}, u32[]{:S(2)}, u32[]{:S(2)}) collective-permute-start(f32[160,128]{1,0:T(8,128)S(1)} %add_add_fusion), channel_id=1, source_target_pairs={{0,4},{2,6},{4,0},{6,2},{8,12},{10,14},{12,8},{14,10},{16,20},{18,... | collective-permute-start | bytes 245768 | tf_op jit(solution)/shard_map/ppermute | solution.py:325
  136.2 5.3 %collective-permute-start.27 = (f32[160,128]{1,0:T(8,128)S(1)}, f32[160,128]{1,0:T(8,128)S(1)}, u32[]{:S(2)}, u32[]{:S(2)}) collective-permute-start(f32[160,128]{1,0:T(8,128)S(1)} %add_add_fusion), channel_id=1, source_target_pairs={{0,6},{2,4},{4,2},{6,0},{8,14},{10,12},{12,10},{14,8},{16,22},{18,... | collective-permute-start | bytes 245768 | tf_op jit(solution)/shard_map/ppermute | solution.py:325
  141.6 1.7 %collective-permute-start.28 = (f32[5,128,128]{2,1,0:T(8,128)S(1)}, f32[5,128,128]{2,1,0:T(8,128)S(1)}, u32[]{:S(2)}, u32[]{:S(2)}) collective-permute-start(f32[5,128,128]{2,1,0:T(8,128)S(1)} %bitcast.79), channel_id=1, source_target_pairs={{0,1},{1,0},{2,3},{3,2},{4,5},{5,4},{6,7},{7,6},{8,9},{9,8},{10,11... | collective-permute-start | bytes 983048 | tf_op jit(solution)/shard_map/ppermute | solution.py:325
  (1 other events, 0.7 us)

commit v3 on v2

--- a/solution.py
+++ b/solution.py
@@ -14,14 +14,16 @@
 f32 = jnp.float32
 bf16 = jnp.bfloat16
 lane = 128
-chunk = 256
-vmem_limit = 48 << 20
+chunks = (256, 256)
 
 COLS = (((0,), (0,)), ((), ()))
 
 
-def params(**kw):
-    return pltpu.CompilerParams(vmem_limit_bytes=vmem_limit, **kw)
+small = pl.CostEstimate(flops=1, bytes_accessed=1, transcendentals=0)
+
+
+def params(limit=24 << 20):
+    return pltpu.CompilerParams(vmem_limit_bytes=limit)
 
 
 def whole():
@@ -32,11 +34,12 @@
     return math.gcd(per_dev, 4)
 
 
-def pack_kernel(per_dev, bound, ids_ref, values_ref, send_ref, position_ref):
+def pack_kernel(per_dev, bound, ids_ref, values_ref, send_ref, position_ref, values):
     k_j, s_dev = ids_ref.shape
     n_dp, slots, width = send_ref.shape
     n_ids = n_dp * per_dev
     joint = joint_of(per_dev)
+    values[...] = values_ref[...].astype(f32)
     ids_rows = ids_ref[...]
     padded = jnp.concatenate([ids_rows.astype(f32), jnp.zeros((lane - k_j, s_dev), f32)], axis=0)
     ids_cols = jnp.transpose(padded)
@@ -47,21 +50,21 @@
     )
     earlier = jnp.where(earlier, 1.0, 0.0).astype(bf16)
     used = jnp.zeros((1, n_ids), f32)
-    total = jnp.zeros((n_ids, bound * width), f32)
-    places = []
+    places, by_rank, named_rows = [], [], []
     for k in range(k_j):
         column = ids_cols[:, k : k + 1]
         named = jnp.where(column == numbers, 1.0, 0.0)
         before = jnp.dot(earlier, named.astype(bf16), preferred_element_type=f32) + used
         rank = jnp.sum(named * before, axis=1, keepdims=True)
         used = used + jnp.sum(named, axis=0, keepdims=True)
-        tile = values_ref[:, k * width : (k + 1) * width].astype(f32)
-        by_rank = jnp.concatenate([jnp.where(rank == r, tile, 0.0).astype(bf16) for r in range(bound)], axis=1)
-        named_rows = jnp.where(ids_rows[k : k + 1, :] == number_rows, 1.0, 0.0).astype(bf16)
-        total = total + jnp.dot(named_rows, by_rank, preferred_element_type=f32)
+        tile = values[pl.ds(k, s_dev, stride=k_j), :]
+        by_rank.append(jnp.concatenate([jnp.where(rank == r, tile, 0.0).astype(bf16) for r in range(bound)], axis=1))
+        named_rows.append(jnp.where(ids_rows[k : k + 1, :] == number_rows, 1.0, 0.0).astype(bf16))
         id_col = column.astype(jnp.int32)
         group = id_col // joint
         places.append((group * bound + rank.astype(jnp.int32)) * joint + id_col - group * joint)
+    named_rows, by_rank = jnp.concatenate(named_rows, axis=1), jnp.concatenate(by_rank, axis=0)
+    total = jnp.dot(named_rows, by_rank, preferred_element_type=f32).astype(bf16)
     position = jnp.concatenate(places + [jnp.zeros((s_dev, lane - k_j), jnp.int32)], axis=1).astype(f32)
     position_ref[...] = jnp.transpose(position)[: position_ref.shape[0]]
     slot = lax.broadcasted_iota(jnp.int32, (slots, slots), 0)
@@ -70,10 +73,15 @@
     rank = (slot - group * (joint * bound)) // joint
     block = group * joint + slot % joint
     order = jnp.where(origin == rank * per_dev + block, 1.0, 0.0).astype(bf16)
+    rows = [
+        jnp.concatenate(
+            [total[to * per_dev : (to + 1) * per_dev, r * width : (r + 1) * width] for r in range(bound)], axis=0
+        )
+        for to in range(n_dp)
+    ]
+    out = jnp.dot(order, jnp.concatenate(rows, axis=1), preferred_element_type=f32).astype(bf16)
     for to in range(n_dp):
-        rows = total[to * per_dev : (to + 1) * per_dev, :]
-        rows = jnp.concatenate([rows[:, r * width : (r + 1) * width] for r in range(bound)], axis=0)
-        send_ref[to] = jnp.dot(order, rows.astype(bf16), preferred_element_type=f32).astype(bf16)
+        send_ref[to] = out[:, to * width : (to + 1) * width]
 
 
 def pack(ids, values, n_dp, per_dev, bound):
@@ -86,15 +94,18 @@
         ),
         in_specs=[whole(), whole()],
         out_specs=(whole(), whole()),
+        scratch_shapes=[pltpu.VMEM(values.shape, f32)],
         compiler_params=params(),
         name="pack",
     )(ids, values)
 
 
-def product_kernel(bound, joint, groups, place_ref, tiles_ref, probe_ref, out_ref):
-    inner, outer, unit, width = out_ref.shape
+def product_kernel(bound, joint, groups, place_ref, tiles_ref, probe_ref, *out_refs):
+    inner = len(out_refs)
+    outer, _, width = out_refs[0].shape
     count = inner * outer
     rows = bound * joint
+    unit = groups * bound * joint
     start = pl.multiple_of(pl.program_id(0) * unit, unit)
     place = place_ref[0]
     tiles = [
@@ -113,7 +124,7 @@
         for b in range(outer):
             at = (a * outer + b) * rows
             value = jnp.concatenate([part[at : at + rows] for part in parts], axis=0)
-            out_ref[a, b] = value.astype(bf16)
+            out_refs[a][b, pl.ds(start, unit), :] = value.astype(bf16)
 
 
 def product(place, tiles, probe, inner, bound, first, width):
@@ -124,16 +135,16 @@
     unit = groups * bound * joint
     return pl.pallas_call(
         functools.partial(product_kernel, bound, joint, groups),
-        out_shape=jax.ShapeDtypeStruct((inner, n_dp // inner, slots, width), bf16),
+        out_shape=[jax.ShapeDtypeStruct((n_dp // inner, slots, width), bf16)] * inner,
         grid=(slots // unit,),
         in_specs=[
             pl.BlockSpec(memory_space=pltpu.SMEM),
-            pl.BlockSpec((n_dp, slots, lane), lambda i: (0, 0, 0)),
+            whole(),
             pl.BlockSpec((groups * joint, lane, width), lambda i: (i, 0, first // width)),
         ],
-        out_specs=pl.BlockSpec((inner, n_dp // inner, unit, width), lambda i: (0, 0, i, 0)),
-        compiler_params=params(),
-        cost_estimate=pl.CostEstimate(flops=2 * n_dp * slots * joint * lane * width, bytes_accessed=1 << 22, transcendentals=0),
+        out_specs=[whole()] * inner,
+        compiler_params=params(48 << 20),
+        cost_estimate=small,
         name="product",
     )(place.reshape(1), tiles, probe)
 
@@ -166,39 +177,39 @@
         in_specs=[pl.BlockSpec(memory_space=pltpu.SMEM)] + [whole()] * len(positions),
         out_specs=whole(),
         compiler_params=params(),
-        cost_estimate=pl.CostEstimate(flops=1 << 24, bytes_accessed=1 << 23, transcendentals=0),
+        cost_estimate=small,
         name="choose",
     )(jnp.stack([place, outer_at]), *positions)
 
 
-def gather_kernel(outer, place_ref, hits_ref, *refs):
-    rows_refs, keep_ref, give_ref = refs[:-2], refs[-2], refs[-1]
-    half = keep_ref.shape[1]
-    slots = rows_refs[0].shape[1]
+def gather_kernel(pieces, place_ref, hits_ref, *refs):
+    count = len(pieces)
+    rows_refs, keep_refs, give_refs = refs[: -2 * count], refs[-2 * count : -count], refs[-count:]
+    half = hits_ref.shape[1] // 2
     feat, outer_at = place_ref[0], place_ref[1]
-    for c in range(outer):
-        rows = jnp.concatenate([ref[outer_at ^ c] for ref in rows_refs], axis=0)
-        give = hits_ref[c, pl.ds(pl.multiple_of((1 - feat) * half, half), half), :]
-        give_ref[c] = jnp.dot(give, rows, preferred_element_type=f32).astype(bf16)
-        keep = hits_ref[c, pl.ds(pl.multiple_of(feat * half, half), half), :]
-        keep_ref[c] = jnp.dot(keep, rows, preferred_element_type=f32)
-
-
-def gather(feat, outer_at, hits, rows):
-    outer, s_dev, _ = hits.shape
-    width = rows[0].shape[2]
-    return pl.pallas_call(
-        functools.partial(gather_kernel, outer),
-        out_shape=(
-            jax.ShapeDtypeStruct((outer, s_dev // 2, width), f32),
-            jax.ShapeDtypeStruct((outer, s_dev // 2, width), bf16),
-        ),
+    for piece, keep_ref, give_ref in zip(pieces, keep_refs, give_refs, strict=True):
+        for at, c in enumerate(piece):
+            rows = jnp.concatenate([ref[outer_at ^ c] for ref in rows_refs], axis=0)
+            give = hits_ref[c, pl.ds(pl.multiple_of((1 - feat) * half, half), half), :]
+            give_ref[at] = jnp.dot(give, rows, preferred_element_type=f32).astype(bf16)
+            keep = hits_ref[c, pl.ds(pl.multiple_of(feat * half, half), half), :]
+            keep_ref[at] = jnp.dot(keep, rows, preferred_element_type=f32)
+
+
+def gather(feat, outer_at, hits, rows, pieces):
+    half, width = hits.shape[1] // 2, rows[0].shape[2]
+    shapes = [(len(piece), half, width) for piece in pieces]
+    count = len(pieces)
+    out = pl.pallas_call(
+        functools.partial(gather_kernel, pieces),
+        out_shape=[jax.ShapeDtypeStruct(shape, kind) for kind in (f32, bf16) for shape in shapes],
         in_specs=[pl.BlockSpec(memory_space=pltpu.SMEM)] + [whole()] * (1 + len(rows)),
-        out_specs=(whole(), whole()),
-        compiler_params=params(),
-        cost_estimate=pl.CostEstimate(flops=2 * hits.size * width, bytes_accessed=1 << 23, transcendentals=0),
+        out_specs=[whole()] * (2 * count),
+        compiler_params=params(),
+        cost_estimate=small,
         name="gather",
     )(jnp.stack([feat, outer_at]), hits, *rows)
+    return out[:count], out[count:]
 
 
 def combine_kernel(k_j, position_ref, rows_ref, out_ref):
@@ -249,7 +260,7 @@
     for at in range(gram_ref.shape[0]):
         left = sketch_ref[:, pl.ds(pl.multiple_of(pairs_ref[2 * at] * lane, lane), lane)]
         right = sketch_ref[:, pl.ds(pl.multiple_of(pairs_ref[2 * at + 1] * lane, lane), lane)]
-        gram_ref[at] = lax.dot_general(left, right, COLS, preferred_element_type=f32)
+        gram_ref[at] = lax.dot_general(left, right, COLS, preferred_element_type=f32).astype(bf16)
 
 
 def gram_blocks(sketch, feat):
@@ -260,7 +271,7 @@
     smem = pl.BlockSpec(memory_space=pltpu.SMEM)
     return pl.pallas_call(
         gram_kernel,
-        out_shape=jax.ShapeDtypeStruct((half, lane, lane), f32),
+        out_shape=jax.ShapeDtypeStruct((half, lane, lane), bf16),
         in_specs=[smem, whole()],
         out_specs=whole(),
         compiler_params=params(),
@@ -287,8 +298,8 @@
     half = len(pairs) // 2
     odd = place_ref[0] % 2 == 1
     for at, (i, j) in enumerate(pairs):
-        mine, other = mine_gram_ref[at % half], other_gram_ref[at % half]
-        block = jnp.where(odd, other, mine) if at < half else jnp.where(odd, mine, other)
+        mine, other = mine_gram_ref[at % half].astype(f32), other_gram_ref[at % half].astype(f32)
+        block = jnp.where(odd == (at < half), other, mine)
         gram[i * lane : (i + 1) * lane, j * lane : (j + 1) * lane] = block
         if i != j:
             gram[j * lane : (j + 1) * lane, i * lane : (i + 1) * lane] = jnp.transpose(block)
@@ -325,32 +336,30 @@
     return lax.ppermute(value, axis, [(source, source ^ bits) for source in range(count)])
 
 
+def total_of(values):
+    total = values[0].astype(f32)
+    for value in values[1:]:
+        total = total + value.astype(f32)
+    return total
+
+
 def sum_over_dp(value):
     n_dp = lax.axis_size("dp")
-    index = lax.axis_index("dp")
     inner = math.gcd(n_dp, 4)
+    me = lax.axis_index("dp") & (inner - 1)
     flat = value.reshape(-1, lane)
     rows = flat.shape[0] // inner
-    me = index % inner
-    part = lax.dynamic_slice_in_dim(flat, me * rows, rows, 0)
-    arrived = [
-        crossed(lax.dynamic_slice_in_dim(flat, (me ^ bits) * rows, rows, 0), "dp", bits) for bits in range(1, inner)
-    ]
-    for other in arrived:
-        part = part + other
+    parts = [lax.dynamic_slice_in_dim(flat, (me ^ bits) * rows, rows, 0) for bits in range(inner)]
+    part = total_of([parts[0]] + [crossed(parts[bits], "dp", bits) for bits in range(1, inner)]).astype(bf16)
     if n_dp // inner == 4:
-        arrived = [crossed(part, "dp", bits * inner) for bits in range(1, 4)]
-        for other in arrived:
-            part = part + other
+        part = total_of([part] + [crossed(part, "dp", bits * inner) for bits in range(1, 4)]).astype(bf16)
     else:
         bits = inner
         while bits < n_dp:
-            part = part + crossed(part, "dp", bits)
+            part = total_of([part, crossed(part, "dp", bits)]).astype(bf16)
             bits *= 2
-    pieces = [part] + [crossed(part, "dp", bits) for bits in range(1, inner)]
-    stacked = jnp.stack(pieces)
-    ordered = [stacked[me ^ at] for at in range(inner)]
-    return jnp.concatenate(ordered, axis=0).reshape(value.shape)
+    pieces = jnp.stack([part] + [crossed(part, "dp", bits) for bits in range(1, inner)])
+    return jnp.concatenate([pieces[me ^ at] for at in range(inner)], axis=0).reshape(value.shape)
 
 
 def sketch_by_all_to_all(products, position, k_j):
@@ -375,17 +384,33 @@
     place, outer_at = index % inner, index // inner
     width = probe.shape[2]
     positions = [position] + [crossed(position, "dp", c * inner) for c in range(1, outer)]
+    mine, others, before = [], [], None
+    firsts = [sum(chunks[:at]) for at in range(len(chunks))]
+    sent = [product(place, tiles, probe, inner, bound, first, size) for first, size in zip(firsts, chunks, strict=True)]
+    arrived = [[block[0]] + [crossed(block[a], "dp", a) for a in range(1, inner)] for block in sent]
+    positions, _ = lax.optimization_barrier((positions, sent))
     hits = choose(place, outer_at, positions, k_j, slots, inner)
-    mine, others = [], []
-    for first in range(0, width, chunk):
-        sent = product(place, tiles, probe, inner, bound, first, chunk)
-        rows = [sent[0]] + [crossed(sent[a], "dp", a) for a in range(1, inner)]
-        keep, give = gather(feat, outer_at, hits, rows)
-        plane = keep + crossed(give, "feat", 1).astype(f32)
-        total = plane[0]
-        for c in range(1, outer):
-            total = total + crossed(plane[c].astype(bf16), "dp", c * inner).astype(f32)
-        mine.append(total.astype(bf16))
+    for at, rows in enumerate(arrived):
+        if at > 0:
+            rows, _ = lax.optimization_barrier((rows, before))
+        last = at + 1 == len(sent)
+        pieces = [(3, 2, 1), (0,)] if last else [(c,) for c in range(outer - 1, -1, -1)]
+        keep, give = gather(feat, outer_at, hits, rows, pieces)
+        plane = {}
+        for piece, a, b in zip(pieces, keep, give, strict=True):
+            both = a + crossed(b, "feat", 1).astype(f32)
+            plane.update({c: both[at] for at, c in enumerate(piece)})
+        plane = [plane[c] for c in range(outer)]
+        if not last:
+            size = 1
+            while size < outer:
+                away = [crossed(one.astype(bf16), "dp", size * inner) for one in plane[1::2]]
+                plane = [total_of(pair) for pair in zip(plane[0::2], away, strict=True)]
+                size *= 2
+            plane = before = plane[0]
+        else:
+            plane = total_of([plane[0]] + [crossed(plane[c].astype(bf16), "dp", c * inner) for c in range(1, outer)])
+        mine.append(plane.astype(bf16))
         others.append(crossed(mine[-1], "feat", 1))
     mine, others = jnp.concatenate(mine, axis=1), jnp.concatenate(others, axis=1)
     return mine, jnp.concatenate([mine, others], axis=0)
@@ -401,7 +426,7 @@
     b_slice = per_dev * n_dp
     bound = max(2, 3 * s_dev * k_j // (2 * b_slice))
     probe = probe[:, 0]
-    send, position = pack(block_ids[0].T, values.reshape(s_dev, k_j * b_width), n_dp, per_dev, bound)
+    send, position = pack(block_ids[0].T, values.reshape(s_dev * k_j, b_width), n_dp, per_dev, bound)
     tiles = lax.all_to_all(send, "dp", split_axis=0, concat_axis=0, tiled=True)
     if n_feat == 2 and n_dp == 16:
         mine, sketch = sketch_by_planes(tiles, probe, position, 4, bound, k_j)

time: 152 us -> 134 us (0.88)
  waiting for transfers between devices: 72.7 us -> 58.5 us
  local copies, waits for them, and re-layouts: 4.58 us -> 1.82 us
  Pallas kernels: 31 us -> 28.4 us
  starting transfers between devices: 41.9 us -> 43.5 us
    ppermute x29 -> x33, waiting for transfers between devices: 53 us -> 38.8 us  [crossed(): lax.ppermute(value, axis, [(source, source ^ bits) for source in range(co...]
    pallas_call x2, Pallas kernels: 5.76 us -> 3.04 us  [gather(): pl.pallas_call(functools.partial(gather_kernel, pieces), out_shape=[jax.S...]
    unnamed x7 -> x6, local copies, waits for them, and re-layouts: 3.45 us -> 1.74 us
    ppermute x29 -> x33, starting transfers between devices: 33.6 us -> 35.2 us  [crossed(): lax.ppermute(value, axis, [(source, source ^ bits) for source in range(co...]
  transfers between devices with their start and end apart: 30 -> 34, of which waited for: 21 -> 20; matrix products, arithmetic and copies ran while one was open for 1% -> 0% of each run, Pallas kernels for 7% -> 5%
where the time goes in v3:
time: 134 us; the launch traced here: 133 us
  waiting for transfers between devices  58.5 us (44%)
  starting transfers between devices  43.5 us (32%)
  Pallas kernels  28.4 us (21%)
  local copies, waits for them, and re-layouts  1.82 us (1%)
    ppermute x33, waiting for transfers between devices, crossed(): lax.ppermute(value, axis, [(source, source ^ bits) for source in range(co...  38.8 us
    ppermute x33, starting transfers between devices, crossed(): lax.ppermute(value, axis, [(source, source ^ bits) for source in range(co...  35.2 us
    all_to_all x1, waiting for transfers between devices, local(): tiles = lax.all_to_all(send, 'dp', split_axis=0, concat_axis=0, tiled=True)  19.7 us
    all_to_all x1, starting transfers between devices, local(): tiles = lax.all_to_all(send, 'dp', split_axis=0, concat_axis=0, tiled=True)  8.31 us
    pallas_call x1, Pallas kernels, whiten(): pl.pallas_call(functools.partial(root_kernel, samples), out_shape=jax.Sha...  8.05 us
    pallas_call x2, Pallas kernels, product(): pl.pallas_call(functools.partial(product_kernel, bound, joint, groups), o...  7.42 us
    pallas_call x1, Pallas kernels, pack(): pl.pallas_call(functools.partial(pack_kernel, per_dev, bound), out_shape=...  5.26 us
    pallas_call x1, Pallas kernels, choose(): pl.pallas_call(functools.partial(choose_kernel, k_j, slots, inner), out_s...  3.73 us
  transfers between devices with their start and end apart: 34, of which 20 were waited for; matrix products, arithmetic and copies ran while one was open for 0% of the time, Pallas kernels for 5%

profile of v3, /device:TPU:0, one launch (start us, length us, event | category | flops | bytes accessed | tf_op | source)
XLA Modules:
  0.0 133.2 jit_solution(9255176423838861908)
XLA Ops:
  1.7 5.3 %pack.1 = (bf16[16,192,128]{2,1,0:T(8,128)(2,1)}, f32[8,512]{1,0:T(8,128)S(1)}) custom-call(s32[4,512]{1,0:T(4,128)S(1)} %bitcast.55, bf16[2048,128]{1,0:T(8,128)(2,1)S(1)} %bitcast.54), custom_call_target="tpu_custom_call" | custom-call | tf_op jit(solution)/shard_map/pack/pallas_call | solution.py:89
  7.0 8.3 %all-to-all-start = ((bf16[16,192,128]{2,1,0:T(8,128)(2,1)}), bf16[16,192,128]{2,1,0:T(8,128)(2,1)S(1)}, u32[]{:S(2)}, u32[]{:S(2)}) async-start(bf16[16,192,128]{2,1,0:T(8,128)(2,1)} %get-tuple-element.36), calls=%async_computation | async-start | bytes 1572864 | tf_op jit(solution)/shard_map/all_to_all | solution.py:430
  15.3 19.7 %all-to-all-done.tiles_ref = bf16[16,192,128]{2,1,0:T(8,128)(2,1)S(1)} async-done(((bf16[16,192,128]{2,1,0:T(8,128)(2,1)}), bf16[16,192,128]{2,1,0:T(8,128)(2,1)S(1)}, u32[]{:S(2)}, u32[]{:S(2)}) %all-to-all-start) | async-done | bytes 786464 | tf_op jit(solution)/shard_map/all_to_all | solution.py:430
  35.1 4.0 %product.2 = (bf16[4,192,256]{2,1,0:T(8,128)(2,1)S(1)}, bf16[4,192,256]{2,1,0:T(8,128)(2,1)}, bf16[4,192,256]{2,1,0:T(8,128)(2,1)S(1)}, bf16[4,192,256]{2,1,0:T(8,128)(2,1)S(1)}) custom-call(s32[1]{0:T(128)} %bitcast.3.place_ref, bf16[16,192,128]{2,1,0:T(8,128)(2,1)S(1)} %all-to-all-done.tiles_ref, bf16[32,128,512]{2,1,0:T(8,128)(2,1)} %bitcast.56), custom_call_target="tpu_custom_call" | custom-call | flops 1 | bytes 1 | tf_op jit(solution)/shard_map/product/pallas_call | solution.py:136
  39.6 1.6 %collective-permute-start.4 = (bf16[4,192,256]{2,1,0:T(8,128)(2,1)S(1)}, bf16[4,192,256]{2,1,0:T(8,128)(2,1)S(1)}, u32[]{:S(2)}, u32[]{:S(2)}) collective-permute-start(bf16[4,192,256]{2,1,0:T(8,128)(2,1)S(1)} %get-tuple-element.39), channel_id=1, source_target_pairs={{0,4},{2,6},{4,0},{6,2},{8,12},{10,14},{12,8},{14,10},{16,20},{18,... | collective-permute-start | bytes 1179656 | tf_op jit(solution)/shard_map/ppermute | solution.py:336
  42.5 2.1 %collective-permute-start = (f32[8,512]{1,0:T(8,128)S(1)}, f32[8,512]{1,0:T(8,128)S(1)}, u32[]{:S(2)}, u32[]{:S(2)}) collective-permute-start(f32[8,512]{1,0:T(8,128)S(1)} %get-tuple-element.45.refs_0_), channel_id=1, source_target_pairs={{0,8},{2,10},{4,12},{6,14},{8,0},{10,2},{12,4},{14,6},{16,24},{18,... | collective-permute-start | bytes 49160 | tf_op jit(solution)/shard_map/ppermute | solution.py:336
  46.4 2.0 %collective-permute-start.2 = (f32[8,512]{1,0:T(8,128)S(1)}, f32[8,512]{1,0:T(8,128)S(1)}, u32[]{:S(2)}, u32[]{:S(2)}) collective-permute-start(f32[8,512]{1,0:T(8,128)S(1)} %get-tuple-element.45.refs_0_), channel_id=1, source_target_pairs={{0,24},{2,26},{4,28},{6,30},{8,16},{10,18},{12,20},{14,22},{16,8},... | collective-permute-start | bytes 49160 | tf_op jit(solution)/shard_map/ppermute | solution.py:336
  48.4 3.5 %product.3 = (bf16[4,192,256]{2,1,0:T(8,128)(2,1)S(1)}, bf16[4,192,256]{2,1,0:T(8,128)(2,1)S(1)}, bf16[4,192,256]{2,1,0:T(8,128)(2,1)S(1)}, bf16[4,192,256]{2,1,0:T(8,128)(2,1)S(1)}) custom-call(s32[1]{0:T(128)} %bitcast.3.place_ref, bf16[16,192,128]{2,1,0:T(8,128)(2,1)S(1)} %all-to-all-done.tiles_ref, bf16[32,128,512]{2,1,0:T(8,128)(2,1)} %bitcast.57), custom_call_target="tpu_custom_call" | custom-call | flops 1 | bytes 1 | tf_op jit(solution)/shard_map/product/pallas_call | solution.py:136
  51.9 3.7 %choose.1.hits_ref = bf16[4,512,768]{2,1,0:T(8,128)(2,1)S(1)} custom-call(s32[2]{0:T(128)S(1)} %pad_add_fusion.1.place_ref, f32[8,512]{1,0:T(8,128)S(1)} %get-tuple-element.45.refs_0_, f32[8,512]{1,0:T(8,128)S(1)} %collective-permute-done.refs_1_, f32[8,512]{1,0:T(8,128)S(1)} %collective-permute-done.1.refs_2_, f32[8,512]{1,0:T(8,128)S(1)} %collective-permute-done.2.refs_3_), custom_call_target="tpu_custom_call" | custom-call | flops 1 | bytes 1 | tf_op jit(solution)/shard_map/choose/pallas_call | solution.py:174
  55.7 1.8 %collective-permute-done.5.refs_3_ = bf16[4,192,256]{2,1,0:T(8,128)(2,1)S(1)} collective-permute-done((bf16[4,192,256]{2,1,0:T(8,128)(2,1)S(1)}, bf16[4,192,256]{2,1,0:T(8,128)(2,1)S(1)}, u32[]{:S(2)}, u32[]{:S(2)}) %collective-permute-start.5) | collective-permute-done | bytes 393248 | tf_op jit(solution)/shard_map/ppermute | solution.py:336
  57.4 1.5 %gather.2 = (f32[1,256,256]{2,1,0:T(8,128)S(1)}, f32[1,256,256]{2,1,0:T(8,128)S(1)}, f32[1,256,256]{2,1,0:T(8,128)S(1)}, f32[1,256,256]{2,1,0:T(8,128)S(1)}, bf1...) custom-call(s32[2]{0:T(128)S(1)} %pad_add_fusion.place_ref, ...), custom_call_target="tpu_custom_call" | custom-call | flops 1 | bytes 1 | tf_op jit(solution)/shard_map/gather/pallas_call | solution.py:203
  59.7 1.5 %collective-permute-start.14 = (bf16[4,192,256]{2,1,0:T(8,128)(2,1)S(1)}, bf16[4,192,256]{2,1,0:T(8,128)(2,1)S(1)}, u32[]{:S(2)}, u32[]{:S(2)}) collective-permute-start(bf16[4,192,256]{2,1,0:T(8,128)(2,1)S(1)} %get-tuple-element.43), channel_id=1, source_target_pairs={{0,4},{2,6},{4,0},{6,2},{8,12},{10,14},{12,8},{14,10},{16,20},{18,... | collective-permute-start | bytes 1179656 | tf_op jit(solution)/shard_map/ppermute | solution.py:336
  64.0 2.7 %collective-permute-start.11 = (bf16[256,256]{1,0:T(8,128)(2,1)S(1)}, bf16[256,256]{1,0:T(8,128)(2,1)S(1)}, u32[]{:S(2)}, u32[]{:S(2)}) collective-permute-start(bf16[256,256]{1,0:T(8,128)(2,1)S(1)} %fusion.6), channel_id=1, source_target_pairs={{0,8},{2,10},{4,12},{6,14},{8,0},{10,2},{12,4},{14,6},{16,24},{18,... | collective-permute-start | bytes 393224 | tf_op jit(solution)/shard_map/ppermute | solution.py:336
  66.8 3.7 %collective-permute-done.11 = bf16[256,256]{1,0:T(8,128)(2,1)S(1)} collective-permute-done((bf16[256,256]{1,0:T(8,128)(2,1)S(1)}, bf16[256,256]{1,0:T(8,128)(2,1)S(1)}, u32[]{:S(2)}, u32[]{:S(2)}) %collective-permute-start.11) | collective-permute-done | bytes 131104 | tf_op jit(solution)/shard_map/ppermute | solution.py:336
  70.4 1.7 %collective-permute-start.8 = (bf16[256,256]{1,0:T(8,128)(2,1)S(1)}, bf16[256,256]{1,0:T(8,128)(2,1)S(1)}, u32[]{:S(2)}, u32[]{:S(2)}) collective-permute-start(bf16[256,256]{1,0:T(8,128)(2,1)S(1)} %fusion.5), channel_id=1, source_target_pairs={{0,8},{2,10},{4,12},{6,14},{8,0},{10,2},{12,4},{14,6},{16,24},{18,... | collective-permute-start | bytes 393224 | tf_op jit(solution)/shard_map/ppermute | solution.py:336
  73.6 2.7 %collective-permute-done.8 = bf16[256,256]{1,0:T(8,128)(2,1)S(1)} collective-permute-done((bf16[256,256]{1,0:T(8,128)(2,1)S(1)}, bf16[256,256]{1,0:T(8,128)(2,1)S(1)}, u32[]{:S(2)}, u32[]{:S(2)}) %collective-permute-start.8) | collective-permute-done | bytes 131104 | tf_op jit(solution)/shard_map/ppermute | solution.py:336
  76.3 4.1 %collective-permute-done.12 = bf16[256,256]{1,0:T(8,128)(2,1)S(1)} collective-permute-done((bf16[256,256]{1,0:T(8,128)(2,1)S(1)}, bf16[256,256]{1,0:T(8,128)(2,1)S(1)}, u32[]{:S(2)}, u32[]{:S(2)}) %collective-permute-start.12) | collective-permute-done | bytes 131104 | tf_op jit(solution)/shard_map/ppermute | solution.py:336
  80.6 1.5 %gather.3 = (f32[3,256,256]{2,1,0:T(8,128)S(1)}, f32[1,256,256]{2,1,0:T(8,128)S(1)}, bf16[3,256,256]{2,1,0:T(8,128)(2,1)S(1)}, bf16[1,256,256]{2,1,0:T(8,128)(2,1)S(1)}) custom-call(s32[2]{0:T(128)S(1)} %pad_add_fusion.place_ref, bf16[4,512,768]{2,1,0:T(8,128)(2,1)S(1)} %choose.1.hits_ref, bf16[4,192,256]{2,1,0:T(8,128)(2,1)S(1)} %get-tuple-element.57.refs_0_, ...), custom_call_target="tpu_custom_call" | custom-call | flops 1 | bytes 1 | tf_op jit(solution)/shard_map/gather/pallas_call | solution.py:203
  84.0 1.5 %collective-permute-start.18 = (bf16[256,256]{1,0:T(8,128)(2,1)S(1)}, bf16[256,256]{1,0:T(8,128)(2,1)S(1)}, u32[]{:S(2)}, u32[]{:S(2)}) collective-permute-start(bf16[256,256]{1,0:T(8,128)(2,1)S(1)} %get-tuple-element.65), channel_id=1, source_target_pairs={{0,8},{2,10},{4,12},{6,14},{8,0},{10,2},{12,4},{14,6},{16,24},{18,... | collective-permute-start | bytes 393224 | tf_op jit(solution)/shard_map/ppermute | solution.py:336
  86.9 1.6 %collective-permute-start.20 = (bf16[256,256]{1,0:T(8,128)(2,1)S(1)}, bf16[256,256]{1,0:T(8,128)(2,1)S(1)}, u32[]{:S(2)}, u32[]{:S(2)}) collective-permute-start(bf16[256,256]{1,0:T(8,128)(2,1)S(1)} %get-tuple-element.66), channel_id=1, source_target_pairs={{0,24},{2,26},{4,28},{6,30},{8,16},{10,18},{12,20},{14,22},{16,8},... | collective-permute-start | bytes 393224 | tf_op jit(solution)/shard_map/ppermute | solution.py:336
  88.5 2.9 %collective-permute-done.18 = bf16[256,256]{1,0:T(8,128)(2,1)S(1)} collective-permute-done((bf16[256,256]{1,0:T(8,128)(2,1)S(1)}, bf16[256,256]{1,0:T(8,128)(2,1)S(1)}, u32[]{:S(2)}, u32[]{:S(2)}) %collective-permute-start.18) | collective-permute-done | bytes 131104 | tf_op jit(solution)/shard_map/ppermute | solution.py:336
  91.4 7.0 %collective-permute-done.19 = bf16[256,256]{1,0:T(8,128)(2,1)S(1)} collective-permute-done((bf16[256,256]{1,0:T(8,128)(2,1)S(1)}, bf16[256,256]{1,0:T(8,128)(2,1)S(1)}, u32[]{:S(2)}, u32[]{:S(2)}) %collective-permute-start.19) | collective-permute-done | bytes 131104 | tf_op jit(solution)/shard_map/ppermute | solution.py:336
  100.9 1.5 %collective-permute-start.23 = (bf16[160,128]{1,0:T(8,128)(2,1)S(1)}, bf16[160,128]{1,0:T(8,128)(2,1)S(1)}, u32[]{:S(2)}, u32[]{:S(2)}) collective-permute-start(bf16[160,128]{1,0:T(8,128)(2,1)S(1)} %get-tuple-element.72), channel_id=1, source_target_pairs={{0,2},{2,0},{4,6},{6,4},{8,10},{10,8},{12,14},{14,12},{16,18},{18,... | collective-permute-start | bytes 122888 | tf_op jit(solution)/shard_map/ppermute | solution.py:336
  103.1 1.4 %collective-permute-start.25 = (bf16[160,128]{1,0:T(8,128)(2,1)S(1)}, bf16[160,128]{1,0:T(8,128)(2,1)S(1)}, u32[]{:S(2)}, u32[]{:S(2)}) collective-permute-start(bf16[160,128]{1,0:T(8,128)(2,1)S(1)} %get-tuple-element.73), channel_id=1, source_target_pairs={{0,6},{2,4},{4,2},{6,0},{8,14},{10,12},{12,10},{14,8},{16,22},{18,... | collective-permute-start | bytes 122888 | tf_op jit(solution)/shard_map/ppermute | solution.py:336
  105.0 1.9 %collective-permute-done.24 = bf16[160,128]{1,0:T(8,128)(2,1)S(1)} collective-permute-done((bf16[160,128]{1,0:T(8,128)(2,1)S(1)}, bf16[160,128]{1,0:T(8,128)(2,1)S(1)}, u32[]{:S(2)}, u32[]{:S(2)}) %collective-permute-start.24) | collective-permute-done | bytes 40992 | tf_op jit(solution)/shard_map/ppermute | solution.py:336
  108.0 2.4 %collective-permute-start.26 = (bf16[160,128]{1,0:T(8,128)(2,1)S(1)}, bf16[160,128]{1,0:T(8,128)(2,1)S(1)}, u32[]{:S(2)}, u32[]{:S(2)}) collective-permute-start(bf16[160,128]{1,0:T(8,128)(2,1)S(1)} %add_convert_fusion.4), channel_id=1, source_target_pairs={{0,8},{2,10},{4,12},{6,14},{8,0},{10,2},{12,4},{14,6},{16,24},{18,... | collective-permute-start | bytes 122888 | tf_op jit(solution)/shard_map/ppermute | solution.py:336
  110.7 2.1 %collective-permute-start.28 = (bf16[160,128]{1,0:T(8,128)(2,1)S(1)}, bf16[160,128]{1,0:T(8,128)(2,1)S(1)}, u32[]{:S(2)}, u32[]{:S(2)}) collective-permute-start(bf16[160,128]{1,0:T(8,128)(2,1)S(1)} %add_convert_fusion.4), channel_id=1, source_target_pairs={{0,24},{2,26},{4,28},{6,30},{8,16},{10,18},{12,20},{14,22},{16,8},... | collective-permute-start | bytes 122888 | tf_op jit(solution)/shard_map/ppermute | solution.py:336
  112.8 2.5 %collective-permute-done.27 = bf16[160,128]{1,0:T(8,128)(2,1)S(1)} collective-permute-done((bf16[160,128]{1,0:T(8,128)(2,1)S(1)}, bf16[160,128]{1,0:T(8,128)(2,1)S(1)}, u32[]{:S(2)}, u32[]{:S(2)}) %collective-permute-start.27) | collective-permute-done | bytes 40992 | tf_op jit(solution)/shard_map/ppermute | solution.py:336
  116.5 1.5 %collective-permute-start.29 = (bf16[160,128]{1,0:T(8,128)(2,1)S(1)}, bf16[160,128]{1,0:T(8,128)(2,1)S(1)}, u32[]{:S(2)}, u32[]{:S(2)}) collective-permute-start(bf16[160,128]{1,0:T(8,128)(2,1)S(1)} %add_convert_fusion.3), channel_id=1, source_target_pairs={{0,2},{2,0},{4,6},{6,4},{8,10},{10,8},{12,14},{14,12},{16,18},{18,... | collective-permute-start | bytes 122888 | tf_op jit(solution)/shard_map/ppermute | solution.py:336
  120.6 1.5 %collective-permute-done.30 = bf16[160,128]{1,0:T(8,128)(2,1)S(1)} collective-permute-done((bf16[160,128]{1,0:T(8,128)(2,1)S(1)}, bf16[160,128]{1,0:T(8,128)(2,1)S(1)}, u32[]{:S(2)}, u32[]{:S(2)}) %collective-permute-start.30) | collective-permute-done | bytes 40992 | tf_op jit(solution)/shard_map/ppermute | solution.py:336
  122.1 1.5 %collective-permute-done.31 = bf16[160,128]{1,0:T(8,128)(2,1)S(1)} collective-permute-done((bf16[160,128]{1,0:T(8,128)(2,1)S(1)}, bf16[160,128]{1,0:T(8,128)(2,1)S(1)}, u32[]{:S(2)}, u32[]{:S(2)}) %collective-permute-start.31) | collective-permute-done | bytes 40992 | tf_op jit(solution)/shard_map/ppermute | solution.py:336
  125.2 8.0 %root.1 = f32[256,512]{1,0:T(8,128)} custom-call(s32[1]{0:T(128)} %bitcast.place_ref, bf16[5,128,128]{2,1,0:T(8,128)(2,1)S(1)} %bitcast.53, bf16[5,128,128]{2,1,0:T(8,128)(2,1)S(1)} %collective-permute-done.32.other_gram_ref, bf16[256,512]{1,0:T(8,128)(2,1)S(1)} %pad_maximum_fusion.mine_ref), custom_call_target="tpu_custom_call" | custom-call | tf_op jit(solution)/shard_map/root/pallas_call | solution.py:323
  (68 shorter events, 24.0 us)
Async XLA Ops:
  7.0 28.1 %all-to-all-start = ((bf16[16,192,128]{2,1,0:T(8,128)(2,1)}), bf16[16,192,128]{2,1,0:T(8,128)(2,1)S(1)}, u32[]{:S(2)}, u32[]{:S(2)}) async-start(bf16[16,192,128]{2,1,0:T(8,128)(2,1)} %get-tuple-element.36), calls=%async_computation | async-start | bytes 1572864 | tf_op jit(solution)/shard_map/all_to_all | solution.py:430
  39.0 16.6 %collective-permute-start.3 = (bf16[4,192,256]{2,1,0:T(8,128)(2,1)}, bf16[4,192,256]{2,1,0:T(8,128)(2,1)S(1)}, u32[]{:S(2)}, u32[]{:S(2)}) collective-permute-start(bf16[4,192,256]{2,1,0:T(8,128)(2,1)} %get-tuple-element.38), channel_id=1, source_target_pairs={{0,2},{2,0},{4,6},{6,4},{8,10},{10,8},{12,14},{14,12},{16,18},{18,... | collective-permute-start | bytes 1179656 | tf_op jit(solution)/shard_map/ppermute | solution.py:336
  39.6 16.1 %collective-permute-start.4 = (bf16[4,192,256]{2,1,0:T(8,128)(2,1)S(1)}, bf16[4,192,256]{2,1,0:T(8,128)(2,1)S(1)}, u32[]{:S(2)}, u32[]{:S(2)}) collective-permute-start(bf16[4,192,256]{2,1,0:T(8,128)(2,1)S(1)} %get-tuple-element.39), channel_id=1, source_target_pairs={{0,4},{2,6},{4,0},{6,2},{8,12},{10,14},{12,8},{14,10},{16,20},{18,... | collective-permute-start | bytes 1179656 | tf_op jit(solution)/shard_map/ppermute | solution.py:336
  41.2 16.2 %collective-permute-start.5 = (bf16[4,192,256]{2,1,0:T(8,128)(2,1)S(1)}, bf16[4,192,256]{2,1,0:T(8,128)(2,1)S(1)}, u32[]{:S(2)}, u32[]{:S(2)}) collective-permute-start(bf16[4,192,256]{2,1,0:T(8,128)(2,1)S(1)} %get-tuple-element.40), channel_id=1, source_target_pairs={{0,6},{2,4},{4,2},{6,0},{8,14},{10,12},{12,10},{14,8},{16,22},{18,... | collective-permute-start | bytes 1179656 | tf_op jit(solution)/shard_map/ppermute | solution.py:336
  42.5 3.9 %collective-permute-start = (f32[8,512]{1,0:T(8,128)S(1)}, f32[8,512]{1,0:T(8,128)S(1)}, u32[]{:S(2)}, u32[]{:S(2)}) collective-permute-start(f32[8,512]{1,0:T(8,128)S(1)} %get-tuple-element.45.refs_0_), channel_id=1, source_target_pairs={{0,8},{2,10},{4,12},{6,14},{8,0},{10,2},{12,4},{14,6},{16,24},{18,... | collective-permute-start | bytes 49160 | tf_op jit(solution)/shard_map/ppermute | solution.py:336
  44.7 7.2 %collective-permute-start.1 = (f32[8,512]{1,0:T(8,128)S(1)}, f32[8,512]{1,0:T(8,128)S(1)}, u32[]{:S(2)}, u32[]{:S(2)}) collective-permute-start(f32[8,512]{1,0:T(8,128)S(1)} %get-tuple-element.45.refs_0_), channel_id=1, source_target_pairs={{0,16},{2,18},{4,20},{6,22},{8,24},{10,26},{12,28},{14,30},{16,0},... | collective-permute-start | bytes 49160 | tf_op jit(solution)/shard_map/ppermute | solution.py:336
  46.4 5.5 %collective-permute-start.2 = (f32[8,512]{1,0:T(8,128)S(1)}, f32[8,512]{1,0:T(8,128)S(1)}, u32[]{:S(2)}, u32[]{:S(2)}) collective-permute-start(f32[8,512]{1,0:T(8,128)S(1)} %get-tuple-element.45.refs_0_), channel_id=1, source_target_pairs={{0,24},{2,26},{4,28},{6,30},{8,16},{10,18},{12,20},{14,22},{16,8},... | collective-permute-start | bytes 49160 | tf_op jit(solution)/shard_map/ppermute | solution.py:336
  59.0 3.6 %collective-permute-start.10 = (bf16[1,256,256]{2,1,0:T(8,128)(2,1)S(1)}, bf16[1,256,256]{2,1,0:T(8,128)(2,1)S(1)}, u32[]{:S(2)}, u32[]{:S(2)}) collective-permute-start(bf16[1,256,256]{2,1,0:T(8,128)(2,1)S(1)} %get-tuple-element.56), channel_id=1, source_target_pairs={{0,1},{1,0},{2,3},{3,2},{4,5},{5,4},{6,7},{7,6},{8,9},{9,8},{10,11... | collective-permute-start | bytes 393224 | tf_op jit(solution)/shard_map/ppermute | solution.py:336
  59.1 21.5 %collective-permute-start.13 = (bf16[4,192,256]{2,1,0:T(8,128)(2,1)S(1)}, bf16[4,192,256]{2,1,0:T(8,128)(2,1)S(1)}, u32[]{:S(2)}, u32[]{:S(2)}) collective-permute-start(bf16[4,192,256]{2,1,0:T(8,128)(2,1)S(1)} %get-tuple-element.42), channel_id=1, source_target_pairs={{0,2},{2,0},{4,6},{6,4},{8,10},{10,8},{12,14},{14,12},{16,18},{18,... | collective-permute-start | bytes 1179656 | tf_op jit(solution)/shard_map/ppermute | solution.py:336
  59.7 20.9 %collective-permute-start.14 = (bf16[4,192,256]{2,1,0:T(8,128)(2,1)S(1)}, bf16[4,192,256]{2,1,0:T(8,128)(2,1)S(1)}, u32[]{:S(2)}, u32[]{:S(2)}) collective-permute-start(bf16[4,192,256]{2,1,0:T(8,128)(2,1)S(1)} %get-tuple-element.43), channel_id=1, source_target_pairs={{0,4},{2,6},{4,0},{6,2},{8,12},{10,14},{12,8},{14,10},{16,20},{18,... | collective-permute-start | bytes 1179656 | tf_op jit(solution)/shard_map/ppermute | solution.py:336
  61.2 19.3 %collective-permute-start.15 = (bf16[4,192,256]{2,1,0:T(8,128)(2,1)S(1)}, bf16[4,192,256]{2,1,0:T(8,128)(2,1)S(1)}, u32[]{:S(2)}, u32[]{:S(2)}) collective-permute-start(bf16[4,192,256]{2,1,0:T(8,128)(2,1)S(1)} %get-tuple-element.44), channel_id=1, source_target_pairs={{0,6},{2,4},{4,2},{6,0},{8,14},{10,12},{12,10},{14,8},{16,22},{18,... | collective-permute-start | bytes 1179656 | tf_op jit(solution)/shard_map/ppermute | solution.py:336
  62.6 4.1 %collective-permute-start.9 = (bf16[1,256,256]{2,1,0:T(8,128)(2,1)S(1)}, bf16[1,256,256]{2,1,0:T(8,128)(2,1)S(1)}, u32[]{:S(2)}, u32[]{:S(2)}) collective-permute-start(bf16[1,256,256]{2,1,0:T(8,128)(2,1)S(1)} %get-tuple-element.54), channel_id=1, source_target_pairs={{0,1},{1,0},{2,3},{3,2},{4,5},{5,4},{6,7},{7,6},{8,9},{9,8},{10,11... | collective-permute-start | bytes 393224 | tf_op jit(solution)/shard_map/ppermute | solution.py:336
  64.0 6.5 %collective-permute-start.11 = (bf16[256,256]{1,0:T(8,128)(2,1)S(1)}, bf16[256,256]{1,0:T(8,128)(2,1)S(1)}, u32[]{:S(2)}, u32[]{:S(2)}) collective-permute-start(bf16[256,256]{1,0:T(8,128)(2,1)S(1)} %fusion.6), channel_id=1, source_target_pairs={{0,8},{2,10},{4,12},{6,14},{8,0},{10,2},{12,4},{14,6},{16,24},{18,... | collective-permute-start | bytes 393224 | tf_op jit(solution)/shard_map/ppermute | solution.py:336
  66.7 5.6 %collective-permute-start.6 = (bf16[1,256,256]{2,1,0:T(8,128)(2,1)S(1)}, bf16[1,256,256]{2,1,0:T(8,128)(2,1)S(1)}, u32[]{:S(2)}, u32[]{:S(2)}) collective-permute-start(bf16[1,256,256]{2,1,0:T(8,128)(2,1)S(1)} %get-tuple-element.50), channel_id=1, source_target_pairs={{0,1},{1,0},{2,3},{3,2},{4,5},{5,4},{6,7},{7,6},{8,9},{9,8},{10,11... | collective-permute-start | bytes 393224 | tf_op jit(solution)/shard_map/ppermute | solution.py:336
  70.4 5.9 %collective-permute-start.8 = (bf16[256,256]{1,0:T(8,128)(2,1)S(1)}, bf16[256,256]{1,0:T(8,128)(2,1)S(1)}, u32[]{:S(2)}, u32[]{:S(2)}) collective-permute-start(bf16[256,256]{1,0:T(8,128)(2,1)S(1)} %fusion.5), channel_id=1, source_target_pairs={{0,8},{2,10},{4,12},{6,14},{8,0},{10,2},{12,4},{14,6},{16,24},{18,... | collective-permute-start | bytes 393224 | tf_op jit(solution)/shard_map/ppermute | solution.py:336
  72.2 8.2 %collective-permute-start.12 = (bf16[256,256]{1,0:T(8,128)(2,1)S(1)}, bf16[256,256]{1,0:T(8,128)(2,1)S(1)}, u32[]{:S(2)}, u32[]{:S(2)}) collective-permute-start(bf16[256,256]{1,0:T(8,128)(2,1)S(1)} %fusion.3), channel_id=1, source_target_pairs={{0,16},{2,18},{4,20},{6,22},{8,24},{10,26},{12,28},{14,30},{16,0},... | collective-permute-start | bytes 393224 | tf_op jit(solution)/shard_map/ppermute | solution.py:336
  82.1 1.8 %collective-permute-start.17 = (bf16[3,256,256]{2,1,0:T(8,128)(2,1)S(1)}, bf16[3,256,256]{2,1,0:T(8,128)(2,1)S(1)}, u32[]{:S(2)}, u32[]{:S(2)}) collective-permute-start(bf16[3,256,256]{2,1,0:T(8,128)(2,1)S(1)} %get-tuple-element.64), channel_id=1, source_target_pairs={{0,1},{1,0},{2,3},{3,2},{4,5},{5,4},{6,7},{7,6},{8,9},{9,8},{10,11... | collective-permute-start | bytes 1179656 | tf_op jit(solution)/shard_map/ppermute | solution.py:336
  82.2 6.3 %collective-permute-start.16 = (bf16[1,256,256]{2,1,0:T(8,128)(2,1)S(1)}, bf16[1,256,256]{2,1,0:T(8,128)(2,1)S(1)}, u32[]{:S(2)}, u32[]{:S(2)}) collective-permute-start(bf16[1,256,256]{2,1,0:T(8,128)(2,1)S(1)} %get-tuple-element.62), channel_id=1, source_target_pairs={{0,1},{1,0},{2,3},{3,2},{4,5},{5,4},{6,7},{7,6},{8,9},{9,8},{10,11... | collective-permute-start | bytes 393224 | tf_op jit(solution)/shard_map/ppermute | solution.py:336
  84.0 7.4 %collective-permute-start.18 = (bf16[256,256]{1,0:T(8,128)(2,1)S(1)}, bf16[256,256]{1,0:T(8,128)(2,1)S(1)}, u32[]{:S(2)}, u32[]{:S(2)}) collective-permute-start(bf16[256,256]{1,0:T(8,128)(2,1)S(1)} %get-tuple-element.65), channel_id=1, source_target_pairs={{0,8},{2,10},{4,12},{6,14},{8,0},{10,2},{12,4},{14,6},{16,24},{18,... | collective-permute-start | bytes 393224 | tf_op jit(solution)/shard_map/ppermute | solution.py:336
  85.5 12.9 %collective-permute-start.19 = (bf16[256,256]{1,0:T(8,128)(2,1)S(1)}, bf16[256,256]{1,0:T(8,128)(2,1)S(1)}, u32[]{:S(2)}, u32[]{:S(2)}) collective-permute-start(bf16[256,256]{1,0:T(8,128)(2,1)S(1)} %get-tuple-element.67), channel_id=1, source_target_pairs={{0,16},{2,18},{4,20},{6,22},{8,24},{10,26},{12,28},{14,30},{16,0},... | collective-permute-start | bytes 393224 | tf_op jit(solution)/shard_map/ppermute | solution.py:336
  86.9 11.5 %collective-permute-start.20 = (bf16[256,256]{1,0:T(8,128)(2,1)S(1)}, bf16[256,256]{1,0:T(8,128)(2,1)S(1)}, u32[]{:S(2)}, u32[]{:S(2)}) collective-permute-start(bf16[256,256]{1,0:T(8,128)(2,1)S(1)} %get-tuple-element.66), channel_id=1, source_target_pairs={{0,24},{2,26},{4,28},{6,30},{8,16},{10,18},{12,20},{14,22},{16,8},... | collective-permute-start | bytes 393224 | tf_op jit(solution)/shard_map/ppermute | solution.py:336
  88.5 10.2 %collective-permute-start.21 = (bf16[256,256]{1,0:T(8,128)(2,1)S(1)}, bf16[256,256]{1,0:T(8,128)(2,1)S(1)}, u32[]{:S(2)}, u32[]{:S(2)}) collective-permute-start(bf16[256,256]{1,0:T(8,128)(2,1)S(1)} %fusion.4), channel_id=1, source_target_pairs={{0,1},{1,0},{2,3},{3,2},{4,5},{5,4},{6,7},{7,6},{8,9},{9,8},{10,11... | collective-permute-start | bytes 393224 | tf_op jit(solution)/shard_map/ppermute | solution.py:336
  100.9 4.1 %collective-permute-start.23 = (bf16[160,128]{1,0:T(8,128)(2,1)S(1)}, bf16[160,128]{1,0:T(8,128)(2,1)S(1)}, u32[]{:S(2)}, u32[]{:S(2)}) collective-permute-start(bf16[160,128]{1,0:T(8,128)(2,1)S(1)} %get-tuple-element.72), channel_id=1, source_target_pairs={{0,2},{2,0},{4,6},{6,4},{8,10},{10,8},{12,14},{14,12},{16,18},{18,... | collective-permute-start | bytes 122888 | tf_op jit(solution)/shard_map/ppermute | solution.py:336
  102.4 4.4 %collective-permute-start.24 = (bf16[160,128]{1,0:T(8,128)(2,1)S(1)}, bf16[160,128]{1,0:T(8,128)(2,1)S(1)}, u32[]{:S(2)}, u32[]{:S(2)}) collective-permute-start(bf16[160,128]{1,0:T(8,128)(2,1)S(1)} %get-tuple-element.74), channel_id=1, source_target_pairs={{0,4},{2,6},{4,0},{6,2},{8,12},{10,14},{12,8},{14,10},{16,20},{18,... | collective-permute-start | bytes 122888 | tf_op jit(solution)/shard_map/ppermute | solution.py:336
  103.1 4.9 %collective-permute-start.25 = (bf16[160,128]{1,0:T(8,128)(2,1)S(1)}, bf16[160,128]{1,0:T(8,128)(2,1)S(1)}, u32[]{:S(2)}, u32[]{:S(2)}) collective-permute-start(bf16[160,128]{1,0:T(8,128)(2,1)S(1)} %get-tuple-element.73), channel_id=1, source_target_pairs={{0,6},{2,4},{4,2},{6,0},{8,14},{10,12},{12,10},{14,8},{16,22},{18,... | collective-permute-start | bytes 122888 | tf_op jit(solution)/shard_map/ppermute | solution.py:336
  108.0 4.8 %collective-permute-start.26 = (bf16[160,128]{1,0:T(8,128)(2,1)S(1)}, bf16[160,128]{1,0:T(8,128)(2,1)S(1)}, u32[]{:S(2)}, u32[]{:S(2)}) collective-permute-start(bf16[160,128]{1,0:T(8,128)(2,1)S(1)} %add_convert_fusion.4), channel_id=1, source_target_pairs={{0,8},{2,10},{4,12},{6,14},{8,0},{10,2},{12,4},{14,6},{16,24},{18,... | collective-permute-start | bytes 122888 | tf_op jit(solution)/shard_map/ppermute | solution.py:336
  110.4 4.9 %collective-permute-start.27 = (bf16[160,128]{1,0:T(8,128)(2,1)S(1)}, bf16[160,128]{1,0:T(8,128)(2,1)S(1)}, u32[]{:S(2)}, u32[]{:S(2)}) collective-permute-start(bf16[160,128]{1,0:T(8,128)(2,1)S(1)} %add_convert_fusion.4), channel_id=1, source_target_pairs={{0,16},{2,18},{4,20},{6,22},{8,24},{10,26},{12,28},{14,30},{16,0},... | collective-permute-start | bytes 122888 | tf_op jit(solution)/shard_map/ppermute | solution.py:336
  110.7 5.8 %collective-permute-start.28 = (bf16[160,128]{1,0:T(8,128)(2,1)S(1)}, bf16[160,128]{1,0:T(8,128)(2,1)S(1)}, u32[]{:S(2)}, u32[]{:S(2)}) collective-permute-start(bf16[160,128]{1,0:T(8,128)(2,1)S(1)} %add_convert_fusion.4), channel_id=1, source_target_pairs={{0,24},{2,26},{4,28},{6,30},{8,16},{10,18},{12,20},{14,22},{16,8},... | collective-permute-start | bytes 122888 | tf_op jit(solution)/shard_map/ppermute | solution.py:336
  116.5 4.1 %collective-permute-start.29 = (bf16[160,128]{1,0:T(8,128)(2,1)S(1)}, bf16[160,128]{1,0:T(8,128)(2,1)S(1)}, u32[]{:S(2)}, u32[]{:S(2)}) collective-permute-start(bf16[160,128]{1,0:T(8,128)(2,1)S(1)} %add_convert_fusion.3), channel_id=1, source_target_pairs={{0,2},{2,0},{4,6},{6,4},{8,10},{10,8},{12,14},{14,12},{16,18},{18,... | collective-permute-start | bytes 122888 | tf_op jit(solution)/shard_map/ppermute | solution.py:336
  118.1 4.0 %collective-permute-start.30 = (bf16[160,128]{1,0:T(8,128)(2,1)S(1)}, bf16[160,128]{1,0:T(8,128)(2,1)S(1)}, u32[]{:S(2)}, u32[]{:S(2)}) collective-permute-start(bf16[160,128]{1,0:T(8,128)(2,1)S(1)} %add_convert_fusion.3), channel_id=1, source_target_pairs={{0,4},{2,6},{4,0},{6,2},{8,12},{10,14},{12,8},{14,10},{16,20},{18,... | collective-permute-start | bytes 122888 | tf_op jit(solution)/shard_map/ppermute | solution.py:336
  118.7 4.9 %collective-permute-start.31 = (bf16[160,128]{1,0:T(8,128)(2,1)S(1)}, bf16[160,128]{1,0:T(8,128)(2,1)S(1)}, u32[]{:S(2)}, u32[]{:S(2)}) collective-permute-start(bf16[160,128]{1,0:T(8,128)(2,1)S(1)} %add_convert_fusion.3), channel_id=1, source_target_pairs={{0,6},{2,4},{4,2},{6,0},{8,14},{10,12},{12,10},{14,8},{16,22},{18,... | collective-permute-start | bytes 122888 | tf_op jit(solution)/shard_map/ppermute | solution.py:336
  123.7 1.5 %collective-permute-start.32 = (bf16[5,128,128]{2,1,0:T(8,128)(2,1)S(1)}, bf16[5,128,128]{2,1,0:T(8,128)(2,1)S(1)}, u32[]{:S(2)}, u32[]{:S(2)}) collective-permute-start(bf16[5,128,128]{2,1,0:T(8,128)(2,1)S(1)} %bitcast.52), channel_id=1, source_target_pairs={{0,1},{1,0},{2,3},{3,2},{4,5},{5,4},{6,7},{7,6},{8,9},{9,8},{10,11... | collective-permute-start | bytes 491528 | tf_op jit(solution)/shard_map/ppermute | solution.py:336
  (5 other events, 22.6 us)

commit v4 on v3

--- a/solution.py
+++ b/solution.py
@@ -14,11 +14,12 @@
 f32 = jnp.float32
 bf16 = jnp.bfloat16
 lane = 128
-chunks = (256, 256)
+stages = ((3,), (2,), (1,), (0,))
 
 COLS = (((0,), (0,)), ((), ()))
 
 
+large = pl.CostEstimate(flops=1 << 34, bytes_accessed=1, transcendentals=0)
 small = pl.CostEstimate(flops=1, bytes_accessed=1, transcendentals=0)
 
 
@@ -100,53 +101,50 @@
     )(ids, values)
 
 
-def product_kernel(bound, joint, groups, place_ref, tiles_ref, probe_ref, *out_refs):
+def product_kernel(bound, joint, groups, away, where_ref, tiles_ref, probe_ref, *out_refs):
     inner = len(out_refs)
-    outer, _, width = out_refs[0].shape
-    count = inner * outer
+    width = out_refs[0].shape[2]
+    count = inner * len(away)
     rows = bound * joint
-    unit = groups * bound * joint
-    start = pl.multiple_of(pl.program_id(0) * unit, unit)
-    place = place_ref[0]
-    tiles = [
-        tiles_ref[b * inner + (place ^ a), pl.ds(start, unit), :].astype(f32)
-        for a in range(inner)
-        for b in range(outer)
-    ]
+    unit = groups * rows
+    blocks = groups * joint
+    units = probe_ref.shape[0] // blocks
+    place, outer_at = where_ref[0], where_ref[1]
     own = lax.broadcasted_iota(jnp.int32, (count * rows, lane), 0) % joint
-    parts = []
-    for g in range(groups):
-        tile = jnp.concatenate([t[g * rows : (g + 1) * rows] for t in tiles], axis=0)
-        spread = jnp.concatenate([jnp.where(own == j, tile, 0.0).astype(bf16) for j in range(joint)], axis=1)
-        probe = probe_ref[g * joint : (g + 1) * joint].reshape(joint * lane, width)
-        parts.append(jnp.dot(spread, probe, preferred_element_type=f32))
-    for a in range(inner):
-        for b in range(outer):
-            at = (a * outer + b) * rows
-            value = jnp.concatenate([part[at : at + rows] for part in parts], axis=0)
-            out_refs[a][b, pl.ds(start, unit), :] = value.astype(bf16)
-
-
-def product(place, tiles, probe, inner, bound, first, width):
+    for u in range(units):
+        tiles = [
+            tiles_ref[(outer_at ^ b) * inner + (place ^ a), u * unit : (u + 1) * unit, :].astype(f32)
+            for a in range(inner)
+            for b in away
+        ]
+        parts = []
+        for g in range(groups):
+            tile = jnp.concatenate([t[g * rows : (g + 1) * rows] for t in tiles], axis=0)
+            spread = jnp.concatenate([jnp.where(own == j, tile, 0.0).astype(bf16) for j in range(joint)], axis=1)
+            first = u * blocks + g * joint
+            probe = probe_ref[first : first + joint].reshape(joint * lane, width)
+            parts.append(jnp.dot(spread, probe, preferred_element_type=f32))
+        for a in range(inner):
+            for b in range(len(away)):
+                at = (a * len(away) + b) * rows
+                value = jnp.concatenate([part[at : at + rows] for part in parts], axis=0)
+                out_refs[a][b, u * unit : (u + 1) * unit, :] = value.astype(bf16)
+
+
+def product(where, tiles, probe, inner, bound, away):
     n_dp, slots, _ = tiles.shape
-    per_dev = probe.shape[0]
+    per_dev, _, width = probe.shape
     joint = joint_of(per_dev)
     groups = 1 if bound * joint % 16 == 0 else 2
-    unit = groups * bound * joint
-    return pl.pallas_call(
-        functools.partial(product_kernel, bound, joint, groups),
-        out_shape=[jax.ShapeDtypeStruct((n_dp // inner, slots, width), bf16)] * inner,
-        grid=(slots // unit,),
-        in_specs=[
-            pl.BlockSpec(memory_space=pltpu.SMEM),
-            whole(),
-            pl.BlockSpec((groups * joint, lane, width), lambda i: (i, 0, first // width)),
-        ],
+    return pl.pallas_call(
+        functools.partial(product_kernel, bound, joint, groups, away),
+        out_shape=[jax.ShapeDtypeStruct((len(away), slots, width), bf16)] * inner,
+        in_specs=[pl.BlockSpec(memory_space=pltpu.SMEM), whole(), whole()],
         out_specs=[whole()] * inner,
-        compiler_params=params(48 << 20),
-        cost_estimate=small,
+        compiler_params=params(),
+        cost_estimate=large,
         name="product",
-    )(place.reshape(1), tiles, probe)
+    )(where, tiles, probe)
 
 
 def choose_kernel(k_j, slots, inner, place_ref, *refs):
@@ -169,7 +167,7 @@
         out_ref[c] = jnp.where(hit, 1.0, 0.0).astype(bf16)
 
 
-def choose(place, outer_at, positions, k_j, slots, inner):
+def choose(where, positions, k_j, slots, inner):
     s_dev = positions[0].shape[1]
     return pl.pallas_call(
         functools.partial(choose_kernel, k_j, slots, inner),
@@ -177,39 +175,33 @@
         in_specs=[pl.BlockSpec(memory_space=pltpu.SMEM)] + [whole()] * len(positions),
         out_specs=whole(),
         compiler_params=params(),
-        cost_estimate=small,
+        cost_estimate=large,
         name="choose",
-    )(jnp.stack([place, outer_at]), *positions)
-
-
-def gather_kernel(pieces, place_ref, hits_ref, *refs):
-    count = len(pieces)
-    rows_refs, keep_refs, give_refs = refs[: -2 * count], refs[-2 * count : -count], refs[-count:]
+    )(where, *positions)
+
+
+def gather_kernel(away, feat_ref, hits_ref, *refs):
+    rows_refs, (keep_ref, give_ref) = refs[:-2], refs[-2:]
     half = hits_ref.shape[1] // 2
-    feat, outer_at = place_ref[0], place_ref[1]
-    for piece, keep_ref, give_ref in zip(pieces, keep_refs, give_refs, strict=True):
-        for at, c in enumerate(piece):
-            rows = jnp.concatenate([ref[outer_at ^ c] for ref in rows_refs], axis=0)
-            give = hits_ref[c, pl.ds(pl.multiple_of((1 - feat) * half, half), half), :]
-            give_ref[at] = jnp.dot(give, rows, preferred_element_type=f32).astype(bf16)
-            keep = hits_ref[c, pl.ds(pl.multiple_of(feat * half, half), half), :]
-            keep_ref[at] = jnp.dot(keep, rows, preferred_element_type=f32)
-
-
-def gather(feat, outer_at, hits, rows, pieces):
-    half, width = hits.shape[1] // 2, rows[0].shape[2]
-    shapes = [(len(piece), half, width) for piece in pieces]
-    count = len(pieces)
-    out = pl.pallas_call(
-        functools.partial(gather_kernel, pieces),
-        out_shape=[jax.ShapeDtypeStruct(shape, kind) for kind in (f32, bf16) for shape in shapes],
+    keep_at = pl.multiple_of(feat_ref[0] * half, half)
+    give_at = pl.multiple_of((1 - feat_ref[0]) * half, half)
+    for at, c in enumerate(away):
+        rows = jnp.concatenate([ref[at] for ref in rows_refs], axis=0)
+        give_ref[at] = jnp.dot(hits_ref[c, pl.ds(give_at, half), :], rows, preferred_element_type=f32).astype(bf16)
+        keep_ref[at] = jnp.dot(hits_ref[c, pl.ds(keep_at, half), :], rows, preferred_element_type=f32)
+
+
+def gather(feat, hits, rows, away):
+    shape = (len(away), hits.shape[1] // 2, rows[0].shape[2])
+    return pl.pallas_call(
+        functools.partial(gather_kernel, away),
+        out_shape=(jax.ShapeDtypeStruct(shape, f32), jax.ShapeDtypeStruct(shape, bf16)),
         in_specs=[pl.BlockSpec(memory_space=pltpu.SMEM)] + [whole()] * (1 + len(rows)),
-        out_specs=[whole()] * (2 * count),
-        compiler_params=params(),
-        cost_estimate=small,
+        out_specs=(whole(), whole()),
+        compiler_params=params(),
+        cost_estimate=large,
         name="gather",
-    )(jnp.stack([feat, outer_at]), hits, *rows)
-    return out[:count], out[count:]
+    )(feat.reshape(1), hits, *rows)
 
 
 def combine_kernel(k_j, position_ref, rows_ref, out_ref):
@@ -377,43 +369,34 @@
     return lax.dynamic_slice_in_dim(sketch, feat * own_rows, own_rows, 0), sketch
 
 
+def tied(value, *others):
+    return lax.optimization_barrier((value, others))[0]
+
+
 def sketch_by_planes(tiles, probe, position, inner, bound, k_j):
     n_dp, slots, _ = tiles.shape
-    outer = n_dp // inner
     index, feat = lax.axis_index("dp"), lax.axis_index("feat")
-    place, outer_at = index % inner, index // inner
-    width = probe.shape[2]
-    positions = [position] + [crossed(position, "dp", c * inner) for c in range(1, outer)]
-    mine, others, before = [], [], None
-    firsts = [sum(chunks[:at]) for at in range(len(chunks))]
-    sent = [product(place, tiles, probe, inner, bound, first, size) for first, size in zip(firsts, chunks, strict=True)]
-    arrived = [[block[0]] + [crossed(block[a], "dp", a) for a in range(1, inner)] for block in sent]
-    positions, _ = lax.optimization_barrier((positions, sent))
-    hits = choose(place, outer_at, positions, k_j, slots, inner)
-    for at, rows in enumerate(arrived):
-        if at > 0:
-            rows, _ = lax.optimization_barrier((rows, before))
-        last = at + 1 == len(sent)
-        pieces = [(3, 2, 1), (0,)] if last else [(c,) for c in range(outer - 1, -1, -1)]
-        keep, give = gather(feat, outer_at, hits, rows, pieces)
-        plane = {}
-        for piece, a, b in zip(pieces, keep, give, strict=True):
-            both = a + crossed(b, "feat", 1).astype(f32)
-            plane.update({c: both[at] for at, c in enumerate(piece)})
-        plane = [plane[c] for c in range(outer)]
-        if not last:
-            size = 1
-            while size < outer:
-                away = [crossed(one.astype(bf16), "dp", size * inner) for one in plane[1::2]]
-                plane = [total_of(pair) for pair in zip(plane[0::2], away, strict=True)]
-                size *= 2
-            plane = before = plane[0]
-        else:
-            plane = total_of([plane[0]] + [crossed(plane[c].astype(bf16), "dp", c * inner) for c in range(1, outer)])
-        mine.append(plane.astype(bf16))
-        others.append(crossed(mine[-1], "feat", 1))
-    mine, others = jnp.concatenate(mine, axis=1), jnp.concatenate(others, axis=1)
-    return mine, jnp.concatenate([mine, others], axis=0)
+    where = jnp.stack([index & (inner - 1), index // inner])
+    positions = [position] + [crossed(position, "dp", c * inner) for c in range(1, n_dp // inner)]
+    sent = []
+    for at, away in enumerate(stages):
+        behind = sent[-1] if at else positions
+        sent.append(product(where, tied(tiles, behind), probe, inner, bound, away))
+    hits = choose(where, tied(positions, sent[-1]), k_j, slots, inner)
+    plane, kept, behind = {}, [], None
+    for at, away in enumerate(stages):
+        rows = [sent[at][0]] + [crossed(sent[at][a], "dp", a) for a in range(1, inner)]
+        if at:
+            rows = tied(rows, kept[-1], plane[2] if at == 2 else kept[-1])
+        keep, give = gather(feat, hits, rows, away)
+        kept.append(keep)
+        both = keep + crossed(give, "feat", 1).astype(f32)
+        plane.update({c: both[i] for i, c in enumerate(away)})
+        if at == 1:
+            plane[2] = plane[2] + crossed(plane[3].astype(bf16), "dp", inner).astype(f32)
+    plane[0] = plane[0] + crossed(plane[1].astype(bf16), "dp", inner).astype(f32)
+    mine = (plane[0] + crossed(plane[2].astype(bf16), "dp", 2 * inner).astype(f32)).astype(bf16)
+    return mine, jnp.concatenate([mine, crossed(mine, "feat", 1)], axis=0)
 
 
 def local(grads, block_ids, probe):
@@ -431,7 +414,7 @@
     if n_feat == 2 and n_dp == 16:
         mine, sketch = sketch_by_planes(tiles, probe, position, 4, bound, k_j)
     else:
-        products = product(jnp.zeros((), jnp.int32), tiles, probe, 1, bound, 0, width)
+        products = product(jnp.zeros((2,), jnp.int32), tiles, probe, 1, bound, tuple(range(n_dp)))
         mine, sketch = sketch_by_all_to_all(products[0], position, k_j)
     mine_gram = sum_over_dp(gram_blocks(sketch, feat))
     other_gram = crossed(mine_gram, "feat", 1)

time: 134 us -> 128 us (0.955)
  waiting for transfers between devices: 58.5 us -> 53.4 us
  Pallas kernels: 28.4 us -> 25.8 us
  local copies, waits for them, and re-layouts: 1.82 us -> 3.98 us
    all_to_all x1, waiting for transfers between devices: 19.7 us -> 0.01 us  [local(): tiles = lax.all_to_all(send, 'dp', split_axis=0, concat_axis=0, tiled=True)]
    ppermute x33, waiting for transfers between devices: 38.8 us -> 53.4 us  [crossed(): lax.ppermute(value, axis, [(source, source ^ bits) for source in range(co...]
    pallas_call x4 -> x8, Pallas kernels: 10.5 us -> 7.59 us  [the longest x4 5.33 us: product(): pl.pallas_call(functools.partial(product_kernel, bound, joint, groups, aw...]
    unnamed x6 -> x8, local copies, waits for them, and re-layouts: 1.74 us -> 3.93 us
  transfers between devices with their start and end apart: 34 -> 34, of which waited for: 20 -> 24; matrix products, arithmetic and copies ran while one was open for 0% -> 0% of each run, Pallas kernels for 5% -> 8%
where the time goes in v4:
time: 128 us; the launch traced here: 127 us
  waiting for transfers between devices  53.4 us (42%)
  starting transfers between devices  43.3 us (34%)
  Pallas kernels  25.8 us (20%)
  local copies, waits for them, and re-layouts  3.98 us (3%)
    ppermute x33, waiting for transfers between devices, crossed(): lax.ppermute(value, axis, [(source, source ^ bits) for source in range(co...  53.4 us
    ppermute x33, starting transfers between devices, crossed(): lax.ppermute(value, axis, [(source, source ^ bits) for source in range(co...  34.8 us
    all_to_all x1, starting transfers between devices, local(): tiles = lax.all_to_all(send, 'dp', split_axis=0, concat_axis=0, tiled=True)  8.49 us
    pallas_call x1, Pallas kernels, whiten(): pl.pallas_call(functools.partial(root_kernel, samples), out_shape=jax.Sha...  8.25 us
    pallas_call x4, Pallas kernels, product(): pl.pallas_call(functools.partial(product_kernel, bound, joint, groups, aw...  5.33 us
    pallas_call x1, Pallas kernels, pack(): pl.pallas_call(functools.partial(pack_kernel, per_dev, bound), out_shape=...  5.26 us
    unnamed x8, local copies, waits for them, and re-layouts  3.93 us
    pallas_call x1, Pallas kernels, choose(): pl.pallas_call(functools.partial(choose_kernel, k_j, slots, inner), out_s...  3.73 us
  transfers between devices with their start and end apart: 34, of which 24 were waited for; matrix products, arithmetic and copies ran while one was open for 0% of the time, Pallas kernels for 8%

profile of v4, /device:TPU:0, one launch (start us, length us, event | category | flops | bytes accessed | tf_op | source)
XLA Modules:
  0.0 127.3 jit_solution(9172449030967474463)
XLA Ops:
  1.7 5.3 %pack.1 = (bf16[16,192,128]{2,1,0:T(8,128)(2,1)}, f32[8,512]{1,0:T(8,128)S(1)}) custom-call(s32[4,512]{1,0:T(4,128)S(1)} %bitcast.41, bf16[2048,128]{1,0:T(8,128)(2,1)S(1)} %bitcast.40), custom_call_target="tpu_custom_call" | custom-call | tf_op jit(solution)/shard_map/pack/pallas_call | solution.py:90
  7.0 8.5 %all-to-all-start = ((bf16[16,192,128]{2,1,0:T(8,128)(2,1)}), bf16[16,192,128]{2,1,0:T(8,128)(2,1)S(1)}, u32[]{:S(2)}, u32[]{:S(2)}) async-start(bf16[16,192,128]{2,1,0:T(8,128)(2,1)} %get-tuple-element.52), calls=%async_computation | async-start | bytes 1572864 | tf_op jit(solution)/shard_map/all_to_all | solution.py:413
  15.5 1.8 %collective-permute-start = (f32[8,512]{1,0:T(8,128)S(1)}, f32[8,512]{1,0:T(8,128)S(1)}, u32[]{:S(2)}, u32[]{:S(2)}) collective-permute-start(f32[8,512]{1,0:T(8,128)S(1)} %get-tuple-element.73.refs_0_), channel_id=1, source_target_pairs={{0,8},{2,10},{4,12},{6,14},{8,0},{10,2},{12,4},{14,6},{16,24},{18,... | collective-permute-start | bytes 49160 | tf_op jit(solution)/shard_map/ppermute | solution.py:328
  17.3 2.4 %collective-permute-start.1 = (f32[8,512]{1,0:T(8,128)S(1)}, f32[8,512]{1,0:T(8,128)S(1)}, u32[]{:S(2)}, u32[]{:S(2)}) collective-permute-start(f32[8,512]{1,0:T(8,128)S(1)} %get-tuple-element.73.refs_0_), channel_id=1, source_target_pairs={{0,16},{2,18},{4,20},{6,22},{8,24},{10,26},{12,28},{14,30},{16,0},... | collective-permute-start | bytes 49160 | tf_op jit(solution)/shard_map/ppermute | solution.py:328
  20.0 8.7 %collective-permute-done.refs_1_ = f32[8,512]{1,0:T(8,128)S(1)} collective-permute-done((f32[8,512]{1,0:T(8,128)S(1)}, f32[8,512]{1,0:T(8,128)S(1)}, u32[]{:S(2)}, u32[]{:S(2)}) %collective-permute-start) | collective-permute-done | bytes 16416 | tf_op jit(solution)/shard_map/ppermute | solution.py:328
  28.7 7.9 %collective-permute-done.1.refs_2_ = f32[8,512]{1,0:T(8,128)S(1)} collective-permute-done((f32[8,512]{1,0:T(8,128)S(1)}, f32[8,512]{1,0:T(8,128)S(1)}, u32[]{:S(2)}, u32[]{:S(2)}) %collective-permute-start.1) | collective-permute-done | bytes 16416 | tf_op jit(solution)/shard_map/ppermute | solution.py:328
  36.6 2.2 %copy-done.2 = bf16[32,1,128,512]{3,2,1,0:T(8,128)(2,1)S(1)} copy-done((bf16[32,1,128,512]{3,2,1,0:T(8,128)(2,1)S(1)}, bf16[32,1,128,512]{3,2,1,0:T(8,128)(2,1)}, u32[]{:S(2)}) %copy-start.2) | copy-done | bytes 4194328
  40.1 1.5 %collective-permute-start.12 = (bf16[1,192,512]{2,1,0:T(8,128)(2,1)S(1)}, bf16[1,192,512]{2,1,0:T(8,128)(2,1)S(1)}, u32[]{:S(2)}, u32[]{:S(2)}) collective-permute-start(bf16[1,192,512]{2,1,0:T(8,128)(2,1)S(1)} %get-tuple-element.55), channel_id=1, source_target_pairs={{0,2},{2,0},{4,6},{6,4},{8,10},{10,8},{12,14},{14,12},{16,18},{18,... | collective-permute-start | bytes 589832 | tf_op jit(solution)/shard_map/ppermute | solution.py:328
  41.7 1.5 %collective-permute-start.13 = (bf16[1,192,512]{2,1,0:T(8,128)(2,1)S(1)}, bf16[1,192,512]{2,1,0:T(8,128)(2,1)S(1)}, u32[]{:S(2)}, u32[]{:S(2)}) collective-permute-start(bf16[1,192,512]{2,1,0:T(8,128)(2,1)S(1)} %get-tuple-element.56), channel_id=1, source_target_pairs={{0,4},{2,6},{4,0},{6,2},{8,12},{10,14},{12,8},{14,10},{16,20},{18,... | collective-permute-start | bytes 589832 | tf_op jit(solution)/shard_map/ppermute | solution.py:328
  45.0 1.5 %collective-permute-start.10 = (bf16[1,192,512]{2,1,0:T(8,128)(2,1)S(1)}, bf16[1,192,512]{2,1,0:T(8,128)(2,1)S(1)}, u32[]{:S(2)}, u32[]{:S(2)}) collective-permute-start(bf16[1,192,512]{2,1,0:T(8,128)(2,1)S(1)} %get-tuple-element.61), channel_id=1, source_target_pairs={{0,4},{2,6},{4,0},{6,2},{8,12},{10,14},{12,8},{14,10},{16,20},{18,... | collective-permute-start | bytes 589832 | tf_op jit(solution)/shard_map/ppermute | solution.py:328
  46.6 1.4 %collective-permute-start.11 = (bf16[1,192,512]{2,1,0:T(8,128)(2,1)S(1)}, bf16[1,192,512]{2,1,0:T(8,128)(2,1)S(1)}, u32[]{:S(2)}, u32[]{:S(2)}) collective-permute-start(bf16[1,192,512]{2,1,0:T(8,128)(2,1)S(1)} %get-tuple-element.62), channel_id=1, source_target_pairs={{0,6},{2,4},{4,2},{6,0},{8,14},{10,12},{12,10},{14,8},{16,22},{18,... | collective-permute-start | bytes 589832 | tf_op jit(solution)/shard_map/ppermute | solution.py:328
  50.7 3.7 %choose.1.hits_ref = bf16[4,512,768]{2,1,0:T(8,128)(2,1)S(1)} custom-call(s32[2]{0:T(128)S(1)} %pad_add_fusion.where_ref.place_ref, f32[8,512]{1,0:T(8,128)S(1)} %get-tuple-element.73.refs_0_, f32[8,512]{1,0:T(8,128)S(1)} %collective-permute-done.refs_1_, f32[8,512]{1,0:T(8,128)S(1)} %collective-permute-done.1.refs_2_, ...), custom_call_target="tpu_custom_call" | custom-call | flops 17179869184 | bytes 1 | tf_op jit(solution)/shard_map/choose/pallas_call | solution.py:172
  55.1 2.2 %collective-permute-done.13.refs_2_ = bf16[1,192,512]{2,1,0:T(8,128)(2,1)S(1)} collective-permute-done((bf16[1,192,512]{2,1,0:T(8,128)(2,1)S(1)}, bf16[1,192,512]{2,1,0:T(8,128)(2,1)S(1)}, u32[]{:S(2)}, u32[]{:S(2)}) %collective-permute-start.13) | collective-permute-done | bytes 196640 | tf_op jit(solution)/shard_map/ppermute | solution.py:328
  57.9 1.8 %collective-permute-done.10.refs_2_ = bf16[1,192,512]{2,1,0:T(8,128)(2,1)S(1)} collective-permute-done((bf16[1,192,512]{2,1,0:T(8,128)(2,1)S(1)}, bf16[1,192,512]{2,1,0:T(8,128)(2,1)S(1)}, u32[]{:S(2)}, u32[]{:S(2)}) %collective-permute-start.10) | collective-permute-done | bytes 196640 | tf_op jit(solution)/shard_map/ppermute | solution.py:328
  62.6 1.5 %collective-permute-start.6 = (bf16[1,192,512]{2,1,0:T(8,128)(2,1)S(1)}, bf16[1,192,512]{2,1,0:T(8,128)(2,1)S(1)}, u32[]{:S(2)}, u32[]{:S(2)}) collective-permute-start(bf16[1,192,512]{2,1,0:T(8,128)(2,1)S(1)} %get-tuple-element.65), channel_id=1, source_target_pairs={{0,2},{2,0},{4,6},{6,4},{8,10},{10,8},{12,14},{14,12},{16,18},{18,... | collective-permute-start | bytes 589832 | tf_op jit(solution)/shard_map/ppermute | solution.py:328
  66.1 1.5 %collective-permute-start.3 = (bf16[1,192,512]{2,1,0:T(8,128)(2,1)S(1)}, bf16[1,192,512]{2,1,0:T(8,128)(2,1)S(1)}, u32[]{:S(2)}, u32[]{:S(2)}) collective-permute-start(bf16[1,192,512]{2,1,0:T(8,128)(2,1)S(1)} %get-tuple-element.70), channel_id=1, source_target_pairs={{0,2},{2,0},{4,6},{6,4},{8,10},{10,8},{12,14},{14,12},{16,18},{18,... | collective-permute-start | bytes 589832 | tf_op jit(solution)/shard_map/ppermute | solution.py:328
  67.6 2.6 %collective-permute-done.17 = bf16[256,512]{1,0:T(8,128)(2,1)S(1)} collective-permute-done((bf16[256,512]{1,0:T(8,128)(2,1)S(1)}, bf16[256,512]{1,0:T(8,128)(2,1)S(1)}, u32[]{:S(2)}, u32[]{:S(2)}) %collective-permute-start.17) | collective-permute-done | bytes 262176 | tf_op jit(solution)/shard_map/ppermute | solution.py:328
  70.2 1.5 %collective-permute-start.4 = (bf16[1,192,512]{2,1,0:T(8,128)(2,1)S(1)}, bf16[1,192,512]{2,1,0:T(8,128)(2,1)S(1)}, u32[]{:S(2)}, u32[]{:S(2)}) collective-permute-start(bf16[1,192,512]{2,1,0:T(8,128)(2,1)S(1)} %get-tuple-element.71), channel_id=1, source_target_pairs={{0,4},{2,6},{4,0},{6,2},{8,12},{10,14},{12,8},{14,10},{16,20},{18,... | collective-permute-start | bytes 589832 | tf_op jit(solution)/shard_map/ppermute | solution.py:328
  72.4 1.6 %collective-permute-done.7.refs_2_ = bf16[1,192,512]{2,1,0:T(8,128)(2,1)S(1)} collective-permute-done((bf16[1,192,512]{2,1,0:T(8,128)(2,1)S(1)}, bf16[1,192,512]{2,1,0:T(8,128)(2,1)S(1)}, u32[]{:S(2)}, u32[]{:S(2)}) %collective-permute-start.7) | collective-permute-done | bytes 196640 | tf_op jit(solution)/shard_map/ppermute | solution.py:328
  74.1 1.4 %collective-permute-start.21 = (bf16[256,512]{1,0:T(8,128)(2,1)S(1)}, bf16[256,512]{1,0:T(8,128)(2,1)S(1)}, u32[]{:S(2)}, u32[]{:S(2)}) collective-permute-start(bf16[256,512]{1,0:T(8,128)(2,1)S(1)} %bitcast_add_fusion.1), channel_id=1, source_target_pairs={{0,16},{2,18},{4,20},{6,22},{8,24},{10,26},{12,28},{14,30},{16,0},... | collective-permute-start | bytes 786440 | tf_op jit(solution)/shard_map/ppermute | solution.py:328
  76.1 2.8 %collective-permute-done.3.refs_1_ = bf16[1,192,512]{2,1,0:T(8,128)(2,1)S(1)} collective-permute-done((bf16[1,192,512]{2,1,0:T(8,128)(2,1)S(1)}, bf16[1,192,512]{2,1,0:T(8,128)(2,1)S(1)}, u32[]{:S(2)}, u32[]{:S(2)}) %collective-permute-start.3) | collective-permute-done | bytes 196640 | tf_op jit(solution)/shard_map/ppermute | solution.py:328
  78.9 4.2 %collective-permute-done.4.refs_2_ = bf16[1,192,512]{2,1,0:T(8,128)(2,1)S(1)} collective-permute-done((bf16[1,192,512]{2,1,0:T(8,128)(2,1)S(1)}, bf16[1,192,512]{2,1,0:T(8,128)(2,1)S(1)}, u32[]{:S(2)}, u32[]{:S(2)}) %collective-permute-start.4) | collective-permute-done | bytes 196640 | tf_op jit(solution)/shard_map/ppermute | solution.py:328
  85.9 7.2 %collective-permute-done.20 = bf16[256,512]{1,0:T(8,128)(2,1)S(1)} collective-permute-done((bf16[256,512]{1,0:T(8,128)(2,1)S(1)}, bf16[256,512]{1,0:T(8,128)(2,1)S(1)}, u32[]{:S(2)}, u32[]{:S(2)}) %collective-permute-start.20) | collective-permute-done | bytes 262176 | tf_op jit(solution)/shard_map/ppermute | solution.py:328
  93.4 1.5 %collective-permute-done.22 = bf16[256,512]{1,0:T(8,128)(2,1)S(1)} collective-permute-done((bf16[256,512]{1,0:T(8,128)(2,1)S(1)}, bf16[256,512]{1,0:T(8,128)(2,1)S(1)}, u32[]{:S(2)}, u32[]{:S(2)}) %collective-permute-start.22) | collective-permute-done | bytes 262176 | tf_op jit(solution)/shard_map/ppermute | solution.py:328
  98.0 1.5 %collective-permute-start.25 = (bf16[160,128]{1,0:T(8,128)(2,1)S(1)}, bf16[160,128]{1,0:T(8,128)(2,1)S(1)}, u32[]{:S(2)}, u32[]{:S(2)}) collective-permute-start(bf16[160,128]{1,0:T(8,128)(2,1)S(1)} %get-tuple-element.102), channel_id=1, source_target_pairs={{0,6},{2,4},{4,2},{6,0},{8,14},{10,12},{12,10},{14,8},{16,22},{18,... | collective-permute-start | bytes 122888 | tf_op jit(solution)/shard_map/ppermute | solution.py:328
  100.8 2.1 %collective-permute-done.25 = bf16[160,128]{1,0:T(8,128)(2,1)S(1)} collective-permute-done((bf16[160,128]{1,0:T(8,128)(2,1)S(1)}, bf16[160,128]{1,0:T(8,128)(2,1)S(1)}, u32[]{:S(2)}, u32[]{:S(2)}) %collective-permute-start.25) | collective-permute-done | bytes 40992 | tf_op jit(solution)/shard_map/ppermute | solution.py:328
  104.9 2.4 %collective-permute-start.28 = (bf16[160,128]{1,0:T(8,128)(2,1)S(1)}, bf16[160,128]{1,0:T(8,128)(2,1)S(1)}, u32[]{:S(2)}, u32[]{:S(2)}) collective-permute-start(bf16[160,128]{1,0:T(8,128)(2,1)S(1)} %add_convert_fusion.3), channel_id=1, source_target_pairs={{0,24},{2,26},{4,28},{6,30},{8,16},{10,18},{12,20},{14,22},{16,8},... | collective-permute-start | bytes 122888 | tf_op jit(solution)/shard_map/ppermute | solution.py:328
  107.3 2.2 %collective-permute-done.27 = bf16[160,128]{1,0:T(8,128)(2,1)S(1)} collective-permute-done((bf16[160,128]{1,0:T(8,128)(2,1)S(1)}, bf16[160,128]{1,0:T(8,128)(2,1)S(1)}, u32[]{:S(2)}, u32[]{:S(2)}) %collective-permute-start.27) | collective-permute-done | bytes 40992 | tf_op jit(solution)/shard_map/ppermute | solution.py:328
  112.6 1.8 %collective-permute-start.31 = (bf16[160,128]{1,0:T(8,128)(2,1)S(1)}, bf16[160,128]{1,0:T(8,128)(2,1)S(1)}, u32[]{:S(2)}, u32[]{:S(2)}) collective-permute-start(bf16[160,128]{1,0:T(8,128)(2,1)S(1)} %add_convert_fusion.2), channel_id=1, source_target_pairs={{0,6},{2,4},{4,2},{6,0},{8,14},{10,12},{12,10},{14,8},{16,22},{18,... | collective-permute-start | bytes 122888 | tf_op jit(solution)/shard_map/ppermute | solution.py:328
  115.7 1.7 %collective-permute-done.31 = bf16[160,128]{1,0:T(8,128)(2,1)S(1)} collective-permute-done((bf16[160,128]{1,0:T(8,128)(2,1)S(1)}, bf16[160,128]{1,0:T(8,128)(2,1)S(1)}, u32[]{:S(2)}, u32[]{:S(2)}) %collective-permute-start.31) | collective-permute-done | bytes 40992 | tf_op jit(solution)/shard_map/ppermute | solution.py:328
  117.6 1.4 %collective-permute-done.32.other_gram_ref = bf16[5,128,128]{2,1,0:T(8,128)(2,1)S(1)} collective-permute-done((bf16[5,128,128]{2,1,0:T(8,128)(2,1)S(1)}, bf16[5,128,128]{2,1,0:T(8,128)(2,1)S(1)}, u32[]{:S(2)}, u32[]{:S(2)}) %collective-permute-start.32) | collective-permute-done | bytes 163872 | tf_op jit(solution)/shard_map/ppermute | solution.py:328
  119.0 8.3 %root.1 = f32[256,512]{1,0:T(8,128)} custom-call(s32[1]{0:T(128)} %bitcast.feat_ref.place_ref, bf16[5,128,128]{2,1,0:T(8,128)(2,1)S(1)} %bitcast.39, bf16[5,128,128]{2,1,0:T(8,128)(2,1)S(1)} %collective-permute-done.32.other_gram_ref, bf16[256,512]{1,0:T(8,128)(2,1)S(1)} %fusion.1.mine_ref), custom_call_target="tpu_custom_call" | custom-call | tf_op jit(solution)/shard_map/root/pallas_call | solution.py:315
  (69 shorter events, 29.5 us)
Async XLA Ops:
  7.0 29.6 %all-to-all-start = ((bf16[16,192,128]{2,1,0:T(8,128)(2,1)}), bf16[16,192,128]{2,1,0:T(8,128)(2,1)S(1)}, u32[]{:S(2)}, u32[]{:S(2)}) async-start(bf16[16,192,128]{2,1,0:T(8,128)(2,1)} %get-tuple-element.52), calls=%async_computation | async-start | bytes 1572864 | tf_op jit(solution)/shard_map/all_to_all | solution.py:413
  15.5 13.2 %collective-permute-start = (f32[8,512]{1,0:T(8,128)S(1)}, f32[8,512]{1,0:T(8,128)S(1)}, u32[]{:S(2)}, u32[]{:S(2)}) collective-permute-start(f32[8,512]{1,0:T(8,128)S(1)} %get-tuple-element.73.refs_0_), channel_id=1, source_target_pairs={{0,8},{2,10},{4,12},{6,14},{8,0},{10,2},{12,4},{14,6},{16,24},{18,... | collective-permute-start | bytes 49160 | tf_op jit(solution)/shard_map/ppermute | solution.py:328
  17.3 19.3 %collective-permute-start.1 = (f32[8,512]{1,0:T(8,128)S(1)}, f32[8,512]{1,0:T(8,128)S(1)}, u32[]{:S(2)}, u32[]{:S(2)}) collective-permute-start(f32[8,512]{1,0:T(8,128)S(1)} %get-tuple-element.73.refs_0_), channel_id=1, source_target_pairs={{0,16},{2,18},{4,20},{6,22},{8,24},{10,26},{12,28},{14,30},{16,0},... | collective-permute-start | bytes 49160 | tf_op jit(solution)/shard_map/ppermute | solution.py:328
  19.7 16.9 %collective-permute-start.2 = (f32[8,512]{1,0:T(8,128)S(1)}, f32[8,512]{1,0:T(8,128)S(1)}, u32[]{:S(2)}, u32[]{:S(2)}) collective-permute-start(f32[8,512]{1,0:T(8,128)S(1)} %get-tuple-element.73.refs_0_), channel_id=1, source_target_pairs={{0,24},{2,26},{4,28},{6,30},{8,16},{10,18},{12,20},{14,22},{16,8},... | collective-permute-start | bytes 49160 | tf_op jit(solution)/shard_map/ppermute | solution.py:328
  40.1 14.3 %collective-permute-start.12 = (bf16[1,192,512]{2,1,0:T(8,128)(2,1)S(1)}, bf16[1,192,512]{2,1,0:T(8,128)(2,1)S(1)}, u32[]{:S(2)}, u32[]{:S(2)}) collective-permute-start(bf16[1,192,512]{2,1,0:T(8,128)(2,1)S(1)} %get-tuple-element.55), channel_id=1, source_target_pairs={{0,2},{2,0},{4,6},{6,4},{8,10},{10,8},{12,14},{14,12},{16,18},{18,... | collective-permute-start | bytes 589832 | tf_op jit(solution)/shard_map/ppermute | solution.py:328
  41.7 15.6 %collective-permute-start.13 = (bf16[1,192,512]{2,1,0:T(8,128)(2,1)S(1)}, bf16[1,192,512]{2,1,0:T(8,128)(2,1)S(1)}, u32[]{:S(2)}, u32[]{:S(2)}) collective-permute-start(bf16[1,192,512]{2,1,0:T(8,128)(2,1)S(1)} %get-tuple-element.56), channel_id=1, source_target_pairs={{0,4},{2,6},{4,0},{6,2},{8,12},{10,14},{12,8},{14,10},{16,20},{18,... | collective-permute-start | bytes 589832 | tf_op jit(solution)/shard_map/ppermute | solution.py:328
  43.1 14.2 %collective-permute-start.14 = (bf16[1,192,512]{2,1,0:T(8,128)(2,1)S(1)}, bf16[1,192,512]{2,1,0:T(8,128)(2,1)S(1)}, u32[]{:S(2)}, u32[]{:S(2)}) collective-permute-start(bf16[1,192,512]{2,1,0:T(8,128)(2,1)S(1)} %get-tuple-element.57), channel_id=1, source_target_pairs={{0,6},{2,4},{4,2},{6,0},{8,14},{10,12},{12,10},{14,8},{16,22},{18,... | collective-permute-start | bytes 589832 | tf_op jit(solution)/shard_map/ppermute | solution.py:328
  45.0 14.6 %collective-permute-start.10 = (bf16[1,192,512]{2,1,0:T(8,128)(2,1)S(1)}, bf16[1,192,512]{2,1,0:T(8,128)(2,1)S(1)}, u32[]{:S(2)}, u32[]{:S(2)}) collective-permute-start(bf16[1,192,512]{2,1,0:T(8,128)(2,1)S(1)} %get-tuple-element.61), channel_id=1, source_target_pairs={{0,4},{2,6},{4,0},{6,2},{8,12},{10,14},{12,8},{14,10},{16,20},{18,... | collective-permute-start | bytes 589832 | tf_op jit(solution)/shard_map/ppermute | solution.py:328
  46.6 13.1 %collective-permute-start.11 = (bf16[1,192,512]{2,1,0:T(8,128)(2,1)S(1)}, bf16[1,192,512]{2,1,0:T(8,128)(2,1)S(1)}, u32[]{:S(2)}, u32[]{:S(2)}) collective-permute-start(bf16[1,192,512]{2,1,0:T(8,128)(2,1)S(1)} %get-tuple-element.62), channel_id=1, source_target_pairs={{0,6},{2,4},{4,2},{6,0},{8,14},{10,12},{12,10},{14,8},{16,22},{18,... | collective-permute-start | bytes 589832 | tf_op jit(solution)/shard_map/ppermute | solution.py:328
  54.4 5.7 %collective-permute-start.9 = (bf16[1,192,512]{2,1,0:T(8,128)(2,1)S(1)}, bf16[1,192,512]{2,1,0:T(8,128)(2,1)S(1)}, u32[]{:S(2)}, u32[]{:S(2)}) collective-permute-start(bf16[1,192,512]{2,1,0:T(8,128)(2,1)S(1)} %get-tuple-element.60), channel_id=1, source_target_pairs={{0,2},{2,0},{4,6},{6,4},{8,10},{10,8},{12,14},{14,12},{16,18},{18,... | collective-permute-start | bytes 589832 | tf_op jit(solution)/shard_map/ppermute | solution.py:328
  60.8 5.3 %collective-permute-start.15 = (bf16[1,256,512]{2,1,0:T(8,128)(2,1)S(1)}, bf16[1,256,512]{2,1,0:T(8,128)(2,1)S(1)}, u32[]{:S(2)}, u32[]{:S(2)}) collective-permute-start(bf16[1,256,512]{2,1,0:T(8,128)(2,1)S(1)} %get-tuple-element.83), channel_id=1, source_target_pairs={{0,1},{1,0},{2,3},{3,2},{4,5},{5,4},{6,7},{7,6},{8,9},{9,8},{10,11... | collective-permute-start | bytes 786440 | tf_op jit(solution)/shard_map/ppermute | solution.py:328
  61.8 8.4 %collective-permute-start.17 = (bf16[256,512]{1,0:T(8,128)(2,1)S(1)}, bf16[256,512]{1,0:T(8,128)(2,1)S(1)}, u32[]{:S(2)}, u32[]{:S(2)}) collective-permute-start(bf16[256,512]{1,0:T(8,128)(2,1)S(1)} %fusion.2), channel_id=1, source_target_pairs={{0,8},{2,10},{4,12},{6,14},{8,0},{10,2},{12,4},{14,6},{16,24},{18,... | collective-permute-start | bytes 786440 | tf_op jit(solution)/shard_map/ppermute | solution.py:328
  62.6 9.2 %collective-permute-start.6 = (bf16[1,192,512]{2,1,0:T(8,128)(2,1)S(1)}, bf16[1,192,512]{2,1,0:T(8,128)(2,1)S(1)}, u32[]{:S(2)}, u32[]{:S(2)}) collective-permute-start(bf16[1,192,512]{2,1,0:T(8,128)(2,1)S(1)} %get-tuple-element.65), channel_id=1, source_target_pairs={{0,2},{2,0},{4,6},{6,4},{8,10},{10,8},{12,14},{14,12},{16,18},{18,... | collective-permute-start | bytes 589832 | tf_op jit(solution)/shard_map/ppermute | solution.py:328
  64.1 10.0 %collective-permute-start.7 = (bf16[1,192,512]{2,1,0:T(8,128)(2,1)S(1)}, bf16[1,192,512]{2,1,0:T(8,128)(2,1)S(1)}, u32[]{:S(2)}, u32[]{:S(2)}) collective-permute-start(bf16[1,192,512]{2,1,0:T(8,128)(2,1)S(1)} %get-tuple-element.66), channel_id=1, source_target_pairs={{0,4},{2,6},{4,0},{6,2},{8,12},{10,14},{12,8},{14,10},{16,20},{18,... | collective-permute-start | bytes 589832 | tf_op jit(solution)/shard_map/ppermute | solution.py:328
  65.2 10.4 %collective-permute-start.8 = (bf16[1,192,512]{2,1,0:T(8,128)(2,1)S(1)}, bf16[1,192,512]{2,1,0:T(8,128)(2,1)S(1)}, u32[]{:S(2)}, u32[]{:S(2)}) collective-permute-start(bf16[1,192,512]{2,1,0:T(8,128)(2,1)S(1)} %get-tuple-element.67), channel_id=1, source_target_pairs={{0,6},{2,4},{4,2},{6,0},{8,14},{10,12},{12,10},{14,8},{16,22},{18,... | collective-permute-start | bytes 589832 | tf_op jit(solution)/shard_map/ppermute | solution.py:328
  66.1 12.8 %collective-permute-start.3 = (bf16[1,192,512]{2,1,0:T(8,128)(2,1)S(1)}, bf16[1,192,512]{2,1,0:T(8,128)(2,1)S(1)}, u32[]{:S(2)}, u32[]{:S(2)}) collective-permute-start(bf16[1,192,512]{2,1,0:T(8,128)(2,1)S(1)} %get-tuple-element.70), channel_id=1, source_target_pairs={{0,2},{2,0},{4,6},{6,4},{8,10},{10,8},{12,14},{14,12},{16,18},{18,... | collective-permute-start | bytes 589832 | tf_op jit(solution)/shard_map/ppermute | solution.py:328
  70.2 12.9 %collective-permute-start.4 = (bf16[1,192,512]{2,1,0:T(8,128)(2,1)S(1)}, bf16[1,192,512]{2,1,0:T(8,128)(2,1)S(1)}, u32[]{:S(2)}, u32[]{:S(2)}) collective-permute-start(bf16[1,192,512]{2,1,0:T(8,128)(2,1)S(1)} %get-tuple-element.71), channel_id=1, source_target_pairs={{0,4},{2,6},{4,0},{6,2},{8,12},{10,14},{12,8},{14,10},{16,20},{18,... | collective-permute-start | bytes 589832 | tf_op jit(solution)/shard_map/ppermute | solution.py:328
  71.8 11.3 %collective-permute-start.5 = (bf16[1,192,512]{2,1,0:T(8,128)(2,1)S(1)}, bf16[1,192,512]{2,1,0:T(8,128)(2,1)S(1)}, u32[]{:S(2)}, u32[]{:S(2)}) collective-permute-start(bf16[1,192,512]{2,1,0:T(8,128)(2,1)S(1)} %get-tuple-element.72), channel_id=1, source_target_pairs={{0,6},{2,4},{4,2},{6,0},{8,14},{10,12},{12,10},{14,8},{16,22},{18,... | collective-permute-start | bytes 589832 | tf_op jit(solution)/shard_map/ppermute | solution.py:328
  74.1 11.8 %collective-permute-start.21 = (bf16[256,512]{1,0:T(8,128)(2,1)S(1)}, bf16[256,512]{1,0:T(8,128)(2,1)S(1)}, u32[]{:S(2)}, u32[]{:S(2)}) collective-permute-start(bf16[256,512]{1,0:T(8,128)(2,1)S(1)} %bitcast_add_fusion.1), channel_id=1, source_target_pairs={{0,16},{2,18},{4,20},{6,22},{8,24},{10,26},{12,28},{14,30},{16,0},... | collective-permute-start | bytes 786440 | tf_op jit(solution)/shard_map/ppermute | solution.py:328
  83.1 1.5 %collective-permute-start.19 = (bf16[1,256,512]{2,1,0:T(8,128)(2,1)S(1)}, bf16[1,256,512]{2,1,0:T(8,128)(2,1)S(1)}, u32[]{:S(2)}, u32[]{:S(2)}) collective-permute-start(bf16[1,256,512]{2,1,0:T(8,128)(2,1)S(1)} %get-tuple-element.96), channel_id=1, source_target_pairs={{0,1},{1,0},{2,3},{3,2},{4,5},{5,4},{6,7},{7,6},{8,9},{9,8},{10,11... | collective-permute-start | bytes 786440 | tf_op jit(solution)/shard_map/ppermute | solution.py:328
  83.7 2.1 %collective-permute-start.18 = (bf16[1,256,512]{2,1,0:T(8,128)(2,1)S(1)}, bf16[1,256,512]{2,1,0:T(8,128)(2,1)S(1)}, u32[]{:S(2)}, u32[]{:S(2)}) collective-permute-start(bf16[1,256,512]{2,1,0:T(8,128)(2,1)S(1)} %get-tuple-element.95), channel_id=1, source_target_pairs={{0,1},{1,0},{2,3},{3,2},{4,5},{5,4},{6,7},{7,6},{8,9},{9,8},{10,11... | collective-permute-start | bytes 786440 | tf_op jit(solution)/shard_map/ppermute | solution.py:328
  84.7 8.4 %collective-permute-start.20 = (bf16[256,512]{1,0:T(8,128)(2,1)S(1)}, bf16[256,512]{1,0:T(8,128)(2,1)S(1)}, u32[]{:S(2)}, u32[]{:S(2)}) collective-permute-start(bf16[256,512]{1,0:T(8,128)(2,1)S(1)} %fusion.3), channel_id=1, source_target_pairs={{0,8},{2,10},{4,12},{6,14},{8,0},{10,2},{12,4},{14,6},{16,24},{18,... | collective-permute-start | bytes 786440 | tf_op jit(solution)/shard_map/ppermute | solution.py:328
  93.3 1.6 %collective-permute-start.22 = (bf16[256,512]{1,0:T(8,128)(2,1)S(1)}, bf16[256,512]{1,0:T(8,128)(2,1)S(1)}, u32[]{:S(2)}, u32[]{:S(2)}) collective-permute-start(bf16[256,512]{1,0:T(8,128)(2,1)S(1)} %fusion.1.mine_ref), channel_id=1, source_target_pairs={{0,1},{1,0},{2,3},{3,2},{4,5},{5,4},{6,7},{7,6},{8,9},{9,8},{10,11... | collective-permute-start | bytes 786440 | tf_op jit(solution)/shard_map/ppermute | solution.py:328
  95.9 4.1 %collective-permute-start.23 = (bf16[160,128]{1,0:T(8,128)(2,1)S(1)}, bf16[160,128]{1,0:T(8,128)(2,1)S(1)}, u32[]{:S(2)}, u32[]{:S(2)}) collective-permute-start(bf16[160,128]{1,0:T(8,128)(2,1)S(1)} %get-tuple-element.101), channel_id=1, source_target_pairs={{0,2},{2,0},{4,6},{6,4},{8,10},{10,8},{12,14},{14,12},{16,18},{18,... | collective-permute-start | bytes 122888 | tf_op jit(solution)/shard_map/ppermute | solution.py:328
  96.8 4.0 %collective-permute-start.24 = (bf16[160,128]{1,0:T(8,128)(2,1)S(1)}, bf16[160,128]{1,0:T(8,128)(2,1)S(1)}, u32[]{:S(2)}, u32[]{:S(2)}) collective-permute-start(bf16[160,128]{1,0:T(8,128)(2,1)S(1)} %get-tuple-element.103), channel_id=1, source_target_pairs={{0,4},{2,6},{4,0},{6,2},{8,12},{10,14},{12,8},{14,10},{16,20},{18,... | collective-permute-start | bytes 122888 | tf_op jit(solution)/shard_map/ppermute | solution.py:328
  98.0 4.9 %collective-permute-start.25 = (bf16[160,128]{1,0:T(8,128)(2,1)S(1)}, bf16[160,128]{1,0:T(8,128)(2,1)S(1)}, u32[]{:S(2)}, u32[]{:S(2)}) collective-permute-start(bf16[160,128]{1,0:T(8,128)(2,1)S(1)} %get-tuple-element.102), channel_id=1, source_target_pairs={{0,6},{2,4},{4,2},{6,0},{8,14},{10,12},{12,10},{14,8},{16,22},{18,... | collective-permute-start | bytes 122888 | tf_op jit(solution)/shard_map/ppermute | solution.py:328
  102.9 4.5 %collective-permute-start.26 = (bf16[160,128]{1,0:T(8,128)(2,1)S(1)}, bf16[160,128]{1,0:T(8,128)(2,1)S(1)}, u32[]{:S(2)}, u32[]{:S(2)}) collective-permute-start(bf16[160,128]{1,0:T(8,128)(2,1)S(1)} %add_convert_fusion.3), channel_id=1, source_target_pairs={{0,8},{2,10},{4,12},{6,14},{8,0},{10,2},{12,4},{14,6},{16,24},{18,... | collective-permute-start | bytes 122888 | tf_op jit(solution)/shard_map/ppermute | solution.py:328
  104.2 5.3 %collective-permute-start.27 = (bf16[160,128]{1,0:T(8,128)(2,1)S(1)}, bf16[160,128]{1,0:T(8,128)(2,1)S(1)}, u32[]{:S(2)}, u32[]{:S(2)}) collective-permute-start(bf16[160,128]{1,0:T(8,128)(2,1)S(1)} %add_convert_fusion.3), channel_id=1, source_target_pairs={{0,16},{2,18},{4,20},{6,22},{8,24},{10,26},{12,28},{14,30},{16,0},... | collective-permute-start | bytes 122888 | tf_op jit(solution)/shard_map/ppermute | solution.py:328
  104.9 5.8 %collective-permute-start.28 = (bf16[160,128]{1,0:T(8,128)(2,1)S(1)}, bf16[160,128]{1,0:T(8,128)(2,1)S(1)}, u32[]{:S(2)}, u32[]{:S(2)}) collective-permute-start(bf16[160,128]{1,0:T(8,128)(2,1)S(1)} %add_convert_fusion.3), channel_id=1, source_target_pairs={{0,24},{2,26},{4,28},{6,30},{8,16},{10,18},{12,20},{14,22},{16,8},... | collective-permute-start | bytes 122888 | tf_op jit(solution)/shard_map/ppermute | solution.py:328
  110.8 4.1 %collective-permute-start.29 = (bf16[160,128]{1,0:T(8,128)(2,1)S(1)}, bf16[160,128]{1,0:T(8,128)(2,1)S(1)}, u32[]{:S(2)}, u32[]{:S(2)}) collective-permute-start(bf16[160,128]{1,0:T(8,128)(2,1)S(1)} %add_convert_fusion.2), channel_id=1, source_target_pairs={{0,2},{2,0},{4,6},{6,4},{8,10},{10,8},{12,14},{14,12},{16,18},{18,... | collective-permute-start | bytes 122888 | tf_op jit(solution)/shard_map/ppermute | solution.py:328
  111.7 4.0 %collective-permute-start.30 = (bf16[160,128]{1,0:T(8,128)(2,1)S(1)}, bf16[160,128]{1,0:T(8,128)(2,1)S(1)}, u32[]{:S(2)}, u32[]{:S(2)}) collective-permute-start(bf16[160,128]{1,0:T(8,128)(2,1)S(1)} %add_convert_fusion.2), channel_id=1, source_target_pairs={{0,4},{2,6},{4,0},{6,2},{8,12},{10,14},{12,8},{14,10},{16,20},{18,... | collective-permute-start | bytes 122888 | tf_op jit(solution)/shard_map/ppermute | solution.py:328
  112.6 4.9 %collective-permute-start.31 = (bf16[160,128]{1,0:T(8,128)(2,1)S(1)}, bf16[160,128]{1,0:T(8,128)(2,1)S(1)}, u32[]{:S(2)}, u32[]{:S(2)}) collective-permute-start(bf16[160,128]{1,0:T(8,128)(2,1)S(1)} %add_convert_fusion.2), channel_id=1, source_target_pairs={{0,6},{2,4},{4,2},{6,0},{8,14},{10,12},{12,10},{14,8},{16,22},{18,... | collective-permute-start | bytes 122888 | tf_op jit(solution)/shard_map/ppermute | solution.py:328
  (6 other events, 17.2 us)

commit v5 on v4

--- a/solution.py
+++ b/solution.py
@@ -35,12 +35,13 @@
     return math.gcd(per_dev, 4)
 
 
-def pack_kernel(per_dev, bound, ids_ref, values_ref, send_ref, position_ref, values):
+def pack_kernel(per_dev, bound, ids_ref, values_ref, send_ref, position_ref, values, raw, arrived):
     k_j, s_dev = ids_ref.shape
     n_dp, slots, width = send_ref.shape
     n_ids = n_dp * per_dev
     joint = joint_of(per_dev)
-    values[...] = values_ref[...].astype(f32)
+    copy = pltpu.make_async_copy(values_ref, raw, arrived)
+    copy.start()
     ids_rows = ids_ref[...]
     padded = jnp.concatenate([ids_rows.astype(f32), jnp.zeros((lane - k_j, s_dev), f32)], axis=0)
     ids_cols = jnp.transpose(padded)
@@ -58,6 +59,9 @@
         before = jnp.dot(earlier, named.astype(bf16), preferred_element_type=f32) + used
         rank = jnp.sum(named * before, axis=1, keepdims=True)
         used = used + jnp.sum(named, axis=0, keepdims=True)
+        if k == 0:
+            copy.wait()
+            values[...] = raw[...].astype(f32)
         tile = values[pl.ds(k, s_dev, stride=k_j), :]
         by_rank.append(jnp.concatenate([jnp.where(rank == r, tile, 0.0).astype(bf16) for r in range(bound)], axis=1))
         named_rows.append(jnp.where(ids_rows[k : k + 1, :] == number_rows, 1.0, 0.0).astype(bf16))
@@ -93,10 +97,10 @@
             jax.ShapeDtypeStruct((n_dp, bound * per_dev, lane), bf16),
             jax.ShapeDtypeStruct((8, s_dev), f32),
         ),
-        in_specs=[whole(), whole()],
+        in_specs=[whole(), pl.BlockSpec(memory_space=pl.ANY)],
         out_specs=(whole(), whole()),
-        scratch_shapes=[pltpu.VMEM(values.shape, f32)],
-        compiler_params=params(),
+        scratch_shapes=[pltpu.VMEM(values.shape, f32), pltpu.VMEM(values.shape, bf16), pltpu.SemaphoreType.DMA],
+        compiler_params=params(62 << 20),
         name="pack",
     )(ids, values)
 
@@ -276,12 +280,18 @@
     return high, (value - high.astype(f32)).astype(bf16)
 
 
+def left(value):
+    high, low = halves(value)
+    return jnp.concatenate([low, high, high], axis=1)
+
+
+def right(value):
+    high, low = halves(value)
+    return jnp.concatenate([high, low, high], axis=0)
+
+
 def dot3(a, b):
-    (ah, al), (bh, bl) = a, b
-    out = jnp.dot(ah, bl, preferred_element_type=f32)
-    if al is not None:
-        out = out + jnp.dot(al, bh, preferred_element_type=f32)
-    return out + jnp.dot(ah, bh, preferred_element_type=f32)
+    return jnp.dot(a, b, preferred_element_type=f32)
 
 
 def root_kernel(samples, place_ref, mine_gram_ref, other_gram_ref, mine_ref, out_ref, gram):
@@ -300,13 +310,18 @@
     total = gram[...] + ridge * samples * ident
     scale = jnp.sum(total * ident, axis=(0, 1), keepdims=True) / width
     current = total / scale
-    result = (mine_ref[...], None)
-    for step in range(root_steps):
-        middle = halves(1.5 * ident - 0.5 * current)
-        if step + 1 < root_steps:
-            current = dot3(halves(dot3(halves(current), middle)), middle)
-        value = dot3(result, middle)
-        result = halves(value)
+    mine = mine_ref[...]
+    for step in range(root_steps - 1):
+        middle = 1.5 * ident - 0.5 * current
+        by = right(middle)
+        if step == 0:
+            value = dot3(jnp.concatenate([mine, mine], axis=1), by[width:])
+        else:
+            value = dot3(left(value), by)
+        if step + 2 < root_steps:
+            current = dot3(left(dot3(left(current), by)), by)
+    moved = dot3(left(dot3(left(dot3(left(value), right(current))), by)), by)
+    value = 1.5 * value - 0.5 * moved
     out_ref[...] = (math.sqrt(samples) * lax.rsqrt(scale)) * value
 
 
@@ -378,16 +393,18 @@
     index, feat = lax.axis_index("dp"), lax.axis_index("feat")
     where = jnp.stack([index & (inner - 1), index // inner])
     positions = [position] + [crossed(position, "dp", c * inner) for c in range(1, n_dp // inner)]
-    sent = []
+    sent, hits = [], None
     for at, away in enumerate(stages):
-        behind = sent[-1] if at else positions
+        behind = positions if not at else sent[-1]
+        if at == 2:
+            hits = choose(where, tied(positions, sent[-1]), k_j, slots, inner)
+            behind = hits
         sent.append(product(where, tied(tiles, behind), probe, inner, bound, away))
-    hits = choose(where, tied(positions, sent[-1]), k_j, slots, inner)
     plane, kept, behind = {}, [], None
     for at, away in enumerate(stages):
         rows = [sent[at][0]] + [crossed(sent[at][a], "dp", a) for a in range(1, inner)]
         if at:
-            rows = tied(rows, kept[-1], plane[2] if at == 2 else kept[-1])
+            rows = tied(rows, kept[-1], (plane[3], sent[3]) if at == 2 else (plane[2], plane[1]) if at == 3 else kept[-1])
         keep, give = gather(feat, hits, rows, away)
         kept.append(keep)
         both = keep + crossed(give, "feat", 1).astype(f32)

time: 128 us -> 120 us (0.938)
  waiting for transfers between devices: 53.4 us -> 47.4 us
  local copies, waits for them, and re-layouts: 3.98 us -> 2.25 us
    ppermute x33, waiting for transfers between devices: 53.4 us -> 47.4 us  [crossed(): lax.ppermute(value, axis, [(source, source ^ bits) for source in range(co...]
    unnamed x8, local copies, waits for them, and re-layouts: 3.93 us -> 2.2 us
    pallas_call x1, Pallas kernels: 5.26 us -> 6.76 us  [pack(): pl.pallas_call(functools.partial(pack_kernel, per_dev, bound), out_shape=...]
  transfers between devices with their start and end apart: 34 -> 34, of which waited for: 24 -> 18; matrix products, arithmetic and copies ran while one was open for 0% -> 0% of each run, Pallas kernels for 8% -> 8%
where the time goes in v5:
time: 120 us; the launch traced here: 119 us
  waiting for transfers between devices  47.4 us (40%)
  starting transfers between devices  42.1 us (35%)
  Pallas kernels  26.6 us (22%)
  local copies, waits for them, and re-layouts  2.25 us (2%)
    ppermute x33, waiting for transfers between devices, crossed(): lax.ppermute(value, axis, [(source, source ^ bits) for source in range(co...  47.4 us
    ppermute x33, starting transfers between devices, crossed(): lax.ppermute(value, axis, [(source, source ^ bits) for source in range(co...  33.6 us
    all_to_all x1, starting transfers between devices, local(): tiles = lax.all_to_all(send, 'dp', split_axis=0, concat_axis=0, tiled=True)  8.51 us
    pallas_call x1, Pallas kernels, whiten(): pl.pallas_call(functools.partial(root_kernel, samples), out_shape=jax.Sha...  7.63 us
    pallas_call x1, Pallas kernels, pack(): pl.pallas_call(functools.partial(pack_kernel, per_dev, bound), out_shape=...  6.76 us
    pallas_call x4, Pallas kernels, product(): pl.pallas_call(functools.partial(product_kernel, bound, joint, groups, aw...  5.32 us
    pallas_call x1, Pallas kernels, choose(): pl.pallas_call(functools.partial(choose_kernel, k_j, slots, inner), out_s...  3.72 us
  transfers between devices with their start and end apart: 34, of which 18 were waited for; matrix products, arithmetic and copies ran while one was open for 0% of the time, Pallas kernels for 8%

profile of v5, /device:TPU:0, one launch (start us, length us, event | category | flops | bytes accessed | tf_op | source)
XLA Modules:
  0.0 119.2 jit_solution(7468110489229015033)
XLA Ops:
  0.0 6.8 %pack.1 = (bf16[16,192,128]{2,1,0:T(8,128)(2,1)}, f32[8,512]{1,0:T(8,128)}) custom-call(s32[4,512]{1,0:T(4,128)} %bitcast.49, bf16[2048,128]{1,0:T(8,128)(2,1)} %bitcast.44), custom_call_target="tpu_custom_call" | custom-call | tf_op jit(solution)/shard_map/pack/pallas_call | solution.py:94
  6.8 8.5 %all-to-all-start = ((bf16[16,192,128]{2,1,0:T(8,128)(2,1)}), bf16[16,192,128]{2,1,0:T(8,128)(2,1)S(1)}, u32[]{:S(2)}, u32[]{:S(2)}) async-start(bf16[16,192,128]{2,1,0:T(8,128)(2,1)} %get-tuple-element.52), calls=%async_computation | async-start | bytes 1572864 | tf_op jit(solution)/shard_map/all_to_all | solution.py:430
  15.3 1.8 %collective-permute-start = (f32[8,512]{1,0:T(8,128)}, f32[8,512]{1,0:T(8,128)S(1)}, u32[]{:S(2)}, u32[]{:S(2)}) collective-permute-start(f32[8,512]{1,0:T(8,128)} %get-tuple-element.63.refs_0_), channel_id=1, source_target_pairs={{0,8},{2,10},{4,12},{6,14},{8,0},{10,2},{12,4},{14,6},{16,24},{18,... | collective-permute-start | bytes 49160 | tf_op jit(solution)/shard_map/ppermute | solution.py:343
  17.1 2.4 %collective-permute-start.1 = (f32[8,512]{1,0:T(8,128)}, f32[8,512]{1,0:T(8,128)S(1)}, u32[]{:S(2)}, u32[]{:S(2)}) collective-permute-start(f32[8,512]{1,0:T(8,128)} %get-tuple-element.63.refs_0_), channel_id=1, source_target_pairs={{0,16},{2,18},{4,20},{6,22},{8,24},{10,26},{12,28},{14,30},{16,0},... | collective-permute-start | bytes 49160 | tf_op jit(solution)/shard_map/ppermute | solution.py:343
  19.8 8.7 %collective-permute-done.refs_1_ = f32[8,512]{1,0:T(8,128)S(1)} collective-permute-done((f32[8,512]{1,0:T(8,128)}, f32[8,512]{1,0:T(8,128)S(1)}, u32[]{:S(2)}, u32[]{:S(2)}) %collective-permute-start) | collective-permute-done | bytes 16416 | tf_op jit(solution)/shard_map/ppermute | solution.py:343
  28.5 7.9 %collective-permute-done.1.refs_2_ = f32[8,512]{1,0:T(8,128)S(1)} collective-permute-done((f32[8,512]{1,0:T(8,128)}, f32[8,512]{1,0:T(8,128)S(1)}, u32[]{:S(2)}, u32[]{:S(2)}) %collective-permute-start.1) | collective-permute-done | bytes 16416 | tf_op jit(solution)/shard_map/ppermute | solution.py:343
  36.4 2.2 %copy-done = bf16[32,1,128,512]{3,2,1,0:T(8,128)(2,1)S(1)} copy-done((bf16[32,1,128,512]{3,2,1,0:T(8,128)(2,1)S(1)}, bf16[32,1,128,512]{3,2,1,0:T(8,128)(2,1)}, u32[]{:S(2)}) %copy-start) | copy-done | bytes 4194328
  39.9 1.5 %collective-permute-start.12 = (bf16[1,192,512]{2,1,0:T(8,128)(2,1)S(1)}, bf16[1,192,512]{2,1,0:T(8,128)(2,1)S(1)}, u32[]{:S(2)}, u32[]{:S(2)}) collective-permute-start(bf16[1,192,512]{2,1,0:T(8,128)(2,1)S(1)} %get-tuple-element.55), channel_id=1, source_target_pairs={{0,2},{2,0},{4,6},{6,4},{8,10},{10,8},{12,14},{14,12},{16,18},{18,... | collective-permute-start | bytes 589832 | tf_op jit(solution)/shard_map/ppermute | solution.py:343
  41.5 1.5 %collective-permute-start.13 = (bf16[1,192,512]{2,1,0:T(8,128)(2,1)S(1)}, bf16[1,192,512]{2,1,0:T(8,128)(2,1)S(1)}, u32[]{:S(2)}, u32[]{:S(2)}) collective-permute-start(bf16[1,192,512]{2,1,0:T(8,128)(2,1)S(1)} %get-tuple-element.56), channel_id=1, source_target_pairs={{0,4},{2,6},{4,0},{6,2},{8,12},{10,14},{12,8},{14,10},{16,20},{18,... | collective-permute-start | bytes 589832 | tf_op jit(solution)/shard_map/ppermute | solution.py:343
  44.8 1.5 %collective-permute-start.9 = (bf16[1,192,512]{2,1,0:T(8,128)(2,1)S(1)}, bf16[1,192,512]{2,1,0:T(8,128)(2,1)S(1)}, u32[]{:S(2)}, u32[]{:S(2)}) collective-permute-start(bf16[1,192,512]{2,1,0:T(8,128)(2,1)S(1)} %get-tuple-element.60), channel_id=1, source_target_pairs={{0,2},{2,0},{4,6},{6,4},{8,10},{10,8},{12,14},{14,12},{16,18},{18,... | collective-permute-start | bytes 589832 | tf_op jit(solution)/shard_map/ppermute | solution.py:343
  46.3 1.5 %collective-permute-start.10 = (bf16[1,192,512]{2,1,0:T(8,128)(2,1)S(1)}, bf16[1,192,512]{2,1,0:T(8,128)(2,1)S(1)}, u32[]{:S(2)}, u32[]{:S(2)}) collective-permute-start(bf16[1,192,512]{2,1,0:T(8,128)(2,1)S(1)} %get-tuple-element.61), channel_id=1, source_target_pairs={{0,4},{2,6},{4,0},{6,2},{8,12},{10,14},{12,8},{14,10},{16,20},{18,... | collective-permute-start | bytes 589832 | tf_op jit(solution)/shard_map/ppermute | solution.py:343
  47.8 3.7 %choose.1.hits_ref = bf16[4,512,768]{2,1,0:T(8,128)(2,1)S(1)} custom-call(s32[2]{0:T(128)S(1)} %pad_add_fusion.where_ref.place_ref, f32[8,512]{1,0:T(8,128)S(1)} %copy-done.2, f32[8,512]{1,0:T(8,128)S(1)} %collective-permute-done.refs_1_, f32[8,512]{1,0:T(8,128)S(1)} %collective-permute-done.1.refs_2_, f32[8,512]{1,0:T(8,128)S(1)} %collective-permute-done.2.refs_3_), custom_call_target="tpu_custom_call" | custom-call | flops 17179869184 | bytes 1 | tf_op jit(solution)/shard_map/choose/pallas_call | solution.py:176
  54.9 1.5 %collective-permute-start.6 = (bf16[1,192,512]{2,1,0:T(8,128)(2,1)S(1)}, bf16[1,192,512]{2,1,0:T(8,128)(2,1)S(1)}, u32[]{:S(2)}, u32[]{:S(2)}) collective-permute-start(bf16[1,192,512]{2,1,0:T(8,128)(2,1)S(1)} %get-tuple-element.69), channel_id=1, source_target_pairs={{0,2},{2,0},{4,6},{6,4},{8,10},{10,8},{12,14},{14,12},{16,18},{18,... | collective-permute-start | bytes 589832 | tf_op jit(solution)/shard_map/ppermute | solution.py:343
  56.3 1.5 %collective-permute-start.7 = (bf16[1,192,512]{2,1,0:T(8,128)(2,1)S(1)}, bf16[1,192,512]{2,1,0:T(8,128)(2,1)S(1)}, u32[]{:S(2)}, u32[]{:S(2)}) collective-permute-start(bf16[1,192,512]{2,1,0:T(8,128)(2,1)S(1)} %get-tuple-element.70), channel_id=1, source_target_pairs={{0,4},{2,6},{4,0},{6,2},{8,12},{10,14},{12,8},{14,10},{16,20},{18,... | collective-permute-start | bytes 589832 | tf_op jit(solution)/shard_map/ppermute | solution.py:343
  59.0 4.1 %collective-permute-done.11.refs_3_ = bf16[1,192,512]{2,1,0:T(8,128)(2,1)S(1)} collective-permute-done((bf16[1,192,512]{2,1,0:T(8,128)(2,1)S(1)}, bf16[1,192,512]{2,1,0:T(8,128)(2,1)S(1)}, u32[]{:S(2)}, u32[]{:S(2)}) %collective-permute-start.11) | collective-permute-done | bytes 196640 | tf_op jit(solution)/shard_map/ppermute | solution.py:343
  64.7 3.2 %collective-permute-done.7.refs_2_ = bf16[1,192,512]{2,1,0:T(8,128)(2,1)S(1)} collective-permute-done((bf16[1,192,512]{2,1,0:T(8,128)(2,1)S(1)}, bf16[1,192,512]{2,1,0:T(8,128)(2,1)S(1)}, u32[]{:S(2)}, u32[]{:S(2)}) %collective-permute-start.7) | collective-permute-done | bytes 196640 | tf_op jit(solution)/shard_map/ppermute | solution.py:343
  70.7 1.4 %collective-permute-start.5 = (bf16[1,192,512]{2,1,0:T(8,128)(2,1)S(1)}, bf16[1,192,512]{2,1,0:T(8,128)(2,1)S(1)}, u32[]{:S(2)}, u32[]{:S(2)}) collective-permute-start(bf16[1,192,512]{2,1,0:T(8,128)(2,1)S(1)} %get-tuple-element.76), channel_id=1, source_target_pairs={{0,6},{2,4},{4,2},{6,0},{8,14},{10,12},{12,10},{14,8},{16,22},{18,... | collective-permute-start | bytes 589832 | tf_op jit(solution)/shard_map/ppermute | solution.py:343
  74.9 1.4 %collective-permute-done.3.refs_1_ = bf16[1,192,512]{2,1,0:T(8,128)(2,1)S(1)} collective-permute-done((bf16[1,192,512]{2,1,0:T(8,128)(2,1)S(1)}, bf16[1,192,512]{2,1,0:T(8,128)(2,1)S(1)}, u32[]{:S(2)}, u32[]{:S(2)}) %collective-permute-start.3) | collective-permute-done | bytes 196640 | tf_op jit(solution)/shard_map/ppermute | solution.py:343
  76.3 3.1 %collective-permute-done.4.refs_2_ = bf16[1,192,512]{2,1,0:T(8,128)(2,1)S(1)} collective-permute-done((bf16[1,192,512]{2,1,0:T(8,128)(2,1)S(1)}, bf16[1,192,512]{2,1,0:T(8,128)(2,1)S(1)}, u32[]{:S(2)}, u32[]{:S(2)}) %collective-permute-start.4) | collective-permute-done | bytes 196640 | tf_op jit(solution)/shard_map/ppermute | solution.py:343
  79.4 1.4 %collective-permute-done.5.refs_3_ = bf16[1,192,512]{2,1,0:T(8,128)(2,1)S(1)} collective-permute-done((bf16[1,192,512]{2,1,0:T(8,128)(2,1)S(1)}, bf16[1,192,512]{2,1,0:T(8,128)(2,1)S(1)}, u32[]{:S(2)}, u32[]{:S(2)}) %collective-permute-start.5) | collective-permute-done | bytes 196640 | tf_op jit(solution)/shard_map/ppermute | solution.py:343
  81.5 5.8 %collective-permute-done.21 = bf16[256,512]{1,0:T(8,128)(2,1)S(1)} collective-permute-done((bf16[256,512]{1,0:T(8,128)(2,1)S(1)}, bf16[256,512]{1,0:T(8,128)(2,1)S(1)}, u32[]{:S(2)}, u32[]{:S(2)}) %collective-permute-start.21) | collective-permute-done | bytes 262176 | tf_op jit(solution)/shard_map/ppermute | solution.py:343
  87.5 1.5 %collective-permute-done.22 = bf16[256,512]{1,0:T(8,128)(2,1)S(1)} collective-permute-done((bf16[256,512]{1,0:T(8,128)(2,1)S(1)}, bf16[256,512]{1,0:T(8,128)(2,1)S(1)}, u32[]{:S(2)}, u32[]{:S(2)}) %collective-permute-start.22) | collective-permute-done | bytes 262176 | tf_op jit(solution)/shard_map/ppermute | solution.py:343
  92.1 1.5 %collective-permute-start.23 = (bf16[160,128]{1,0:T(8,128)(2,1)S(1)}, bf16[160,128]{1,0:T(8,128)(2,1)S(1)}, u32[]{:S(2)}, u32[]{:S(2)}) collective-permute-start(bf16[160,128]{1,0:T(8,128)(2,1)S(1)} %get-tuple-element.101), channel_id=1, source_target_pairs={{0,2},{2,0},{4,6},{6,4},{8,10},{10,8},{12,14},{14,12},{16,18},{18,... | collective-permute-start | bytes 122888 | tf_op jit(solution)/shard_map/ppermute | solution.py:343
  93.6 1.8 %collective-permute-done.25 = bf16[160,128]{1,0:T(8,128)(2,1)S(1)} collective-permute-done((bf16[160,128]{1,0:T(8,128)(2,1)S(1)}, bf16[160,128]{1,0:T(8,128)(2,1)S(1)}, u32[]{:S(2)}, u32[]{:S(2)}) %collective-permute-start.25) | collective-permute-done | bytes 40992 | tf_op jit(solution)/shard_map/ppermute | solution.py:343
  96.1 2.6 %collective-permute-start.28 = (bf16[160,128]{1,0:T(8,128)(2,1)S(1)}, bf16[160,128]{1,0:T(8,128)(2,1)S(1)}, u32[]{:S(2)}, u32[]{:S(2)}) collective-permute-start(bf16[160,128]{1,0:T(8,128)(2,1)S(1)} %add_convert_fusion.1), channel_id=1, source_target_pairs={{0,24},{2,26},{4,28},{6,30},{8,16},{10,18},{12,20},{14,22},{16,8},... | collective-permute-start | bytes 122888 | tf_op jit(solution)/shard_map/ppermute | solution.py:343
  98.8 1.8 %collective-permute-start.26 = (bf16[160,128]{1,0:T(8,128)(2,1)S(1)}, bf16[160,128]{1,0:T(8,128)(2,1)S(1)}, u32[]{:S(2)}, u32[]{:S(2)}) collective-permute-start(bf16[160,128]{1,0:T(8,128)(2,1)S(1)} %add_convert_fusion.1), channel_id=1, source_target_pairs={{0,8},{2,10},{4,12},{6,14},{8,0},{10,2},{12,4},{14,6},{16,24},{18,... | collective-permute-start | bytes 122888 | tf_op jit(solution)/shard_map/ppermute | solution.py:343
  100.6 1.6 %collective-permute-done.28 = bf16[160,128]{1,0:T(8,128)(2,1)S(1)} collective-permute-done((bf16[160,128]{1,0:T(8,128)(2,1)S(1)}, bf16[160,128]{1,0:T(8,128)(2,1)S(1)}, u32[]{:S(2)}, u32[]{:S(2)}) %collective-permute-start.28) | collective-permute-done | bytes 40992 | tf_op jit(solution)/shard_map/ppermute | solution.py:343
  102.2 1.5 %collective-permute-done.27 = bf16[160,128]{1,0:T(8,128)(2,1)S(1)} collective-permute-done((bf16[160,128]{1,0:T(8,128)(2,1)S(1)}, bf16[160,128]{1,0:T(8,128)(2,1)S(1)}, u32[]{:S(2)}, u32[]{:S(2)}) %collective-permute-start.27) | collective-permute-done | bytes 40992 | tf_op jit(solution)/shard_map/ppermute | solution.py:343
  103.7 1.3 %collective-permute-start.31 = (bf16[160,128]{1,0:T(8,128)(2,1)S(1)}, bf16[160,128]{1,0:T(8,128)(2,1)S(1)}, u32[]{:S(2)}, u32[]{:S(2)}) collective-permute-start(bf16[160,128]{1,0:T(8,128)(2,1)S(1)} %add_convert_fusion), channel_id=1, source_target_pairs={{0,6},{2,4},{4,2},{6,0},{8,14},{10,12},{12,10},{14,8},{16,22},{18,... | collective-permute-start | bytes 122888 | tf_op jit(solution)/shard_map/ppermute | solution.py:343
  107.3 1.4 %collective-permute-done.31 = bf16[160,128]{1,0:T(8,128)(2,1)S(1)} collective-permute-done((bf16[160,128]{1,0:T(8,128)(2,1)S(1)}, bf16[160,128]{1,0:T(8,128)(2,1)S(1)}, u32[]{:S(2)}, u32[]{:S(2)}) %collective-permute-start.31) | collective-permute-done | bytes 40992 | tf_op jit(solution)/shard_map/ppermute | solution.py:343
  110.2 1.4 %collective-permute-done.32.other_gram_ref = bf16[5,128,128]{2,1,0:T(8,128)(2,1)S(1)} collective-permute-done((bf16[5,128,128]{2,1,0:T(8,128)(2,1)S(1)}, bf16[5,128,128]{2,1,0:T(8,128)(2,1)S(1)}, u32[]{:S(2)}, u32[]{:S(2)}) %collective-permute-start.32) | collective-permute-done | bytes 163872 | tf_op jit(solution)/shard_map/ppermute | solution.py:343
  111.6 7.6 %root.1 = f32[256,512]{1,0:T(8,128)} custom-call(s32[1]{0:T(128)} %bitcast.feat_ref.place_ref, bf16[5,128,128]{2,1,0:T(8,128)(2,1)S(1)} %bitcast.39, bf16[5,128,128]{2,1,0:T(8,128)(2,1)S(1)} %collective-permute-done.32.other_gram_ref, bf16[256,512]{1,0:T(8,128)(2,1)S(1)} %fusion.1.mine_ref), custom_call_target="tpu_custom_call" | custom-call | tf_op jit(solution)/shard_map/root/pallas_call | solution.py:330
  (69 shorter events, 23.6 us)
Async XLA Ops:
  6.8 29.6 %all-to-all-start = ((bf16[16,192,128]{2,1,0:T(8,128)(2,1)}), bf16[16,192,128]{2,1,0:T(8,128)(2,1)S(1)}, u32[]{:S(2)}, u32[]{:S(2)}) async-start(bf16[16,192,128]{2,1,0:T(8,128)(2,1)} %get-tuple-element.52), calls=%async_computation | async-start | bytes 1572864 | tf_op jit(solution)/shard_map/all_to_all | solution.py:430
  15.3 13.2 %collective-permute-start = (f32[8,512]{1,0:T(8,128)}, f32[8,512]{1,0:T(8,128)S(1)}, u32[]{:S(2)}, u32[]{:S(2)}) collective-permute-start(f32[8,512]{1,0:T(8,128)} %get-tuple-element.63.refs_0_), channel_id=1, source_target_pairs={{0,8},{2,10},{4,12},{6,14},{8,0},{10,2},{12,4},{14,6},{16,24},{18,... | collective-permute-start | bytes 49160 | tf_op jit(solution)/shard_map/ppermute | solution.py:343
  17.1 19.3 %collective-permute-start.1 = (f32[8,512]{1,0:T(8,128)}, f32[8,512]{1,0:T(8,128)S(1)}, u32[]{:S(2)}, u32[]{:S(2)}) collective-permute-start(f32[8,512]{1,0:T(8,128)} %get-tuple-element.63.refs_0_), channel_id=1, source_target_pairs={{0,16},{2,18},{4,20},{6,22},{8,24},{10,26},{12,28},{14,30},{16,0},... | collective-permute-start | bytes 49160 | tf_op jit(solution)/shard_map/ppermute | solution.py:343
  19.5 16.9 %collective-permute-start.2 = (f32[8,512]{1,0:T(8,128)}, f32[8,512]{1,0:T(8,128)S(1)}, u32[]{:S(2)}, u32[]{:S(2)}) collective-permute-start(f32[8,512]{1,0:T(8,128)} %get-tuple-element.63.refs_0_), channel_id=1, source_target_pairs={{0,24},{2,26},{4,28},{6,30},{8,16},{10,18},{12,20},{14,22},{16,8},... | collective-permute-start | bytes 49160 | tf_op jit(solution)/shard_map/ppermute | solution.py:343
  39.9 14.3 %collective-permute-start.12 = (bf16[1,192,512]{2,1,0:T(8,128)(2,1)S(1)}, bf16[1,192,512]{2,1,0:T(8,128)(2,1)S(1)}, u32[]{:S(2)}, u32[]{:S(2)}) collective-permute-start(bf16[1,192,512]{2,1,0:T(8,128)(2,1)S(1)} %get-tuple-element.55), channel_id=1, source_target_pairs={{0,2},{2,0},{4,6},{6,4},{8,10},{10,8},{12,14},{14,12},{16,18},{18,... | collective-permute-start | bytes 589832 | tf_op jit(solution)/shard_map/ppermute | solution.py:343
  41.5 13.4 %collective-permute-start.13 = (bf16[1,192,512]{2,1,0:T(8,128)(2,1)S(1)}, bf16[1,192,512]{2,1,0:T(8,128)(2,1)S(1)}, u32[]{:S(2)}, u32[]{:S(2)}) collective-permute-start(bf16[1,192,512]{2,1,0:T(8,128)(2,1)S(1)} %get-tuple-element.56), channel_id=1, source_target_pairs={{0,4},{2,6},{4,0},{6,2},{8,12},{10,14},{12,8},{14,10},{16,20},{18,... | collective-permute-start | bytes 589832 | tf_op jit(solution)/shard_map/ppermute | solution.py:343
  42.9 13.4 %collective-permute-start.14 = (bf16[1,192,512]{2,1,0:T(8,128)(2,1)S(1)}, bf16[1,192,512]{2,1,0:T(8,128)(2,1)S(1)}, u32[]{:S(2)}, u32[]{:S(2)}) collective-permute-start(bf16[1,192,512]{2,1,0:T(8,128)(2,1)S(1)} %get-tuple-element.57), channel_id=1, source_target_pairs={{0,6},{2,4},{4,2},{6,0},{8,14},{10,12},{12,10},{14,8},{16,22},{18,... | collective-permute-start | bytes 589832 | tf_op jit(solution)/shard_map/ppermute | solution.py:343
  44.8 13.6 %collective-permute-start.9 = (bf16[1,192,512]{2,1,0:T(8,128)(2,1)S(1)}, bf16[1,192,512]{2,1,0:T(8,128)(2,1)S(1)}, u32[]{:S(2)}, u32[]{:S(2)}) collective-permute-start(bf16[1,192,512]{2,1,0:T(8,128)(2,1)S(1)} %get-tuple-element.60), channel_id=1, source_target_pairs={{0,2},{2,0},{4,6},{6,4},{8,10},{10,8},{12,14},{14,12},{16,18},{18,... | collective-permute-start | bytes 589832 | tf_op jit(solution)/shard_map/ppermute | solution.py:343
  46.3 12.7 %collective-permute-start.10 = (bf16[1,192,512]{2,1,0:T(8,128)(2,1)S(1)}, bf16[1,192,512]{2,1,0:T(8,128)(2,1)S(1)}, u32[]{:S(2)}, u32[]{:S(2)}) collective-permute-start(bf16[1,192,512]{2,1,0:T(8,128)(2,1)S(1)} %get-tuple-element.61), channel_id=1, source_target_pairs={{0,4},{2,6},{4,0},{6,2},{8,12},{10,14},{12,8},{14,10},{16,20},{18,... | collective-permute-start | bytes 589832 | tf_op jit(solution)/shard_map/ppermute | solution.py:343
  54.2 8.9 %collective-permute-start.11 = (bf16[1,192,512]{2,1,0:T(8,128)(2,1)S(1)}, bf16[1,192,512]{2,1,0:T(8,128)(2,1)S(1)}, u32[]{:S(2)}, u32[]{:S(2)}) collective-permute-start(bf16[1,192,512]{2,1,0:T(8,128)(2,1)S(1)} %get-tuple-element.62), channel_id=1, source_target_pairs={{0,6},{2,4},{4,2},{6,0},{8,14},{10,12},{12,10},{14,8},{16,22},{18,... | collective-permute-start | bytes 589832 | tf_op jit(solution)/shard_map/ppermute | solution.py:343
  54.9 9.9 %collective-permute-start.6 = (bf16[1,192,512]{2,1,0:T(8,128)(2,1)S(1)}, bf16[1,192,512]{2,1,0:T(8,128)(2,1)S(1)}, u32[]{:S(2)}, u32[]{:S(2)}) collective-permute-start(bf16[1,192,512]{2,1,0:T(8,128)(2,1)S(1)} %get-tuple-element.69), channel_id=1, source_target_pairs={{0,2},{2,0},{4,6},{6,4},{8,10},{10,8},{12,14},{14,12},{16,18},{18,... | collective-permute-start | bytes 589832 | tf_op jit(solution)/shard_map/ppermute | solution.py:343
  56.3 11.5 %collective-permute-start.7 = (bf16[1,192,512]{2,1,0:T(8,128)(2,1)S(1)}, bf16[1,192,512]{2,1,0:T(8,128)(2,1)S(1)}, u32[]{:S(2)}, u32[]{:S(2)}) collective-permute-start(bf16[1,192,512]{2,1,0:T(8,128)(2,1)S(1)} %get-tuple-element.70), channel_id=1, source_target_pairs={{0,4},{2,6},{4,0},{6,2},{8,12},{10,14},{12,8},{14,10},{16,20},{18,... | collective-permute-start | bytes 589832 | tf_op jit(solution)/shard_map/ppermute | solution.py:343
  58.4 9.5 %collective-permute-start.8 = (bf16[1,192,512]{2,1,0:T(8,128)(2,1)S(1)}, bf16[1,192,512]{2,1,0:T(8,128)(2,1)S(1)}, u32[]{:S(2)}, u32[]{:S(2)}) collective-permute-start(bf16[1,192,512]{2,1,0:T(8,128)(2,1)S(1)} %get-tuple-element.71), channel_id=1, source_target_pairs={{0,6},{2,4},{4,2},{6,0},{8,14},{10,12},{12,10},{14,8},{16,22},{18,... | collective-permute-start | bytes 589832 | tf_op jit(solution)/shard_map/ppermute | solution.py:343
  59.0 4.8 %collective-permute-start.15 = (bf16[1,256,512]{2,1,0:T(8,128)(2,1)S(1)}, bf16[1,256,512]{2,1,0:T(8,128)(2,1)S(1)}, u32[]{:S(2)}, u32[]{:S(2)}) collective-permute-start(bf16[1,256,512]{2,1,0:T(8,128)(2,1)S(1)} %get-tuple-element.83), channel_id=1, source_target_pairs={{0,1},{1,0},{2,3},{3,2},{4,5},{5,4},{6,7},{7,6},{8,9},{9,8},{10,11... | collective-permute-start | bytes 786440 | tf_op jit(solution)/shard_map/ppermute | solution.py:343
  63.7 7.0 %collective-permute-start.16 = (bf16[1,256,512]{2,1,0:T(8,128)(2,1)S(1)}, bf16[1,256,512]{2,1,0:T(8,128)(2,1)S(1)}, u32[]{:S(2)}, u32[]{:S(2)}) collective-permute-start(bf16[1,256,512]{2,1,0:T(8,128)(2,1)S(1)} %get-tuple-element.89), channel_id=1, source_target_pairs={{0,1},{1,0},{2,3},{3,2},{4,5},{5,4},{6,7},{7,6},{8,9},{9,8},{10,11... | collective-permute-start | bytes 786440 | tf_op jit(solution)/shard_map/ppermute | solution.py:343
  63.9 8.8 %collective-permute-start.17 = (bf16[256,512]{1,0:T(8,128)(2,1)S(1)}, bf16[256,512]{1,0:T(8,128)(2,1)S(1)}, u32[]{:S(2)}, u32[]{:S(2)}) collective-permute-start(bf16[256,512]{1,0:T(8,128)(2,1)S(1)} %add_bitcast_fusion.1), channel_id=1, source_target_pairs={{0,8},{2,10},{4,12},{6,14},{8,0},{10,2},{12,4},{14,6},{16,24},{18,... | collective-permute-start | bytes 786440 | tf_op jit(solution)/shard_map/ppermute | solution.py:343
  68.5 5.3 %collective-permute-start.18 = (bf16[1,256,512]{2,1,0:T(8,128)(2,1)S(1)}, bf16[1,256,512]{2,1,0:T(8,128)(2,1)S(1)}, u32[]{:S(2)}, u32[]{:S(2)}) collective-permute-start(bf16[1,256,512]{2,1,0:T(8,128)(2,1)S(1)} %get-tuple-element.90), channel_id=1, source_target_pairs={{0,1},{1,0},{2,3},{3,2},{4,5},{5,4},{6,7},{7,6},{8,9},{9,8},{10,11... | collective-permute-start | bytes 786440 | tf_op jit(solution)/shard_map/ppermute | solution.py:343
  68.5 7.8 %collective-permute-start.3 = (bf16[1,192,512]{2,1,0:T(8,128)(2,1)S(1)}, bf16[1,192,512]{2,1,0:T(8,128)(2,1)S(1)}, u32[]{:S(2)}, u32[]{:S(2)}) collective-permute-start(bf16[1,192,512]{2,1,0:T(8,128)(2,1)S(1)} %get-tuple-element.74), channel_id=1, source_target_pairs={{0,2},{2,0},{4,6},{6,4},{8,10},{10,8},{12,14},{14,12},{16,18},{18,... | collective-permute-start | bytes 589832 | tf_op jit(solution)/shard_map/ppermute | solution.py:343
  69.6 9.8 %collective-permute-start.4 = (bf16[1,192,512]{2,1,0:T(8,128)(2,1)S(1)}, bf16[1,192,512]{2,1,0:T(8,128)(2,1)S(1)}, u32[]{:S(2)}, u32[]{:S(2)}) collective-permute-start(bf16[1,192,512]{2,1,0:T(8,128)(2,1)S(1)} %get-tuple-element.75), channel_id=1, source_target_pairs={{0,4},{2,6},{4,0},{6,2},{8,12},{10,14},{12,8},{14,10},{16,20},{18,... | collective-permute-start | bytes 589832 | tf_op jit(solution)/shard_map/ppermute | solution.py:343
  70.7 10.1 %collective-permute-start.5 = (bf16[1,192,512]{2,1,0:T(8,128)(2,1)S(1)}, bf16[1,192,512]{2,1,0:T(8,128)(2,1)S(1)}, u32[]{:S(2)}, u32[]{:S(2)}) collective-permute-start(bf16[1,192,512]{2,1,0:T(8,128)(2,1)S(1)} %get-tuple-element.76), channel_id=1, source_target_pairs={{0,6},{2,4},{4,2},{6,0},{8,14},{10,12},{12,10},{14,8},{16,22},{18,... | collective-permute-start | bytes 589832 | tf_op jit(solution)/shard_map/ppermute | solution.py:343
  72.8 14.5 %collective-permute-start.21 = (bf16[256,512]{1,0:T(8,128)(2,1)S(1)}, bf16[256,512]{1,0:T(8,128)(2,1)S(1)}, u32[]{:S(2)}, u32[]{:S(2)}) collective-permute-start(bf16[256,512]{1,0:T(8,128)(2,1)S(1)} %bitcast_add_fusion.1), channel_id=1, source_target_pairs={{0,16},{2,18},{4,20},{6,22},{8,24},{10,26},{12,28},{14,30},{16,0},... | collective-permute-start | bytes 786440 | tf_op jit(solution)/shard_map/ppermute | solution.py:343
  73.9 13.4 %collective-permute-start.20 = (bf16[256,512]{1,0:T(8,128)(2,1)S(1)}, bf16[256,512]{1,0:T(8,128)(2,1)S(1)}, u32[]{:S(2)}, u32[]{:S(2)}) collective-permute-start(bf16[256,512]{1,0:T(8,128)(2,1)S(1)} %add_bitcast_fusion), channel_id=1, source_target_pairs={{0,8},{2,10},{4,12},{6,14},{8,0},{10,2},{12,4},{14,6},{16,24},{18,... | collective-permute-start | bytes 786440 | tf_op jit(solution)/shard_map/ppermute | solution.py:343
  81.4 5.9 %collective-permute-start.19 = (bf16[1,256,512]{2,1,0:T(8,128)(2,1)S(1)}, bf16[1,256,512]{2,1,0:T(8,128)(2,1)S(1)}, u32[]{:S(2)}, u32[]{:S(2)}) collective-permute-start(bf16[1,256,512]{2,1,0:T(8,128)(2,1)S(1)} %get-tuple-element.96), channel_id=1, source_target_pairs={{0,1},{1,0},{2,3},{3,2},{4,5},{5,4},{6,7},{7,6},{8,9},{9,8},{10,11... | collective-permute-start | bytes 786440 | tf_op jit(solution)/shard_map/ppermute | solution.py:343
  90.0 5.4 %collective-permute-start.25 = (bf16[160,128]{1,0:T(8,128)(2,1)S(1)}, bf16[160,128]{1,0:T(8,128)(2,1)S(1)}, u32[]{:S(2)}, u32[]{:S(2)}) collective-permute-start(bf16[160,128]{1,0:T(8,128)(2,1)S(1)} %get-tuple-element.102), channel_id=1, source_target_pairs={{0,6},{2,4},{4,2},{6,0},{8,14},{10,12},{12,10},{14,8},{16,22},{18,... | collective-permute-start | bytes 122888 | tf_op jit(solution)/shard_map/ppermute | solution.py:343
  90.9 4.5 %collective-permute-start.24 = (bf16[160,128]{1,0:T(8,128)(2,1)S(1)}, bf16[160,128]{1,0:T(8,128)(2,1)S(1)}, u32[]{:S(2)}, u32[]{:S(2)}) collective-permute-start(bf16[160,128]{1,0:T(8,128)(2,1)S(1)} %get-tuple-element.103), channel_id=1, source_target_pairs={{0,4},{2,6},{4,0},{6,2},{8,12},{10,14},{12,8},{14,10},{16,20},{18,... | collective-permute-start | bytes 122888 | tf_op jit(solution)/shard_map/ppermute | solution.py:343
  92.1 4.0 %collective-permute-start.23 = (bf16[160,128]{1,0:T(8,128)(2,1)S(1)}, bf16[160,128]{1,0:T(8,128)(2,1)S(1)}, u32[]{:S(2)}, u32[]{:S(2)}) collective-permute-start(bf16[160,128]{1,0:T(8,128)(2,1)S(1)} %get-tuple-element.101), channel_id=1, source_target_pairs={{0,2},{2,0},{4,6},{6,4},{8,10},{10,8},{12,14},{14,12},{16,18},{18,... | collective-permute-start | bytes 122888 | tf_op jit(solution)/shard_map/ppermute | solution.py:343
  96.1 6.1 %collective-permute-start.28 = (bf16[160,128]{1,0:T(8,128)(2,1)S(1)}, bf16[160,128]{1,0:T(8,128)(2,1)S(1)}, u32[]{:S(2)}, u32[]{:S(2)}) collective-permute-start(bf16[160,128]{1,0:T(8,128)(2,1)S(1)} %add_convert_fusion.1), channel_id=1, source_target_pairs={{0,24},{2,26},{4,28},{6,30},{8,16},{10,18},{12,20},{14,22},{16,8},... | collective-permute-start | bytes 122888 | tf_op jit(solution)/shard_map/ppermute | solution.py:343
  98.8 4.9 %collective-permute-start.27 = (bf16[160,128]{1,0:T(8,128)(2,1)S(1)}, bf16[160,128]{1,0:T(8,128)(2,1)S(1)}, u32[]{:S(2)}, u32[]{:S(2)}) collective-permute-start(bf16[160,128]{1,0:T(8,128)(2,1)S(1)} %add_convert_fusion.1), channel_id=1, source_target_pairs={{0,16},{2,18},{4,20},{6,22},{8,24},{10,26},{12,28},{14,30},{16,0},... | collective-permute-start | bytes 122888 | tf_op jit(solution)/shard_map/ppermute | solution.py:343
  98.8 4.9 %collective-permute-start.26 = (bf16[160,128]{1,0:T(8,128)(2,1)S(1)}, bf16[160,128]{1,0:T(8,128)(2,1)S(1)}, u32[]{:S(2)}, u32[]{:S(2)}) collective-permute-start(bf16[160,128]{1,0:T(8,128)(2,1)S(1)} %add_convert_fusion.1), channel_id=1, source_target_pairs={{0,8},{2,10},{4,12},{6,14},{8,0},{10,2},{12,4},{14,6},{16,24},{18,... | collective-permute-start | bytes 122888 | tf_op jit(solution)/shard_map/ppermute | solution.py:343
  103.7 5.0 %collective-permute-start.31 = (bf16[160,128]{1,0:T(8,128)(2,1)S(1)}, bf16[160,128]{1,0:T(8,128)(2,1)S(1)}, u32[]{:S(2)}, u32[]{:S(2)}) collective-permute-start(bf16[160,128]{1,0:T(8,128)(2,1)S(1)} %add_convert_fusion), channel_id=1, source_target_pairs={{0,6},{2,4},{4,2},{6,0},{8,14},{10,12},{12,10},{14,8},{16,22},{18,... | collective-permute-start | bytes 122888 | tf_op jit(solution)/shard_map/ppermute | solution.py:343
  105.0 4.1 %collective-permute-start.30 = (bf16[160,128]{1,0:T(8,128)(2,1)S(1)}, bf16[160,128]{1,0:T(8,128)(2,1)S(1)}, u32[]{:S(2)}, u32[]{:S(2)}) collective-permute-start(bf16[160,128]{1,0:T(8,128)(2,1)S(1)} %add_convert_fusion), channel_id=1, source_target_pairs={{0,4},{2,6},{4,0},{6,2},{8,12},{10,14},{12,8},{14,10},{16,20},{18,... | collective-permute-start | bytes 122888 | tf_op jit(solution)/shard_map/ppermute | solution.py:343
  106.0 4.0 %collective-permute-start.29 = (bf16[160,128]{1,0:T(8,128)(2,1)S(1)}, bf16[160,128]{1,0:T(8,128)(2,1)S(1)}, u32[]{:S(2)}, u32[]{:S(2)}) collective-permute-start(bf16[160,128]{1,0:T(8,128)(2,1)S(1)} %add_convert_fusion), channel_id=1, source_target_pairs={{0,2},{2,0},{4,6},{6,4},{8,10},{10,8},{12,14},{14,12},{16,18},{18,... | collective-permute-start | bytes 122888 | tf_op jit(solution)/shard_map/ppermute | solution.py:343
  (6 other events, 27.0 us)

commit v6 on v5

--- a/solution.py
+++ b/solution.py
@@ -280,18 +280,13 @@
     return high, (value - high.astype(f32)).astype(bf16)
 
 
-def left(value):
-    high, low = halves(value)
-    return jnp.concatenate([low, high, high], axis=1)
-
-
-def right(value):
-    high, low = halves(value)
-    return jnp.concatenate([high, low, high], axis=0)
+def dot(a, b):
+    return jnp.dot(a, b, preferred_element_type=f32)
 
 
 def dot3(a, b):
-    return jnp.dot(a, b, preferred_element_type=f32)
+    (ah, al), (bh, bl) = halves(a), halves(b)
+    return dot(jnp.concatenate([al, ah, ah], axis=1), jnp.concatenate([bh, bl, bh], axis=0))
 
 
 def root_kernel(samples, place_ref, mine_gram_ref, other_gram_ref, mine_ref, out_ref, gram):
@@ -309,19 +304,21 @@
     ident = jnp.where(rows == lax.broadcasted_iota(jnp.int32, (width, width), 1), 1.0, 0.0)
     total = gram[...] + ridge * samples * ident
     scale = jnp.sum(total * ident, axis=(0, 1), keepdims=True) / width
-    current = total / scale
+    gap = 0.5 * ident - 0.5 * (total / scale)
+    high, low = halves(gap)
     mine = mine_ref[...]
-    for step in range(root_steps - 1):
-        middle = 1.5 * ident - 0.5 * current
-        by = right(middle)
-        if step == 0:
-            value = dot3(jnp.concatenate([mine, mine], axis=1), by[width:])
-        else:
-            value = dot3(left(value), by)
-        if step + 2 < root_steps:
-            current = dot3(left(dot3(left(current), by)), by)
-    moved = dot3(left(dot3(left(dot3(left(value), right(current))), by)), by)
-    value = 1.5 * value - 0.5 * moved
+    value = mine.astype(f32) + dot(jnp.concatenate([mine, mine], axis=1), jnp.concatenate([low, high], axis=0))
+    square = dot3(gap, gap)
+    gap = 1.5 * square + dot3(square, gap)
+    for _ in range(root_steps - 3):
+        high = gap.astype(bf16)
+        value = value + dot(value.astype(bf16), high)
+        square = dot(high, high)
+        gap = 1.5 * square + dot(square.astype(bf16), high)
+    high = gap.astype(bf16)
+    value = value + dot(value.astype(bf16), high)
+    moved = dot(dot(value.astype(bf16), high).astype(bf16), high)
+    value = value + 1.5 * moved + dot(moved.astype(bf16), high)
     out_ref[...] = (math.sqrt(samples) * lax.rsqrt(scale)) * value
 
 

time: 120 us -> 117 us (0.975)
  Pallas kernels: 26.6 us -> 24.1 us
    pallas_call x1, Pallas kernels: 7.63 us -> 5.11 us  [whiten(): pl.pallas_call(functools.partial(root_kernel, samples), out_shape=jax.Sha...]
  transfers between devices with their start and end apart: 34 -> 34, of which waited for: 18 -> 18; matrix products, arithmetic and copies ran while one was open for 0% -> 0% of each run, Pallas kernels for 8% -> 9%
where the time goes in v6:
time: 117 us
  waiting for transfers between devices  47.4 us (41%)
  starting transfers between devices  42.1 us (36%)
  Pallas kernels  24.1 us (21%)
  local copies, waits for them, and re-layouts  2.25 us (2%)
    ppermute x33, waiting for transfers between devices, crossed(): lax.ppermute(value, axis, [(source, source ^ bits) for source in range(co...  47.4 us
    ppermute x33, starting transfers between devices, crossed(): lax.ppermute(value, axis, [(source, source ^ bits) for source in range(co...  33.6 us
    all_to_all x1, starting transfers between devices, local(): tiles = lax.all_to_all(send, 'dp', split_axis=0, concat_axis=0, tiled=True)  8.51 us
    pallas_call x1, Pallas kernels, pack(): pl.pallas_call(functools.partial(pack_kernel, per_dev, bound), out_shape=...  6.76 us
    pallas_call x4, Pallas kernels, product(): pl.pallas_call(functools.partial(product_kernel, bound, joint, groups, aw...  5.32 us
    pallas_call x1, Pallas kernels, whiten(): pl.pallas_call(functools.partial(root_kernel, samples), out_shape=jax.Sha...  5.11 us
    pallas_call x1, Pallas kernels, choose(): pl.pallas_call(functools.partial(choose_kernel, k_j, slots, inner), out_s...  3.72 us
  transfers between devices with their start and end apart: 34, of which 18 were waited for; matrix products, arithmetic and copies ran while one was open for 0% of the time, Pallas kernels for 9%

profile of v6, /device:TPU:0, one launch (start us, length us, event | category | flops | bytes accessed | tf_op | source)
XLA Modules:
  0.0 116.7 jit_solution(10725897694584829284)
XLA Ops:
  0.0 6.8 %pack.1 = (bf16[16,192,128]{2,1,0:T(8,128)(2,1)}, f32[8,512]{1,0:T(8,128)}) custom-call(s32[4,512]{1,0:T(4,128)} %bitcast.49, bf16[2048,128]{1,0:T(8,128)(2,1)} %bitcast.44), custom_call_target="tpu_custom_call" | custom-call | tf_op jit(solution)/shard_map/pack/pallas_call | solution.py:94
  6.8 8.5 %all-to-all-start = ((bf16[16,192,128]{2,1,0:T(8,128)(2,1)}), bf16[16,192,128]{2,1,0:T(8,128)(2,1)S(1)}, u32[]{:S(2)}, u32[]{:S(2)}) async-start(bf16[16,192,128]{2,1,0:T(8,128)(2,1)} %get-tuple-element.52), calls=%async_computation | async-start | bytes 1572864 | tf_op jit(solution)/shard_map/all_to_all | solution.py:427
  15.3 1.8 %collective-permute-start = (f32[8,512]{1,0:T(8,128)}, f32[8,512]{1,0:T(8,128)S(1)}, u32[]{:S(2)}, u32[]{:S(2)}) collective-permute-start(f32[8,512]{1,0:T(8,128)} %get-tuple-element.63.refs_0_), channel_id=1, source_target_pairs={{0,8},{2,10},{4,12},{6,14},{8,0},{10,2},{12,4},{14,6},{16,24},{18,... | collective-permute-start | bytes 49160 | tf_op jit(solution)/shard_map/ppermute | solution.py:340
  17.1 2.4 %collective-permute-start.1 = (f32[8,512]{1,0:T(8,128)}, f32[8,512]{1,0:T(8,128)S(1)}, u32[]{:S(2)}, u32[]{:S(2)}) collective-permute-start(f32[8,512]{1,0:T(8,128)} %get-tuple-element.63.refs_0_), channel_id=1, source_target_pairs={{0,16},{2,18},{4,20},{6,22},{8,24},{10,26},{12,28},{14,30},{16,0},... | collective-permute-start | bytes 49160 | tf_op jit(solution)/shard_map/ppermute | solution.py:340
  19.8 8.7 %collective-permute-done.refs_1_ = f32[8,512]{1,0:T(8,128)S(1)} collective-permute-done((f32[8,512]{1,0:T(8,128)}, f32[8,512]{1,0:T(8,128)S(1)}, u32[]{:S(2)}, u32[]{:S(2)}) %collective-permute-start) | collective-permute-done | bytes 16416 | tf_op jit(solution)/shard_map/ppermute | solution.py:340
  28.5 7.9 %collective-permute-done.1.refs_2_ = f32[8,512]{1,0:T(8,128)S(1)} collective-permute-done((f32[8,512]{1,0:T(8,128)}, f32[8,512]{1,0:T(8,128)S(1)}, u32[]{:S(2)}, u32[]{:S(2)}) %collective-permute-start.1) | collective-permute-done | bytes 16416 | tf_op jit(solution)/shard_map/ppermute | solution.py:340
  36.4 2.2 %copy-done = bf16[32,1,128,512]{3,2,1,0:T(8,128)(2,1)S(1)} copy-done((bf16[32,1,128,512]{3,2,1,0:T(8,128)(2,1)S(1)}, bf16[32,1,128,512]{3,2,1,0:T(8,128)(2,1)}, u32[]{:S(2)}) %copy-start) | copy-done | bytes 4194328
  39.9 1.5 %collective-permute-start.12 = (bf16[1,192,512]{2,1,0:T(8,128)(2,1)S(1)}, bf16[1,192,512]{2,1,0:T(8,128)(2,1)S(1)}, u32[]{:S(2)}, u32[]{:S(2)}) collective-permute-start(bf16[1,192,512]{2,1,0:T(8,128)(2,1)S(1)} %get-tuple-element.55), channel_id=1, source_target_pairs={{0,2},{2,0},{4,6},{6,4},{8,10},{10,8},{12,14},{14,12},{16,18},{18,... | collective-permute-start | bytes 589832 | tf_op jit(solution)/shard_map/ppermute | solution.py:340
  41.5 1.5 %collective-permute-start.13 = (bf16[1,192,512]{2,1,0:T(8,128)(2,1)S(1)}, bf16[1,192,512]{2,1,0:T(8,128)(2,1)S(1)}, u32[]{:S(2)}, u32[]{:S(2)}) collective-permute-start(bf16[1,192,512]{2,1,0:T(8,128)(2,1)S(1)} %get-tuple-element.56), channel_id=1, source_target_pairs={{0,4},{2,6},{4,0},{6,2},{8,12},{10,14},{12,8},{14,10},{16,20},{18,... | collective-permute-start | bytes 589832 | tf_op jit(solution)/shard_map/ppermute | solution.py:340
  44.8 1.5 %collective-permute-start.9 = (bf16[1,192,512]{2,1,0:T(8,128)(2,1)S(1)}, bf16[1,192,512]{2,1,0:T(8,128)(2,1)S(1)}, u32[]{:S(2)}, u32[]{:S(2)}) collective-permute-start(bf16[1,192,512]{2,1,0:T(8,128)(2,1)S(1)} %get-tuple-element.60), channel_id=1, source_target_pairs={{0,2},{2,0},{4,6},{6,4},{8,10},{10,8},{12,14},{14,12},{16,18},{18,... | collective-permute-start | bytes 589832 | tf_op jit(solution)/shard_map/ppermute | solution.py:340
  46.3 1.5 %collective-permute-start.10 = (bf16[1,192,512]{2,1,0:T(8,128)(2,1)S(1)}, bf16[1,192,512]{2,1,0:T(8,128)(2,1)S(1)}, u32[]{:S(2)}, u32[]{:S(2)}) collective-permute-start(bf16[1,192,512]{2,1,0:T(8,128)(2,1)S(1)} %get-tuple-element.61), channel_id=1, source_target_pairs={{0,4},{2,6},{4,0},{6,2},{8,12},{10,14},{12,8},{14,10},{16,20},{18,... | collective-permute-start | bytes 589832 | tf_op jit(solution)/shard_map/ppermute | solution.py:340
  47.8 3.7 %choose.1.hits_ref = bf16[4,512,768]{2,1,0:T(8,128)(2,1)S(1)} custom-call(s32[2]{0:T(128)S(1)} %pad_add_fusion.where_ref.place_ref, f32[8,512]{1,0:T(8,128)S(1)} %copy-done.2, f32[8,512]{1,0:T(8,128)S(1)} %collective-permute-done.refs_1_, f32[8,512]{1,0:T(8,128)S(1)} %collective-permute-done.1.refs_2_, f32[8,512]{1,0:T(8,128)S(1)} %collective-permute-done.2.refs_3_), custom_call_target="tpu_custom_call" | custom-call | flops 17179869184 | bytes 1 | tf_op jit(solution)/shard_map/choose/pallas_call | solution.py:176
  54.9 1.5 %collective-permute-start.6 = (bf16[1,192,512]{2,1,0:T(8,128)(2,1)S(1)}, bf16[1,192,512]{2,1,0:T(8,128)(2,1)S(1)}, u32[]{:S(2)}, u32[]{:S(2)}) collective-permute-start(bf16[1,192,512]{2,1,0:T(8,128)(2,1)S(1)} %get-tuple-element.69), channel_id=1, source_target_pairs={{0,2},{2,0},{4,6},{6,4},{8,10},{10,8},{12,14},{14,12},{16,18},{18,... | collective-permute-start | bytes 589832 | tf_op jit(solution)/shard_map/ppermute | solution.py:340
  56.3 1.5 %collective-permute-start.7 = (bf16[1,192,512]{2,1,0:T(8,128)(2,1)S(1)}, bf16[1,192,512]{2,1,0:T(8,128)(2,1)S(1)}, u32[]{:S(2)}, u32[]{:S(2)}) collective-permute-start(bf16[1,192,512]{2,1,0:T(8,128)(2,1)S(1)} %get-tuple-element.70), channel_id=1, source_target_pairs={{0,4},{2,6},{4,0},{6,2},{8,12},{10,14},{12,8},{14,10},{16,20},{18,... | collective-permute-start | bytes 589832 | tf_op jit(solution)/shard_map/ppermute | solution.py:340
  59.0 4.1 %collective-permute-done.11.refs_3_ = bf16[1,192,512]{2,1,0:T(8,128)(2,1)S(1)} collective-permute-done((bf16[1,192,512]{2,1,0:T(8,128)(2,1)S(1)}, bf16[1,192,512]{2,1,0:T(8,128)(2,1)S(1)}, u32[]{:S(2)}, u32[]{:S(2)}) %collective-permute-start.11) | collective-permute-done | bytes 196640 | tf_op jit(solution)/shard_map/ppermute | solution.py:340
  64.7 3.2 %collective-permute-done.7.refs_2_ = bf16[1,192,512]{2,1,0:T(8,128)(2,1)S(1)} collective-permute-done((bf16[1,192,512]{2,1,0:T(8,128)(2,1)S(1)}, bf16[1,192,512]{2,1,0:T(8,128)(2,1)S(1)}, u32[]{:S(2)}, u32[]{:S(2)}) %collective-permute-start.7) | collective-permute-done | bytes 196640 | tf_op jit(solution)/shard_map/ppermute | solution.py:340
  70.7 1.4 %collective-permute-start.5 = (bf16[1,192,512]{2,1,0:T(8,128)(2,1)S(1)}, bf16[1,192,512]{2,1,0:T(8,128)(2,1)S(1)}, u32[]{:S(2)}, u32[]{:S(2)}) collective-permute-start(bf16[1,192,512]{2,1,0:T(8,128)(2,1)S(1)} %get-tuple-element.76), channel_id=1, source_target_pairs={{0,6},{2,4},{4,2},{6,0},{8,14},{10,12},{12,10},{14,8},{16,22},{18,... | collective-permute-start | bytes 589832 | tf_op jit(solution)/shard_map/ppermute | solution.py:340
  74.9 1.4 %collective-permute-done.3.refs_1_ = bf16[1,192,512]{2,1,0:T(8,128)(2,1)S(1)} collective-permute-done((bf16[1,192,512]{2,1,0:T(8,128)(2,1)S(1)}, bf16[1,192,512]{2,1,0:T(8,128)(2,1)S(1)}, u32[]{:S(2)}, u32[]{:S(2)}) %collective-permute-start.3) | collective-permute-done | bytes 196640 | tf_op jit(solution)/shard_map/ppermute | solution.py:340
  76.3 3.1 %collective-permute-done.4.refs_2_ = bf16[1,192,512]{2,1,0:T(8,128)(2,1)S(1)} collective-permute-done((bf16[1,192,512]{2,1,0:T(8,128)(2,1)S(1)}, bf16[1,192,512]{2,1,0:T(8,128)(2,1)S(1)}, u32[]{:S(2)}, u32[]{:S(2)}) %collective-permute-start.4) | collective-permute-done | bytes 196640 | tf_op jit(solution)/shard_map/ppermute | solution.py:340
  79.4 1.4 %collective-permute-done.5.refs_3_ = bf16[1,192,512]{2,1,0:T(8,128)(2,1)S(1)} collective-permute-done((bf16[1,192,512]{2,1,0:T(8,128)(2,1)S(1)}, bf16[1,192,512]{2,1,0:T(8,128)(2,1)S(1)}, u32[]{:S(2)}, u32[]{:S(2)}) %collective-permute-start.5) | collective-permute-done | bytes 196640 | tf_op jit(solution)/shard_map/ppermute | solution.py:340
  81.5 5.8 %collective-permute-done.21 = bf16[256,512]{1,0:T(8,128)(2,1)S(1)} collective-permute-done((bf16[256,512]{1,0:T(8,128)(2,1)S(1)}, bf16[256,512]{1,0:T(8,128)(2,1)S(1)}, u32[]{:S(2)}, u32[]{:S(2)}) %collective-permute-start.21) | collective-permute-done | bytes 262176 | tf_op jit(solution)/shard_map/ppermute | solution.py:340
  87.5 1.5 %collective-permute-done.22 = bf16[256,512]{1,0:T(8,128)(2,1)S(1)} collective-permute-done((bf16[256,512]{1,0:T(8,128)(2,1)S(1)}, bf16[256,512]{1,0:T(8,128)(2,1)S(1)}, u32[]{:S(2)}, u32[]{:S(2)}) %collective-permute-start.22) | collective-permute-done | bytes 262176 | tf_op jit(solution)/shard_map/ppermute | solution.py:340
  92.1 1.5 %collective-permute-start.23 = (bf16[160,128]{1,0:T(8,128)(2,1)S(1)}, bf16[160,128]{1,0:T(8,128)(2,1)S(1)}, u32[]{:S(2)}, u32[]{:S(2)}) collective-permute-start(bf16[160,128]{1,0:T(8,128)(2,1)S(1)} %get-tuple-element.101), channel_id=1, source_target_pairs={{0,2},{2,0},{4,6},{6,4},{8,10},{10,8},{12,14},{14,12},{16,18},{18,... | collective-permute-start | bytes 122888 | tf_op jit(solution)/shard_map/ppermute | solution.py:340
  93.6 1.8 %collective-permute-done.25 = bf16[160,128]{1,0:T(8,128)(2,1)S(1)} collective-permute-done((bf16[160,128]{1,0:T(8,128)(2,1)S(1)}, bf16[160,128]{1,0:T(8,128)(2,1)S(1)}, u32[]{:S(2)}, u32[]{:S(2)}) %collective-permute-start.25) | collective-permute-done | bytes 40992 | tf_op jit(solution)/shard_map/ppermute | solution.py:340
  96.1 2.6 %collective-permute-start.28 = (bf16[160,128]{1,0:T(8,128)(2,1)S(1)}, bf16[160,128]{1,0:T(8,128)(2,1)S(1)}, u32[]{:S(2)}, u32[]{:S(2)}) collective-permute-start(bf16[160,128]{1,0:T(8,128)(2,1)S(1)} %add_convert_fusion.1), channel_id=1, source_target_pairs={{0,24},{2,26},{4,28},{6,30},{8,16},{10,18},{12,20},{14,22},{16,8},... | collective-permute-start | bytes 122888 | tf_op jit(solution)/shard_map/ppermute | solution.py:340
  98.8 1.8 %collective-permute-start.26 = (bf16[160,128]{1,0:T(8,128)(2,1)S(1)}, bf16[160,128]{1,0:T(8,128)(2,1)S(1)}, u32[]{:S(2)}, u32[]{:S(2)}) collective-permute-start(bf16[160,128]{1,0:T(8,128)(2,1)S(1)} %add_convert_fusion.1), channel_id=1, source_target_pairs={{0,8},{2,10},{4,12},{6,14},{8,0},{10,2},{12,4},{14,6},{16,24},{18,... | collective-permute-start | bytes 122888 | tf_op jit(solution)/shard_map/ppermute | solution.py:340
  100.6 1.6 %collective-permute-done.28 = bf16[160,128]{1,0:T(8,128)(2,1)S(1)} collective-permute-done((bf16[160,128]{1,0:T(8,128)(2,1)S(1)}, bf16[160,128]{1,0:T(8,128)(2,1)S(1)}, u32[]{:S(2)}, u32[]{:S(2)}) %collective-permute-start.28) | collective-permute-done | bytes 40992 | tf_op jit(solution)/shard_map/ppermute | solution.py:340
  102.2 1.5 %collective-permute-done.27 = bf16[160,128]{1,0:T(8,128)(2,1)S(1)} collective-permute-done((bf16[160,128]{1,0:T(8,128)(2,1)S(1)}, bf16[160,128]{1,0:T(8,128)(2,1)S(1)}, u32[]{:S(2)}, u32[]{:S(2)}) %collective-permute-start.27) | collective-permute-done | bytes 40992 | tf_op jit(solution)/shard_map/ppermute | solution.py:340
  103.7 1.3 %collective-permute-start.31 = (bf16[160,128]{1,0:T(8,128)(2,1)S(1)}, bf16[160,128]{1,0:T(8,128)(2,1)S(1)}, u32[]{:S(2)}, u32[]{:S(2)}) collective-permute-start(bf16[160,128]{1,0:T(8,128)(2,1)S(1)} %add_convert_fusion), channel_id=1, source_target_pairs={{0,6},{2,4},{4,2},{6,0},{8,14},{10,12},{12,10},{14,8},{16,22},{18,... | collective-permute-start | bytes 122888 | tf_op jit(solution)/shard_map/ppermute | solution.py:340
  107.3 1.4 %collective-permute-done.31 = bf16[160,128]{1,0:T(8,128)(2,1)S(1)} collective-permute-done((bf16[160,128]{1,0:T(8,128)(2,1)S(1)}, bf16[160,128]{1,0:T(8,128)(2,1)S(1)}, u32[]{:S(2)}, u32[]{:S(2)}) %collective-permute-start.31) | collective-permute-done | bytes 40992 | tf_op jit(solution)/shard_map/ppermute | solution.py:340
  110.2 1.4 %collective-permute-done.32.other_gram_ref = bf16[5,128,128]{2,1,0:T(8,128)(2,1)S(1)} collective-permute-done((bf16[5,128,128]{2,1,0:T(8,128)(2,1)S(1)}, bf16[5,128,128]{2,1,0:T(8,128)(2,1)S(1)}, u32[]{:S(2)}, u32[]{:S(2)}) %collective-permute-start.32) | collective-permute-done | bytes 163872 | tf_op jit(solution)/shard_map/ppermute | solution.py:340
  111.6 5.1 %root.1 = f32[256,512]{1,0:T(8,128)} custom-call(s32[1]{0:T(128)} %bitcast.feat_ref.place_ref, bf16[5,128,128]{2,1,0:T(8,128)(2,1)S(1)} %bitcast.39, bf16[5,128,128]{2,1,0:T(8,128)(2,1)S(1)} %collective-permute-done.32.other_gram_ref, bf16[256,512]{1,0:T(8,128)(2,1)S(1)} %fusion.1.mine_ref), custom_call_target="tpu_custom_call" | custom-call | tf_op jit(solution)/shard_map/root/pallas_call | solution.py:327
  (69 shorter events, 23.6 us)
Async XLA Ops:
  6.8 29.6 %all-to-all-start = ((bf16[16,192,128]{2,1,0:T(8,128)(2,1)}), bf16[16,192,128]{2,1,0:T(8,128)(2,1)S(1)}, u32[]{:S(2)}, u32[]{:S(2)}) async-start(bf16[16,192,128]{2,1,0:T(8,128)(2,1)} %get-tuple-element.52), calls=%async_computation | async-start | bytes 1572864 | tf_op jit(solution)/shard_map/all_to_all | solution.py:427
  15.3 13.2 %collective-permute-start = (f32[8,512]{1,0:T(8,128)}, f32[8,512]{1,0:T(8,128)S(1)}, u32[]{:S(2)}, u32[]{:S(2)}) collective-permute-start(f32[8,512]{1,0:T(8,128)} %get-tuple-element.63.refs_0_), channel_id=1, source_target_pairs={{0,8},{2,10},{4,12},{6,14},{8,0},{10,2},{12,4},{14,6},{16,24},{18,... | collective-permute-start | bytes 49160 | tf_op jit(solution)/shard_map/ppermute | solution.py:340
  17.1 19.3 %collective-permute-start.1 = (f32[8,512]{1,0:T(8,128)}, f32[8,512]{1,0:T(8,128)S(1)}, u32[]{:S(2)}, u32[]{:S(2)}) collective-permute-start(f32[8,512]{1,0:T(8,128)} %get-tuple-element.63.refs_0_), channel_id=1, source_target_pairs={{0,16},{2,18},{4,20},{6,22},{8,24},{10,26},{12,28},{14,30},{16,0},... | collective-permute-start | bytes 49160 | tf_op jit(solution)/shard_map/ppermute | solution.py:340
  19.5 16.9 %collective-permute-start.2 = (f32[8,512]{1,0:T(8,128)}, f32[8,512]{1,0:T(8,128)S(1)}, u32[]{:S(2)}, u32[]{:S(2)}) collective-permute-start(f32[8,512]{1,0:T(8,128)} %get-tuple-element.63.refs_0_), channel_id=1, source_target_pairs={{0,24},{2,26},{4,28},{6,30},{8,16},{10,18},{12,20},{14,22},{16,8},... | collective-permute-start | bytes 49160 | tf_op jit(solution)/shard_map/ppermute | solution.py:340
  39.9 14.3 %collective-permute-start.12 = (bf16[1,192,512]{2,1,0:T(8,128)(2,1)S(1)}, bf16[1,192,512]{2,1,0:T(8,128)(2,1)S(1)}, u32[]{:S(2)}, u32[]{:S(2)}) collective-permute-start(bf16[1,192,512]{2,1,0:T(8,128)(2,1)S(1)} %get-tuple-element.55), channel_id=1, source_target_pairs={{0,2},{2,0},{4,6},{6,4},{8,10},{10,8},{12,14},{14,12},{16,18},{18,... | collective-permute-start | bytes 589832 | tf_op jit(solution)/shard_map/ppermute | solution.py:340
  41.5 13.4 %collective-permute-start.13 = (bf16[1,192,512]{2,1,0:T(8,128)(2,1)S(1)}, bf16[1,192,512]{2,1,0:T(8,128)(2,1)S(1)}, u32[]{:S(2)}, u32[]{:S(2)}) collective-permute-start(bf16[1,192,512]{2,1,0:T(8,128)(2,1)S(1)} %get-tuple-element.56), channel_id=1, source_target_pairs={{0,4},{2,6},{4,0},{6,2},{8,12},{10,14},{12,8},{14,10},{16,20},{18,... | collective-permute-start | bytes 589832 | tf_op jit(solution)/shard_map/ppermute | solution.py:340
  42.9 13.4 %collective-permute-start.14 = (bf16[1,192,512]{2,1,0:T(8,128)(2,1)S(1)}, bf16[1,192,512]{2,1,0:T(8,128)(2,1)S(1)}, u32[]{:S(2)}, u32[]{:S(2)}) collective-permute-start(bf16[1,192,512]{2,1,0:T(8,128)(2,1)S(1)} %get-tuple-element.57), channel_id=1, source_target_pairs={{0,6},{2,4},{4,2},{6,0},{8,14},{10,12},{12,10},{14,8},{16,22},{18,... | collective-permute-start | bytes 589832 | tf_op jit(solution)/shard_map/ppermute | solution.py:340
  44.8 13.6 %collective-permute-start.9 = (bf16[1,192,512]{2,1,0:T(8,128)(2,1)S(1)}, bf16[1,192,512]{2,1,0:T(8,128)(2,1)S(1)}, u32[]{:S(2)}, u32[]{:S(2)}) collective-permute-start(bf16[1,192,512]{2,1,0:T(8,128)(2,1)S(1)} %get-tuple-element.60), channel_id=1, source_target_pairs={{0,2},{2,0},{4,6},{6,4},{8,10},{10,8},{12,14},{14,12},{16,18},{18,... | collective-permute-start | bytes 589832 | tf_op jit(solution)/shard_map/ppermute | solution.py:340
  46.3 12.7 %collective-permute-start.10 = (bf16[1,192,512]{2,1,0:T(8,128)(2,1)S(1)}, bf16[1,192,512]{2,1,0:T(8,128)(2,1)S(1)}, u32[]{:S(2)}, u32[]{:S(2)}) collective-permute-start(bf16[1,192,512]{2,1,0:T(8,128)(2,1)S(1)} %get-tuple-element.61), channel_id=1, source_target_pairs={{0,4},{2,6},{4,0},{6,2},{8,12},{10,14},{12,8},{14,10},{16,20},{18,... | collective-permute-start | bytes 589832 | tf_op jit(solution)/shard_map/ppermute | solution.py:340
  54.2 8.9 %collective-permute-start.11 = (bf16[1,192,512]{2,1,0:T(8,128)(2,1)S(1)}, bf16[1,192,512]{2,1,0:T(8,128)(2,1)S(1)}, u32[]{:S(2)}, u32[]{:S(2)}) collective-permute-start(bf16[1,192,512]{2,1,0:T(8,128)(2,1)S(1)} %get-tuple-element.62), channel_id=1, source_target_pairs={{0,6},{2,4},{4,2},{6,0},{8,14},{10,12},{12,10},{14,8},{16,22},{18,... | collective-permute-start | bytes 589832 | tf_op jit(solution)/shard_map/ppermute | solution.py:340
  54.9 9.9 %collective-permute-start.6 = (bf16[1,192,512]{2,1,0:T(8,128)(2,1)S(1)}, bf16[1,192,512]{2,1,0:T(8,128)(2,1)S(1)}, u32[]{:S(2)}, u32[]{:S(2)}) collective-permute-start(bf16[1,192,512]{2,1,0:T(8,128)(2,1)S(1)} %get-tuple-element.69), channel_id=1, source_target_pairs={{0,2},{2,0},{4,6},{6,4},{8,10},{10,8},{12,14},{14,12},{16,18},{18,... | collective-permute-start | bytes 589832 | tf_op jit(solution)/shard_map/ppermute | solution.py:340
  56.3 11.5 %collective-permute-start.7 = (bf16[1,192,512]{2,1,0:T(8,128)(2,1)S(1)}, bf16[1,192,512]{2,1,0:T(8,128)(2,1)S(1)}, u32[]{:S(2)}, u32[]{:S(2)}) collective-permute-start(bf16[1,192,512]{2,1,0:T(8,128)(2,1)S(1)} %get-tuple-element.70), channel_id=1, source_target_pairs={{0,4},{2,6},{4,0},{6,2},{8,12},{10,14},{12,8},{14,10},{16,20},{18,... | collective-permute-start | bytes 589832 | tf_op jit(solution)/shard_map/ppermute | solution.py:340
  58.4 9.5 %collective-permute-start.8 = (bf16[1,192,512]{2,1,0:T(8,128)(2,1)S(1)}, bf16[1,192,512]{2,1,0:T(8,128)(2,1)S(1)}, u32[]{:S(2)}, u32[]{:S(2)}) collective-permute-start(bf16[1,192,512]{2,1,0:T(8,128)(2,1)S(1)} %get-tuple-element.71), channel_id=1, source_target_pairs={{0,6},{2,4},{4,2},{6,0},{8,14},{10,12},{12,10},{14,8},{16,22},{18,... | collective-permute-start | bytes 589832 | tf_op jit(solution)/shard_map/ppermute | solution.py:340
  59.0 4.8 %collective-permute-start.15 = (bf16[1,256,512]{2,1,0:T(8,128)(2,1)S(1)}, bf16[1,256,512]{2,1,0:T(8,128)(2,1)S(1)}, u32[]{:S(2)}, u32[]{:S(2)}) collective-permute-start(bf16[1,256,512]{2,1,0:T(8,128)(2,1)S(1)} %get-tuple-element.83), channel_id=1, source_target_pairs={{0,1},{1,0},{2,3},{3,2},{4,5},{5,4},{6,7},{7,6},{8,9},{9,8},{10,11... | collective-permute-start | bytes 786440 | tf_op jit(solution)/shard_map/ppermute | solution.py:340
  63.7 7.0 %collective-permute-start.16 = (bf16[1,256,512]{2,1,0:T(8,128)(2,1)S(1)}, bf16[1,256,512]{2,1,0:T(8,128)(2,1)S(1)}, u32[]{:S(2)}, u32[]{:S(2)}) collective-permute-start(bf16[1,256,512]{2,1,0:T(8,128)(2,1)S(1)} %get-tuple-element.89), channel_id=1, source_target_pairs={{0,1},{1,0},{2,3},{3,2},{4,5},{5,4},{6,7},{7,6},{8,9},{9,8},{10,11... | collective-permute-start | bytes 786440 | tf_op jit(solution)/shard_map/ppermute | solution.py:340
  63.9 8.8 %collective-permute-start.17 = (bf16[256,512]{1,0:T(8,128)(2,1)S(1)}, bf16[256,512]{1,0:T(8,128)(2,1)S(1)}, u32[]{:S(2)}, u32[]{:S(2)}) collective-permute-start(bf16[256,512]{1,0:T(8,128)(2,1)S(1)} %add_bitcast_fusion.1), channel_id=1, source_target_pairs={{0,8},{2,10},{4,12},{6,14},{8,0},{10,2},{12,4},{14,6},{16,24},{18,... | collective-permute-start | bytes 786440 | tf_op jit(solution)/shard_map/ppermute | solution.py:340
  68.5 5.3 %collective-permute-start.18 = (bf16[1,256,512]{2,1,0:T(8,128)(2,1)S(1)}, bf16[1,256,512]{2,1,0:T(8,128)(2,1)S(1)}, u32[]{:S(2)}, u32[]{:S(2)}) collective-permute-start(bf16[1,256,512]{2,1,0:T(8,128)(2,1)S(1)} %get-tuple-element.90), channel_id=1, source_target_pairs={{0,1},{1,0},{2,3},{3,2},{4,5},{5,4},{6,7},{7,6},{8,9},{9,8},{10,11... | collective-permute-start | bytes 786440 | tf_op jit(solution)/shard_map/ppermute | solution.py:340
  68.5 7.8 %collective-permute-start.3 = (bf16[1,192,512]{2,1,0:T(8,128)(2,1)S(1)}, bf16[1,192,512]{2,1,0:T(8,128)(2,1)S(1)}, u32[]{:S(2)}, u32[]{:S(2)}) collective-permute-start(bf16[1,192,512]{2,1,0:T(8,128)(2,1)S(1)} %get-tuple-element.74), channel_id=1, source_target_pairs={{0,2},{2,0},{4,6},{6,4},{8,10},{10,8},{12,14},{14,12},{16,18},{18,... | collective-permute-start | bytes 589832 | tf_op jit(solution)/shard_map/ppermute | solution.py:340
  69.6 9.8 %collective-permute-start.4 = (bf16[1,192,512]{2,1,0:T(8,128)(2,1)S(1)}, bf16[1,192,512]{2,1,0:T(8,128)(2,1)S(1)}, u32[]{:S(2)}, u32[]{:S(2)}) collective-permute-start(bf16[1,192,512]{2,1,0:T(8,128)(2,1)S(1)} %get-tuple-element.75), channel_id=1, source_target_pairs={{0,4},{2,6},{4,0},{6,2},{8,12},{10,14},{12,8},{14,10},{16,20},{18,... | collective-permute-start | bytes 589832 | tf_op jit(solution)/shard_map/ppermute | solution.py:340
  70.7 10.1 %collective-permute-start.5 = (bf16[1,192,512]{2,1,0:T(8,128)(2,1)S(1)}, bf16[1,192,512]{2,1,0:T(8,128)(2,1)S(1)}, u32[]{:S(2)}, u32[]{:S(2)}) collective-permute-start(bf16[1,192,512]{2,1,0:T(8,128)(2,1)S(1)} %get-tuple-element.76), channel_id=1, source_target_pairs={{0,6},{2,4},{4,2},{6,0},{8,14},{10,12},{12,10},{14,8},{16,22},{18,... | collective-permute-start | bytes 589832 | tf_op jit(solution)/shard_map/ppermute | solution.py:340
  72.8 14.5 %collective-permute-start.21 = (bf16[256,512]{1,0:T(8,128)(2,1)S(1)}, bf16[256,512]{1,0:T(8,128)(2,1)S(1)}, u32[]{:S(2)}, u32[]{:S(2)}) collective-permute-start(bf16[256,512]{1,0:T(8,128)(2,1)S(1)} %bitcast_add_fusion.1), channel_id=1, source_target_pairs={{0,16},{2,18},{4,20},{6,22},{8,24},{10,26},{12,28},{14,30},{16,0},... | collective-permute-start | bytes 786440 | tf_op jit(solution)/shard_map/ppermute | solution.py:340
  73.9 13.4 %collective-permute-start.20 = (bf16[256,512]{1,0:T(8,128)(2,1)S(1)}, bf16[256,512]{1,0:T(8,128)(2,1)S(1)}, u32[]{:S(2)}, u32[]{:S(2)}) collective-permute-start(bf16[256,512]{1,0:T(8,128)(2,1)S(1)} %add_bitcast_fusion), channel_id=1, source_target_pairs={{0,8},{2,10},{4,12},{6,14},{8,0},{10,2},{12,4},{14,6},{16,24},{18,... | collective-permute-start | bytes 786440 | tf_op jit(solution)/shard_map/ppermute | solution.py:340
  81.4 5.9 %collective-permute-start.19 = (bf16[1,256,512]{2,1,0:T(8,128)(2,1)S(1)}, bf16[1,256,512]{2,1,0:T(8,128)(2,1)S(1)}, u32[]{:S(2)}, u32[]{:S(2)}) collective-permute-start(bf16[1,256,512]{2,1,0:T(8,128)(2,1)S(1)} %get-tuple-element.96), channel_id=1, source_target_pairs={{0,1},{1,0},{2,3},{3,2},{4,5},{5,4},{6,7},{7,6},{8,9},{9,8},{10,11... | collective-permute-start | bytes 786440 | tf_op jit(solution)/shard_map/ppermute | solution.py:340
  90.0 5.4 %collective-permute-start.25 = (bf16[160,128]{1,0:T(8,128)(2,1)S(1)}, bf16[160,128]{1,0:T(8,128)(2,1)S(1)}, u32[]{:S(2)}, u32[]{:S(2)}) collective-permute-start(bf16[160,128]{1,0:T(8,128)(2,1)S(1)} %get-tuple-element.102), channel_id=1, source_target_pairs={{0,6},{2,4},{4,2},{6,0},{8,14},{10,12},{12,10},{14,8},{16,22},{18,... | collective-permute-start | bytes 122888 | tf_op jit(solution)/shard_map/ppermute | solution.py:340
  90.9 4.5 %collective-permute-start.24 = (bf16[160,128]{1,0:T(8,128)(2,1)S(1)}, bf16[160,128]{1,0:T(8,128)(2,1)S(1)}, u32[]{:S(2)}, u32[]{:S(2)}) collective-permute-start(bf16[160,128]{1,0:T(8,128)(2,1)S(1)} %get-tuple-element.103), channel_id=1, source_target_pairs={{0,4},{2,6},{4,0},{6,2},{8,12},{10,14},{12,8},{14,10},{16,20},{18,... | collective-permute-start | bytes 122888 | tf_op jit(solution)/shard_map/ppermute | solution.py:340
  92.1 4.0 %collective-permute-start.23 = (bf16[160,128]{1,0:T(8,128)(2,1)S(1)}, bf16[160,128]{1,0:T(8,128)(2,1)S(1)}, u32[]{:S(2)}, u32[]{:S(2)}) collective-permute-start(bf16[160,128]{1,0:T(8,128)(2,1)S(1)} %get-tuple-element.101), channel_id=1, source_target_pairs={{0,2},{2,0},{4,6},{6,4},{8,10},{10,8},{12,14},{14,12},{16,18},{18,... | collective-permute-start | bytes 122888 | tf_op jit(solution)/shard_map/ppermute | solution.py:340
  96.1 6.1 %collective-permute-start.28 = (bf16[160,128]{1,0:T(8,128)(2,1)S(1)}, bf16[160,128]{1,0:T(8,128)(2,1)S(1)}, u32[]{:S(2)}, u32[]{:S(2)}) collective-permute-start(bf16[160,128]{1,0:T(8,128)(2,1)S(1)} %add_convert_fusion.1), channel_id=1, source_target_pairs={{0,24},{2,26},{4,28},{6,30},{8,16},{10,18},{12,20},{14,22},{16,8},... | collective-permute-start | bytes 122888 | tf_op jit(solution)/shard_map/ppermute | solution.py:340
  98.8 4.9 %collective-permute-start.27 = (bf16[160,128]{1,0:T(8,128)(2,1)S(1)}, bf16[160,128]{1,0:T(8,128)(2,1)S(1)}, u32[]{:S(2)}, u32[]{:S(2)}) collective-permute-start(bf16[160,128]{1,0:T(8,128)(2,1)S(1)} %add_convert_fusion.1), channel_id=1, source_target_pairs={{0,16},{2,18},{4,20},{6,22},{8,24},{10,26},{12,28},{14,30},{16,0},... | collective-permute-start | bytes 122888 | tf_op jit(solution)/shard_map/ppermute | solution.py:340
  98.8 4.9 %collective-permute-start.26 = (bf16[160,128]{1,0:T(8,128)(2,1)S(1)}, bf16[160,128]{1,0:T(8,128)(2,1)S(1)}, u32[]{:S(2)}, u32[]{:S(2)}) collective-permute-start(bf16[160,128]{1,0:T(8,128)(2,1)S(1)} %add_convert_fusion.1), channel_id=1, source_target_pairs={{0,8},{2,10},{4,12},{6,14},{8,0},{10,2},{12,4},{14,6},{16,24},{18,... | collective-permute-start | bytes 122888 | tf_op jit(solution)/shard_map/ppermute | solution.py:340
  103.7 5.0 %collective-permute-start.31 = (bf16[160,128]{1,0:T(8,128)(2,1)S(1)}, bf16[160,128]{1,0:T(8,128)(2,1)S(1)}, u32[]{:S(2)}, u32[]{:S(2)}) collective-permute-start(bf16[160,128]{1,0:T(8,128)(2,1)S(1)} %add_convert_fusion), channel_id=1, source_target_pairs={{0,6},{2,4},{4,2},{6,0},{8,14},{10,12},{12,10},{14,8},{16,22},{18,... | collective-permute-start | bytes 122888 | tf_op jit(solution)/shard_map/ppermute | solution.py:340
  105.0 4.1 %collective-permute-start.30 = (bf16[160,128]{1,0:T(8,128)(2,1)S(1)}, bf16[160,128]{1,0:T(8,128)(2,1)S(1)}, u32[]{:S(2)}, u32[]{:S(2)}) collective-permute-start(bf16[160,128]{1,0:T(8,128)(2,1)S(1)} %add_convert_fusion), channel_id=1, source_target_pairs={{0,4},{2,6},{4,0},{6,2},{8,12},{10,14},{12,8},{14,10},{16,20},{18,... | collective-permute-start | bytes 122888 | tf_op jit(solution)/shard_map/ppermute | solution.py:340
  106.0 4.0 %collective-permute-start.29 = (bf16[160,128]{1,0:T(8,128)(2,1)S(1)}, bf16[160,128]{1,0:T(8,128)(2,1)S(1)}, u32[]{:S(2)}, u32[]{:S(2)}) collective-permute-start(bf16[160,128]{1,0:T(8,128)(2,1)S(1)} %add_convert_fusion), channel_id=1, source_target_pairs={{0,2},{2,0},{4,6},{6,4},{8,10},{10,8},{12,14},{14,12},{16,18},{18,... | collective-permute-start | bytes 122888 | tf_op jit(solution)/shard_map/ppermute | solution.py:340
  (6 other events, 27.0 us)

commit v7 on v6

--- a/solution.py
+++ b/solution.py
@@ -61,7 +61,7 @@
         used = used + jnp.sum(named, axis=0, keepdims=True)
         if k == 0:
             copy.wait()
-            values[...] = raw[...].astype(f32)
+            values[: raw.shape[0], :] = raw[...].astype(f32)
         tile = values[pl.ds(k, s_dev, stride=k_j), :]
         by_rank.append(jnp.concatenate([jnp.where(rank == r, tile, 0.0).astype(bf16) for r in range(bound)], axis=1))
         named_rows.append(jnp.where(ids_rows[k : k + 1, :] == number_rows, 1.0, 0.0).astype(bf16))
@@ -99,7 +99,11 @@
         ),
         in_specs=[whole(), pl.BlockSpec(memory_space=pl.ANY)],
         out_specs=(whole(), whole()),
-        scratch_shapes=[pltpu.VMEM(values.shape, f32), pltpu.VMEM(values.shape, bf16), pltpu.SemaphoreType.DMA],
+        scratch_shapes=[
+            pltpu.VMEM((values.shape[0] + 8, lane), f32),
+            pltpu.VMEM(values.shape, bf16),
+            pltpu.SemaphoreType.DMA,
+        ],
         compiler_params=params(62 << 20),
         name="pack",
     )(ids, values)

time: 117 us -> 117 us (level)
  no operation moved by 1% of the time
where the time goes in v7:
time: 117 us
  waiting for transfers between devices  47.4 us (41%)
  starting transfers between devices  42.1 us (36%)
  Pallas kernels  24.1 us (21%)
  local copies, waits for them, and re-layouts  2.25 us (2%)
    ppermute x33, waiting for transfers between devices, crossed(): lax.ppermute(value, axis, [(source, source ^ bits) for source in range(co...  47.4 us
    ppermute x33, starting transfers between devices, crossed(): lax.ppermute(value, axis, [(source, source ^ bits) for source in range(co...  33.6 us
    all_to_all x1, starting transfers between devices, local(): tiles = lax.all_to_all(send, 'dp', split_axis=0, concat_axis=0, tiled=True)  8.5 us
    pallas_call x1, Pallas kernels, pack(): pl.pallas_call(functools.partial(pack_kernel, per_dev, bound), out_shape=...  6.76 us
    pallas_call x4, Pallas kernels, product(): pl.pallas_call(functools.partial(product_kernel, bound, joint, groups, aw...  5.32 us
    pallas_call x1, Pallas kernels, whiten(): pl.pallas_call(functools.partial(root_kernel, samples), out_shape=jax.Sha...  5.11 us
    pallas_call x1, Pallas kernels, choose(): pl.pallas_call(functools.partial(choose_kernel, k_j, slots, inner), out_s...  3.72 us
  transfers between devices with their start and end apart: 34, of which 18 were waited for; matrix products, arithmetic and copies ran while one was open for 0% of the time, Pallas kernels for 9%

profile of v7, /device:TPU:0, one launch (start us, length us, event | category | flops | bytes accessed | tf_op | source)
XLA Modules:
  0.0 116.7 jit_solution(1734766199218191762)
XLA Ops:
  0.0 6.8 %pack.1 = (bf16[16,192,128]{2,1,0:T(8,128)(2,1)}, f32[8,512]{1,0:T(8,128)}) custom-call(s32[4,512]{1,0:T(4,128)} %bitcast.49, bf16[2048,128]{1,0:T(8,128)(2,1)} %bitcast.44), custom_call_target="tpu_custom_call" | custom-call | tf_op jit(solution)/shard_map/pack/pallas_call | solution.py:94
  6.8 8.5 %all-to-all-start = ((bf16[16,192,128]{2,1,0:T(8,128)(2,1)}), bf16[16,192,128]{2,1,0:T(8,128)(2,1)S(1)}, u32[]{:S(2)}, u32[]{:S(2)}) async-start(bf16[16,192,128]{2,1,0:T(8,128)(2,1)} %get-tuple-element.52), calls=%async_computation | async-start | bytes 1572864 | tf_op jit(solution)/shard_map/all_to_all | solution.py:431
  15.3 1.8 %collective-permute-start = (f32[8,512]{1,0:T(8,128)}, f32[8,512]{1,0:T(8,128)S(1)}, u32[]{:S(2)}, u32[]{:S(2)}) collective-permute-start(f32[8,512]{1,0:T(8,128)} %get-tuple-element.63.refs_0_), channel_id=1, source_target_pairs={{0,8},{2,10},{4,12},{6,14},{8,0},{10,2},{12,4},{14,6},{16,24},{18,... | collective-permute-start | bytes 49160 | tf_op jit(solution)/shard_map/ppermute | solution.py:344
  17.1 2.4 %collective-permute-start.1 = (f32[8,512]{1,0:T(8,128)}, f32[8,512]{1,0:T(8,128)S(1)}, u32[]{:S(2)}, u32[]{:S(2)}) collective-permute-start(f32[8,512]{1,0:T(8,128)} %get-tuple-element.63.refs_0_), channel_id=1, source_target_pairs={{0,16},{2,18},{4,20},{6,22},{8,24},{10,26},{12,28},{14,30},{16,0},... | collective-permute-start | bytes 49160 | tf_op jit(solution)/shard_map/ppermute | solution.py:344
  19.8 8.7 %collective-permute-done.refs_1_ = f32[8,512]{1,0:T(8,128)S(1)} collective-permute-done((f32[8,512]{1,0:T(8,128)}, f32[8,512]{1,0:T(8,128)S(1)}, u32[]{:S(2)}, u32[]{:S(2)}) %collective-permute-start) | collective-permute-done | bytes 16416 | tf_op jit(solution)/shard_map/ppermute | solution.py:344
  28.5 7.9 %collective-permute-done.1.refs_2_ = f32[8,512]{1,0:T(8,128)S(1)} collective-permute-done((f32[8,512]{1,0:T(8,128)}, f32[8,512]{1,0:T(8,128)S(1)}, u32[]{:S(2)}, u32[]{:S(2)}) %collective-permute-start.1) | collective-permute-done | bytes 16416 | tf_op jit(solution)/shard_map/ppermute | solution.py:344
  36.4 2.2 %copy-done = bf16[32,1,128,512]{3,2,1,0:T(8,128)(2,1)S(1)} copy-done((bf16[32,1,128,512]{3,2,1,0:T(8,128)(2,1)S(1)}, bf16[32,1,128,512]{3,2,1,0:T(8,128)(2,1)}, u32[]{:S(2)}) %copy-start) | copy-done | bytes 4194328
  39.9 1.5 %collective-permute-start.12 = (bf16[1,192,512]{2,1,0:T(8,128)(2,1)S(1)}, bf16[1,192,512]{2,1,0:T(8,128)(2,1)S(1)}, u32[]{:S(2)}, u32[]{:S(2)}) collective-permute-start(bf16[1,192,512]{2,1,0:T(8,128)(2,1)S(1)} %get-tuple-element.55), channel_id=1, source_target_pairs={{0,2},{2,0},{4,6},{6,4},{8,10},{10,8},{12,14},{14,12},{16,18},{18,... | collective-permute-start | bytes 589832 | tf_op jit(solution)/shard_map/ppermute | solution.py:344
  41.5 1.5 %collective-permute-start.13 = (bf16[1,192,512]{2,1,0:T(8,128)(2,1)S(1)}, bf16[1,192,512]{2,1,0:T(8,128)(2,1)S(1)}, u32[]{:S(2)}, u32[]{:S(2)}) collective-permute-start(bf16[1,192,512]{2,1,0:T(8,128)(2,1)S(1)} %get-tuple-element.56), channel_id=1, source_target_pairs={{0,4},{2,6},{4,0},{6,2},{8,12},{10,14},{12,8},{14,10},{16,20},{18,... | collective-permute-start | bytes 589832 | tf_op jit(solution)/shard_map/ppermute | solution.py:344
  44.8 1.5 %collective-permute-start.9 = (bf16[1,192,512]{2,1,0:T(8,128)(2,1)S(1)}, bf16[1,192,512]{2,1,0:T(8,128)(2,1)S(1)}, u32[]{:S(2)}, u32[]{:S(2)}) collective-permute-start(bf16[1,192,512]{2,1,0:T(8,128)(2,1)S(1)} %get-tuple-element.60), channel_id=1, source_target_pairs={{0,2},{2,0},{4,6},{6,4},{8,10},{10,8},{12,14},{14,12},{16,18},{18,... | collective-permute-start | bytes 589832 | tf_op jit(solution)/shard_map/ppermute | solution.py:344
  46.3 1.5 %collective-permute-start.10 = (bf16[1,192,512]{2,1,0:T(8,128)(2,1)S(1)}, bf16[1,192,512]{2,1,0:T(8,128)(2,1)S(1)}, u32[]{:S(2)}, u32[]{:S(2)}) collective-permute-start(bf16[1,192,512]{2,1,0:T(8,128)(2,1)S(1)} %get-tuple-element.61), channel_id=1, source_target_pairs={{0,4},{2,6},{4,0},{6,2},{8,12},{10,14},{12,8},{14,10},{16,20},{18,... | collective-permute-start | bytes 589832 | tf_op jit(solution)/shard_map/ppermute | solution.py:344
  47.8 3.7 %choose.1.hits_ref = bf16[4,512,768]{2,1,0:T(8,128)(2,1)S(1)} custom-call(s32[2]{0:T(128)S(1)} %pad_add_fusion.where_ref.place_ref, f32[8,512]{1,0:T(8,128)S(1)} %copy-done.2, f32[8,512]{1,0:T(8,128)S(1)} %collective-permute-done.refs_1_, f32[8,512]{1,0:T(8,128)S(1)} %collective-permute-done.1.refs_2_, f32[8,512]{1,0:T(8,128)S(1)} %collective-permute-done.2.refs_3_), custom_call_target="tpu_custom_call" | custom-call | flops 17179869184 | bytes 1 | tf_op jit(solution)/shard_map/choose/pallas_call | solution.py:180
  54.9 1.5 %collective-permute-start.6 = (bf16[1,192,512]{2,1,0:T(8,128)(2,1)S(1)}, bf16[1,192,512]{2,1,0:T(8,128)(2,1)S(1)}, u32[]{:S(2)}, u32[]{:S(2)}) collective-permute-start(bf16[1,192,512]{2,1,0:T(8,128)(2,1)S(1)} %get-tuple-element.69), channel_id=1, source_target_pairs={{0,2},{2,0},{4,6},{6,4},{8,10},{10,8},{12,14},{14,12},{16,18},{18,... | collective-permute-start | bytes 589832 | tf_op jit(solution)/shard_map/ppermute | solution.py:344
  56.3 1.5 %collective-permute-start.7 = (bf16[1,192,512]{2,1,0:T(8,128)(2,1)S(1)}, bf16[1,192,512]{2,1,0:T(8,128)(2,1)S(1)}, u32[]{:S(2)}, u32[]{:S(2)}) collective-permute-start(bf16[1,192,512]{2,1,0:T(8,128)(2,1)S(1)} %get-tuple-element.70), channel_id=1, source_target_pairs={{0,4},{2,6},{4,0},{6,2},{8,12},{10,14},{12,8},{14,10},{16,20},{18,... | collective-permute-start | bytes 589832 | tf_op jit(solution)/shard_map/ppermute | solution.py:344
  59.0 4.1 %collective-permute-done.11.refs_3_ = bf16[1,192,512]{2,1,0:T(8,128)(2,1)S(1)} collective-permute-done((bf16[1,192,512]{2,1,0:T(8,128)(2,1)S(1)}, bf16[1,192,512]{2,1,0:T(8,128)(2,1)S(1)}, u32[]{:S(2)}, u32[]{:S(2)}) %collective-permute-start.11) | collective-permute-done | bytes 196640 | tf_op jit(solution)/shard_map/ppermute | solution.py:344
  64.7 3.2 %collective-permute-done.7.refs_2_ = bf16[1,192,512]{2,1,0:T(8,128)(2,1)S(1)} collective-permute-done((bf16[1,192,512]{2,1,0:T(8,128)(2,1)S(1)}, bf16[1,192,512]{2,1,0:T(8,128)(2,1)S(1)}, u32[]{:S(2)}, u32[]{:S(2)}) %collective-permute-start.7) | collective-permute-done | bytes 196640 | tf_op jit(solution)/shard_map/ppermute | solution.py:344
  70.7 1.4 %collective-permute-start.5 = (bf16[1,192,512]{2,1,0:T(8,128)(2,1)S(1)}, bf16[1,192,512]{2,1,0:T(8,128)(2,1)S(1)}, u32[]{:S(2)}, u32[]{:S(2)}) collective-permute-start(bf16[1,192,512]{2,1,0:T(8,128)(2,1)S(1)} %get-tuple-element.76), channel_id=1, source_target_pairs={{0,6},{2,4},{4,2},{6,0},{8,14},{10,12},{12,10},{14,8},{16,22},{18,... | collective-permute-start | bytes 589832 | tf_op jit(solution)/shard_map/ppermute | solution.py:344
  74.9 1.4 %collective-permute-done.3.refs_1_ = bf16[1,192,512]{2,1,0:T(8,128)(2,1)S(1)} collective-permute-done((bf16[1,192,512]{2,1,0:T(8,128)(2,1)S(1)}, bf16[1,192,512]{2,1,0:T(8,128)(2,1)S(1)}, u32[]{:S(2)}, u32[]{:S(2)}) %collective-permute-start.3) | collective-permute-done | bytes 196640 | tf_op jit(solution)/shard_map/ppermute | solution.py:344
  76.3 3.1 %collective-permute-done.4.refs_2_ = bf16[1,192,512]{2,1,0:T(8,128)(2,1)S(1)} collective-permute-done((bf16[1,192,512]{2,1,0:T(8,128)(2,1)S(1)}, bf16[1,192,512]{2,1,0:T(8,128)(2,1)S(1)}, u32[]{:S(2)}, u32[]{:S(2)}) %collective-permute-start.4) | collective-permute-done | bytes 196640 | tf_op jit(solution)/shard_map/ppermute | solution.py:344
  79.4 1.4 %collective-permute-done.5.refs_3_ = bf16[1,192,512]{2,1,0:T(8,128)(2,1)S(1)} collective-permute-done((bf16[1,192,512]{2,1,0:T(8,128)(2,1)S(1)}, bf16[1,192,512]{2,1,0:T(8,128)(2,1)S(1)}, u32[]{:S(2)}, u32[]{:S(2)}) %collective-permute-start.5) | collective-permute-done | bytes 196640 | tf_op jit(solution)/shard_map/ppermute | solution.py:344
  81.5 5.8 %collective-permute-done.21 = bf16[256,512]{1,0:T(8,128)(2,1)S(1)} collective-permute-done((bf16[256,512]{1,0:T(8,128)(2,1)S(1)}, bf16[256,512]{1,0:T(8,128)(2,1)S(1)}, u32[]{:S(2)}, u32[]{:S(2)}) %collective-permute-start.21) | collective-permute-done | bytes 262176 | tf_op jit(solution)/shard_map/ppermute | solution.py:344
  87.5 1.5 %collective-permute-done.22 = bf16[256,512]{1,0:T(8,128)(2,1)S(1)} collective-permute-done((bf16[256,512]{1,0:T(8,128)(2,1)S(1)}, bf16[256,512]{1,0:T(8,128)(2,1)S(1)}, u32[]{:S(2)}, u32[]{:S(2)}) %collective-permute-start.22) | collective-permute-done | bytes 262176 | tf_op jit(solution)/shard_map/ppermute | solution.py:344
  92.1 1.5 %collective-permute-start.23 = (bf16[160,128]{1,0:T(8,128)(2,1)S(1)}, bf16[160,128]{1,0:T(8,128)(2,1)S(1)}, u32[]{:S(2)}, u32[]{:S(2)}) collective-permute-start(bf16[160,128]{1,0:T(8,128)(2,1)S(1)} %get-tuple-element.101), channel_id=1, source_target_pairs={{0,2},{2,0},{4,6},{6,4},{8,10},{10,8},{12,14},{14,12},{16,18},{18,... | collective-permute-start | bytes 122888 | tf_op jit(solution)/shard_map/ppermute | solution.py:344
  93.6 1.8 %collective-permute-done.25 = bf16[160,128]{1,0:T(8,128)(2,1)S(1)} collective-permute-done((bf16[160,128]{1,0:T(8,128)(2,1)S(1)}, bf16[160,128]{1,0:T(8,128)(2,1)S(1)}, u32[]{:S(2)}, u32[]{:S(2)}) %collective-permute-start.25) | collective-permute-done | bytes 40992 | tf_op jit(solution)/shard_map/ppermute | solution.py:344
  96.1 2.6 %collective-permute-start.28 = (bf16[160,128]{1,0:T(8,128)(2,1)S(1)}, bf16[160,128]{1,0:T(8,128)(2,1)S(1)}, u32[]{:S(2)}, u32[]{:S(2)}) collective-permute-start(bf16[160,128]{1,0:T(8,128)(2,1)S(1)} %add_convert_fusion.1), channel_id=1, source_target_pairs={{0,24},{2,26},{4,28},{6,30},{8,16},{10,18},{12,20},{14,22},{16,8},... | collective-permute-start | bytes 122888 | tf_op jit(solution)/shard_map/ppermute | solution.py:344
  98.8 1.8 %collective-permute-start.26 = (bf16[160,128]{1,0:T(8,128)(2,1)S(1)}, bf16[160,128]{1,0:T(8,128)(2,1)S(1)}, u32[]{:S(2)}, u32[]{:S(2)}) collective-permute-start(bf16[160,128]{1,0:T(8,128)(2,1)S(1)} %add_convert_fusion.1), channel_id=1, source_target_pairs={{0,8},{2,10},{4,12},{6,14},{8,0},{10,2},{12,4},{14,6},{16,24},{18,... | collective-permute-start | bytes 122888 | tf_op jit(solution)/shard_map/ppermute | solution.py:344
  100.6 1.6 %collective-permute-done.28 = bf16[160,128]{1,0:T(8,128)(2,1)S(1)} collective-permute-done((bf16[160,128]{1,0:T(8,128)(2,1)S(1)}, bf16[160,128]{1,0:T(8,128)(2,1)S(1)}, u32[]{:S(2)}, u32[]{:S(2)}) %collective-permute-start.28) | collective-permute-done | bytes 40992 | tf_op jit(solution)/shard_map/ppermute | solution.py:344
  102.2 1.5 %collective-permute-done.27 = bf16[160,128]{1,0:T(8,128)(2,1)S(1)} collective-permute-done((bf16[160,128]{1,0:T(8,128)(2,1)S(1)}, bf16[160,128]{1,0:T(8,128)(2,1)S(1)}, u32[]{:S(2)}, u32[]{:S(2)}) %collective-permute-start.27) | collective-permute-done | bytes 40992 | tf_op jit(solution)/shard_map/ppermute | solution.py:344
  103.7 1.3 %collective-permute-start.31 = (bf16[160,128]{1,0:T(8,128)(2,1)S(1)}, bf16[160,128]{1,0:T(8,128)(2,1)S(1)}, u32[]{:S(2)}, u32[]{:S(2)}) collective-permute-start(bf16[160,128]{1,0:T(8,128)(2,1)S(1)} %add_convert_fusion), channel_id=1, source_target_pairs={{0,6},{2,4},{4,2},{6,0},{8,14},{10,12},{12,10},{14,8},{16,22},{18,... | collective-permute-start | bytes 122888 | tf_op jit(solution)/shard_map/ppermute | solution.py:344
  107.3 1.4 %collective-permute-done.31 = bf16[160,128]{1,0:T(8,128)(2,1)S(1)} collective-permute-done((bf16[160,128]{1,0:T(8,128)(2,1)S(1)}, bf16[160,128]{1,0:T(8,128)(2,1)S(1)}, u32[]{:S(2)}, u32[]{:S(2)}) %collective-permute-start.31) | collective-permute-done | bytes 40992 | tf_op jit(solution)/shard_map/ppermute | solution.py:344
  110.2 1.4 %collective-permute-done.32.other_gram_ref = bf16[5,128,128]{2,1,0:T(8,128)(2,1)S(1)} collective-permute-done((bf16[5,128,128]{2,1,0:T(8,128)(2,1)S(1)}, bf16[5,128,128]{2,1,0:T(8,128)(2,1)S(1)}, u32[]{:S(2)}, u32[]{:S(2)}) %collective-permute-start.32) | collective-permute-done | bytes 163872 | tf_op jit(solution)/shard_map/ppermute | solution.py:344
  111.6 5.1 %root.1 = f32[256,512]{1,0:T(8,128)} custom-call(s32[1]{0:T(128)} %bitcast.feat_ref.place_ref, bf16[5,128,128]{2,1,0:T(8,128)(2,1)S(1)} %bitcast.39, bf16[5,128,128]{2,1,0:T(8,128)(2,1)S(1)} %collective-permute-done.32.other_gram_ref, bf16[256,512]{1,0:T(8,128)(2,1)S(1)} %fusion.1.mine_ref), custom_call_target="tpu_custom_call" | custom-call | tf_op jit(solution)/shard_map/root/pallas_call | solution.py:331
  (69 shorter events, 23.6 us)
Async XLA Ops:
  6.8 29.6 %all-to-all-start = ((bf16[16,192,128]{2,1,0:T(8,128)(2,1)}), bf16[16,192,128]{2,1,0:T(8,128)(2,1)S(1)}, u32[]{:S(2)}, u32[]{:S(2)}) async-start(bf16[16,192,128]{2,1,0:T(8,128)(2,1)} %get-tuple-element.52), calls=%async_computation | async-start | bytes 1572864 | tf_op jit(solution)/shard_map/all_to_all | solution.py:431
  15.3 13.2 %collective-permute-start = (f32[8,512]{1,0:T(8,128)}, f32[8,512]{1,0:T(8,128)S(1)}, u32[]{:S(2)}, u32[]{:S(2)}) collective-permute-start(f32[8,512]{1,0:T(8,128)} %get-tuple-element.63.refs_0_), channel_id=1, source_target_pairs={{0,8},{2,10},{4,12},{6,14},{8,0},{10,2},{12,4},{14,6},{16,24},{18,... | collective-permute-start | bytes 49160 | tf_op jit(solution)/shard_map/ppermute | solution.py:344
  17.1 19.3 %collective-permute-start.1 = (f32[8,512]{1,0:T(8,128)}, f32[8,512]{1,0:T(8,128)S(1)}, u32[]{:S(2)}, u32[]{:S(2)}) collective-permute-start(f32[8,512]{1,0:T(8,128)} %get-tuple-element.63.refs_0_), channel_id=1, source_target_pairs={{0,16},{2,18},{4,20},{6,22},{8,24},{10,26},{12,28},{14,30},{16,0},... | collective-permute-start | bytes 49160 | tf_op jit(solution)/shard_map/ppermute | solution.py:344
  19.5 16.9 %collective-permute-start.2 = (f32[8,512]{1,0:T(8,128)}, f32[8,512]{1,0:T(8,128)S(1)}, u32[]{:S(2)}, u32[]{:S(2)}) collective-permute-start(f32[8,512]{1,0:T(8,128)} %get-tuple-element.63.refs_0_), channel_id=1, source_target_pairs={{0,24},{2,26},{4,28},{6,30},{8,16},{10,18},{12,20},{14,22},{16,8},... | collective-permute-start | bytes 49160 | tf_op jit(solution)/shard_map/ppermute | solution.py:344
  39.9 14.3 %collective-permute-start.12 = (bf16[1,192,512]{2,1,0:T(8,128)(2,1)S(1)}, bf16[1,192,512]{2,1,0:T(8,128)(2,1)S(1)}, u32[]{:S(2)}, u32[]{:S(2)}) collective-permute-start(bf16[1,192,512]{2,1,0:T(8,128)(2,1)S(1)} %get-tuple-element.55), channel_id=1, source_target_pairs={{0,2},{2,0},{4,6},{6,4},{8,10},{10,8},{12,14},{14,12},{16,18},{18,... | collective-permute-start | bytes 589832 | tf_op jit(solution)/shard_map/ppermute | solution.py:344
  41.5 13.4 %collective-permute-start.13 = (bf16[1,192,512]{2,1,0:T(8,128)(2,1)S(1)}, bf16[1,192,512]{2,1,0:T(8,128)(2,1)S(1)}, u32[]{:S(2)}, u32[]{:S(2)}) collective-permute-start(bf16[1,192,512]{2,1,0:T(8,128)(2,1)S(1)} %get-tuple-element.56), channel_id=1, source_target_pairs={{0,4},{2,6},{4,0},{6,2},{8,12},{10,14},{12,8},{14,10},{16,20},{18,... | collective-permute-start | bytes 589832 | tf_op jit(solution)/shard_map/ppermute | solution.py:344
  42.9 13.4 %collective-permute-start.14 = (bf16[1,192,512]{2,1,0:T(8,128)(2,1)S(1)}, bf16[1,192,512]{2,1,0:T(8,128)(2,1)S(1)}, u32[]{:S(2)}, u32[]{:S(2)}) collective-permute-start(bf16[1,192,512]{2,1,0:T(8,128)(2,1)S(1)} %get-tuple-element.57), channel_id=1, source_target_pairs={{0,6},{2,4},{4,2},{6,0},{8,14},{10,12},{12,10},{14,8},{16,22},{18,... | collective-permute-start | bytes 589832 | tf_op jit(solution)/shard_map/ppermute | solution.py:344
  44.8 13.6 %collective-permute-start.9 = (bf16[1,192,512]{2,1,0:T(8,128)(2,1)S(1)}, bf16[1,192,512]{2,1,0:T(8,128)(2,1)S(1)}, u32[]{:S(2)}, u32[]{:S(2)}) collective-permute-start(bf16[1,192,512]{2,1,0:T(8,128)(2,1)S(1)} %get-tuple-element.60), channel_id=1, source_target_pairs={{0,2},{2,0},{4,6},{6,4},{8,10},{10,8},{12,14},{14,12},{16,18},{18,... | collective-permute-start | bytes 589832 | tf_op jit(solution)/shard_map/ppermute | solution.py:344
  46.3 12.7 %collective-permute-start.10 = (bf16[1,192,512]{2,1,0:T(8,128)(2,1)S(1)}, bf16[1,192,512]{2,1,0:T(8,128)(2,1)S(1)}, u32[]{:S(2)}, u32[]{:S(2)}) collective-permute-start(bf16[1,192,512]{2,1,0:T(8,128)(2,1)S(1)} %get-tuple-element.61), channel_id=1, source_target_pairs={{0,4},{2,6},{4,0},{6,2},{8,12},{10,14},{12,8},{14,10},{16,20},{18,... | collective-permute-start | bytes 589832 | tf_op jit(solution)/shard_map/ppermute | solution.py:344
  54.2 8.9 %collective-permute-start.11 = (bf16[1,192,512]{2,1,0:T(8,128)(2,1)S(1)}, bf16[1,192,512]{2,1,0:T(8,128)(2,1)S(1)}, u32[]{:S(2)}, u32[]{:S(2)}) collective-permute-start(bf16[1,192,512]{2,1,0:T(8,128)(2,1)S(1)} %get-tuple-element.62), channel_id=1, source_target_pairs={{0,6},{2,4},{4,2},{6,0},{8,14},{10,12},{12,10},{14,8},{16,22},{18,... | collective-permute-start | bytes 589832 | tf_op jit(solution)/shard_map/ppermute | solution.py:344
  54.9 9.9 %collective-permute-start.6 = (bf16[1,192,512]{2,1,0:T(8,128)(2,1)S(1)}, bf16[1,192,512]{2,1,0:T(8,128)(2,1)S(1)}, u32[]{:S(2)}, u32[]{:S(2)}) collective-permute-start(bf16[1,192,512]{2,1,0:T(8,128)(2,1)S(1)} %get-tuple-element.69), channel_id=1, source_target_pairs={{0,2},{2,0},{4,6},{6,4},{8,10},{10,8},{12,14},{14,12},{16,18},{18,... | collective-permute-start | bytes 589832 | tf_op jit(solution)/shard_map/ppermute | solution.py:344
  56.3 11.5 %collective-permute-start.7 = (bf16[1,192,512]{2,1,0:T(8,128)(2,1)S(1)}, bf16[1,192,512]{2,1,0:T(8,128)(2,1)S(1)}, u32[]{:S(2)}, u32[]{:S(2)}) collective-permute-start(bf16[1,192,512]{2,1,0:T(8,128)(2,1)S(1)} %get-tuple-element.70), channel_id=1, source_target_pairs={{0,4},{2,6},{4,0},{6,2},{8,12},{10,14},{12,8},{14,10},{16,20},{18,... | collective-permute-start | bytes 589832 | tf_op jit(solution)/shard_map/ppermute | solution.py:344
  58.4 9.5 %collective-permute-start.8 = (bf16[1,192,512]{2,1,0:T(8,128)(2,1)S(1)}, bf16[1,192,512]{2,1,0:T(8,128)(2,1)S(1)}, u32[]{:S(2)}, u32[]{:S(2)}) collective-permute-start(bf16[1,192,512]{2,1,0:T(8,128)(2,1)S(1)} %get-tuple-element.71), channel_id=1, source_target_pairs={{0,6},{2,4},{4,2},{6,0},{8,14},{10,12},{12,10},{14,8},{16,22},{18,... | collective-permute-start | bytes 589832 | tf_op jit(solution)/shard_map/ppermute | solution.py:344
  59.0 4.8 %collective-permute-start.15 = (bf16[1,256,512]{2,1,0:T(8,128)(2,1)S(1)}, bf16[1,256,512]{2,1,0:T(8,128)(2,1)S(1)}, u32[]{:S(2)}, u32[]{:S(2)}) collective-permute-start(bf16[1,256,512]{2,1,0:T(8,128)(2,1)S(1)} %get-tuple-element.83), channel_id=1, source_target_pairs={{0,1},{1,0},{2,3},{3,2},{4,5},{5,4},{6,7},{7,6},{8,9},{9,8},{10,11... | collective-permute-start | bytes 786440 | tf_op jit(solution)/shard_map/ppermute | solution.py:344
  63.7 7.0 %collective-permute-start.16 = (bf16[1,256,512]{2,1,0:T(8,128)(2,1)S(1)}, bf16[1,256,512]{2,1,0:T(8,128)(2,1)S(1)}, u32[]{:S(2)}, u32[]{:S(2)}) collective-permute-start(bf16[1,256,512]{2,1,0:T(8,128)(2,1)S(1)} %get-tuple-element.89), channel_id=1, source_target_pairs={{0,1},{1,0},{2,3},{3,2},{4,5},{5,4},{6,7},{7,6},{8,9},{9,8},{10,11... | collective-permute-start | bytes 786440 | tf_op jit(solution)/shard_map/ppermute | solution.py:344
  63.9 8.8 %collective-permute-start.17 = (bf16[256,512]{1,0:T(8,128)(2,1)S(1)}, bf16[256,512]{1,0:T(8,128)(2,1)S(1)}, u32[]{:S(2)}, u32[]{:S(2)}) collective-permute-start(bf16[256,512]{1,0:T(8,128)(2,1)S(1)} %add_bitcast_fusion.1), channel_id=1, source_target_pairs={{0,8},{2,10},{4,12},{6,14},{8,0},{10,2},{12,4},{14,6},{16,24},{18,... | collective-permute-start | bytes 786440 | tf_op jit(solution)/shard_map/ppermute | solution.py:344
  68.5 5.3 %collective-permute-start.18 = (bf16[1,256,512]{2,1,0:T(8,128)(2,1)S(1)}, bf16[1,256,512]{2,1,0:T(8,128)(2,1)S(1)}, u32[]{:S(2)}, u32[]{:S(2)}) collective-permute-start(bf16[1,256,512]{2,1,0:T(8,128)(2,1)S(1)} %get-tuple-element.90), channel_id=1, source_target_pairs={{0,1},{1,0},{2,3},{3,2},{4,5},{5,4},{6,7},{7,6},{8,9},{9,8},{10,11... | collective-permute-start | bytes 786440 | tf_op jit(solution)/shard_map/ppermute | solution.py:344
  68.5 7.8 %collective-permute-start.3 = (bf16[1,192,512]{2,1,0:T(8,128)(2,1)S(1)}, bf16[1,192,512]{2,1,0:T(8,128)(2,1)S(1)}, u32[]{:S(2)}, u32[]{:S(2)}) collective-permute-start(bf16[1,192,512]{2,1,0:T(8,128)(2,1)S(1)} %get-tuple-element.74), channel_id=1, source_target_pairs={{0,2},{2,0},{4,6},{6,4},{8,10},{10,8},{12,14},{14,12},{16,18},{18,... | collective-permute-start | bytes 589832 | tf_op jit(solution)/shard_map/ppermute | solution.py:344
  69.6 9.8 %collective-permute-start.4 = (bf16[1,192,512]{2,1,0:T(8,128)(2,1)S(1)}, bf16[1,192,512]{2,1,0:T(8,128)(2,1)S(1)}, u32[]{:S(2)}, u32[]{:S(2)}) collective-permute-start(bf16[1,192,512]{2,1,0:T(8,128)(2,1)S(1)} %get-tuple-element.75), channel_id=1, source_target_pairs={{0,4},{2,6},{4,0},{6,2},{8,12},{10,14},{12,8},{14,10},{16,20},{18,... | collective-permute-start | bytes 589832 | tf_op jit(solution)/shard_map/ppermute | solution.py:344
  70.7 10.1 %collective-permute-start.5 = (bf16[1,192,512]{2,1,0:T(8,128)(2,1)S(1)}, bf16[1,192,512]{2,1,0:T(8,128)(2,1)S(1)}, u32[]{:S(2)}, u32[]{:S(2)}) collective-permute-start(bf16[1,192,512]{2,1,0:T(8,128)(2,1)S(1)} %get-tuple-element.76), channel_id=1, source_target_pairs={{0,6},{2,4},{4,2},{6,0},{8,14},{10,12},{12,10},{14,8},{16,22},{18,... | collective-permute-start | bytes 589832 | tf_op jit(solution)/shard_map/ppermute | solution.py:344
  72.8 14.5 %collective-permute-start.21 = (bf16[256,512]{1,0:T(8,128)(2,1)S(1)}, bf16[256,512]{1,0:T(8,128)(2,1)S(1)}, u32[]{:S(2)}, u32[]{:S(2)}) collective-permute-start(bf16[256,512]{1,0:T(8,128)(2,1)S(1)} %bitcast_add_fusion.1), channel_id=1, source_target_pairs={{0,16},{2,18},{4,20},{6,22},{8,24},{10,26},{12,28},{14,30},{16,0},... | collective-permute-start | bytes 786440 | tf_op jit(solution)/shard_map/ppermute | solution.py:344
  73.9 13.4 %collective-permute-start.20 = (bf16[256,512]{1,0:T(8,128)(2,1)S(1)}, bf16[256,512]{1,0:T(8,128)(2,1)S(1)}, u32[]{:S(2)}, u32[]{:S(2)}) collective-permute-start(bf16[256,512]{1,0:T(8,128)(2,1)S(1)} %add_bitcast_fusion), channel_id=1, source_target_pairs={{0,8},{2,10},{4,12},{6,14},{8,0},{10,2},{12,4},{14,6},{16,24},{18,... | collective-permute-start | bytes 786440 | tf_op jit(solution)/shard_map/ppermute | solution.py:344
  81.4 5.9 %collective-permute-start.19 = (bf16[1,256,512]{2,1,0:T(8,128)(2,1)S(1)}, bf16[1,256,512]{2,1,0:T(8,128)(2,1)S(1)}, u32[]{:S(2)}, u32[]{:S(2)}) collective-permute-start(bf16[1,256,512]{2,1,0:T(8,128)(2,1)S(1)} %get-tuple-element.96), channel_id=1, source_target_pairs={{0,1},{1,0},{2,3},{3,2},{4,5},{5,4},{6,7},{7,6},{8,9},{9,8},{10,11... | collective-permute-start | bytes 786440 | tf_op jit(solution)/shard_map/ppermute | solution.py:344
  90.0 5.4 %collective-permute-start.25 = (bf16[160,128]{1,0:T(8,128)(2,1)S(1)}, bf16[160,128]{1,0:T(8,128)(2,1)S(1)}, u32[]{:S(2)}, u32[]{:S(2)}) collective-permute-start(bf16[160,128]{1,0:T(8,128)(2,1)S(1)} %get-tuple-element.102), channel_id=1, source_target_pairs={{0,6},{2,4},{4,2},{6,0},{8,14},{10,12},{12,10},{14,8},{16,22},{18,... | collective-permute-start | bytes 122888 | tf_op jit(solution)/shard_map/ppermute | solution.py:344
  90.9 4.5 %collective-permute-start.24 = (bf16[160,128]{1,0:T(8,128)(2,1)S(1)}, bf16[160,128]{1,0:T(8,128)(2,1)S(1)}, u32[]{:S(2)}, u32[]{:S(2)}) collective-permute-start(bf16[160,128]{1,0:T(8,128)(2,1)S(1)} %get-tuple-element.103), channel_id=1, source_target_pairs={{0,4},{2,6},{4,0},{6,2},{8,12},{10,14},{12,8},{14,10},{16,20},{18,... | collective-permute-start | bytes 122888 | tf_op jit(solution)/shard_map/ppermute | solution.py:344
  92.1 4.0 %collective-permute-start.23 = (bf16[160,128]{1,0:T(8,128)(2,1)S(1)}, bf16[160,128]{1,0:T(8,128)(2,1)S(1)}, u32[]{:S(2)}, u32[]{:S(2)}) collective-permute-start(bf16[160,128]{1,0:T(8,128)(2,1)S(1)} %get-tuple-element.101), channel_id=1, source_target_pairs={{0,2},{2,0},{4,6},{6,4},{8,10},{10,8},{12,14},{14,12},{16,18},{18,... | collective-permute-start | bytes 122888 | tf_op jit(solution)/shard_map/ppermute | solution.py:344
  96.1 6.1 %collective-permute-start.28 = (bf16[160,128]{1,0:T(8,128)(2,1)S(1)}, bf16[160,128]{1,0:T(8,128)(2,1)S(1)}, u32[]{:S(2)}, u32[]{:S(2)}) collective-permute-start(bf16[160,128]{1,0:T(8,128)(2,1)S(1)} %add_convert_fusion.1), channel_id=1, source_target_pairs={{0,24},{2,26},{4,28},{6,30},{8,16},{10,18},{12,20},{14,22},{16,8},... | collective-permute-start | bytes 122888 | tf_op jit(solution)/shard_map/ppermute | solution.py:344
  98.8 4.9 %collective-permute-start.27 = (bf16[160,128]{1,0:T(8,128)(2,1)S(1)}, bf16[160,128]{1,0:T(8,128)(2,1)S(1)}, u32[]{:S(2)}, u32[]{:S(2)}) collective-permute-start(bf16[160,128]{1,0:T(8,128)(2,1)S(1)} %add_convert_fusion.1), channel_id=1, source_target_pairs={{0,16},{2,18},{4,20},{6,22},{8,24},{10,26},{12,28},{14,30},{16,0},... | collective-permute-start | bytes 122888 | tf_op jit(solution)/shard_map/ppermute | solution.py:344
  98.8 4.9 %collective-permute-start.26 = (bf16[160,128]{1,0:T(8,128)(2,1)S(1)}, bf16[160,128]{1,0:T(8,128)(2,1)S(1)}, u32[]{:S(2)}, u32[]{:S(2)}) collective-permute-start(bf16[160,128]{1,0:T(8,128)(2,1)S(1)} %add_convert_fusion.1), channel_id=1, source_target_pairs={{0,8},{2,10},{4,12},{6,14},{8,0},{10,2},{12,4},{14,6},{16,24},{18,... | collective-permute-start | bytes 122888 | tf_op jit(solution)/shard_map/ppermute | solution.py:344
  103.7 5.0 %collective-permute-start.31 = (bf16[160,128]{1,0:T(8,128)(2,1)S(1)}, bf16[160,128]{1,0:T(8,128)(2,1)S(1)}, u32[]{:S(2)}, u32[]{:S(2)}) collective-permute-start(bf16[160,128]{1,0:T(8,128)(2,1)S(1)} %add_convert_fusion), channel_id=1, source_target_pairs={{0,6},{2,4},{4,2},{6,0},{8,14},{10,12},{12,10},{14,8},{16,22},{18,... | collective-permute-start | bytes 122888 | tf_op jit(solution)/shard_map/ppermute | solution.py:344
  105.0 4.1 %collective-permute-start.30 = (bf16[160,128]{1,0:T(8,128)(2,1)S(1)}, bf16[160,128]{1,0:T(8,128)(2,1)S(1)}, u32[]{:S(2)}, u32[]{:S(2)}) collective-permute-start(bf16[160,128]{1,0:T(8,128)(2,1)S(1)} %add_convert_fusion), channel_id=1, source_target_pairs={{0,4},{2,6},{4,0},{6,2},{8,12},{10,14},{12,8},{14,10},{16,20},{18,... | collective-permute-start | bytes 122888 | tf_op jit(solution)/shard_map/ppermute | solution.py:344
  106.0 4.0 %collective-permute-start.29 = (bf16[160,128]{1,0:T(8,128)(2,1)S(1)}, bf16[160,128]{1,0:T(8,128)(2,1)S(1)}, u32[]{:S(2)}, u32[]{:S(2)}) collective-permute-start(bf16[160,128]{1,0:T(8,128)(2,1)S(1)} %add_convert_fusion), channel_id=1, source_target_pairs={{0,2},{2,0},{4,6},{6,4},{8,10},{10,8},{12,14},{14,12},{16,18},{18,... | collective-permute-start | bytes 122888 | tf_op jit(solution)/shard_map/ppermute | solution.py:344
  (6 other events, 27.0 us)

commit v8 on v7

--- a/solution.py
+++ b/solution.py
@@ -395,7 +395,7 @@
     where = jnp.stack([index & (inner - 1), index // inner])
     positions = [position] + [crossed(position, "dp", c * inner) for c in range(1, n_dp // inner)]
     sent, hits = [], None
-    for at, away in enumerate(stages):
+    for at, away in enumerate(stages[:3]):
         behind = positions if not at else sent[-1]
         if at == 2:
             hits = choose(where, tied(positions, sent[-1]), k_j, slots, inner)
@@ -403,9 +403,11 @@
         sent.append(product(where, tied(tiles, behind), probe, inner, bound, away))
     plane, kept, behind = {}, [], None
     for at, away in enumerate(stages):
+        if at == 1:
+            sent.append(product(where, tied(tiles, kept[0]), probe, inner, bound, stages[3]))
         rows = [sent[at][0]] + [crossed(sent[at][a], "dp", a) for a in range(1, inner)]
         if at:
-            rows = tied(rows, kept[-1], (plane[3], sent[3]) if at == 2 else (plane[2], plane[1]) if at == 3 else kept[-1])
+            rows = tied(rows, kept[-1], (plane[3], sent[3]) if at == 2 else (plane[2], plane[1]) if at == 3 else sent[3])
         keep, give = gather(feat, hits, rows, away)
         kept.append(keep)
         both = keep + crossed(give, "feat", 1).astype(f32)

time: 117 us -> 117 us (level)
  transfers between devices with their start and end apart: 34 -> 34, of which waited for: 18 -> 20; matrix products, arithmetic and copies ran while one was open for 0% -> 0% of each run, Pallas kernels for 9% -> 9%
where the time goes in v8:
time: 117 us; the launch traced here: 116 us
  waiting for transfers between devices  46.7 us (40%)
  starting transfers between devices  42.4 us (36%)
  Pallas kernels  24.1 us (21%)
  local copies, waits for them, and re-layouts  2.25 us (2%)
    ppermute x33, waiting for transfers between devices, crossed(): lax.ppermute(value, axis, [(source, source ^ bits) for source in range(co...  46.7 us
    ppermute x33, starting transfers between devices, crossed(): lax.ppermute(value, axis, [(source, source ^ bits) for source in range(co...  33.9 us
    all_to_all x1, starting transfers between devices, local(): tiles = lax.all_to_all(send, 'dp', split_axis=0, concat_axis=0, tiled=True)  8.5 us
    pallas_call x1, Pallas kernels, pack(): pl.pallas_call(functools.partial(pack_kernel, per_dev, bound), out_shape=...  6.76 us
    pallas_call x4, Pallas kernels, product(): pl.pallas_call(functools.partial(product_kernel, bound, joint, groups, aw...  5.32 us
    pallas_call x1, Pallas kernels, whiten(): pl.pallas_call(functools.partial(root_kernel, samples), out_shape=jax.Sha...  5.11 us
    pallas_call x1, Pallas kernels, choose(): pl.pallas_call(functools.partial(choose_kernel, k_j, slots, inner), out_s...  3.72 us
  transfers between devices with their start and end apart: 34, of which 20 were waited for; matrix products, arithmetic and copies ran while one was open for 0% of the time, Pallas kernels for 9%

profile of v8, /device:TPU:0, one launch (start us, length us, event | category | flops | bytes accessed | tf_op | source)
XLA Modules:
  0.0 116.4 jit_solution(6276043893173233337)
XLA Ops:
  0.0 6.8 %pack.1 = (bf16[16,192,128]{2,1,0:T(8,128)(2,1)}, f32[8,512]{1,0:T(8,128)}) custom-call(s32[4,512]{1,0:T(4,128)} %bitcast.49, bf16[2048,128]{1,0:T(8,128)(2,1)} %bitcast.44), custom_call_target="tpu_custom_call" | custom-call | tf_op jit(solution)/shard_map/pack/pallas_call | solution.py:94
  6.8 8.5 %all-to-all-start = ((bf16[16,192,128]{2,1,0:T(8,128)(2,1)}), bf16[16,192,128]{2,1,0:T(8,128)(2,1)S(1)}, u32[]{:S(2)}, u32[]{:S(2)}) async-start(bf16[16,192,128]{2,1,0:T(8,128)(2,1)} %get-tuple-element.52), calls=%async_computation | async-start | bytes 1572864 | tf_op jit(solution)/shard_map/all_to_all | solution.py:433
  15.3 1.8 %collective-permute-start = (f32[8,512]{1,0:T(8,128)}, f32[8,512]{1,0:T(8,128)S(1)}, u32[]{:S(2)}, u32[]{:S(2)}) collective-permute-start(f32[8,512]{1,0:T(8,128)} %get-tuple-element.63.refs_0_), channel_id=1, source_target_pairs={{0,8},{2,10},{4,12},{6,14},{8,0},{10,2},{12,4},{14,6},{16,24},{18,... | collective-permute-start | bytes 49160 | tf_op jit(solution)/shard_map/ppermute | solution.py:344
  17.1 2.4 %collective-permute-start.1 = (f32[8,512]{1,0:T(8,128)}, f32[8,512]{1,0:T(8,128)S(1)}, u32[]{:S(2)}, u32[]{:S(2)}) collective-permute-start(f32[8,512]{1,0:T(8,128)} %get-tuple-element.63.refs_0_), channel_id=1, source_target_pairs={{0,16},{2,18},{4,20},{6,22},{8,24},{10,26},{12,28},{14,30},{16,0},... | collective-permute-start | bytes 49160 | tf_op jit(solution)/shard_map/ppermute | solution.py:344
  19.8 8.7 %collective-permute-done.refs_1_ = f32[8,512]{1,0:T(8,128)S(1)} collective-permute-done((f32[8,512]{1,0:T(8,128)}, f32[8,512]{1,0:T(8,128)S(1)}, u32[]{:S(2)}, u32[]{:S(2)}) %collective-permute-start) | collective-permute-done | bytes 16416 | tf_op jit(solution)/shard_map/ppermute | solution.py:344
  28.5 7.9 %collective-permute-done.1.refs_2_ = f32[8,512]{1,0:T(8,128)S(1)} collective-permute-done((f32[8,512]{1,0:T(8,128)}, f32[8,512]{1,0:T(8,128)S(1)}, u32[]{:S(2)}, u32[]{:S(2)}) %collective-permute-start.1) | collective-permute-done | bytes 16416 | tf_op jit(solution)/shard_map/ppermute | solution.py:344
  36.4 2.2 %copy-done = bf16[32,1,128,512]{3,2,1,0:T(8,128)(2,1)S(1)} copy-done((bf16[32,1,128,512]{3,2,1,0:T(8,128)(2,1)S(1)}, bf16[32,1,128,512]{3,2,1,0:T(8,128)(2,1)}, u32[]{:S(2)}) %copy-start) | copy-done | bytes 4194328
  39.9 1.5 %collective-permute-start.3 = (bf16[1,192,512]{2,1,0:T(8,128)(2,1)S(1)}, bf16[1,192,512]{2,1,0:T(8,128)(2,1)S(1)}, u32[]{:S(2)}, u32[]{:S(2)}) collective-permute-start(bf16[1,192,512]{2,1,0:T(8,128)(2,1)S(1)} %get-tuple-element.55), channel_id=1, source_target_pairs={{0,2},{2,0},{4,6},{6,4},{8,10},{10,8},{12,14},{14,12},{16,18},{18,... | collective-permute-start | bytes 589832 | tf_op jit(solution)/shard_map/ppermute | solution.py:344
  41.5 1.5 %collective-permute-start.4 = (bf16[1,192,512]{2,1,0:T(8,128)(2,1)S(1)}, bf16[1,192,512]{2,1,0:T(8,128)(2,1)S(1)}, u32[]{:S(2)}, u32[]{:S(2)}) collective-permute-start(bf16[1,192,512]{2,1,0:T(8,128)(2,1)S(1)} %get-tuple-element.56), channel_id=1, source_target_pairs={{0,4},{2,6},{4,0},{6,2},{8,12},{10,14},{12,8},{14,10},{16,20},{18,... | collective-permute-start | bytes 589832 | tf_op jit(solution)/shard_map/ppermute | solution.py:344
  44.8 1.5 %collective-permute-start.12 = (bf16[1,192,512]{2,1,0:T(8,128)(2,1)S(1)}, bf16[1,192,512]{2,1,0:T(8,128)(2,1)S(1)}, u32[]{:S(2)}, u32[]{:S(2)}) collective-permute-start(bf16[1,192,512]{2,1,0:T(8,128)(2,1)S(1)} %get-tuple-element.60), channel_id=1, source_target_pairs={{0,2},{2,0},{4,6},{6,4},{8,10},{10,8},{12,14},{14,12},{16,18},{18,... | collective-permute-start | bytes 589832 | tf_op jit(solution)/shard_map/ppermute | solution.py:344
  46.3 1.5 %collective-permute-start.13 = (bf16[1,192,512]{2,1,0:T(8,128)(2,1)S(1)}, bf16[1,192,512]{2,1,0:T(8,128)(2,1)S(1)}, u32[]{:S(2)}, u32[]{:S(2)}) collective-permute-start(bf16[1,192,512]{2,1,0:T(8,128)(2,1)S(1)} %get-tuple-element.61), channel_id=1, source_target_pairs={{0,4},{2,6},{4,0},{6,2},{8,12},{10,14},{12,8},{14,10},{16,20},{18,... | collective-permute-start | bytes 589832 | tf_op jit(solution)/shard_map/ppermute | solution.py:344
  47.8 3.7 %choose.1.hits_ref = bf16[4,512,768]{2,1,0:T(8,128)(2,1)S(1)} custom-call(s32[2]{0:T(128)S(1)} %pad_add_fusion.where_ref.place_ref, f32[8,512]{1,0:T(8,128)S(1)} %copy-done.2, f32[8,512]{1,0:T(8,128)S(1)} %collective-permute-done.refs_1_, f32[8,512]{1,0:T(8,128)S(1)} %collective-permute-done.1.refs_2_, f32[8,512]{1,0:T(8,128)S(1)} %collective-permute-done.2.refs_3_), custom_call_target="tpu_custom_call" | custom-call | flops 17179869184 | bytes 1 | tf_op jit(solution)/shard_map/choose/pallas_call | solution.py:180
  53.5 1.5 %collective-permute-start.9 = (bf16[1,192,512]{2,1,0:T(8,128)(2,1)S(1)}, bf16[1,192,512]{2,1,0:T(8,128)(2,1)S(1)}, u32[]{:S(2)}, u32[]{:S(2)}) collective-permute-start(bf16[1,192,512]{2,1,0:T(8,128)(2,1)S(1)} %get-tuple-element.75), channel_id=1, source_target_pairs={{0,2},{2,0},{4,6},{6,4},{8,10},{10,8},{12,14},{14,12},{16,18},{18,... | collective-permute-start | bytes 589832 | tf_op jit(solution)/shard_map/ppermute | solution.py:344
  55.0 1.5 %collective-permute-start.10 = (bf16[1,192,512]{2,1,0:T(8,128)(2,1)S(1)}, bf16[1,192,512]{2,1,0:T(8,128)(2,1)S(1)}, u32[]{:S(2)}, u32[]{:S(2)}) collective-permute-start(bf16[1,192,512]{2,1,0:T(8,128)(2,1)S(1)} %get-tuple-element.76), channel_id=1, source_target_pairs={{0,4},{2,6},{4,0},{6,2},{8,12},{10,14},{12,8},{14,10},{16,20},{18,... | collective-permute-start | bytes 589832 | tf_op jit(solution)/shard_map/ppermute | solution.py:344
  59.6 2.1 %collective-permute-done.14.refs_3_ = bf16[1,192,512]{2,1,0:T(8,128)(2,1)S(1)} collective-permute-done((bf16[1,192,512]{2,1,0:T(8,128)(2,1)S(1)}, bf16[1,192,512]{2,1,0:T(8,128)(2,1)S(1)}, u32[]{:S(2)}, u32[]{:S(2)}) %collective-permute-start.14) | collective-permute-done | bytes 196640 | tf_op jit(solution)/shard_map/ppermute | solution.py:344
  63.3 1.4 %collective-permute-done.9.refs_1_ = bf16[1,192,512]{2,1,0:T(8,128)(2,1)S(1)} collective-permute-done((bf16[1,192,512]{2,1,0:T(8,128)(2,1)S(1)}, bf16[1,192,512]{2,1,0:T(8,128)(2,1)S(1)}, u32[]{:S(2)}, u32[]{:S(2)}) %collective-permute-start.9) | collective-permute-done | bytes 196640 | tf_op jit(solution)/shard_map/ppermute | solution.py:344
  64.6 3.3 %collective-permute-done.10.refs_2_ = bf16[1,192,512]{2,1,0:T(8,128)(2,1)S(1)} collective-permute-done((bf16[1,192,512]{2,1,0:T(8,128)(2,1)S(1)}, bf16[1,192,512]{2,1,0:T(8,128)(2,1)S(1)}, u32[]{:S(2)}, u32[]{:S(2)}) %collective-permute-start.10) | collective-permute-done | bytes 196640 | tf_op jit(solution)/shard_map/ppermute | solution.py:344
  70.7 1.4 %collective-permute-start.8 = (bf16[1,192,512]{2,1,0:T(8,128)(2,1)S(1)}, bf16[1,192,512]{2,1,0:T(8,128)(2,1)S(1)}, u32[]{:S(2)}, u32[]{:S(2)}) collective-permute-start(bf16[1,192,512]{2,1,0:T(8,128)(2,1)S(1)} %get-tuple-element.72), channel_id=1, source_target_pairs={{0,6},{2,4},{4,2},{6,0},{8,14},{10,12},{12,10},{14,8},{16,22},{18,... | collective-permute-start | bytes 589832 | tf_op jit(solution)/shard_map/ppermute | solution.py:344
  72.2 1.5 %collective-permute-start.21 = (bf16[256,512]{1,0:T(8,128)(2,1)S(1)}, bf16[256,512]{1,0:T(8,128)(2,1)S(1)}, u32[]{:S(2)}, u32[]{:S(2)}) collective-permute-start(bf16[256,512]{1,0:T(8,128)(2,1)S(1)} %bitcast_add_fusion.1), channel_id=1, source_target_pairs={{0,16},{2,18},{4,20},{6,22},{8,24},{10,26},{12,28},{14,30},{16,0},... | collective-permute-start | bytes 786440 | tf_op jit(solution)/shard_map/ppermute | solution.py:344
  74.8 1.5 %collective-permute-done.6.refs_1_ = bf16[1,192,512]{2,1,0:T(8,128)(2,1)S(1)} collective-permute-done((bf16[1,192,512]{2,1,0:T(8,128)(2,1)S(1)}, bf16[1,192,512]{2,1,0:T(8,128)(2,1)S(1)}, u32[]{:S(2)}, u32[]{:S(2)}) %collective-permute-start.6) | collective-permute-done | bytes 196640 | tf_op jit(solution)/shard_map/ppermute | solution.py:344
  76.3 3.1 %collective-permute-done.7.refs_2_ = bf16[1,192,512]{2,1,0:T(8,128)(2,1)S(1)} collective-permute-done((bf16[1,192,512]{2,1,0:T(8,128)(2,1)S(1)}, bf16[1,192,512]{2,1,0:T(8,128)(2,1)S(1)}, u32[]{:S(2)}, u32[]{:S(2)}) %collective-permute-start.7) | collective-permute-done | bytes 196640 | tf_op jit(solution)/shard_map/ppermute | solution.py:344
  81.4 5.3 %collective-permute-done.21 = bf16[256,512]{1,0:T(8,128)(2,1)S(1)} collective-permute-done((bf16[256,512]{1,0:T(8,128)(2,1)S(1)}, bf16[256,512]{1,0:T(8,128)(2,1)S(1)}, u32[]{:S(2)}, u32[]{:S(2)}) %collective-permute-start.21) | collective-permute-done | bytes 262176 | tf_op jit(solution)/shard_map/ppermute | solution.py:344
  86.9 1.5 %collective-permute-done.22 = bf16[256,512]{1,0:T(8,128)(2,1)S(1)} collective-permute-done((bf16[256,512]{1,0:T(8,128)(2,1)S(1)}, bf16[256,512]{1,0:T(8,128)(2,1)S(1)}, u32[]{:S(2)}, u32[]{:S(2)}) %collective-permute-start.22) | collective-permute-done | bytes 262176 | tf_op jit(solution)/shard_map/ppermute | solution.py:344
  89.4 1.6 %collective-permute-start.25 = (bf16[160,128]{1,0:T(8,128)(2,1)S(1)}, bf16[160,128]{1,0:T(8,128)(2,1)S(1)}, u32[]{:S(2)}, u32[]{:S(2)}) collective-permute-start(bf16[160,128]{1,0:T(8,128)(2,1)S(1)} %get-tuple-element.102), channel_id=1, source_target_pairs={{0,6},{2,4},{4,2},{6,0},{8,14},{10,12},{12,10},{14,8},{16,22},{18,... | collective-permute-start | bytes 122888 | tf_op jit(solution)/shard_map/ppermute | solution.py:344
  92.9 1.5 %collective-permute-done.25 = bf16[160,128]{1,0:T(8,128)(2,1)S(1)} collective-permute-done((bf16[160,128]{1,0:T(8,128)(2,1)S(1)}, bf16[160,128]{1,0:T(8,128)(2,1)S(1)}, u32[]{:S(2)}, u32[]{:S(2)}) %collective-permute-start.25) | collective-permute-done | bytes 40992 | tf_op jit(solution)/shard_map/ppermute | solution.py:344
  95.8 2.7 %collective-permute-start.28 = (bf16[160,128]{1,0:T(8,128)(2,1)S(1)}, bf16[160,128]{1,0:T(8,128)(2,1)S(1)}, u32[]{:S(2)}, u32[]{:S(2)}) collective-permute-start(bf16[160,128]{1,0:T(8,128)(2,1)S(1)} %add_convert_fusion.1), channel_id=1, source_target_pairs={{0,24},{2,26},{4,28},{6,30},{8,16},{10,18},{12,20},{14,22},{16,8},... | collective-permute-start | bytes 122888 | tf_op jit(solution)/shard_map/ppermute | solution.py:344
  98.5 1.8 %collective-permute-start.26 = (bf16[160,128]{1,0:T(8,128)(2,1)S(1)}, bf16[160,128]{1,0:T(8,128)(2,1)S(1)}, u32[]{:S(2)}, u32[]{:S(2)}) collective-permute-start(bf16[160,128]{1,0:T(8,128)(2,1)S(1)} %add_convert_fusion.1), channel_id=1, source_target_pairs={{0,8},{2,10},{4,12},{6,14},{8,0},{10,2},{12,4},{14,6},{16,24},{18,... | collective-permute-start | bytes 122888 | tf_op jit(solution)/shard_map/ppermute | solution.py:344
  100.3 1.5 %collective-permute-done.28 = bf16[160,128]{1,0:T(8,128)(2,1)S(1)} collective-permute-done((bf16[160,128]{1,0:T(8,128)(2,1)S(1)}, bf16[160,128]{1,0:T(8,128)(2,1)S(1)}, u32[]{:S(2)}, u32[]{:S(2)}) %collective-permute-start.28) | collective-permute-done | bytes 40992 | tf_op jit(solution)/shard_map/ppermute | solution.py:344
  101.8 1.6 %collective-permute-done.27 = bf16[160,128]{1,0:T(8,128)(2,1)S(1)} collective-permute-done((bf16[160,128]{1,0:T(8,128)(2,1)S(1)}, bf16[160,128]{1,0:T(8,128)(2,1)S(1)}, u32[]{:S(2)}, u32[]{:S(2)}) %collective-permute-start.27) | collective-permute-done | bytes 40992 | tf_op jit(solution)/shard_map/ppermute | solution.py:344
  103.5 1.6 %collective-permute-start.31 = (bf16[160,128]{1,0:T(8,128)(2,1)S(1)}, bf16[160,128]{1,0:T(8,128)(2,1)S(1)}, u32[]{:S(2)}, u32[]{:S(2)}) collective-permute-start(bf16[160,128]{1,0:T(8,128)(2,1)S(1)} %add_convert_fusion), channel_id=1, source_target_pairs={{0,6},{2,4},{4,2},{6,0},{8,14},{10,12},{12,10},{14,8},{16,22},{18,... | collective-permute-start | bytes 122888 | tf_op jit(solution)/shard_map/ppermute | solution.py:344
  107.0 1.4 %collective-permute-done.31 = bf16[160,128]{1,0:T(8,128)(2,1)S(1)} collective-permute-done((bf16[160,128]{1,0:T(8,128)(2,1)S(1)}, bf16[160,128]{1,0:T(8,128)(2,1)S(1)}, u32[]{:S(2)}, u32[]{:S(2)}) %collective-permute-start.31) | collective-permute-done | bytes 40992 | tf_op jit(solution)/shard_map/ppermute | solution.py:344
  111.2 5.1 %root.1 = f32[256,512]{1,0:T(8,128)} custom-call(s32[1]{0:T(128)} %bitcast.feat_ref.place_ref, bf16[5,128,128]{2,1,0:T(8,128)(2,1)S(1)} %bitcast.39, bf16[5,128,128]{2,1,0:T(8,128)(2,1)S(1)} %collective-permute-done.32.other_gram_ref, bf16[256,512]{1,0:T(8,128)(2,1)S(1)} %fusion.1.mine_ref), custom_call_target="tpu_custom_call" | custom-call | tf_op jit(solution)/shard_map/root/pallas_call | solution.py:331
  (69 shorter events, 25.5 us)
Async XLA Ops:
  6.8 29.6 %all-to-all-start = ((bf16[16,192,128]{2,1,0:T(8,128)(2,1)}), bf16[16,192,128]{2,1,0:T(8,128)(2,1)S(1)}, u32[]{:S(2)}, u32[]{:S(2)}) async-start(bf16[16,192,128]{2,1,0:T(8,128)(2,1)} %get-tuple-element.52), calls=%async_computation | async-start | bytes 1572864 | tf_op jit(solution)/shard_map/all_to_all | solution.py:433
  15.3 13.2 %collective-permute-start = (f32[8,512]{1,0:T(8,128)}, f32[8,512]{1,0:T(8,128)S(1)}, u32[]{:S(2)}, u32[]{:S(2)}) collective-permute-start(f32[8,512]{1,0:T(8,128)} %get-tuple-element.63.refs_0_), channel_id=1, source_target_pairs={{0,8},{2,10},{4,12},{6,14},{8,0},{10,2},{12,4},{14,6},{16,24},{18,... | collective-permute-start | bytes 49160 | tf_op jit(solution)/shard_map/ppermute | solution.py:344
  17.1 19.3 %collective-permute-start.1 = (f32[8,512]{1,0:T(8,128)}, f32[8,512]{1,0:T(8,128)S(1)}, u32[]{:S(2)}, u32[]{:S(2)}) collective-permute-start(f32[8,512]{1,0:T(8,128)} %get-tuple-element.63.refs_0_), channel_id=1, source_target_pairs={{0,16},{2,18},{4,20},{6,22},{8,24},{10,26},{12,28},{14,30},{16,0},... | collective-permute-start | bytes 49160 | tf_op jit(solution)/shard_map/ppermute | solution.py:344
  19.5 16.9 %collective-permute-start.2 = (f32[8,512]{1,0:T(8,128)}, f32[8,512]{1,0:T(8,128)S(1)}, u32[]{:S(2)}, u32[]{:S(2)}) collective-permute-start(f32[8,512]{1,0:T(8,128)} %get-tuple-element.63.refs_0_), channel_id=1, source_target_pairs={{0,24},{2,26},{4,28},{6,30},{8,16},{10,18},{12,20},{14,22},{16,8},... | collective-permute-start | bytes 49160 | tf_op jit(solution)/shard_map/ppermute | solution.py:344
  39.9 13.0 %collective-permute-start.3 = (bf16[1,192,512]{2,1,0:T(8,128)(2,1)S(1)}, bf16[1,192,512]{2,1,0:T(8,128)(2,1)S(1)}, u32[]{:S(2)}, u32[]{:S(2)}) collective-permute-start(bf16[1,192,512]{2,1,0:T(8,128)(2,1)S(1)} %get-tuple-element.55), channel_id=1, source_target_pairs={{0,2},{2,0},{4,6},{6,4},{8,10},{10,8},{12,14},{14,12},{16,18},{18,... | collective-permute-start | bytes 589832 | tf_op jit(solution)/shard_map/ppermute | solution.py:344
  41.5 12.1 %collective-permute-start.4 = (bf16[1,192,512]{2,1,0:T(8,128)(2,1)S(1)}, bf16[1,192,512]{2,1,0:T(8,128)(2,1)S(1)}, u32[]{:S(2)}, u32[]{:S(2)}) collective-permute-start(bf16[1,192,512]{2,1,0:T(8,128)(2,1)S(1)} %get-tuple-element.56), channel_id=1, source_target_pairs={{0,4},{2,6},{4,0},{6,2},{8,12},{10,14},{12,8},{14,10},{16,20},{18,... | collective-permute-start | bytes 589832 | tf_op jit(solution)/shard_map/ppermute | solution.py:344
  42.9 12.1 %collective-permute-start.5 = (bf16[1,192,512]{2,1,0:T(8,128)(2,1)S(1)}, bf16[1,192,512]{2,1,0:T(8,128)(2,1)S(1)}, u32[]{:S(2)}, u32[]{:S(2)}) collective-permute-start(bf16[1,192,512]{2,1,0:T(8,128)(2,1)S(1)} %get-tuple-element.57), channel_id=1, source_target_pairs={{0,6},{2,4},{4,2},{6,0},{8,14},{10,12},{12,10},{14,8},{16,22},{18,... | collective-permute-start | bytes 589832 | tf_op jit(solution)/shard_map/ppermute | solution.py:344
  44.8 13.6 %collective-permute-start.12 = (bf16[1,192,512]{2,1,0:T(8,128)(2,1)S(1)}, bf16[1,192,512]{2,1,0:T(8,128)(2,1)S(1)}, u32[]{:S(2)}, u32[]{:S(2)}) collective-permute-start(bf16[1,192,512]{2,1,0:T(8,128)(2,1)S(1)} %get-tuple-element.60), channel_id=1, source_target_pairs={{0,2},{2,0},{4,6},{6,4},{8,10},{10,8},{12,14},{14,12},{16,18},{18,... | collective-permute-start | bytes 589832 | tf_op jit(solution)/shard_map/ppermute | solution.py:344
  46.3 13.3 %collective-permute-start.13 = (bf16[1,192,512]{2,1,0:T(8,128)(2,1)S(1)}, bf16[1,192,512]{2,1,0:T(8,128)(2,1)S(1)}, u32[]{:S(2)}, u32[]{:S(2)}) collective-permute-start(bf16[1,192,512]{2,1,0:T(8,128)(2,1)S(1)} %get-tuple-element.61), channel_id=1, source_target_pairs={{0,4},{2,6},{4,0},{6,2},{8,12},{10,14},{12,8},{14,10},{16,20},{18,... | collective-permute-start | bytes 589832 | tf_op jit(solution)/shard_map/ppermute | solution.py:344
  52.9 8.9 %collective-permute-start.14 = (bf16[1,192,512]{2,1,0:T(8,128)(2,1)S(1)}, bf16[1,192,512]{2,1,0:T(8,128)(2,1)S(1)}, u32[]{:S(2)}, u32[]{:S(2)}) collective-permute-start(bf16[1,192,512]{2,1,0:T(8,128)(2,1)S(1)} %get-tuple-element.62), channel_id=1, source_target_pairs={{0,6},{2,4},{4,2},{6,0},{8,14},{10,12},{12,10},{14,8},{16,22},{18,... | collective-permute-start | bytes 589832 | tf_op jit(solution)/shard_map/ppermute | solution.py:344
  53.5 11.1 %collective-permute-start.9 = (bf16[1,192,512]{2,1,0:T(8,128)(2,1)S(1)}, bf16[1,192,512]{2,1,0:T(8,128)(2,1)S(1)}, u32[]{:S(2)}, u32[]{:S(2)}) collective-permute-start(bf16[1,192,512]{2,1,0:T(8,128)(2,1)S(1)} %get-tuple-element.75), channel_id=1, source_target_pairs={{0,2},{2,0},{4,6},{6,4},{8,10},{10,8},{12,14},{14,12},{16,18},{18,... | collective-permute-start | bytes 589832 | tf_op jit(solution)/shard_map/ppermute | solution.py:344
  55.0 12.9 %collective-permute-start.10 = (bf16[1,192,512]{2,1,0:T(8,128)(2,1)S(1)}, bf16[1,192,512]{2,1,0:T(8,128)(2,1)S(1)}, u32[]{:S(2)}, u32[]{:S(2)}) collective-permute-start(bf16[1,192,512]{2,1,0:T(8,128)(2,1)S(1)} %get-tuple-element.76), channel_id=1, source_target_pairs={{0,4},{2,6},{4,0},{6,2},{8,12},{10,14},{12,8},{14,10},{16,20},{18,... | collective-permute-start | bytes 589832 | tf_op jit(solution)/shard_map/ppermute | solution.py:344
  58.4 9.5 %collective-permute-start.11 = (bf16[1,192,512]{2,1,0:T(8,128)(2,1)S(1)}, bf16[1,192,512]{2,1,0:T(8,128)(2,1)S(1)}, u32[]{:S(2)}, u32[]{:S(2)}) collective-permute-start(bf16[1,192,512]{2,1,0:T(8,128)(2,1)S(1)} %get-tuple-element.77), channel_id=1, source_target_pairs={{0,6},{2,4},{4,2},{6,0},{8,14},{10,12},{12,10},{14,8},{16,22},{18,... | collective-permute-start | bytes 589832 | tf_op jit(solution)/shard_map/ppermute | solution.py:344
  59.6 2.8 %collective-permute-start.15 = (bf16[1,256,512]{2,1,0:T(8,128)(2,1)S(1)}, bf16[1,256,512]{2,1,0:T(8,128)(2,1)S(1)}, u32[]{:S(2)}, u32[]{:S(2)}) collective-permute-start(bf16[1,256,512]{2,1,0:T(8,128)(2,1)S(1)} %get-tuple-element.83), channel_id=1, source_target_pairs={{0,1},{1,0},{2,3},{3,2},{4,5},{5,4},{6,7},{7,6},{8,9},{9,8},{10,11... | collective-permute-start | bytes 786440 | tf_op jit(solution)/shard_map/ppermute | solution.py:344
  62.3 8.3 %collective-permute-start.16 = (bf16[1,256,512]{2,1,0:T(8,128)(2,1)S(1)}, bf16[1,256,512]{2,1,0:T(8,128)(2,1)S(1)}, u32[]{:S(2)}, u32[]{:S(2)}) collective-permute-start(bf16[1,256,512]{2,1,0:T(8,128)(2,1)S(1)} %get-tuple-element.89), channel_id=1, source_target_pairs={{0,1},{1,0},{2,3},{3,2},{4,5},{5,4},{6,7},{7,6},{8,9},{9,8},{10,11... | collective-permute-start | bytes 786440 | tf_op jit(solution)/shard_map/ppermute | solution.py:344
  62.5 9.6 %collective-permute-start.17 = (bf16[256,512]{1,0:T(8,128)(2,1)S(1)}, bf16[256,512]{1,0:T(8,128)(2,1)S(1)}, u32[]{:S(2)}, u32[]{:S(2)}) collective-permute-start(bf16[256,512]{1,0:T(8,128)(2,1)S(1)} %add_bitcast_fusion.1), channel_id=1, source_target_pairs={{0,8},{2,10},{4,12},{6,14},{8,0},{10,2},{12,4},{14,6},{16,24},{18,... | collective-permute-start | bytes 786440 | tf_op jit(solution)/shard_map/ppermute | solution.py:344
  68.5 5.3 %collective-permute-start.18 = (bf16[1,256,512]{2,1,0:T(8,128)(2,1)S(1)}, bf16[1,256,512]{2,1,0:T(8,128)(2,1)S(1)}, u32[]{:S(2)}, u32[]{:S(2)}) collective-permute-start(bf16[1,256,512]{2,1,0:T(8,128)(2,1)S(1)} %get-tuple-element.90), channel_id=1, source_target_pairs={{0,1},{1,0},{2,3},{3,2},{4,5},{5,4},{6,7},{7,6},{8,9},{9,8},{10,11... | collective-permute-start | bytes 786440 | tf_op jit(solution)/shard_map/ppermute | solution.py:344
  68.5 7.8 %collective-permute-start.6 = (bf16[1,192,512]{2,1,0:T(8,128)(2,1)S(1)}, bf16[1,192,512]{2,1,0:T(8,128)(2,1)S(1)}, u32[]{:S(2)}, u32[]{:S(2)}) collective-permute-start(bf16[1,192,512]{2,1,0:T(8,128)(2,1)S(1)} %get-tuple-element.70), channel_id=1, source_target_pairs={{0,2},{2,0},{4,6},{6,4},{8,10},{10,8},{12,14},{14,12},{16,18},{18,... | collective-permute-start | bytes 589832 | tf_op jit(solution)/shard_map/ppermute | solution.py:344
  69.5 9.9 %collective-permute-start.7 = (bf16[1,192,512]{2,1,0:T(8,128)(2,1)S(1)}, bf16[1,192,512]{2,1,0:T(8,128)(2,1)S(1)}, u32[]{:S(2)}, u32[]{:S(2)}) collective-permute-start(bf16[1,192,512]{2,1,0:T(8,128)(2,1)S(1)} %get-tuple-element.71), channel_id=1, source_target_pairs={{0,4},{2,6},{4,0},{6,2},{8,12},{10,14},{12,8},{14,10},{16,20},{18,... | collective-permute-start | bytes 589832 | tf_op jit(solution)/shard_map/ppermute | solution.py:344
  70.7 10.0 %collective-permute-start.8 = (bf16[1,192,512]{2,1,0:T(8,128)(2,1)S(1)}, bf16[1,192,512]{2,1,0:T(8,128)(2,1)S(1)}, u32[]{:S(2)}, u32[]{:S(2)}) collective-permute-start(bf16[1,192,512]{2,1,0:T(8,128)(2,1)S(1)} %get-tuple-element.72), channel_id=1, source_target_pairs={{0,6},{2,4},{4,2},{6,0},{8,14},{10,12},{12,10},{14,8},{16,22},{18,... | collective-permute-start | bytes 589832 | tf_op jit(solution)/shard_map/ppermute | solution.py:344
  72.2 14.4 %collective-permute-start.21 = (bf16[256,512]{1,0:T(8,128)(2,1)S(1)}, bf16[256,512]{1,0:T(8,128)(2,1)S(1)}, u32[]{:S(2)}, u32[]{:S(2)}) collective-permute-start(bf16[256,512]{1,0:T(8,128)(2,1)S(1)} %bitcast_add_fusion.1), channel_id=1, source_target_pairs={{0,16},{2,18},{4,20},{6,22},{8,24},{10,26},{12,28},{14,30},{16,0},... | collective-permute-start | bytes 786440 | tf_op jit(solution)/shard_map/ppermute | solution.py:344
  73.9 12.8 %collective-permute-start.20 = (bf16[256,512]{1,0:T(8,128)(2,1)S(1)}, bf16[256,512]{1,0:T(8,128)(2,1)S(1)}, u32[]{:S(2)}, u32[]{:S(2)}) collective-permute-start(bf16[256,512]{1,0:T(8,128)(2,1)S(1)} %add_bitcast_fusion), channel_id=1, source_target_pairs={{0,8},{2,10},{4,12},{6,14},{8,0},{10,2},{12,4},{14,6},{16,24},{18,... | collective-permute-start | bytes 786440 | tf_op jit(solution)/shard_map/ppermute | solution.py:344
  81.3 5.3 %collective-permute-start.19 = (bf16[1,256,512]{2,1,0:T(8,128)(2,1)S(1)}, bf16[1,256,512]{2,1,0:T(8,128)(2,1)S(1)}, u32[]{:S(2)}, u32[]{:S(2)}) collective-permute-start(bf16[1,256,512]{2,1,0:T(8,128)(2,1)S(1)} %get-tuple-element.96), channel_id=1, source_target_pairs={{0,1},{1,0},{2,3},{3,2},{4,5},{5,4},{6,7},{7,6},{8,9},{9,8},{10,11... | collective-permute-start | bytes 786440 | tf_op jit(solution)/shard_map/ppermute | solution.py:344
  89.4 5.0 %collective-permute-start.25 = (bf16[160,128]{1,0:T(8,128)(2,1)S(1)}, bf16[160,128]{1,0:T(8,128)(2,1)S(1)}, u32[]{:S(2)}, u32[]{:S(2)}) collective-permute-start(bf16[160,128]{1,0:T(8,128)(2,1)S(1)} %get-tuple-element.102), channel_id=1, source_target_pairs={{0,6},{2,4},{4,2},{6,0},{8,14},{10,12},{12,10},{14,8},{16,22},{18,... | collective-permute-start | bytes 122888 | tf_op jit(solution)/shard_map/ppermute | solution.py:344
  90.9 4.0 %collective-permute-start.24 = (bf16[160,128]{1,0:T(8,128)(2,1)S(1)}, bf16[160,128]{1,0:T(8,128)(2,1)S(1)}, u32[]{:S(2)}, u32[]{:S(2)}) collective-permute-start(bf16[160,128]{1,0:T(8,128)(2,1)S(1)} %get-tuple-element.103), channel_id=1, source_target_pairs={{0,4},{2,6},{4,0},{6,2},{8,12},{10,14},{12,8},{14,10},{16,20},{18,... | collective-permute-start | bytes 122888 | tf_op jit(solution)/shard_map/ppermute | solution.py:344
  91.8 4.0 %collective-permute-start.23 = (bf16[160,128]{1,0:T(8,128)(2,1)S(1)}, bf16[160,128]{1,0:T(8,128)(2,1)S(1)}, u32[]{:S(2)}, u32[]{:S(2)}) collective-permute-start(bf16[160,128]{1,0:T(8,128)(2,1)S(1)} %get-tuple-element.101), channel_id=1, source_target_pairs={{0,2},{2,0},{4,6},{6,4},{8,10},{10,8},{12,14},{14,12},{16,18},{18,... | collective-permute-start | bytes 122888 | tf_op jit(solution)/shard_map/ppermute | solution.py:344
  95.8 6.0 %collective-permute-start.28 = (bf16[160,128]{1,0:T(8,128)(2,1)S(1)}, bf16[160,128]{1,0:T(8,128)(2,1)S(1)}, u32[]{:S(2)}, u32[]{:S(2)}) collective-permute-start(bf16[160,128]{1,0:T(8,128)(2,1)S(1)} %add_convert_fusion.1), channel_id=1, source_target_pairs={{0,24},{2,26},{4,28},{6,30},{8,16},{10,18},{12,20},{14,22},{16,8},... | collective-permute-start | bytes 122888 | tf_op jit(solution)/shard_map/ppermute | solution.py:344
  98.5 4.9 %collective-permute-start.27 = (bf16[160,128]{1,0:T(8,128)(2,1)S(1)}, bf16[160,128]{1,0:T(8,128)(2,1)S(1)}, u32[]{:S(2)}, u32[]{:S(2)}) collective-permute-start(bf16[160,128]{1,0:T(8,128)(2,1)S(1)} %add_convert_fusion.1), channel_id=1, source_target_pairs={{0,16},{2,18},{4,20},{6,22},{8,24},{10,26},{12,28},{14,30},{16,0},... | collective-permute-start | bytes 122888 | tf_op jit(solution)/shard_map/ppermute | solution.py:344
  98.5 4.9 %collective-permute-start.26 = (bf16[160,128]{1,0:T(8,128)(2,1)S(1)}, bf16[160,128]{1,0:T(8,128)(2,1)S(1)}, u32[]{:S(2)}, u32[]{:S(2)}) collective-permute-start(bf16[160,128]{1,0:T(8,128)(2,1)S(1)} %add_convert_fusion.1), channel_id=1, source_target_pairs={{0,8},{2,10},{4,12},{6,14},{8,0},{10,2},{12,4},{14,6},{16,24},{18,... | collective-permute-start | bytes 122888 | tf_op jit(solution)/shard_map/ppermute | solution.py:344
  103.5 5.0 %collective-permute-start.31 = (bf16[160,128]{1,0:T(8,128)(2,1)S(1)}, bf16[160,128]{1,0:T(8,128)(2,1)S(1)}, u32[]{:S(2)}, u32[]{:S(2)}) collective-permute-start(bf16[160,128]{1,0:T(8,128)(2,1)S(1)} %add_convert_fusion), channel_id=1, source_target_pairs={{0,6},{2,4},{4,2},{6,0},{8,14},{10,12},{12,10},{14,8},{16,22},{18,... | collective-permute-start | bytes 122888 | tf_op jit(solution)/shard_map/ppermute | solution.py:344
  105.0 4.0 %collective-permute-start.30 = (bf16[160,128]{1,0:T(8,128)(2,1)S(1)}, bf16[160,128]{1,0:T(8,128)(2,1)S(1)}, u32[]{:S(2)}, u32[]{:S(2)}) collective-permute-start(bf16[160,128]{1,0:T(8,128)(2,1)S(1)} %add_convert_fusion), channel_id=1, source_target_pairs={{0,4},{2,6},{4,0},{6,2},{8,12},{10,14},{12,8},{14,10},{16,20},{18,... | collective-permute-start | bytes 122888 | tf_op jit(solution)/shard_map/ppermute | solution.py:344
  105.7 4.0 %collective-permute-start.29 = (bf16[160,128]{1,0:T(8,128)(2,1)S(1)}, bf16[160,128]{1,0:T(8,128)(2,1)S(1)}, u32[]{:S(2)}, u32[]{:S(2)}) collective-permute-start(bf16[160,128]{1,0:T(8,128)(2,1)S(1)} %add_convert_fusion), channel_id=1, source_target_pairs={{0,2},{2,0},{4,6},{6,4},{8,10},{10,8},{12,14},{14,12},{16,18},{18,... | collective-permute-start | bytes 122888 | tf_op jit(solution)/shard_map/ppermute | solution.py:344
  (6 other events, 26.4 us)

commit v9 on v8

--- a/solution.py
+++ b/solution.py
@@ -313,7 +313,8 @@
     mine = mine_ref[...]
     value = mine.astype(f32) + dot(jnp.concatenate([mine, mine], axis=1), jnp.concatenate([low, high], axis=0))
     square = dot3(gap, gap)
-    gap = 1.5 * square + dot3(square, gap)
+    part, rest = halves(square)
+    gap = 1.5 * square + dot(jnp.concatenate([rest, part], axis=1), jnp.concatenate([high, high], axis=0))
     for _ in range(root_steps - 3):
         high = gap.astype(bf16)
         value = value + dot(value.astype(bf16), high)

time: 117 us -> 116 us (level)
  no operation moved by 1% of the time
where the time goes in v9:
time: 116 us
  waiting for transfers between devices  46.7 us (40%)
  starting transfers between devices  42.4 us (37%)
  Pallas kernels  23.8 us (21%)
  local copies, waits for them, and re-layouts  2.25 us (2%)
    ppermute x33, waiting for transfers between devices, crossed(): lax.ppermute(value, axis, [(source, source ^ bits) for source in range(co...  46.7 us
    ppermute x33, starting transfers between devices, crossed(): lax.ppermute(value, axis, [(source, source ^ bits) for source in range(co...  33.9 us
    all_to_all x1, starting transfers between devices, local(): tiles = lax.all_to_all(send, 'dp', split_axis=0, concat_axis=0, tiled=True)  8.5 us
    pallas_call x1, Pallas kernels, pack(): pl.pallas_call(functools.partial(pack_kernel, per_dev, bound), out_shape=...  6.76 us
    pallas_call x4, Pallas kernels, product(): pl.pallas_call(functools.partial(product_kernel, bound, joint, groups, aw...  5.32 us
    pallas_call x1, Pallas kernels, whiten(): pl.pallas_call(functools.partial(root_kernel, samples), out_shape=jax.Sha...  4.82 us
    pallas_call x1, Pallas kernels, choose(): pl.pallas_call(functools.partial(choose_kernel, k_j, slots, inner), out_s...  3.72 us
  transfers between devices with their start and end apart: 34, of which 20 were waited for; matrix products, arithmetic and copies ran while one was open for 0% of the time, Pallas kernels for 9%

profile of v9, /device:TPU:0, one launch (start us, length us, event | category | flops | bytes accessed | tf_op | source)
XLA Modules:
  0.0 116.1 jit_solution(16110646253861500952)
XLA Ops:
  0.0 6.8 %pack.1 = (bf16[16,192,128]{2,1,0:T(8,128)(2,1)}, f32[8,512]{1,0:T(8,128)}) custom-call(s32[4,512]{1,0:T(4,128)} %bitcast.49, bf16[2048,128]{1,0:T(8,128)(2,1)} %bitcast.44), custom_call_target="tpu_custom_call" | custom-call | tf_op jit(solution)/shard_map/pack/pallas_call | solution.py:94
  6.8 8.5 %all-to-all-start = ((bf16[16,192,128]{2,1,0:T(8,128)(2,1)}), bf16[16,192,128]{2,1,0:T(8,128)(2,1)S(1)}, u32[]{:S(2)}, u32[]{:S(2)}) async-start(bf16[16,192,128]{2,1,0:T(8,128)(2,1)} %get-tuple-element.52), calls=%async_computation | async-start | bytes 1572864 | tf_op jit(solution)/shard_map/all_to_all | solution.py:434
  15.3 1.8 %collective-permute-start = (f32[8,512]{1,0:T(8,128)}, f32[8,512]{1,0:T(8,128)S(1)}, u32[]{:S(2)}, u32[]{:S(2)}) collective-permute-start(f32[8,512]{1,0:T(8,128)} %get-tuple-element.63.refs_0_), channel_id=1, source_target_pairs={{0,8},{2,10},{4,12},{6,14},{8,0},{10,2},{12,4},{14,6},{16,24},{18,... | collective-permute-start | bytes 49160 | tf_op jit(solution)/shard_map/ppermute | solution.py:345
  17.1 2.4 %collective-permute-start.1 = (f32[8,512]{1,0:T(8,128)}, f32[8,512]{1,0:T(8,128)S(1)}, u32[]{:S(2)}, u32[]{:S(2)}) collective-permute-start(f32[8,512]{1,0:T(8,128)} %get-tuple-element.63.refs_0_), channel_id=1, source_target_pairs={{0,16},{2,18},{4,20},{6,22},{8,24},{10,26},{12,28},{14,30},{16,0},... | collective-permute-start | bytes 49160 | tf_op jit(solution)/shard_map/ppermute | solution.py:345
  19.8 8.7 %collective-permute-done.refs_1_ = f32[8,512]{1,0:T(8,128)S(1)} collective-permute-done((f32[8,512]{1,0:T(8,128)}, f32[8,512]{1,0:T(8,128)S(1)}, u32[]{:S(2)}, u32[]{:S(2)}) %collective-permute-start) | collective-permute-done | bytes 16416 | tf_op jit(solution)/shard_map/ppermute | solution.py:345
  28.5 7.9 %collective-permute-done.1.refs_2_ = f32[8,512]{1,0:T(8,128)S(1)} collective-permute-done((f32[8,512]{1,0:T(8,128)}, f32[8,512]{1,0:T(8,128)S(1)}, u32[]{:S(2)}, u32[]{:S(2)}) %collective-permute-start.1) | collective-permute-done | bytes 16416 | tf_op jit(solution)/shard_map/ppermute | solution.py:345
  36.4 2.2 %copy-done = bf16[32,1,128,512]{3,2,1,0:T(8,128)(2,1)S(1)} copy-done((bf16[32,1,128,512]{3,2,1,0:T(8,128)(2,1)S(1)}, bf16[32,1,128,512]{3,2,1,0:T(8,128)(2,1)}, u32[]{:S(2)}) %copy-start) | copy-done | bytes 4194328
  39.9 1.5 %collective-permute-start.3 = (bf16[1,192,512]{2,1,0:T(8,128)(2,1)S(1)}, bf16[1,192,512]{2,1,0:T(8,128)(2,1)S(1)}, u32[]{:S(2)}, u32[]{:S(2)}) collective-permute-start(bf16[1,192,512]{2,1,0:T(8,128)(2,1)S(1)} %get-tuple-element.55), channel_id=1, source_target_pairs={{0,2},{2,0},{4,6},{6,4},{8,10},{10,8},{12,14},{14,12},{16,18},{18,... | collective-permute-start | bytes 589832 | tf_op jit(solution)/shard_map/ppermute | solution.py:345
  41.5 1.5 %collective-permute-start.4 = (bf16[1,192,512]{2,1,0:T(8,128)(2,1)S(1)}, bf16[1,192,512]{2,1,0:T(8,128)(2,1)S(1)}, u32[]{:S(2)}, u32[]{:S(2)}) collective-permute-start(bf16[1,192,512]{2,1,0:T(8,128)(2,1)S(1)} %get-tuple-element.56), channel_id=1, source_target_pairs={{0,4},{2,6},{4,0},{6,2},{8,12},{10,14},{12,8},{14,10},{16,20},{18,... | collective-permute-start | bytes 589832 | tf_op jit(solution)/shard_map/ppermute | solution.py:345
  44.8 1.5 %collective-permute-start.12 = (bf16[1,192,512]{2,1,0:T(8,128)(2,1)S(1)}, bf16[1,192,512]{2,1,0:T(8,128)(2,1)S(1)}, u32[]{:S(2)}, u32[]{:S(2)}) collective-permute-start(bf16[1,192,512]{2,1,0:T(8,128)(2,1)S(1)} %get-tuple-element.60), channel_id=1, source_target_pairs={{0,2},{2,0},{4,6},{6,4},{8,10},{10,8},{12,14},{14,12},{16,18},{18,... | collective-permute-start | bytes 589832 | tf_op jit(solution)/shard_map/ppermute | solution.py:345
  46.3 1.5 %collective-permute-start.13 = (bf16[1,192,512]{2,1,0:T(8,128)(2,1)S(1)}, bf16[1,192,512]{2,1,0:T(8,128)(2,1)S(1)}, u32[]{:S(2)}, u32[]{:S(2)}) collective-permute-start(bf16[1,192,512]{2,1,0:T(8,128)(2,1)S(1)} %get-tuple-element.61), channel_id=1, source_target_pairs={{0,4},{2,6},{4,0},{6,2},{8,12},{10,14},{12,8},{14,10},{16,20},{18,... | collective-permute-start | bytes 589832 | tf_op jit(solution)/shard_map/ppermute | solution.py:345
  47.8 3.7 %choose.1.hits_ref = bf16[4,512,768]{2,1,0:T(8,128)(2,1)S(1)} custom-call(s32[2]{0:T(128)S(1)} %pad_add_fusion.where_ref.place_ref, f32[8,512]{1,0:T(8,128)S(1)} %copy-done.2, f32[8,512]{1,0:T(8,128)S(1)} %collective-permute-done.refs_1_, f32[8,512]{1,0:T(8,128)S(1)} %collective-permute-done.1.refs_2_, f32[8,512]{1,0:T(8,128)S(1)} %collective-permute-done.2.refs_3_), custom_call_target="tpu_custom_call" | custom-call | flops 17179869184 | bytes 1 | tf_op jit(solution)/shard_map/choose/pallas_call | solution.py:180
  53.5 1.5 %collective-permute-start.9 = (bf16[1,192,512]{2,1,0:T(8,128)(2,1)S(1)}, bf16[1,192,512]{2,1,0:T(8,128)(2,1)S(1)}, u32[]{:S(2)}, u32[]{:S(2)}) collective-permute-start(bf16[1,192,512]{2,1,0:T(8,128)(2,1)S(1)} %get-tuple-element.75), channel_id=1, source_target_pairs={{0,2},{2,0},{4,6},{6,4},{8,10},{10,8},{12,14},{14,12},{16,18},{18,... | collective-permute-start | bytes 589832 | tf_op jit(solution)/shard_map/ppermute | solution.py:345
  55.0 1.5 %collective-permute-start.10 = (bf16[1,192,512]{2,1,0:T(8,128)(2,1)S(1)}, bf16[1,192,512]{2,1,0:T(8,128)(2,1)S(1)}, u32[]{:S(2)}, u32[]{:S(2)}) collective-permute-start(bf16[1,192,512]{2,1,0:T(8,128)(2,1)S(1)} %get-tuple-element.76), channel_id=1, source_target_pairs={{0,4},{2,6},{4,0},{6,2},{8,12},{10,14},{12,8},{14,10},{16,20},{18,... | collective-permute-start | bytes 589832 | tf_op jit(solution)/shard_map/ppermute | solution.py:345
  59.6 2.1 %collective-permute-done.14.refs_3_ = bf16[1,192,512]{2,1,0:T(8,128)(2,1)S(1)} collective-permute-done((bf16[1,192,512]{2,1,0:T(8,128)(2,1)S(1)}, bf16[1,192,512]{2,1,0:T(8,128)(2,1)S(1)}, u32[]{:S(2)}, u32[]{:S(2)}) %collective-permute-start.14) | collective-permute-done | bytes 196640 | tf_op jit(solution)/shard_map/ppermute | solution.py:345
  63.3 1.4 %collective-permute-done.9.refs_1_ = bf16[1,192,512]{2,1,0:T(8,128)(2,1)S(1)} collective-permute-done((bf16[1,192,512]{2,1,0:T(8,128)(2,1)S(1)}, bf16[1,192,512]{2,1,0:T(8,128)(2,1)S(1)}, u32[]{:S(2)}, u32[]{:S(2)}) %collective-permute-start.9) | collective-permute-done | bytes 196640 | tf_op jit(solution)/shard_map/ppermute | solution.py:345
  64.6 3.3 %collective-permute-done.10.refs_2_ = bf16[1,192,512]{2,1,0:T(8,128)(2,1)S(1)} collective-permute-done((bf16[1,192,512]{2,1,0:T(8,128)(2,1)S(1)}, bf16[1,192,512]{2,1,0:T(8,128)(2,1)S(1)}, u32[]{:S(2)}, u32[]{:S(2)}) %collective-permute-start.10) | collective-permute-done | bytes 196640 | tf_op jit(solution)/shard_map/ppermute | solution.py:345
  70.7 1.4 %collective-permute-start.8 = (bf16[1,192,512]{2,1,0:T(8,128)(2,1)S(1)}, bf16[1,192,512]{2,1,0:T(8,128)(2,1)S(1)}, u32[]{:S(2)}, u32[]{:S(2)}) collective-permute-start(bf16[1,192,512]{2,1,0:T(8,128)(2,1)S(1)} %get-tuple-element.72), channel_id=1, source_target_pairs={{0,6},{2,4},{4,2},{6,0},{8,14},{10,12},{12,10},{14,8},{16,22},{18,... | collective-permute-start | bytes 589832 | tf_op jit(solution)/shard_map/ppermute | solution.py:345
  72.2 1.5 %collective-permute-start.21 = (bf16[256,512]{1,0:T(8,128)(2,1)S(1)}, bf16[256,512]{1,0:T(8,128)(2,1)S(1)}, u32[]{:S(2)}, u32[]{:S(2)}) collective-permute-start(bf16[256,512]{1,0:T(8,128)(2,1)S(1)} %bitcast_add_fusion.1), channel_id=1, source_target_pairs={{0,16},{2,18},{4,20},{6,22},{8,24},{10,26},{12,28},{14,30},{16,0},... | collective-permute-start | bytes 786440 | tf_op jit(solution)/shard_map/ppermute | solution.py:345
  74.8 1.5 %collective-permute-done.6.refs_1_ = bf16[1,192,512]{2,1,0:T(8,128)(2,1)S(1)} collective-permute-done((bf16[1,192,512]{2,1,0:T(8,128)(2,1)S(1)}, bf16[1,192,512]{2,1,0:T(8,128)(2,1)S(1)}, u32[]{:S(2)}, u32[]{:S(2)}) %collective-permute-start.6) | collective-permute-done | bytes 196640 | tf_op jit(solution)/shard_map/ppermute | solution.py:345
  76.3 3.1 %collective-permute-done.7.refs_2_ = bf16[1,192,512]{2,1,0:T(8,128)(2,1)S(1)} collective-permute-done((bf16[1,192,512]{2,1,0:T(8,128)(2,1)S(1)}, bf16[1,192,512]{2,1,0:T(8,128)(2,1)S(1)}, u32[]{:S(2)}, u32[]{:S(2)}) %collective-permute-start.7) | collective-permute-done | bytes 196640 | tf_op jit(solution)/shard_map/ppermute | solution.py:345
  81.4 5.3 %collective-permute-done.21 = bf16[256,512]{1,0:T(8,128)(2,1)S(1)} collective-permute-done((bf16[256,512]{1,0:T(8,128)(2,1)S(1)}, bf16[256,512]{1,0:T(8,128)(2,1)S(1)}, u32[]{:S(2)}, u32[]{:S(2)}) %collective-permute-start.21) | collective-permute-done | bytes 262176 | tf_op jit(solution)/shard_map/ppermute | solution.py:345
  86.9 1.5 %collective-permute-done.22 = bf16[256,512]{1,0:T(8,128)(2,1)S(1)} collective-permute-done((bf16[256,512]{1,0:T(8,128)(2,1)S(1)}, bf16[256,512]{1,0:T(8,128)(2,1)S(1)}, u32[]{:S(2)}, u32[]{:S(2)}) %collective-permute-start.22) | collective-permute-done | bytes 262176 | tf_op jit(solution)/shard_map/ppermute | solution.py:345
  89.4 1.6 %collective-permute-start.25 = (bf16[160,128]{1,0:T(8,128)(2,1)S(1)}, bf16[160,128]{1,0:T(8,128)(2,1)S(1)}, u32[]{:S(2)}, u32[]{:S(2)}) collective-permute-start(bf16[160,128]{1,0:T(8,128)(2,1)S(1)} %get-tuple-element.102), channel_id=1, source_target_pairs={{0,6},{2,4},{4,2},{6,0},{8,14},{10,12},{12,10},{14,8},{16,22},{18,... | collective-permute-start | bytes 122888 | tf_op jit(solution)/shard_map/ppermute | solution.py:345
  92.9 1.5 %collective-permute-done.25 = bf16[160,128]{1,0:T(8,128)(2,1)S(1)} collective-permute-done((bf16[160,128]{1,0:T(8,128)(2,1)S(1)}, bf16[160,128]{1,0:T(8,128)(2,1)S(1)}, u32[]{:S(2)}, u32[]{:S(2)}) %collective-permute-start.25) | collective-permute-done | bytes 40992 | tf_op jit(solution)/shard_map/ppermute | solution.py:345
  95.8 2.7 %collective-permute-start.28 = (bf16[160,128]{1,0:T(8,128)(2,1)S(1)}, bf16[160,128]{1,0:T(8,128)(2,1)S(1)}, u32[]{:S(2)}, u32[]{:S(2)}) collective-permute-start(bf16[160,128]{1,0:T(8,128)(2,1)S(1)} %add_convert_fusion.1), channel_id=1, source_target_pairs={{0,24},{2,26},{4,28},{6,30},{8,16},{10,18},{12,20},{14,22},{16,8},... | collective-permute-start | bytes 122888 | tf_op jit(solution)/shard_map/ppermute | solution.py:345
  98.5 1.8 %collective-permute-start.26 = (bf16[160,128]{1,0:T(8,128)(2,1)S(1)}, bf16[160,128]{1,0:T(8,128)(2,1)S(1)}, u32[]{:S(2)}, u32[]{:S(2)}) collective-permute-start(bf16[160,128]{1,0:T(8,128)(2,1)S(1)} %add_convert_fusion.1), channel_id=1, source_target_pairs={{0,8},{2,10},{4,12},{6,14},{8,0},{10,2},{12,4},{14,6},{16,24},{18,... | collective-permute-start | bytes 122888 | tf_op jit(solution)/shard_map/ppermute | solution.py:345
  100.3 1.5 %collective-permute-done.28 = bf16[160,128]{1,0:T(8,128)(2,1)S(1)} collective-permute-done((bf16[160,128]{1,0:T(8,128)(2,1)S(1)}, bf16[160,128]{1,0:T(8,128)(2,1)S(1)}, u32[]{:S(2)}, u32[]{:S(2)}) %collective-permute-start.28) | collective-permute-done | bytes 40992 | tf_op jit(solution)/shard_map/ppermute | solution.py:345
  101.8 1.6 %collective-permute-done.27 = bf16[160,128]{1,0:T(8,128)(2,1)S(1)} collective-permute-done((bf16[160,128]{1,0:T(8,128)(2,1)S(1)}, bf16[160,128]{1,0:T(8,128)(2,1)S(1)}, u32[]{:S(2)}, u32[]{:S(2)}) %collective-permute-start.27) | collective-permute-done | bytes 40992 | tf_op jit(solution)/shard_map/ppermute | solution.py:345
  103.5 1.6 %collective-permute-start.31 = (bf16[160,128]{1,0:T(8,128)(2,1)S(1)}, bf16[160,128]{1,0:T(8,128)(2,1)S(1)}, u32[]{:S(2)}, u32[]{:S(2)}) collective-permute-start(bf16[160,128]{1,0:T(8,128)(2,1)S(1)} %add_convert_fusion), channel_id=1, source_target_pairs={{0,6},{2,4},{4,2},{6,0},{8,14},{10,12},{12,10},{14,8},{16,22},{18,... | collective-permute-start | bytes 122888 | tf_op jit(solution)/shard_map/ppermute | solution.py:345
  107.0 1.4 %collective-permute-done.31 = bf16[160,128]{1,0:T(8,128)(2,1)S(1)} collective-permute-done((bf16[160,128]{1,0:T(8,128)(2,1)S(1)}, bf16[160,128]{1,0:T(8,128)(2,1)S(1)}, u32[]{:S(2)}, u32[]{:S(2)}) %collective-permute-start.31) | collective-permute-done | bytes 40992 | tf_op jit(solution)/shard_map/ppermute | solution.py:345
  111.2 4.8 %root.1 = f32[256,512]{1,0:T(8,128)} custom-call(s32[1]{0:T(128)} %bitcast.feat_ref.place_ref, bf16[5,128,128]{2,1,0:T(8,128)(2,1)S(1)} %bitcast.39, bf16[5,128,128]{2,1,0:T(8,128)(2,1)S(1)} %collective-permute-done.32.other_gram_ref, bf16[256,512]{1,0:T(8,128)(2,1)S(1)} %fusion.1.mine_ref), custom_call_target="tpu_custom_call" | custom-call | tf_op jit(solution)/shard_map/root/pallas_call | solution.py:332
  (69 shorter events, 25.5 us)
Async XLA Ops:
  6.8 29.6 %all-to-all-start = ((bf16[16,192,128]{2,1,0:T(8,128)(2,1)}), bf16[16,192,128]{2,1,0:T(8,128)(2,1)S(1)}, u32[]{:S(2)}, u32[]{:S(2)}) async-start(bf16[16,192,128]{2,1,0:T(8,128)(2,1)} %get-tuple-element.52), calls=%async_computation | async-start | bytes 1572864 | tf_op jit(solution)/shard_map/all_to_all | solution.py:434
  15.3 13.2 %collective-permute-start = (f32[8,512]{1,0:T(8,128)}, f32[8,512]{1,0:T(8,128)S(1)}, u32[]{:S(2)}, u32[]{:S(2)}) collective-permute-start(f32[8,512]{1,0:T(8,128)} %get-tuple-element.63.refs_0_), channel_id=1, source_target_pairs={{0,8},{2,10},{4,12},{6,14},{8,0},{10,2},{12,4},{14,6},{16,24},{18,... | collective-permute-start | bytes 49160 | tf_op jit(solution)/shard_map/ppermute | solution.py:345
  17.1 19.3 %collective-permute-start.1 = (f32[8,512]{1,0:T(8,128)}, f32[8,512]{1,0:T(8,128)S(1)}, u32[]{:S(2)}, u32[]{:S(2)}) collective-permute-start(f32[8,512]{1,0:T(8,128)} %get-tuple-element.63.refs_0_), channel_id=1, source_target_pairs={{0,16},{2,18},{4,20},{6,22},{8,24},{10,26},{12,28},{14,30},{16,0},... | collective-permute-start | bytes 49160 | tf_op jit(solution)/shard_map/ppermute | solution.py:345
  19.5 16.9 %collective-permute-start.2 = (f32[8,512]{1,0:T(8,128)}, f32[8,512]{1,0:T(8,128)S(1)}, u32[]{:S(2)}, u32[]{:S(2)}) collective-permute-start(f32[8,512]{1,0:T(8,128)} %get-tuple-element.63.refs_0_), channel_id=1, source_target_pairs={{0,24},{2,26},{4,28},{6,30},{8,16},{10,18},{12,20},{14,22},{16,8},... | collective-permute-start | bytes 49160 | tf_op jit(solution)/shard_map/ppermute | solution.py:345
  39.9 13.0 %collective-permute-start.3 = (bf16[1,192,512]{2,1,0:T(8,128)(2,1)S(1)}, bf16[1,192,512]{2,1,0:T(8,128)(2,1)S(1)}, u32[]{:S(2)}, u32[]{:S(2)}) collective-permute-start(bf16[1,192,512]{2,1,0:T(8,128)(2,1)S(1)} %get-tuple-element.55), channel_id=1, source_target_pairs={{0,2},{2,0},{4,6},{6,4},{8,10},{10,8},{12,14},{14,12},{16,18},{18,... | collective-permute-start | bytes 589832 | tf_op jit(solution)/shard_map/ppermute | solution.py:345
  41.5 12.1 %collective-permute-start.4 = (bf16[1,192,512]{2,1,0:T(8,128)(2,1)S(1)}, bf16[1,192,512]{2,1,0:T(8,128)(2,1)S(1)}, u32[]{:S(2)}, u32[]{:S(2)}) collective-permute-start(bf16[1,192,512]{2,1,0:T(8,128)(2,1)S(1)} %get-tuple-element.56), channel_id=1, source_target_pairs={{0,4},{2,6},{4,0},{6,2},{8,12},{10,14},{12,8},{14,10},{16,20},{18,... | collective-permute-start | bytes 589832 | tf_op jit(solution)/shard_map/ppermute | solution.py:345
  42.9 12.1 %collective-permute-start.5 = (bf16[1,192,512]{2,1,0:T(8,128)(2,1)S(1)}, bf16[1,192,512]{2,1,0:T(8,128)(2,1)S(1)}, u32[]{:S(2)}, u32[]{:S(2)}) collective-permute-start(bf16[1,192,512]{2,1,0:T(8,128)(2,1)S(1)} %get-tuple-element.57), channel_id=1, source_target_pairs={{0,6},{2,4},{4,2},{6,0},{8,14},{10,12},{12,10},{14,8},{16,22},{18,... | collective-permute-start | bytes 589832 | tf_op jit(solution)/shard_map/ppermute | solution.py:345
  44.8 13.6 %collective-permute-start.12 = (bf16[1,192,512]{2,1,0:T(8,128)(2,1)S(1)}, bf16[1,192,512]{2,1,0:T(8,128)(2,1)S(1)}, u32[]{:S(2)}, u32[]{:S(2)}) collective-permute-start(bf16[1,192,512]{2,1,0:T(8,128)(2,1)S(1)} %get-tuple-element.60), channel_id=1, source_target_pairs={{0,2},{2,0},{4,6},{6,4},{8,10},{10,8},{12,14},{14,12},{16,18},{18,... | collective-permute-start | bytes 589832 | tf_op jit(solution)/shard_map/ppermute | solution.py:345
  46.3 13.3 %collective-permute-start.13 = (bf16[1,192,512]{2,1,0:T(8,128)(2,1)S(1)}, bf16[1,192,512]{2,1,0:T(8,128)(2,1)S(1)}, u32[]{:S(2)}, u32[]{:S(2)}) collective-permute-start(bf16[1,192,512]{2,1,0:T(8,128)(2,1)S(1)} %get-tuple-element.61), channel_id=1, source_target_pairs={{0,4},{2,6},{4,0},{6,2},{8,12},{10,14},{12,8},{14,10},{16,20},{18,... | collective-permute-start | bytes 589832 | tf_op jit(solution)/shard_map/ppermute | solution.py:345
  52.9 8.9 %collective-permute-start.14 = (bf16[1,192,512]{2,1,0:T(8,128)(2,1)S(1)}, bf16[1,192,512]{2,1,0:T(8,128)(2,1)S(1)}, u32[]{:S(2)}, u32[]{:S(2)}) collective-permute-start(bf16[1,192,512]{2,1,0:T(8,128)(2,1)S(1)} %get-tuple-element.62), channel_id=1, source_target_pairs={{0,6},{2,4},{4,2},{6,0},{8,14},{10,12},{12,10},{14,8},{16,22},{18,... | collective-permute-start | bytes 589832 | tf_op jit(solution)/shard_map/ppermute | solution.py:345
  53.5 11.1 %collective-permute-start.9 = (bf16[1,192,512]{2,1,0:T(8,128)(2,1)S(1)}, bf16[1,192,512]{2,1,0:T(8,128)(2,1)S(1)}, u32[]{:S(2)}, u32[]{:S(2)}) collective-permute-start(bf16[1,192,512]{2,1,0:T(8,128)(2,1)S(1)} %get-tuple-element.75), channel_id=1, source_target_pairs={{0,2},{2,0},{4,6},{6,4},{8,10},{10,8},{12,14},{14,12},{16,18},{18,... | collective-permute-start | bytes 589832 | tf_op jit(solution)/shard_map/ppermute | solution.py:345
  55.0 12.9 %collective-permute-start.10 = (bf16[1,192,512]{2,1,0:T(8,128)(2,1)S(1)}, bf16[1,192,512]{2,1,0:T(8,128)(2,1)S(1)}, u32[]{:S(2)}, u32[]{:S(2)}) collective-permute-start(bf16[1,192,512]{2,1,0:T(8,128)(2,1)S(1)} %get-tuple-element.76), channel_id=1, source_target_pairs={{0,4},{2,6},{4,0},{6,2},{8,12},{10,14},{12,8},{14,10},{16,20},{18,... | collective-permute-start | bytes 589832 | tf_op jit(solution)/shard_map/ppermute | solution.py:345
  58.4 9.5 %collective-permute-start.11 = (bf16[1,192,512]{2,1,0:T(8,128)(2,1)S(1)}, bf16[1,192,512]{2,1,0:T(8,128)(2,1)S(1)}, u32[]{:S(2)}, u32[]{:S(2)}) collective-permute-start(bf16[1,192,512]{2,1,0:T(8,128)(2,1)S(1)} %get-tuple-element.77), channel_id=1, source_target_pairs={{0,6},{2,4},{4,2},{6,0},{8,14},{10,12},{12,10},{14,8},{16,22},{18,... | collective-permute-start | bytes 589832 | tf_op jit(solution)/shard_map/ppermute | solution.py:345
  59.6 2.8 %collective-permute-start.15 = (bf16[1,256,512]{2,1,0:T(8,128)(2,1)S(1)}, bf16[1,256,512]{2,1,0:T(8,128)(2,1)S(1)}, u32[]{:S(2)}, u32[]{:S(2)}) collective-permute-start(bf16[1,256,512]{2,1,0:T(8,128)(2,1)S(1)} %get-tuple-element.83), channel_id=1, source_target_pairs={{0,1},{1,0},{2,3},{3,2},{4,5},{5,4},{6,7},{7,6},{8,9},{9,8},{10,11... | collective-permute-start | bytes 786440 | tf_op jit(solution)/shard_map/ppermute | solution.py:345
  62.3 8.3 %collective-permute-start.16 = (bf16[1,256,512]{2,1,0:T(8,128)(2,1)S(1)}, bf16[1,256,512]{2,1,0:T(8,128)(2,1)S(1)}, u32[]{:S(2)}, u32[]{:S(2)}) collective-permute-start(bf16[1,256,512]{2,1,0:T(8,128)(2,1)S(1)} %get-tuple-element.89), channel_id=1, source_target_pairs={{0,1},{1,0},{2,3},{3,2},{4,5},{5,4},{6,7},{7,6},{8,9},{9,8},{10,11... | collective-permute-start | bytes 786440 | tf_op jit(solution)/shard_map/ppermute | solution.py:345
  62.5 9.6 %collective-permute-start.17 = (bf16[256,512]{1,0:T(8,128)(2,1)S(1)}, bf16[256,512]{1,0:T(8,128)(2,1)S(1)}, u32[]{:S(2)}, u32[]{:S(2)}) collective-permute-start(bf16[256,512]{1,0:T(8,128)(2,1)S(1)} %add_bitcast_fusion.1), channel_id=1, source_target_pairs={{0,8},{2,10},{4,12},{6,14},{8,0},{10,2},{12,4},{14,6},{16,24},{18,... | collective-permute-start | bytes 786440 | tf_op jit(solution)/shard_map/ppermute | solution.py:345
  68.5 5.3 %collective-permute-start.18 = (bf16[1,256,512]{2,1,0:T(8,128)(2,1)S(1)}, bf16[1,256,512]{2,1,0:T(8,128)(2,1)S(1)}, u32[]{:S(2)}, u32[]{:S(2)}) collective-permute-start(bf16[1,256,512]{2,1,0:T(8,128)(2,1)S(1)} %get-tuple-element.90), channel_id=1, source_target_pairs={{0,1},{1,0},{2,3},{3,2},{4,5},{5,4},{6,7},{7,6},{8,9},{9,8},{10,11... | collective-permute-start | bytes 786440 | tf_op jit(solution)/shard_map/ppermute | solution.py:345
  68.5 7.8 %collective-permute-start.6 = (bf16[1,192,512]{2,1,0:T(8,128)(2,1)S(1)}, bf16[1,192,512]{2,1,0:T(8,128)(2,1)S(1)}, u32[]{:S(2)}, u32[]{:S(2)}) collective-permute-start(bf16[1,192,512]{2,1,0:T(8,128)(2,1)S(1)} %get-tuple-element.70), channel_id=1, source_target_pairs={{0,2},{2,0},{4,6},{6,4},{8,10},{10,8},{12,14},{14,12},{16,18},{18,... | collective-permute-start | bytes 589832 | tf_op jit(solution)/shard_map/ppermute | solution.py:345
  69.5 9.9 %collective-permute-start.7 = (bf16[1,192,512]{2,1,0:T(8,128)(2,1)S(1)}, bf16[1,192,512]{2,1,0:T(8,128)(2,1)S(1)}, u32[]{:S(2)}, u32[]{:S(2)}) collective-permute-start(bf16[1,192,512]{2,1,0:T(8,128)(2,1)S(1)} %get-tuple-element.71), channel_id=1, source_target_pairs={{0,4},{2,6},{4,0},{6,2},{8,12},{10,14},{12,8},{14,10},{16,20},{18,... | collective-permute-start | bytes 589832 | tf_op jit(solution)/shard_map/ppermute | solution.py:345
  70.7 10.0 %collective-permute-start.8 = (bf16[1,192,512]{2,1,0:T(8,128)(2,1)S(1)}, bf16[1,192,512]{2,1,0:T(8,128)(2,1)S(1)}, u32[]{:S(2)}, u32[]{:S(2)}) collective-permute-start(bf16[1,192,512]{2,1,0:T(8,128)(2,1)S(1)} %get-tuple-element.72), channel_id=1, source_target_pairs={{0,6},{2,4},{4,2},{6,0},{8,14},{10,12},{12,10},{14,8},{16,22},{18,... | collective-permute-start | bytes 589832 | tf_op jit(solution)/shard_map/ppermute | solution.py:345
  72.2 14.4 %collective-permute-start.21 = (bf16[256,512]{1,0:T(8,128)(2,1)S(1)}, bf16[256,512]{1,0:T(8,128)(2,1)S(1)}, u32[]{:S(2)}, u32[]{:S(2)}) collective-permute-start(bf16[256,512]{1,0:T(8,128)(2,1)S(1)} %bitcast_add_fusion.1), channel_id=1, source_target_pairs={{0,16},{2,18},{4,20},{6,22},{8,24},{10,26},{12,28},{14,30},{16,0},... | collective-permute-start | bytes 786440 | tf_op jit(solution)/shard_map/ppermute | solution.py:345
  73.9 12.8 %collective-permute-start.20 = (bf16[256,512]{1,0:T(8,128)(2,1)S(1)}, bf16[256,512]{1,0:T(8,128)(2,1)S(1)}, u32[]{:S(2)}, u32[]{:S(2)}) collective-permute-start(bf16[256,512]{1,0:T(8,128)(2,1)S(1)} %add_bitcast_fusion), channel_id=1, source_target_pairs={{0,8},{2,10},{4,12},{6,14},{8,0},{10,2},{12,4},{14,6},{16,24},{18,... | collective-permute-start | bytes 786440 | tf_op jit(solution)/shard_map/ppermute | solution.py:345
  81.3 5.3 %collective-permute-start.19 = (bf16[1,256,512]{2,1,0:T(8,128)(2,1)S(1)}, bf16[1,256,512]{2,1,0:T(8,128)(2,1)S(1)}, u32[]{:S(2)}, u32[]{:S(2)}) collective-permute-start(bf16[1,256,512]{2,1,0:T(8,128)(2,1)S(1)} %get-tuple-element.96), channel_id=1, source_target_pairs={{0,1},{1,0},{2,3},{3,2},{4,5},{5,4},{6,7},{7,6},{8,9},{9,8},{10,11... | collective-permute-start | bytes 786440 | tf_op jit(solution)/shard_map/ppermute | solution.py:345
  89.4 5.0 %collective-permute-start.25 = (bf16[160,128]{1,0:T(8,128)(2,1)S(1)}, bf16[160,128]{1,0:T(8,128)(2,1)S(1)}, u32[]{:S(2)}, u32[]{:S(2)}) collective-permute-start(bf16[160,128]{1,0:T(8,128)(2,1)S(1)} %get-tuple-element.102), channel_id=1, source_target_pairs={{0,6},{2,4},{4,2},{6,0},{8,14},{10,12},{12,10},{14,8},{16,22},{18,... | collective-permute-start | bytes 122888 | tf_op jit(solution)/shard_map/ppermute | solution.py:345
  90.9 4.0 %collective-permute-start.24 = (bf16[160,128]{1,0:T(8,128)(2,1)S(1)}, bf16[160,128]{1,0:T(8,128)(2,1)S(1)}, u32[]{:S(2)}, u32[]{:S(2)}) collective-permute-start(bf16[160,128]{1,0:T(8,128)(2,1)S(1)} %get-tuple-element.103), channel_id=1, source_target_pairs={{0,4},{2,6},{4,0},{6,2},{8,12},{10,14},{12,8},{14,10},{16,20},{18,... | collective-permute-start | bytes 122888 | tf_op jit(solution)/shard_map/ppermute | solution.py:345
  91.8 4.0 %collective-permute-start.23 = (bf16[160,128]{1,0:T(8,128)(2,1)S(1)}, bf16[160,128]{1,0:T(8,128)(2,1)S(1)}, u32[]{:S(2)}, u32[]{:S(2)}) collective-permute-start(bf16[160,128]{1,0:T(8,128)(2,1)S(1)} %get-tuple-element.101), channel_id=1, source_target_pairs={{0,2},{2,0},{4,6},{6,4},{8,10},{10,8},{12,14},{14,12},{16,18},{18,... | collective-permute-start | bytes 122888 | tf_op jit(solution)/shard_map/ppermute | solution.py:345
  95.8 6.0 %collective-permute-start.28 = (bf16[160,128]{1,0:T(8,128)(2,1)S(1)}, bf16[160,128]{1,0:T(8,128)(2,1)S(1)}, u32[]{:S(2)}, u32[]{:S(2)}) collective-permute-start(bf16[160,128]{1,0:T(8,128)(2,1)S(1)} %add_convert_fusion.1), channel_id=1, source_target_pairs={{0,24},{2,26},{4,28},{6,30},{8,16},{10,18},{12,20},{14,22},{16,8},... | collective-permute-start | bytes 122888 | tf_op jit(solution)/shard_map/ppermute | solution.py:345
  98.5 4.9 %collective-permute-start.27 = (bf16[160,128]{1,0:T(8,128)(2,1)S(1)}, bf16[160,128]{1,0:T(8,128)(2,1)S(1)}, u32[]{:S(2)}, u32[]{:S(2)}) collective-permute-start(bf16[160,128]{1,0:T(8,128)(2,1)S(1)} %add_convert_fusion.1), channel_id=1, source_target_pairs={{0,16},{2,18},{4,20},{6,22},{8,24},{10,26},{12,28},{14,30},{16,0},... | collective-permute-start | bytes 122888 | tf_op jit(solution)/shard_map/ppermute | solution.py:345
  98.5 4.9 %collective-permute-start.26 = (bf16[160,128]{1,0:T(8,128)(2,1)S(1)}, bf16[160,128]{1,0:T(8,128)(2,1)S(1)}, u32[]{:S(2)}, u32[]{:S(2)}) collective-permute-start(bf16[160,128]{1,0:T(8,128)(2,1)S(1)} %add_convert_fusion.1), channel_id=1, source_target_pairs={{0,8},{2,10},{4,12},{6,14},{8,0},{10,2},{12,4},{14,6},{16,24},{18,... | collective-permute-start | bytes 122888 | tf_op jit(solution)/shard_map/ppermute | solution.py:345
  103.5 5.0 %collective-permute-start.31 = (bf16[160,128]{1,0:T(8,128)(2,1)S(1)}, bf16[160,128]{1,0:T(8,128)(2,1)S(1)}, u32[]{:S(2)}, u32[]{:S(2)}) collective-permute-start(bf16[160,128]{1,0:T(8,128)(2,1)S(1)} %add_convert_fusion), channel_id=1, source_target_pairs={{0,6},{2,4},{4,2},{6,0},{8,14},{10,12},{12,10},{14,8},{16,22},{18,... | collective-permute-start | bytes 122888 | tf_op jit(solution)/shard_map/ppermute | solution.py:345
  105.0 4.0 %collective-permute-start.30 = (bf16[160,128]{1,0:T(8,128)(2,1)S(1)}, bf16[160,128]{1,0:T(8,128)(2,1)S(1)}, u32[]{:S(2)}, u32[]{:S(2)}) collective-permute-start(bf16[160,128]{1,0:T(8,128)(2,1)S(1)} %add_convert_fusion), channel_id=1, source_target_pairs={{0,4},{2,6},{4,0},{6,2},{8,12},{10,14},{12,8},{14,10},{16,20},{18,... | collective-permute-start | bytes 122888 | tf_op jit(solution)/shard_map/ppermute | solution.py:345
  105.7 4.0 %collective-permute-start.29 = (bf16[160,128]{1,0:T(8,128)(2,1)S(1)}, bf16[160,128]{1,0:T(8,128)(2,1)S(1)}, u32[]{:S(2)}, u32[]{:S(2)}) collective-permute-start(bf16[160,128]{1,0:T(8,128)(2,1)S(1)} %add_convert_fusion), channel_id=1, source_target_pairs={{0,2},{2,0},{4,6},{6,4},{8,10},{10,8},{12,14},{14,12},{16,18},{18,... | collective-permute-start | bytes 122888 | tf_op jit(solution)/shard_map/ppermute | solution.py:345
  (6 other events, 26.4 us)
